TPU v7x, 128 devices: a whole 4x4x4 slice. The times are simulated.
128 devices in a mesh: ctx: 16 (over z_hi, y, core), exp: 8 (over z_lo, x).
Axes of the slice: x: 4, y: 4, z: 4 (z_hi: 2, z_lo: 2; z = z_hi * 2 + z_lo), core: 2. Of those that a mesh axis runs over, the one named last changes fastest.
Arguments:
- tokens: bfloat16 [8, 3072, 1024], P('exp', 'ctx'), may hold values from -40 to 40
- cotangent: bfloat16 [8, 3072, 1024], P('exp', 'ctx'), may hold values from -6 to 6
- lengths: int32 [8, 4], P('exp'), may hold values from 1 to 2048, 3072 in all within a row
- deal_perm: int32 [8, 16, 16], P('exp'), may hold values from 0 to 15, each once within a row
- routes: int32 [8, 3072, 8], P('exp', 'ctx'), may hold values from 0 to 31, all different within a row; in each aligned block of 192 rows (0 to 191, 192 to 383, ..., all dimensions but the last counted through in order) at most 72 rows name the same one
- gate_logits: float32 [8, 3072, 8], P('exp', 'ctx'), may hold values from -2.5 to 2.5
- norm_attn: bfloat16 [1024], P('exp'), may hold values from 0.25 to 1.75
- norm_query: bfloat16 [1024], P('exp'), may hold values from 0.25 to 1.75
- norm_key: bfloat16 [512], P('exp'), may hold values from 0.25 to 1.75
- norm_ffn: bfloat16 [1024], P('exp'), may hold values from 0.25 to 1.75
- w_query: bfloat16 [1024, 1024], P('exp'), may hold values from -0.1875 to 0.1875
- w_key: bfloat16 [1024, 512], P('exp'), may hold values from -0.1875 to 0.1875
- w_value: bfloat16 [1024, 512], P('exp'), may hold values from -0.1875 to 0.1875
- w_out: bfloat16 [1024, 1024], P('exp'), may hold values from -1.5 to 1.5
- w_gate: bfloat16 [32, 1024, 512], P('exp'), may hold values from -0.1875 to 0.1875
- w_up: bfloat16 [32, 1024, 512], P('exp'), may hold values from -0.1875 to 0.1875
- w_down: bfloat16 [32, 512, 1024], P('exp'), may hold values from -1 to 1
Outputs:
- layer_out: bfloat16 [8, 3072, 1024], P('exp', 'ctx')
- input_grad: float32 [8, 3072, 1024], P('exp', 'ctx')
- w_query_grad: float32 [1024, 1024], P('exp')
- w_key_grad: float32 [1024, 512], P('exp')
- w_value_grad: float32 [1024, 512], P('exp')
- w_out_grad: float32 [1024, 1024], P('exp')
- norm_attn_grad: float32 [1024], P('exp')
- norm_query_grad: float32 [1024], P('exp')
- norm_key_grad: float32 [512], P('exp')
- norm_ffn_grad: float32 [1024], P('exp')
- w_gate_grad: float32 [32, 1024, 512], P('exp', 'ctx')
- w_up_grad: float32 [32, 1024, 512], P('exp', 'ctx')
- w_down_grad: float32 [32, 512, 1024], P('exp', 'ctx')
Inputs may be any that keep to these rules, and one draw needn't show every extreme that they name: Each group's 4 lengths sum to 3072; the longest is exactly 2048. Each deal_perm[g, j] is a permutation of the 16 indices. `routes`: A row names 8 different experts; among the 192 rows of one device no expert is named more than 72 times, a bound that some block reaches.
All inputs are finite; a program needn't handle non-finite values.
Results may differ from a plain program's by a relative error of at most 0.029.
Values may be sent and summed in bfloat16 or wider, within the bound.
A program may use at most 320 MiB of HBM per device.

v0:
```python
import jax
import jax.numpy as jnp
from jax import lax
from jax.sharding import PartitionSpec as P

HEADS = 16
KV_HEADS = 8


EPSILON = 1e-05
ROPE_BASE = 10000.0
MASKED = -1e30


def norm_forward(values, norm_gain):
    inv_scale = lax.rsqrt(jnp.mean(values * values, axis=-1, keepdims=True) + EPSILON)
    return (values * inv_scale * norm_gain, inv_scale)


def norm_backward(values, inv_scale, norm_gain, incoming):
    weighted = incoming * norm_gain
    gain_grad = jnp.sum(incoming * values * inv_scale, axis=0)
    inner = jnp.mean(weighted * values, axis=-1, keepdims=True)
    return (inv_scale * weighted - values * (inv_scale * inv_scale * inv_scale) * inner, gain_grad)


def rotate(values, offsets, head_count, direction):
    row_total = values.shape[0]
    head_width = values.shape[1] // head_count
    half_width = head_width // 2
    shaped = values.reshape(row_total, head_count, head_width)
    inverse_freq = ROPE_BASE ** (-jnp.arange(half_width).astype(jnp.float32) * 2.0 / head_width)
    angles = offsets.astype(jnp.float32)[:, None] * inverse_freq[None, :]
    cosine = jnp.cos(angles)[:, None, :]
    sine_part = direction * jnp.sin(angles)[:, None, :]
    first_half = shaped[..., :half_width]
    second_half = shaped[..., half_width:]
    turned = jnp.concatenate(
        [
            first_half * cosine - second_half * sine_part,
            second_half * cosine + first_half * sine_part,
        ],
        axis=-1,
    )
    return turned.reshape(row_total, head_count * head_width)


def documents(positions, seq_lengths):
    seq_ends = jnp.cumsum(seq_lengths)
    seq_starts = seq_ends - seq_lengths
    doc_index = jnp.sum((positions[:, None] >= seq_ends[None, :]).astype(jnp.int32), axis=1)
    inside = (positions[:, None] >= seq_starts[None, :]) & (positions[:, None] < seq_ends[None, :])
    offsets = positions - jnp.sum(jnp.where(inside, seq_starts[None, :], 0), axis=1)
    return (doc_index, offsets)


def contract_rows(left_side, right_side):
    return lax.dot_general(
        left_side, right_side, (((0,), (0,)), ((), ())), preferred_element_type=jnp.float32
    )


def contract_cols(left_side, right_side):
    return lax.dot_general(
        left_side, right_side, (((1,), (1,)), ((), ())), preferred_element_type=jnp.float32
    )


def float_gains(gathered):
    query_full, key_full, value_full, out_full, attn_gain, query_gain, key_gain, ffn_gain = gathered
    return (
        query_full,
        key_full,
        value_full,
        out_full,
        attn_gain.astype(jnp.float32),
        query_gain.astype(jnp.float32),
        key_gain.astype(jnp.float32),
        ffn_gain.astype(jnp.float32),
    )


def per_device(
    tokens,
    cotangent,
    lengths,
    deal_perm,
    routes,
    gate_logits,
    norm_attn,
    norm_query,
    norm_key,
    norm_ffn,
    w_query,
    w_key,
    w_value,
    w_out,
    w_gate,
    w_up,
    w_down,
):
    ctx_count = lax.axis_size("ctx")
    exp_count = lax.axis_size("exp")
    ctx_index = lax.axis_index("ctx")
    row_count = tokens.shape[1]
    model_width = tokens.shape[2]
    piece_rows = row_count // ctx_count
    group_rows = row_count * ctx_count
    top_count = routes.shape[2]
    local_experts = w_gate.shape[0]
    expert_count = local_experts * exp_count
    capacity = 3 * row_count * top_count // (2 * expert_count)
    group_share = HEADS // KV_HEADS
    head_width = model_width // HEADS
    kv_width = KV_HEADS * head_width
    score_scale = head_width ** (-0.5)
    deal_order = lax.dynamic_index_in_dim(deal_perm[0], ctx_index, 0, keepdims=False)
    ctx_slots = jnp.arange(ctx_count, dtype=jnp.int32)
    deal_inverse = jnp.sum(
        jnp.where(deal_order[None, :] == ctx_slots[:, None], ctx_slots[None, :], 0), axis=1
    )

    def deal(given_rows):
        prepared = jnp.take(
            given_rows.reshape(ctx_count, piece_rows, given_rows.shape[1]), deal_inverse, axis=0
        )
        arrived = lax.all_to_all(prepared, "ctx", split_axis=0, concat_axis=0, tiled=True)
        return arrived.reshape(row_count, given_rows.shape[1])

    def undeal(causal_rows):
        returned = lax.all_to_all(
            causal_rows.reshape(ctx_count, piece_rows, causal_rows.shape[1]),
            "ctx",
            split_axis=0,
            concat_axis=0,
            tiled=True,
        )
        return jnp.take(returned, deal_order, axis=0).reshape(row_count, causal_rows.shape[1])

    within = jnp.arange(piece_rows, dtype=jnp.int32)
    own_pos = ((ctx_slots[:, None] * ctx_count + ctx_index) * piece_rows + within[None, :]).reshape(
        row_count
    )
    key_pos = (
        (ctx_slots[None, :, None] * ctx_count + ctx_slots[:, None, None]) * piece_rows
        + within[None, None, :]
    ).reshape(group_rows)
    own_doc, own_offset = documents(own_pos, lengths[0])
    key_doc, key_offset = documents(key_pos, lengths[0])
    allowed = (own_doc[:, None] == key_doc[None, :]) & (key_pos[None, :] <= own_pos[:, None])
    dense_set = float_gains(
        (
            lax.all_gather(w_query, "exp", axis=0, tiled=True),
            lax.all_gather(w_key, "exp", axis=0, tiled=True),
            lax.all_gather(w_value, "exp", axis=0, tiled=True),
            lax.all_gather(w_out, "exp", axis=0, tiled=True),
            lax.all_gather(norm_attn, "exp", axis=0, tiled=True),
            lax.all_gather(norm_query, "exp", axis=0, tiled=True),
            lax.all_gather(norm_key, "exp", axis=0, tiled=True),
            lax.all_gather(norm_ffn, "exp", axis=0, tiled=True),
        )
    )
    query_full, key_full, value_full, out_full, attn_gain, query_gain, key_gain, ffn_gain = (
        dense_set
    )
    layer_in = tokens[0].astype(jnp.float32)
    normed, inv_attn = norm_forward(layer_in, attn_gain)
    ordered = deal(normed.astype(jnp.bfloat16))
    query_lin = jnp.dot(ordered, query_full, preferred_element_type=jnp.float32)
    key_lin = jnp.dot(ordered, key_full, preferred_element_type=jnp.float32)
    value_rows = jnp.dot(ordered, value_full, preferred_element_type=jnp.float32).astype(
        jnp.bfloat16
    )
    query_normed, inv_query = norm_forward(query_lin, query_gain)
    key_normed, inv_key = norm_forward(key_lin, key_gain)
    query_rows = rotate(query_normed, own_offset, HEADS, 1.0).astype(jnp.bfloat16)
    key_rows = rotate(key_normed, own_offset, KV_HEADS, 1.0).astype(jnp.bfloat16)
    keys_all, values_all = (
        lax.all_gather(key_rows, "ctx", axis=0, tiled=True),
        lax.all_gather(value_rows, "ctx", axis=0, tiled=True),
    )
    key_heads = keys_all.reshape(group_rows, KV_HEADS, head_width)
    value_heads = values_all.reshape(group_rows, KV_HEADS, head_width)
    query_heads = query_rows.reshape(row_count, KV_HEADS, group_share, head_width)

    def masked_scores():
        raw_scores = (
            jnp.einsum("qgsd,kgd->gsqk", query_heads, key_heads, preferred_element_type=jnp.float32)
            * score_scale
        )
        return jnp.where(allowed[None, None], raw_scores, MASKED)

    scores = masked_scores()
    row_top = jnp.max(scores, axis=-1, keepdims=True)
    log_total = row_top + jnp.log(jnp.sum(jnp.exp(scores - row_top), axis=-1, keepdims=True))
    probs = jnp.exp(scores - log_total).astype(jnp.bfloat16)
    attended = jnp.einsum("gsqk,kgd->qgsd", probs, value_heads, preferred_element_type=jnp.float32)
    attended = attended.reshape(row_count, model_width).astype(jnp.bfloat16)
    branch = jnp.dot(attended, out_full, preferred_element_type=jnp.float32).astype(jnp.bfloat16)
    resid = layer_in + undeal(branch).astype(jnp.float32)
    ffn_in, inv_ffn = norm_forward(resid, ffn_gain)
    ffn_rows = ffn_in.astype(jnp.bfloat16)
    flat_routes = routes[0].reshape(-1)
    choice_row = jnp.arange(row_count * top_count, dtype=jnp.int32) // top_count
    onehot = (flat_routes[:, None] == jnp.arange(expert_count, dtype=jnp.int32)[None, :]).astype(
        jnp.int32
    )
    rank_in = jnp.sum((jnp.cumsum(onehot, axis=0) - onehot) * onehot, axis=1)
    slot_index = flat_routes * capacity + rank_in

    def to_experts(choice_rows):
        buffer_rows = (
            jnp.zeros((expert_count * capacity, model_width), jnp.bfloat16)
            .at[slot_index]
            .set(choice_rows)
        )
        moved = lax.all_to_all(
            buffer_rows.reshape(exp_count, local_experts, capacity, model_width),
            "exp",
            split_axis=0,
            concat_axis=2,
            tiled=True,
        )
        return moved.reshape(local_experts, exp_count * capacity, model_width)

    def from_experts(expert_rows):
        moved = lax.all_to_all(
            expert_rows.reshape(1, local_experts, exp_count * capacity, model_width),
            "exp",
            split_axis=2,
            concat_axis=0,
            tiled=True,
        )
        return moved.reshape(expert_count * capacity, model_width)[slot_index].reshape(
            row_count, top_count, model_width
        )

    expert_in = to_experts(ffn_rows[choice_row])
    pre_gate = jnp.einsum("emd,edf->emf", expert_in, w_gate, preferred_element_type=jnp.float32)
    pre_up = jnp.einsum("emd,edf->emf", expert_in, w_up, preferred_element_type=jnp.float32)
    act_rows = (jax.nn.silu(pre_gate) * pre_up).astype(jnp.bfloat16)
    expert_out = jnp.einsum(
        "emf,efd->emd", act_rows, w_down, preferred_element_type=jnp.float32
    ).astype(jnp.bfloat16)
    picked = from_experts(expert_out)
    gates = jax.nn.softmax(gate_logits[0], axis=-1)
    layer_out = (resid + jnp.sum(gates[:, :, None] * picked.astype(jnp.float32), axis=1)).astype(
        jnp.bfloat16
    )
    dense_set = float_gains(
        (
            lax.all_gather(w_query, "exp", axis=0, tiled=True),
            lax.all_gather(w_key, "exp", axis=0, tiled=True),
            lax.all_gather(w_value, "exp", axis=0, tiled=True),
            lax.all_gather(w_out, "exp", axis=0, tiled=True),
            lax.all_gather(norm_attn, "exp", axis=0, tiled=True),
            lax.all_gather(norm_query, "exp", axis=0, tiled=True),
            lax.all_gather(norm_key, "exp", axis=0, tiled=True),
            lax.all_gather(norm_ffn, "exp", axis=0, tiled=True),
        )
    )
    query_full, key_full, value_full, out_full, attn_gain, query_gain, key_gain, ffn_gain = (
        dense_set
    )
    grad_out = cotangent[0].astype(jnp.float32)
    d_expert = (
        (gates[:, :, None] * grad_out[:, None, :])
        .astype(jnp.bfloat16)
        .reshape(row_count * top_count, model_width)
    )
    d_rows = to_experts(d_expert)
    d_act = jnp.einsum("emd,efd->emf", d_rows, w_down, preferred_element_type=jnp.float32)
    sigmoid_gate = jax.nn.sigmoid(pre_gate)
    d_gate = (d_act * pre_up * sigmoid_gate * (1.0 + pre_gate * (1.0 - sigmoid_gate))).astype(
        jnp.bfloat16
    )
    d_up = (d_act * pre_gate * sigmoid_gate).astype(jnp.bfloat16)
    d_choice = jnp.einsum("emf,edf->emd", d_gate, w_gate, preferred_element_type=jnp.float32)
    d_choice = (
        d_choice + jnp.einsum("emf,edf->emd", d_up, w_up, preferred_element_type=jnp.float32)
    ).astype(jnp.bfloat16)
    d_ffn_in = jnp.sum(from_experts(d_choice).astype(jnp.float32), axis=1)
    full_grads = (
        jnp.einsum("emd,emf->edf", expert_in, d_gate, preferred_element_type=jnp.float32),
        jnp.einsum("emd,emf->edf", expert_in, d_up, preferred_element_type=jnp.float32),
        jnp.einsum("emf,emd->efd", act_rows, d_rows, preferred_element_type=jnp.float32),
    )
    gate_grad, up_grad, down_grad = (
        lax.psum_scatter(
            full_grads[0].astype(jnp.bfloat16), "ctx", scatter_dimension=1, tiled=True
        ).astype(jnp.float32),
        lax.psum_scatter(
            full_grads[1].astype(jnp.bfloat16), "ctx", scatter_dimension=1, tiled=True
        ).astype(jnp.float32),
        lax.psum_scatter(
            full_grads[2].astype(jnp.bfloat16), "ctx", scatter_dimension=1, tiled=True
        ).astype(jnp.float32),
    )
    d_resid_norm, ffn_gain_grad = norm_backward(resid, inv_ffn, ffn_gain, d_ffn_in)
    d_resid = grad_out + d_resid_norm
    d_branch = deal(d_resid.astype(jnp.bfloat16))
    out_grad = contract_rows(attended, d_branch)
    d_attended = contract_cols(d_branch, out_full).astype(jnp.bfloat16)
    d_attended_heads = d_attended.reshape(row_count, KV_HEADS, group_share, head_width)
    soft_probs = jnp.exp(masked_scores() - log_total)
    rounded_probs = soft_probs.astype(jnp.bfloat16)
    d_probs = jnp.einsum(
        "qgsd,kgd->gsqk", d_attended_heads, value_heads, preferred_element_type=jnp.float32
    )
    d_scores = (
        soft_probs * (d_probs - jnp.sum(soft_probs * d_probs, axis=-1, keepdims=True))
    ).astype(jnp.bfloat16)
    d_query = (
        jnp.einsum(
            "gsqk,kgd->qgsd", d_scores, key_heads, preferred_element_type=jnp.float32
        ).reshape(row_count, model_width)
        * score_scale
    )
    d_keys_all = (
        jnp.einsum(
            "gsqk,qgsd->kgd", d_scores, query_heads, preferred_element_type=jnp.float32
        ).reshape(group_rows, kv_width)
        * score_scale
    )
    d_values_all = jnp.einsum(
        "gsqk,qgsd->kgd", rounded_probs, d_attended_heads, preferred_element_type=jnp.float32
    ).reshape(group_rows, kv_width)
    key_sum, value_sum = (
        lax.psum_scatter(
            d_keys_all.astype(jnp.bfloat16), "ctx", scatter_dimension=0, tiled=True
        ).astype(jnp.float32),
        lax.psum_scatter(
            d_values_all.astype(jnp.bfloat16), "ctx", scatter_dimension=0, tiled=True
        ).astype(jnp.float32),
    )
    d_value = value_sum.astype(jnp.bfloat16)
    d_query_lin, query_gain_grad = norm_backward(
        query_lin, inv_query, query_gain, rotate(d_query, own_offset, HEADS, -1.0)
    )
    d_key_lin, key_gain_grad = norm_backward(
        key_lin, inv_key, key_gain, rotate(key_sum, own_offset, KV_HEADS, -1.0)
    )
    d_query_low = d_query_lin.astype(jnp.bfloat16)
    d_key_low = d_key_lin.astype(jnp.bfloat16)
    query_grad = contract_rows(ordered, d_query_low)
    key_grad = contract_rows(ordered, d_key_low)
    value_grad = contract_rows(ordered, d_value)
    d_ordered = (
        contract_cols(d_query_low, query_full)
        + contract_cols(d_key_low, key_full)
        + contract_cols(d_value, value_full)
    )
    d_normed = undeal(d_ordered.astype(jnp.bfloat16)).astype(jnp.float32)
    d_input_norm, attn_gain_grad = norm_backward(layer_in, inv_attn, attn_gain, d_normed)
    input_grad = d_resid + d_input_norm
    shard_grads = (
        lax.psum_scatter(
            query_grad.astype(jnp.bfloat16), "exp", scatter_dimension=0, tiled=True
        ).astype(jnp.float32),
        lax.psum_scatter(
            key_grad.astype(jnp.bfloat16), "exp", scatter_dimension=0, tiled=True
        ).astype(jnp.float32),
        lax.psum_scatter(
            value_grad.astype(jnp.bfloat16), "exp", scatter_dimension=0, tiled=True
        ).astype(jnp.float32),
        lax.psum_scatter(
            out_grad.astype(jnp.bfloat16), "exp", scatter_dimension=0, tiled=True
        ).astype(jnp.float32),
        lax.psum_scatter(
            attn_gain_grad.astype(jnp.bfloat16), "exp", scatter_dimension=0, tiled=True
        ).astype(jnp.float32),
        lax.psum_scatter(
            query_gain_grad.astype(jnp.bfloat16), "exp", scatter_dimension=0, tiled=True
        ).astype(jnp.float32),
        lax.psum_scatter(
            key_gain_grad.astype(jnp.bfloat16), "exp", scatter_dimension=0, tiled=True
        ).astype(jnp.float32),
        lax.psum_scatter(
            ffn_gain_grad.astype(jnp.bfloat16), "exp", scatter_dimension=0, tiled=True
        ).astype(jnp.float32),
    )
    summed = (
        lax.psum(shard_grads[0].astype(jnp.bfloat16), "ctx").astype(jnp.float32),
        lax.psum(shard_grads[1].astype(jnp.bfloat16), "ctx").astype(jnp.float32),
        lax.psum(shard_grads[2].astype(jnp.bfloat16), "ctx").astype(jnp.float32),
        lax.psum(shard_grads[3].astype(jnp.bfloat16), "ctx").astype(jnp.float32),
        lax.psum(shard_grads[4].astype(jnp.bfloat16), "ctx").astype(jnp.float32),
        lax.psum(shard_grads[5].astype(jnp.bfloat16), "ctx").astype(jnp.float32),
        lax.psum(shard_grads[6].astype(jnp.bfloat16), "ctx").astype(jnp.float32),
        lax.psum(shard_grads[7].astype(jnp.bfloat16), "ctx").astype(jnp.float32),
    )
    return (
        layer_out[None],
        input_grad[None],
        summed[0],
        summed[1],
        summed[2],
        summed[3],
        summed[4],
        summed[5],
        summed[6],
        summed[7],
        gate_grad,
        up_grad,
        down_grad,
    )


def solution(mesh):
    in_specs = (
        P("exp", "ctx", None),
        P("exp", "ctx", None),
        P("exp", None),
        P("exp", None, None),
        P("exp", "ctx", None),
        P("exp", "ctx", None),
        P("exp"),
        P("exp"),
        P("exp"),
        P("exp"),
        P("exp", None),
        P("exp", None),
        P("exp", None),
        P("exp", None),
        P("exp", None, None),
        P("exp", None, None),
        P("exp", None, None),
    )
    out_specs = (
        P("exp", "ctx", None),
        P("exp", "ctx", None),
        P("exp", None),
        P("exp", None),
        P("exp", None),
        P("exp", None),
        P("exp"),
        P("exp"),
        P("exp"),
        P("exp"),
        P("exp", "ctx", None),
        P("exp", "ctx", None),
        P("exp", "ctx", None),
    )
    return jax.shard_map(
        per_device, mesh=mesh, in_specs=in_specs, out_specs=out_specs, check_vma=False
    )
```

profile of v0, /device:TPU:1, one launch (start us, length us, event | category | flops | bytes accessed | tf_op | source)
XLA Modules:
  0.0 1456.0 jit_solution(2752745678326680709)
XLA Ops:
  12.3 16.3 %all-gather = bf16[8,1,128]{2,1,0:T(2,128)(2,1)S(1)} all-gather(bf16[1,1,128]{2,1,0:T(2,128)(2,1)} %bitcast.281), channel_id=1, replica_groups=mesh['ctx'=16,'exp'=8] {'exp'}, dimensions={0}, use_global_device_ids=true | all-gather | bytes 2304 | tf_op jit(solution)/shard_map/all_gather | solution.py:157
  64.9 22.2 %all-gather.10.cloned.1.call-done = bf16[1024,512]{1,0:T(8,128)(2,1)} async-done(((bf16[128,512]{1,0:T(8,128)(2,1)}), bf16[1024,512]{1,0:T(8,128)(2,1)}) %all-gather.10.cloned.1.call-update) | async-done | bytes 1048592 | tf_op jit(solution)/shard_map/all_gather | solution.py:155
  135.6 53.8 %all-gather.16.cloned.1.call-done = bf16[3072,512]{1,0:T(8,128)(2,1)} async-done(((bf16[192,512]{1,0:T(8,128)(2,1)}), bf16[3072,512]{1,0:T(8,128)(2,1)}) %all-gather.16.cloned.1.call-update) | async-done | bytes 3145744 | tf_op jit(solution)/shard_map/all_gather | solution.py:179
  194.1 17.6 %fusion.4 = (f32[8,2,192]{2,1,0:T(2,128)S(1)}, f32[8,3072,192,2]{1,2,3,0:T(8,128)}) fusion(pred[192,3072]{1,0:T(8,128)(4,1)S(1)} %compare_and_fusion, bf16[3072,8,64,1]{0,2,3,1:T(8,128)(2,1)} %bitcast.231, bf16[192,8,2,64]{0,3,2,1:T(8,128)(2,1)S(1)} %bitcast.238), kind=kOutput, calls=%fused_computation.18 | convolution fusion | flops 1236268032 | bytes 41889792 | tf_op jit(solution)/shard_map/qgsd,kgd->gsqk/dot_general | solution.py:188
  211.6 17.1 %exponential_reduce_fusion = f32[8,2,192]{2,1,0:T(2,128)S(1)} fusion(f32[8,3072,192,2]{1,2,3,0:T(8,128)} %get-tuple-element.69, f32[8,2,192]{2,1,0:T(2,128)S(1)} %get-tuple-element.68, pred[192,3072]{1,0:T(8,128)(4,1)S(1)} %compare_and_fusion), kind=kLoop, calls=%fused_computation.16 | loop fusion | flops 37745664 | bytes 38363136 | tf_op jit(solution)/shard_map/reduce_sum | solution.py:195
  248.0 16.3 %convolution_convert_fusion.7 = bf16[8,64,2,192]{3,1,2,0:T(8,128)(2,1)S(1)} fusion(bf16[3072,8,64,1]{0,2,3,1:T(8,128)(2,1)} %bitcast.235, f32[8,3072,192,2]{1,2,3,0:T(8,128)} %get-tuple-element.69, f32[8,2,192]{2,1,0:T(2,128)S(1)} %bitcast.262, pred[192,3072]{1,0:T(8,128)(4,1)S(1)} %compare_and_fusion), kind=kOutput, calls=%fused_computation.52 | convolution fusion | flops 1245904896 | bytes 41889792 | tf_op jit(solution)/shard_map/gsqk,kgd->qgsd/dot_general | solution.py:197
  313.6 76.4 %all-gather.2 = bf16[8,1,128]{2,1,0:T(2,128)(2,1)S(1)} all-gather(bf16[1,1,128]{2,1,0:T(2,128)(2,1)S(1)} %bitcast.283), channel_id=1, replica_groups=mesh['ctx'=16,'exp'=8] {'exp'}, dimensions={0}, use_global_device_ids=true | all-gather | bytes 2304 | tf_op jit(solution)/shard_map/all_gather | solution.py:160
  395.6 24.2 %scatter_custom_fusion = bf16[2304,1024]{1,0:T(8,128)(2,1)} fusion(s32[1536]{0:T(1024)S(1)} %copy-done.46, bf16[192,1024]{1,0:T(8,128)(2,1)} %multiply_convert_fusion.4, s32[2048]{0:T(1024)S(1)} %pad_clamp_fusion.1, bf16[]{:T(256)} %constant.91.clone.1), kind=kCustom, calls=%fused_computation.35 | custom fusion | bytes 4719104 | tf_op jit(solution)/shard_map/scatter | solution.py:215
  429.7 50.1 %all-to-all-done.2 = bf16[8,4,72,1024]{3,2,1,0:T(8,128)(2,1)} async-done(((bf16[8,4,72,1024]{3,2,1,0:T(8,128)(2,1)}), bf16[8,4,72,1024]{3,2,1,0:T(8,128)(2,1)}, u32[]{:S(2)}, u32[]{:S(2)}) %all-to-all-start.2) | async-done | bytes 4718624 | tf_op jit(solution)/shard_map/all_to_all | solution.py:217
  538.5 34.1 %all-to-all-done.3 = bf16[1,4,576,1024]{3,1,0,2:T(4,128)(2,1)} async-done(((bf16[1,4,576,1024]{3,1,0,2:T(4,128)(2,1)}), bf16[1,4,576,1024]{3,1,0,2:T(4,128)(2,1)}, u32[]{:S(2)}, u32[]{:S(2)}) %all-to-all-start.3) | async-done | bytes 4718624 | tf_op jit(solution)/shard_map/all_to_all | solution.py:227
  584.8 47.6 %all-to-all-done.5 = bf16[1,4,576,1024]{3,1,0,2:T(4,128)(2,1)} async-done(((bf16[1,4,576,1024]{3,1,0,2:T(4,128)(2,1)}), bf16[1,4,576,1024]{3,1,0,2:T(4,128)(2,1)}, u32[]{:S(2)}, u32[]{:S(2)}) %all-to-all-start.5) | async-done | bytes 4718624 | tf_op jit(solution)/shard_map/all_to_all | solution.py:227
  676.4 16.2 %all_to_all.80 = bf16[16,12,1024]{2,1,0:T(8,128)(2,1)S(1)} all-to-all(bf16[16,12,1024]{2,1,0:T(8,128)(2,1)S(1)} %broadcast_select_fusion), channel_id=1, replica_groups=mesh['ctx'=16,'exp'=8] {'ctx'}, dimensions={0} | all-to-all | bytes 786432 | tf_op jit(solution)/shard_map/all_to_all | solution.py:127
  695.5 17.8 %bitcast_convert_fusion = bf16[8,64,3072]{2,1,0:T(8,128)(2,1)} fusion(bf16[192,8,2,64]{0,3,2,1:T(8,128)(2,1)S(1)} %bitcast.252, f32[8,3072,192,2]{1,2,3,0:T(8,128)} %get-tuple-element.69, f32[8,2,192]{2,1,0:T(2,128)S(1)} %bitcast.263, pred[192,3072]{1,0:T(8,128)(4,1)S(1)} %compare_and_fusion), kind=kOutput, calls=%fused_computation.23 | convolution fusion | flops 1247281152 | bytes 41889792 | tf_op jit(solution)/shard_map/gsqk,qgsd->kgd/dot_general | solution.py:325
  718.0 28.8 %fusion = (f32[8,2,192]{2,1,0:T(2,128)S(1)}, f32[8,3072,192,2]{1,2,3,0:T(8,128)}) fusion(f32[8,3072,192,2]{1,2,3,0:T(8,128)} %get-tuple-element.69, f32[8,2,192]{2,1,0:T(2,128)S(1)} %bitcast.264, pred[192,3072]{1,0:T(8,128)(4,1)S(1)} %compare_and_fusion, bf16[3072,8,64,1]{0,2,3,1:T(8,128)(2,1)} %bitcast.236, bf16[192,8,2,64]{0,3,2,1:T(8,128)(2,1)S(1)} %bitcast.253), kind=kOutput, calls=%fused_computation.11 | convolution fusion | flops 1255142400 | bytes 79650816 | tf_op jit(solution)/shard_map/qgsd,kgd->gsqk/dot_general | solution.py:307
  746.8 31.9 %fusion.2 = bf16[8,2,192,3072]{3,2,1,0:T(8,128)(2,1)} fusion(f32[8,3072,192,2]{1,2,3,0:T(8,128)} %get-tuple-element.71, f32[8,3072,192,2]{1,2,3,0:T(8,128)} %get-tuple-element.69, f32[8,2,192]{2,1,0:T(2,128)S(1)} %get-tuple-element.70, f32[8,2,192]{2,1,0:T(2,128)S(1)} %bitcast.265, pred[192,3072]{1,0:T(8,128)(4,1)S(1)} %compare_and_fusion), kind=kLoop, calls=%fused_computation.13 | loop fusion | flops 56623104 | bytes 94986240 | tf_op jit(solution)/shard_map/convert_element_type | solution.py:312
  838.8 42.9 %reduce-scatter.28.cloned.1.call-done = bf16[192,512]{1,0:T(8,128)(2,1)} async-done(((bf16[3072,512]{1,0:T(8,128)(2,1)}), bf16[192,512]{1,0:T(8,128)(2,1)}) %reduce-scatter.28.cloned.1.call-update) | async-done | bytes 196624
  902.9 62.0 %reduce-scatter.26.cloned.1.call-done = bf16[4,32,1024]{2,1,0:T(8,128)(2,1)} async-done(((bf16[4,512,1024]{2,1,0:T(8,128)(2,1)}), bf16[4,32,1024]{2,1,0:T(8,128)(2,1)}) %reduce-scatter.26.cloned.1.call-update) | async-done | bytes 262160 | tf_op jit(solution)/shard_map/reduce_scatter | solution.py:295
  966.6 81.6 %reduce-scatter.24.cloned.1.call-done = bf16[4,64,512]{2,1,0:T(8,128)(2,1)} async-done(((bf16[4,1024,512]{2,1,0:T(8,128)(2,1)}), bf16[4,64,512]{2,1,0:T(8,128)(2,1)}) %reduce-scatter.24.cloned.1.call-update) | async-done | bytes 262160 | tf_op jit(solution)/shard_map/reduce_scatter | solution.py:292
  1050.1 81.2 %reduce-scatter.22.cloned.1.call-done = bf16[4,64,512]{2,1,0:T(8,128)(2,1)} async-done(((bf16[4,1024,512]{2,1,0:T(8,128)(2,1)}), bf16[4,64,512]{2,1,0:T(8,128)(2,1)}) %reduce-scatter.22.cloned.1.call-update) | async-done | bytes 262160 | tf_op jit(solution)/shard_map/reduce_scatter | solution.py:289
  1151.7 37.9 %all-reduce.5 = (bf16[128]{0:T(256)(128)(2,1)S(1)}, bf16[128]{0:T(256)(128)(2,1)S(1)}, bf16[64]{0:T(256)(128)(2,1)S(1)}, bf16[128]{0:T(256)(128)(2,1)S(1)}) all-reduce(bf16[128]{0:T(256)(128)(2,1)S(1)} %dynamic-slice.3, bf16[128]{0:T(256)(128)(2,1)S(1)} %dynamic-slice.5, ...), channel_id=1, replica_groups=mesh['ctx'=16,'exp'=8] {'ctx'}, use_global_device_ids=true, to_apply=%region_37.39 | all-reduce | flops 448 | bytes 1792 | tf_op jit(solution)/shard_map/psum | solution.py:387
  1191.6 23.2 %reduce-scatter.14.cloned.1.call-done = bf16[128,1024]{1,0:T(8,128)(2,1)} async-done(((bf16[1024,1024]{1,0:T(8,128)(2,1)}), bf16[128,1024]{1,0:T(8,128)(2,1)}) %reduce-scatter.14.cloned.1.call-update) | async-done | bytes 262160 | tf_op jit(solution)/shard_map/reduce_scatter | solution.py:357
  1214.8 40.9 %reduce-scatter.18.cloned.1.call-done = bf16[128,512]{1,0:T(8,128)(2,1)} async-done(((bf16[1024,512]{1,0:T(8,128)(2,1)}), bf16[128,512]{1,0:T(8,128)(2,1)}) %reduce-scatter.18.cloned.1.call-update) | async-done | bytes 131088 | tf_op jit(solution)/shard_map/reduce_scatter | solution.py:363
  1255.7 40.2 %reduce-scatter.16.cloned.1.call-done = bf16[128,512]{1,0:T(8,128)(2,1)} async-done(((bf16[1024,512]{1,0:T(8,128)(2,1)}), bf16[128,512]{1,0:T(8,128)(2,1)}) %reduce-scatter.16.cloned.1.call-update) | async-done | bytes 131088 | tf_op jit(solution)/shard_map/reduce_scatter | solution.py:360
  1300.3 142.1 %all-reduce.10.cloned.1.call-done = (bf16[128,1024]{1,0:T(8,128)(2,1)}, bf16[128,512]{1,0:T(8,128)(2,1)}, bf16[128,512]{1,0:T(8,128)(2,1)}, bf16[128,1024]{1,0:T(8,128)(2,1)}) async-done(((bf16[128,1024]{1,0:T(8,128)(2,1)}, bf16[128,512]{1,0:T(8,128)(2,1)}, bf16[128,512]{1,0:T(8,128)(2,1)}, bf16[128,1024]{1,0:T(8,128)(2,1)}), (bf16[128,1024]{1,0:T(8,128)(2,1)}, bf16[128,512]{1,0:T(8,128)(2,1)}, ...) | async-done | bytes 786448 | tf_op jit(solution)/shard_map/psum | solution.py:383
  (396 shorter events, 415.8 us)
Async XLA Ops:
  7.2 53.7 %all-gather.14.cloned.1.call-start = ((), (), s32[]{:S(2)}) async-start(), calls=%async_computation.19 | async-start | bytes 1179648 | tf_op jit(solution)/shard_map/all_gather | solution.py:154
  7.9 79.2 %all-gather.10.cloned.1.call-start = ((), (), s32[]{:S(2)}) async-start(), calls=%async_computation.17 | async-start | bytes 1179648 | tf_op jit(solution)/shard_map/all_gather | solution.py:155
  8.7 121.0 %all-gather.18.cloned.1.call-start = ((), (), s32[]{:S(2)}) async-start(), calls=%async_computation.21 | async-start | bytes 2359296 | tf_op jit(solution)/shard_map/all_gather | solution.py:153
  12.2 659.7 %copy-start.3 = (f32[16,12,1024]{2,1,0:T(8,128)}, f32[16,12,1024]{2,1,0:T(8,128)S(1)}, u32[]{:S(2)}) copy-start(f32[16,12,1024]{2,1,0:T(8,128)S(1)} %reshape.838) | copy-start | bytes 2359300
  32.7 28.2 %all-to-all-start = ((bf16[16,12,1024]{2,1,0:T(8,128)(2,1)}), bf16[16,12,1024]{2,1,0:T(8,128)(2,1)S(1)}, u32[]{:S(2)}, u32[]{:S(2)}) async-start(bf16[16,12,1024]{2,1,0:T(8,128)(2,1)} %broadcast_select_fusion.1), calls=%async_computation | async-start | bytes 1048576 | tf_op jit(solution)/shard_map/all_to_all | solution.py:127
  44.7 144.7 %all-gather.16.cloned.1.call-start = ((), (), s32[]{:S(2)}) async-start(), calls=%async_computation.20 | async-start | bytes 3342336 | tf_op jit(solution)/shard_map/all_gather | solution.py:179
  64.8 178.4 %all-gather.12.cloned.1.call-start = ((), (), s32[]{:S(2)}) async-start(), calls=%async_computation.18 | async-start | bytes 3342336 | tf_op jit(solution)/shard_map/all_gather | solution.py:180
  89.4 190.2 %all-gather.20.cloned.1.call-start = ((), (), s32[]{:S(2)}) async-start(), calls=%async_computation.22 | async-start | bytes 2359296 | tf_op jit(solution)/shard_map/all_gather | solution.py:156
  282.7 25.2 %all-to-all-start.1 = ((bf16[16,12,1024]{2,1,0:T(8,128)(2,1)}), bf16[16,12,1024]{2,1,0:T(8,128)(2,1)S(1)}, u32[]{:S(2)}, u32[]{:S(2)}) async-start(bf16[16,12,1024]{2,1,0:T(8,128)(2,1)} %reshape.821), calls=%async_computation.1 | async-start | bytes 1048576 | tf_op jit(solution)/shard_map/all_to_all | solution.py:131
  308.8 111.0 %all-to-all-start.4 = ((bf16[8,4,72,1024]{3,2,1,0:T(8,128)(2,1)}), bf16[8,4,72,1024]{3,2,1,0:T(8,128)(2,1)}, u32[]{:S(2)}, u32[]{:S(2)}) async-start(bf16[8,4,72,1024]{3,2,1,0:T(8,128)(2,1)} %bitcast.233), calls=%async_computation.4 | async-start | bytes 9437184 | tf_op jit(solution)/shard_map/all_to_all | solution.py:217
  419.8 60.0 %all-to-all-start.2 = ((bf16[8,4,72,1024]{3,2,1,0:T(8,128)(2,1)}), bf16[8,4,72,1024]{3,2,1,0:T(8,128)(2,1)}, u32[]{:S(2)}, u32[]{:S(2)}) async-start(bf16[8,4,72,1024]{3,2,1,0:T(8,128)(2,1)} %bitcast.234), calls=%async_computation.2 | async-start | bytes 9437184 | tf_op jit(solution)/shard_map/all_to_all | solution.py:217
  509.4 63.2 %all-to-all-start.3 = ((bf16[1,4,576,1024]{3,1,0,2:T(4,128)(2,1)}), bf16[1,4,576,1024]{3,1,0,2:T(4,128)(2,1)}, u32[]{:S(2)}, u32[]{:S(2)}) async-start(bf16[1,4,576,1024]{3,1,0,2:T(4,128)(2,1)} %copy.100), calls=%async_computation.3 | async-start | bytes 9437184 | tf_op jit(solution)/shard_map/all_to_all | solution.py:227
  572.6 59.7 %all-to-all-start.5 = ((bf16[1,4,576,1024]{3,1,0,2:T(4,128)(2,1)}), bf16[1,4,576,1024]{3,1,0,2:T(4,128)(2,1)}, u32[]{:S(2)}, u32[]{:S(2)}) async-start(bf16[1,4,576,1024]{3,1,0,2:T(4,128)(2,1)} %copy.106), calls=%async_computation.5 | async-start | bytes 9437184 | tf_op jit(solution)/shard_map/all_to_all | solution.py:227
  577.2 258.9 %reduce-scatter.30.cloned.1.call-start = ((), (), s32[]{:S(2)}) async-start(), calls=%async_computation.31 | async-start | bytes 3342336
  718.0 163.8 %reduce-scatter.28.cloned.1.call-start = ((), (), s32[]{:S(2)}) async-start(), calls=%async_computation.30 | async-start | bytes 3342336
  791.8 173.0 %reduce-scatter.26.cloned.1.call-start = ((), (), s32[]{:S(2)}) async-start(), calls=%async_computation.29 | async-start | bytes 4456448 | tf_op jit(solution)/shard_map/reduce_scatter | solution.py:295
  800.4 247.9 %reduce-scatter.24.cloned.1.call-start = ((), (), s32[]{:S(2)}) async-start(), calls=%async_computation.28 | async-start | bytes 4456448 | tf_op jit(solution)/shard_map/reduce_scatter | solution.py:292
  809.7 321.6 %reduce-scatter.22.cloned.1.call-start = ((), (), s32[]{:S(2)}) async-start(), calls=%async_computation.27 | async-start | bytes 4456448 | tf_op jit(solution)/shard_map/reduce_scatter | solution.py:289
  818.0 373.6 %reduce-scatter.20.cloned.1.call-start = ((), (), s32[]{:S(2)}) async-start(), calls=%async_computation.26 | async-start | bytes 2359296 | tf_op jit(solution)/shard_map/reduce_scatter | solution.py:366
  821.4 393.4 %reduce-scatter.14.cloned.1.call-start = ((), (), s32[]{:S(2)}) async-start(), calls=%async_computation.23 | async-start | bytes 2359296 | tf_op jit(solution)/shard_map/reduce_scatter | solution.py:357
  836.1 419.6 %reduce-scatter.18.cloned.1.call-start = ((), (), s32[]{:S(2)}) async-start(), calls=%async_computation.25 | async-start | bytes 1179648 | tf_op jit(solution)/shard_map/reduce_scatter | solution.py:363
  838.6 457.3 %reduce-scatter.16.cloned.1.call-start = ((), (), s32[]{:S(2)}) async-start(), calls=%async_computation.24 | async-start | bytes 1179648 | tf_op jit(solution)/shard_map/reduce_scatter | solution.py:360
  894.3 238.8 %all-to-all-start.7 = ((bf16[16,12,1024]{2,1,0:T(8,128)(2,1)}), bf16[16,12,1024]{2,1,0:T(8,128)(2,1)}, u32[]{:S(2)}, u32[]{:S(2)}) async-start(bf16[16,12,1024]{2,1,0:T(8,128)(2,1)} %reshape.837), calls=%async_computation.7 | async-start | bytes 1048576 | tf_op jit(solution)/shard_map/all_to_all | solution.py:131
  900.5 542.0 %all-reduce.10.cloned.1.call-start = ((), (), s32[]{:S(2)}) async-start(), calls=%async_computation.32 | async-start | bytes 1572864 | tf_op jit(solution)/shard_map/psum | solution.py:383
  (84 other events, 7274.9 us)
Sparse Core Ops, SparseCore 0:
  9.7 37.2 all-gather.13
  48.7 38.4 all-gather.9
  88.8 40.8 all-gather.17
  132.5 56.8 all-gather.15
  192.3 50.9 all-gather.11
  244.8 34.8 all-gather.19
  718.1 85.4 reduce-scatter.29
  807.7 74.0 reduce-scatter.27
  885.8 78.9 reduce-scatter.25
  969.3 78.9 reduce-scatter.23
  1052.3 78.9 reduce-scatter.21
  1133.7 37.8 reduce-scatter.19
  1174.1 40.6 reduce-scatter.13
  1217.2 38.5 reduce-scatter.17
  1258.1 37.8 reduce-scatter.15
  1298.7 143.6 all-reduce.9
where the time goes:
time: 1460 us
  waiting for transfers between devices  769 us (53%)
  blocking collectives  189 us (13%)
  matrix products  186 us (13%)
  local copies, waits for them, and re-layouts  125 us (9%)
  other arithmetic  115 us (8%)
  starting transfers between devices  54.3 us (4%)
  between operations  17.5 us (1%)
    psum x1, waiting for transfers between devices, per_device(): lax.psum(shard_grads[0].astype(jnp.bfloat16), 'ctx').astype(jnp.float32)  142 us
    all_to_all x2, waiting for transfers between devices, from_experts(): lax.all_to_all(expert_rows.reshape(1, local_experts, exp_count * capacity...  81.7 us
    reduce_scatter x1, waiting for transfers between devices, per_device(): lax.psum_scatter(full_grads[1].astype(jnp.bfloat16), 'ctx', scatter_dimen...  81.6 us
    reduce_scatter x1, waiting for transfers between devices, per_device(): lax.psum_scatter(full_grads[0].astype(jnp.bfloat16), 'ctx', scatter_dimen...  81.2 us
    all_gather x1, blocking collectives, per_device(): lax.all_gather(norm_ffn, 'exp', axis=0, tiled=True)  76.4 us
    reduce_scatter x1, waiting for transfers between devices, per_device(): lax.psum_scatter(full_grads[2].astype(jnp.bfloat16), 'ctx', scatter_dimen...  62 us
    all_gather x1, waiting for transfers between devices, per_device(): lax.all_gather(key_rows, 'ctx', axis=0, tiled=True)  53.8 us
    all_to_all x2, waiting for transfers between devices, to_experts(): lax.all_to_all(buffer_rows.reshape(exp_count, local_experts, capacity, mo...  50.1 us
  transfers between devices with their start and end apart: 23, of which 16 were waited for; matrix products, arithmetic and copies ran while one was open for 22% of the time, Pallas kernels for 0%

commit v1 on v0

v1 whole, which is shorter than its diff:
```python
import jax
import jax.numpy as jnp
from jax import lax
from jax.experimental import pallas as pl
from jax.experimental.pallas import tpu as pltpu
from jax.sharding import PartitionSpec as P

HEADS = 16
KV_HEADS = 8
EPSILON = 1e-05
ROPE_BASE = 10000.0
MASKED = -1e30

MESH = pl.DeviceIdType.MESH
CTX = 16
EXP = 8
CHIPS = 8
ROWS = 192
WIDTH = 1024
FF = 512
LOCAL = 4
CAP = 72
PAIRS = EXP // 2
PAIR_ROWS = 2 * ROWS
PAIR_CAP = 2 * CAP
SLOTS = EXP * CAP
PAIR_SLOTS = LOCAL * PAIR_CAP
KEYS = CTX * ROWS
CHUNK = 2 * ROWS
MIB = 1 << 20

ANY_SPEC = pl.BlockSpec(memory_space=pl.ANY)
F32 = jnp.float32
BF16 = jnp.bfloat16


def dot(a, b, dims=((1,), (0,))):
    return lax.dot_general(a, b, (dims, ((), ())), preferred_element_type=F32)


NT = ((1,), (1,))
TN = ((0,), (0,))


def comm_call(body, name, collective_id, outs, ins, copies):
    return pl.pallas_call(
        body,
        name=name,
        out_shape=outs,
        in_specs=[ANY_SPEC] * len(ins),
        out_specs=[ANY_SPEC] * len(outs),
        scratch_shapes=[
            pltpu.SemaphoreType.DMA((copies,)),
            pltpu.SemaphoreType.DMA((copies,)),
            pltpu.SemaphoreType.DMA((8,)),
        ],
        compiler_params=pltpu.CompilerParams(collective_id=collective_id, has_side_effects=True),
    )(*ins)


class Copier:
    def __init__(self, send_sem, recv_sem, local_sem):
        self.send_sem, self.recv_sem, self.local_sem = send_sem, recv_sem, local_sem
        self.remote, self.local = [], []

    def send(self, src, dst, axis, index):
        at = len(self.remote)
        copy = pltpu.make_async_remote_copy(
            src_ref=src,
            dst_ref=dst,
            send_sem=self.send_sem.at[at],
            recv_sem=self.recv_sem.at[at],
            device_id={axis: index},
            device_id_type=MESH,
        )
        copy.start()
        self.remote.append([copy, False])
        return at

    def keep(self, src, dst):
        copy = pltpu.make_async_copy(src, dst, self.local_sem.at[len(self.local)])
        copy.start()
        self.local.append(copy)

    def arrived(self, at):
        self.remote[at][0].wait_recv()
        self.remote[at][1] = True

    def finish(self):
        for copy, seen in self.remote:
            if not seen:
                copy.wait_recv()
        for copy, _ in self.remote:
            copy.wait_send()
        for copy in self.local:
            copy.wait()


def meet(partners):
    barrier = pltpu.get_barrier_semaphore()
    for axis, index in partners:
        pl.semaphore_signal(barrier, inc=1, device_id={axis: index}, device_id_type=MESH)
    pl.semaphore_wait(barrier, len(partners))


def place():
    ctx = lax.axis_index("ctx")
    core = lax.rem(ctx, 2)
    return ctx, ctx // 2, core, ctx + 1 - 2 * core


def exp_ring():
    me = lax.axis_index("exp")
    half, spot = me // 4, lax.rem(me, 4)
    right = half * 4 + lax.rem(spot + 1, 4)
    left = half * 4 + lax.rem(spot + 3, 4)
    over = (1 - half) * 4
    return (
        me,
        right,
        left,
        half * 4 + lax.rem(spot + 2, 4),
        over + spot,
        over + lax.rem(spot + 1, 4),
        over + lax.rem(spot + 3, 4),
        over + lax.rem(spot + 2, 4),
    )


def relay(copier, own, slot, rows, ring, forward):
    me, right, left, far, over, over_right, over_left, over_far = ring
    half = rows // 2
    low, high = pl.ds(0, half), pl.ds(half, half)
    to_over = copier.send(own, slot(me), "exp", over)
    to_right = copier.send(own, slot(me), "exp", right)
    to_left = copier.send(own, slot(me), "exp", left)
    copier.arrived(to_over)
    over_r = copier.send(slot(over), slot(over), "exp", right)
    over_l = copier.send(slot(over), slot(over), "exp", left)
    copier.arrived(to_right)
    far_r = copier.send(slot(left).at[low], slot(left).at[low], "exp", right)
    copier.arrived(to_left)
    far_l = copier.send(slot(right).at[high], slot(right).at[high], "exp", left)
    for partner in (over, left, right):
        forward(partner)
    copier.arrived(over_r)
    ofar_r = copier.send(slot(over_left).at[low], slot(over_left).at[low], "exp", right)
    copier.arrived(over_l)
    ofar_l = copier.send(slot(over_right).at[high], slot(over_right).at[high], "exp", left)
    forward(over_left)
    forward(over_right)
    copier.arrived(far_r)
    copier.arrived(far_l)
    forward(far)
    copier.arrived(ofar_r)
    copier.arrived(ofar_l)
    forward(over_far)


def gather_weights(shards, gains):
    def body(x_ref, g_ref, w_ref, go_ref, send_sem, recv_sem, local_sem):
        ring = exp_ring()
        me = ring[0]
        _, _, core, sibling = place()
        copier = Copier(send_sem, recv_sem, local_sem)
        meet([("exp", partner) for partner in ring[1:]] + [("ctx", sibling)])
        copier.keep(x_ref.at[0], w_ref.at[0, me])
        copier.keep(x_ref.at[1], w_ref.at[1, me])
        copier.keep(g_ref, go_ref.at[me])
        for partner in ring[1:]:
            copier.send(g_ref, go_ref.at[me], "exp", partner)
        relay(
            copier,
            x_ref.at[core],
            lambda s: w_ref.at[core, s],
            shards.shape[1],
            ring,
            lambda s: copier.send(w_ref.at[core, s], w_ref.at[core, s], "ctx", sibling),
        )
        copier.finish()

    return comm_call(
        body,
        "gather_weights",
        1,
        [
            jax.ShapeDtypeStruct((2, EXP) + shards.shape[1:], shards.dtype),
            jax.ShapeDtypeStruct((EXP,) + gains.shape, gains.dtype),
        ],
        [shards, gains],
        23,
    )


def gather_rows(rows):
    def body(x_ref, o_ref, send_sem, recv_sem, local_sem):
        ring = exp_ring()
        copier = Copier(send_sem, recv_sem, local_sem)
        meet([("exp", ring[1]), ("exp", ring[2]), ("exp", ring[4])])
        copier.keep(x_ref, o_ref.at[ring[0]])
        relay(copier, x_ref, lambda s: o_ref.at[s], rows.shape[0], ring, lambda s: None)
        copier.finish()

    return comm_call(
        body, "gather_rows", 2, [jax.ShapeDtypeStruct((EXP,) + rows.shape, rows.dtype)], [rows], 9
    )[0]


def spread_heads(q_send, kv_send, meta):
    def body(q_ref, kv_ref, m_ref, qo_ref, kvo_ref, mo_ref, send_sem, recv_sem, local_sem):
        _, chip, core, sibling = place()
        me = lax.axis_index("exp")
        chips = [lax.rem(chip + d, CHIPS) for d in range(1, CHIPS)]
        experts = [lax.rem(me + d, EXP) for d in range(1, EXP)]
        copier = Copier(send_sem, recv_sem, local_sem)
        meet([("ctx", 2 * p + core) for p in chips] + [("ctx", sibling)] + [("exp", p) for p in experts])
        own = 2 * chip + core
        first = [copier.send(kv_ref.at[p], kvo_ref.at[own], "ctx", 2 * p + core) for p in chips]
        copier.send(kv_ref.at[chip], kvo_ref.at[own], "ctx", sibling)
        for p in chips:
            copier.send(q_ref.at[p], qo_ref.at[chip], "ctx", 2 * p + core)
        for p in experts:
            copier.send(m_ref.at[p], mo_ref.at[me], "exp", p)
        copier.keep(q_ref.at[chip], qo_ref.at[chip])
        copier.keep(kv_ref.at[chip], kvo_ref.at[own])
        copier.keep(m_ref.at[me], mo_ref.at[me])
        for d, at in enumerate(first, 1):
            copier.arrived(at)
            source = 2 * lax.rem(chip + CHIPS - d, CHIPS) + core
            copier.send(kvo_ref.at[source], kvo_ref.at[source], "ctx", sibling)
        copier.finish()

    return comm_call(
        body,
        "spread_heads",
        3,
        [
            jax.ShapeDtypeStruct((CHIPS, ROWS, 128), BF16),
            jax.ShapeDtypeStruct((CTX, ROWS, 128), BF16),
            jax.ShapeDtypeStruct(meta.shape, F32),
        ],
        [q_send, kv_send, meta],
        29,
    )


def lanes(index):
    return pl.ds(pl.multiple_of(index * 128, 128), 128)


def collect_heads(blocks):
    def body(x_ref, o_ref, send_sem, recv_sem, local_sem):
        _, chip, core, _ = place()
        chips = [lax.rem(chip + d, CHIPS) for d in range(1, CHIPS)]
        copier = Copier(send_sem, recv_sem, local_sem)
        meet([("ctx", 2 * p + core) for p in chips])
        for p in chips:
            copier.send(x_ref.at[p], o_ref.at[:, lanes(chip)], "ctx", 2 * p + core)
        copier.keep(x_ref.at[chip], o_ref.at[:, lanes(chip)])
        copier.finish()

    return comm_call(
        body, "collect_heads", 4, [jax.ShapeDtypeStruct((ROWS, WIDTH), BF16)], [blocks], 7
    )[0]


def spread_grads(rows):
    def body(x_ref, o_ref, send_sem, recv_sem, local_sem):
        _, chip, core, _ = place()
        chips = [lax.rem(chip + d, CHIPS) for d in range(1, CHIPS)]
        copier = Copier(send_sem, recv_sem, local_sem)
        meet([("ctx", 2 * p + core) for p in chips])
        for p in chips:
            copier.send(x_ref.at[:, lanes(p)], o_ref.at[chip], "ctx", 2 * p + core)
        copier.keep(x_ref.at[:, lanes(chip)], o_ref.at[chip])
        copier.finish()

    return comm_call(
        body, "spread_grads", 5, [jax.ShapeDtypeStruct((CHIPS, ROWS, 128), BF16)], [rows], 7
    )[0]


def collect_grads(dq, dkv):
    def body(q_ref, kv_ref, qo_ref, kvo_ref, send_sem, recv_sem, local_sem):
        ctx, chip, core, _ = place()
        chips = [lax.rem(chip + d, CHIPS) for d in range(1, CHIPS)]
        others = [lax.rem(ctx + d, CTX) for d in range(1, CTX)]
        copier = Copier(send_sem, recv_sem, local_sem)
        meet([("ctx", p) for p in others])
        for p in others:
            copier.send(kv_ref.at[p], kvo_ref.at[core, :, lanes(chip)], "ctx", p)
        for p in chips:
            copier.send(q_ref.at[p], qo_ref.at[:, lanes(chip)], "ctx", 2 * p + core)
        copier.keep(q_ref.at[chip], qo_ref.at[:, lanes(chip)])
        copier.keep(kv_ref.at[ctx], kvo_ref.at[core, :, lanes(chip)])
        copier.finish()

    return comm_call(
        body,
        "collect_grads",
        6,
        [
            jax.ShapeDtypeStruct((ROWS, WIDTH), BF16),
            jax.ShapeDtypeStruct((2, ROWS, WIDTH), BF16),
        ],
        [dq, dkv],
        22,
    )


def swap_cores(grads):
    def body(x_ref, o_ref, send_sem, recv_sem, local_sem):
        _, _, core, sibling = place()
        copier = Copier(send_sem, recv_sem, local_sem)
        meet([("ctx", sibling)])
        copier.send(x_ref.at[:, 1 - core], o_ref, "ctx", sibling)
        copier.finish()

    shape = (grads.shape[0],) + grads.shape[2:]
    return comm_call(body, "swap_cores", 7, [jax.ShapeDtypeStruct(shape, BF16)], [grads], 1)[0]


def trade_exp(blocks, collective_id):
    def body(x_ref, o_ref, send_sem, recv_sem, local_sem):
        me = lax.axis_index("exp")
        others = [lax.rem(me + d, EXP) for d in range(1, EXP)]
        copier = Copier(send_sem, recv_sem, local_sem)
        meet([("exp", p) for p in others])
        for p in others:
            copier.send(x_ref.at[p], o_ref.at[me], "exp", p)
        copier.keep(x_ref.at[me], o_ref.at[me])
        copier.finish()

    return comm_call(
        body, "trade_exp", collective_id, [jax.ShapeDtypeStruct(blocks.shape, BF16)], [blocks], 7
    )[0]


def trade_chips(rows):
    def body(x_ref, o_ref, send_sem, recv_sem, local_sem):
        _, chip, core, _ = place()
        chips = [lax.rem(chip + d, CHIPS) for d in range(1, CHIPS)]
        copier = Copier(send_sem, recv_sem, local_sem)
        meet([("ctx", 2 * p + core) for p in chips])
        for p in chips:
            copier.send(x_ref.at[:, lanes(p)], o_ref.at[chip], "ctx", 2 * p + core)
        copier.keep(x_ref.at[:, lanes(chip)], o_ref.at[chip])
        copier.finish()

    return comm_call(
        body, "trade_chips", 9, [jax.ShapeDtypeStruct((CHIPS, rows.shape[0], 128), BF16)], [rows], 7
    )[0]


def share_all(part):
    def body(x_ref, o_ref, send_sem, recv_sem, local_sem):
        _, chip, core, sibling = place()
        chips = [lax.rem(chip + d, CHIPS) for d in range(1, CHIPS)]
        copier = Copier(send_sem, recv_sem, local_sem)
        meet([("ctx", 2 * p + core) for p in chips] + [("ctx", sibling)])
        mine = o_ref.at[core, :, lanes(chip)]
        first = [copier.send(x_ref, mine, "ctx", 2 * p + core) for p in chips]
        copier.send(x_ref, mine, "ctx", sibling)
        copier.keep(x_ref, mine)
        for d, at in enumerate(first, 1):
            copier.arrived(at)
            got = o_ref.at[core, :, lanes(lax.rem(chip + CHIPS - d, CHIPS))]
            copier.send(got, got, "ctx", sibling)
        copier.finish()

    return comm_call(
        body, "share_all", 10, [jax.ShapeDtypeStruct((2, part.shape[0], WIDTH), BF16)], [part], 15
    )[0]


def compute_call(body, name, outs, ins, vmem=48, cost=None, **kw):
    return pl.pallas_call(
        body,
        name=name,
        out_shape=outs,
        compiler_params=pltpu.CompilerParams(vmem_limit_bytes=vmem * MIB),
        **kw,
    )(*ins)


def turn(values, cosine, down, up):
    return values * cosine + pltpu.roll(values, 96, 1) * down + pltpu.roll(values, 32, 1) * up


def row_scale(total, width):
    return lax.rsqrt(total * (1.0 / width) + EPSILON)


def key_lanes():
    return lax.broadcasted_iota(jnp.int32, (1, 128), 1) < 64


def project(tokens, w_q, w_kv, gains, tables, routes_t, logits_t):
    def body(t_ref, wq_ref, wkv_ref, g_ref, tab_ref, r_ref, l_ref, n_ref, q_ref, kv_ref, qs_ref, kvs_ref, m_ref):
        x = t_ref[...].astype(F32)
        scale = row_scale(jnp.sum(x * x, axis=1, keepdims=True), WIDTH)
        normed = (x * scale * g_ref[0:1, :]).astype(BF16)
        n_ref[...] = normed
        q = dot(normed, wq_ref[...])
        kv = dot(normed, wkv_ref[...])
        q_ref[...] = q
        kv_ref[...] = kv
        q_scale = row_scale(jnp.sum(q * q, axis=1, keepdims=True), WIDTH)
        keys = key_lanes()
        total = jnp.zeros((ROWS, 128), F32)
        for c in range(CHIPS):
            piece = kv[:, c * 128 : (c + 1) * 128]
            total = total + jnp.where(keys, piece * piece, 0.0)
        k_scale = row_scale(jnp.sum(total, axis=1, keepdims=True), WIDTH // 2)
        kv_scale = jnp.where(keys, k_scale, 1.0)
        for c in range(CHIPS):
            at = slice(c * 128, (c + 1) * 128)
            qn = q[:, at] * q_scale * g_ref[1:2, at]
            qr = turn(qn, tab_ref[0], tab_ref[1], tab_ref[2])
            qs_ref[c] = (qr.astype(BF16).astype(F32) * 0.125).astype(BF16)
            kn = kv[:, at] * kv_scale * g_ref[2:3, at]
            kvs_ref[c] = turn(kn, tab_ref[3], tab_ref[4], tab_ref[5]).astype(BF16)
        logits = l_ref[...]
        raised = jnp.exp(logits - jnp.max(logits, axis=0, keepdims=True))
        gates = raised / jnp.sum(raised, axis=0, keepdims=True)
        experts = lax.broadcasted_iota(jnp.int32, (32, ROWS), 0)
        member = jnp.zeros((32, ROWS), F32)
        weight = jnp.zeros((32, ROWS), F32)
        for c in range(8):
            hit = r_ref[c : c + 1, :] == experts
            member = member + jnp.where(hit, 1.0, 0.0)
            weight = weight + jnp.where(hit, gates[c : c + 1, :], 0.0)
        before = lax.broadcasted_iota(jnp.int32, (ROWS, ROWS), 0) < lax.broadcasted_iota(
            jnp.int32, (ROWS, ROWS), 1
        )
        rank = dot(member.astype(BF16), jnp.where(before, 1.0, 0.0).astype(BF16))
        spot = jnp.where(member > 0.5, rank, -1.0)
        for e in range(EXP):
            m_ref[e, 0:4, :] = spot[e * 4 : e * 4 + 4, :]
            m_ref[e, 4:8, :] = weight[e * 4 : e * 4 + 4, :]

    return compute_call(
        body,
        "project",
        [
            jax.ShapeDtypeStruct((ROWS, WIDTH), BF16),
            jax.ShapeDtypeStruct((ROWS, WIDTH), F32),
            jax.ShapeDtypeStruct((ROWS, WIDTH), F32),
            jax.ShapeDtypeStruct((CHIPS, ROWS, 128), BF16),
            jax.ShapeDtypeStruct((CHIPS, ROWS, 128), BF16),
            jax.ShapeDtypeStruct((EXP, 8, ROWS), F32),
        ],
        [tokens, w_q, w_kv, gains, tables, routes_t, logits_t],
    )


def split_kv(kv_ref, klo, khi, vlo, vhi):
    low = key_lanes()
    both = kv_ref[...].astype(F32)
    other = pltpu.roll(both, 64, 1)
    if klo is not None:
        klo[...] = jnp.where(low, both, 0.0).astype(BF16)
        khi[...] = jnp.where(low, 0.0, other).astype(BF16)
    vlo[...] = jnp.where(low, other, 0.0).astype(BF16)
    vhi[...] = jnp.where(low, 0.0, both).astype(BF16)


def attend(q, kv, key_pos, query_pos, query_start, first_chunk):
    def body(first_ref, q_ref, kv_ref, kp_ref, qp_ref, qb_ref, o_ref, of_ref, l_ref, klo, khi, vlo, vhi):
        i = pl.program_id(0)

        @pl.when(i == 0)
        def _():
            split_kv(kv_ref, klo, khi, vlo, vhi)

        q_block = q_ref[0]
        at_row, start_row = qp_ref[0], qb_ref[0]
        low = key_lanes()

        def step(p, carry):
            m0, m1, l0, l1, acc = carry
            rows = pl.ds(pl.multiple_of(p * CHUNK, CHUNK), CHUNK)
            at_key = kp_ref[p]
            seen = (at_key >= start_row) & (at_key <= at_row)
            s0 = jnp.where(seen, dot(q_block, klo[rows, :], NT), MASKED)
            s1 = jnp.where(seen, dot(q_block, khi[rows, :], NT), MASKED)
            n0 = jnp.maximum(m0, jnp.max(s0, axis=1, keepdims=True))
            n1 = jnp.maximum(m1, jnp.max(s1, axis=1, keepdims=True))
            p0 = jnp.exp(s0 - n0)
            p1 = jnp.exp(s1 - n1)
            a0 = jnp.exp(m0 - n0)
            a1 = jnp.exp(m1 - n1)
            l0 = l0 * a0 + jnp.sum(p0, axis=1, keepdims=True)
            l1 = l1 * a1 + jnp.sum(p1, axis=1, keepdims=True)
            acc = acc * jnp.where(low, a0, a1)
            acc = acc + dot(p0.astype(BF16), vlo[rows, :]) + dot(p1.astype(BF16), vhi[rows, :])
            return n0, n1, l0, l1, acc

        top = jnp.full((ROWS, 1), MASKED, F32)
        none = jnp.zeros((ROWS, 1), F32)
        m0, m1, l0, l1, acc = lax.fori_loop(
            first_ref[i], i + 1, step, (top, top, none, none, jnp.zeros((ROWS, 128), F32))
        )
        out = acc / jnp.where(low, l0, l1)
        of_ref[0] = out
        o_ref[0] = out.astype(BF16)
        l_ref[0] = jnp.where(low, m0 + jnp.log(l0), m1 + jnp.log(l1))

    def block(*shape):
        return pl.BlockSpec((1,) + shape, lambda i, first: (i, 0, 0))

    return pl.pallas_call(
        body,
        name="attend",
        out_shape=[
            jax.ShapeDtypeStruct((CHIPS, ROWS, 128), BF16),
            jax.ShapeDtypeStruct((CHIPS, ROWS, 128), F32),
            jax.ShapeDtypeStruct((CHIPS, ROWS, 128), F32),
        ],
        grid_spec=pltpu.PrefetchScalarGridSpec(
            num_scalar_prefetch=1,
            grid=(CHIPS,),
            in_specs=[
                block(ROWS, 128),
                pl.BlockSpec((KEYS, 128), lambda i, first: (0, 0)),
                pl.BlockSpec((CHIPS, 1, CHUNK), lambda i, first: (0, 0, 0)),
                block(ROWS, 1),
                block(ROWS, 1),
            ],
            out_specs=[block(ROWS, 128)] * 3,
            scratch_shapes=[pltpu.VMEM((KEYS, 128), BF16)] * 4,
        ),
        compiler_params=pltpu.CompilerParams(vmem_limit_bytes=48 * MIB),
    )(first_chunk, q, kv, key_pos, query_pos, query_start)


def attend_back(q, kv, d_out, out, log_total, key_pos, query_pos, query_start, first_chunk):
    def body(
        first_ref, q_ref, kv_ref, do_ref, o_ref, l_ref, kp_ref, qp_ref, qb_ref, dq_ref, dkv_ref, klo, khi, vlo, vhi, acc
    ):
        i = pl.program_id(0)

        @pl.when(i == 0)
        def _():
            split_kv(kv_ref, klo, khi, vlo, vhi)
            acc[...] = jnp.zeros_like(acc)

        low = key_lanes()
        q_block, do_block = q_ref[0], do_ref[0]
        do_wide, q_wide = do_block.astype(F32), q_block.astype(F32)
        q_turned, do_turned = pltpu.roll(q_wide, 64, 1), pltpu.roll(do_wide, 64, 1)
        right = jnp.concatenate(
            [
                jnp.where(low, q_wide, 0.0).astype(BF16),
                jnp.where(low, q_turned, 0.0).astype(BF16),
                jnp.where(low, 0.0, do_turned).astype(BF16),
                jnp.where(low, 0.0, do_wide).astype(BF16),
            ],
            axis=0,
        )
        row_id = lax.broadcasted_iota(jnp.int32, (8, 128), 0)
        lane_id = lax.broadcasted_iota(jnp.int32, (8, 128), 1)
        halves = jnp.where(lane_id // 64 == row_id, 1.0, 0.0)
        picks = jnp.where(lane_id == 64 * row_id, 1.0, 0.0)

        def across(select, values):
            return lax.dot_general(
                select, values, (NT, ((), ())), precision=lax.Precision.HIGHEST, preferred_element_type=F32
            )

        delta = across(halves, do_wide * o_ref[0])
        total = across(picks, l_ref[0])
        at_row, start_row = qp_ref[0], qb_ref[0]

        def step(p, dq):
            rows = pl.ds(pl.multiple_of(p * CHUNK, CHUNK), CHUNK)
            at_key = kp_ref[p]
            seen = (at_key >= start_row) & (at_key <= at_row)
            k0, k1 = klo[rows, :], khi[rows, :]
            s0 = jnp.where(seen, dot(k0, q_block, NT), MASKED)
            s1 = jnp.where(seen, dot(k1, q_block, NT), MASKED)
            p0 = jnp.exp(s0 - total[0:1, :])
            p1 = jnp.exp(s1 - total[1:2, :])
            d0 = (p0 * (dot(vlo[rows, :], do_block, NT) - delta[0:1, :])).astype(BF16)
            d1 = (p1 * (dot(vhi[rows, :], do_block, NT) - delta[1:2, :])).astype(BF16)
            left = jnp.concatenate([d0, d1, p0.astype(BF16), p1.astype(BF16)], axis=1)
            acc[rows, :] += dot(left, right)
            return dq + dot(d0, k0, TN) + dot(d1, k1, TN)

        dq = lax.fori_loop(first_ref[i], i + 1, step, jnp.zeros((ROWS, 128), F32))
        dq_ref[0] = (dq * 0.125).astype(BF16)

        @pl.when(i == CHIPS - 1)
        def _():
            dkv_ref[...] = acc[...].astype(BF16)

    def block(*shape):
        return pl.BlockSpec((1,) + shape, lambda i, first: (i, 0, 0))

    whole = pl.BlockSpec((KEYS, 128), lambda i, first: (0, 0))
    return pl.pallas_call(
        body,
        name="attend_back",
        out_shape=[
            jax.ShapeDtypeStruct((CHIPS, ROWS, 128), BF16),
            jax.ShapeDtypeStruct((KEYS, 128), BF16),
        ],
        grid_spec=pltpu.PrefetchScalarGridSpec(
            num_scalar_prefetch=1,
            grid=(CHIPS,),
            in_specs=[
                block(ROWS, 128),
                whole,
                block(ROWS, 128),
                block(ROWS, 128),
                block(ROWS, 128),
                pl.BlockSpec((CHIPS, CHUNK, 1), lambda i, first: (0, 0, 0)),
                block(1, ROWS),
                block(1, ROWS),
            ],
            out_specs=[block(ROWS, 128), whole],
            scratch_shapes=[pltpu.VMEM((KEYS, 128), BF16)] * 4 + [pltpu.VMEM((KEYS, 128), F32)],
        ),
        compiler_params=pltpu.CompilerParams(vmem_limit_bytes=48 * MIB),
    )(first_chunk, q, kv, d_out, out, log_total, key_pos, query_pos, query_start)


def finish_attention(attended, w_out, tokens, gains):
    def body(a_ref, w_ref, t_ref, g_ref, r_ref, f_ref):
        branch = dot(a_ref[...], w_ref[...]).astype(BF16).astype(F32)
        resid = t_ref[...].astype(F32) + branch
        r_ref[...] = resid
        scale = row_scale(jnp.sum(resid * resid, axis=1, keepdims=True), WIDTH)
        f_ref[...] = (resid * scale * g_ref[3:4, :]).astype(BF16)

    return compute_call(
        body,
        "finish_attention",
        [jax.ShapeDtypeStruct((ROWS, WIDTH), F32), jax.ShapeDtypeStruct((ROWS, WIDTH), BF16)],
        [attended, w_out, tokens, gains],
    )


def experts(rows, grads, meta, meta_t, w_gate, w_up, w_down):
    half = SLOTS // 2

    def body(
        x_ref, g_ref, m_ref, mt_ref, wg_ref, wu_ref, wd_ref,
        xin_ref, dr_ref, act_ref, dg_ref, du_ref, out_ref, dx_ref,
        made, back, weight,
    ):
        e = pl.program_id(0)

        @pl.when(e == 0)
        def _():
            slot_id = lax.broadcasted_iota(jnp.int32, (PAIR_CAP, PAIR_ROWS), 0).astype(F32)

            def pick(p, _):
                meta_p = m_ref[p]
                parts, gates = [], []
                for k in range(LOCAL):
                    hit = slot_id == meta_p[k : k + 1, :]
                    parts.append(jnp.where(hit, 1.0, 0.0).astype(BF16))
                    gates.append(
                        jnp.sum(jnp.where(hit, meta_p[4 + k : 5 + k, :], 0.0), axis=1, keepdims=True)
                    )
                chosen = jnp.concatenate(parts, axis=0)
                rows_p = dot(chosen, x_ref[p]).astype(BF16)
                grads_p = dot(chosen, g_ref[p])
                at = pl.ds(pl.multiple_of(p * PAIR_CAP, PAIR_CAP), PAIR_CAP)
                for k in range(LOCAL):
                    piece = slice(k * PAIR_CAP, (k + 1) * PAIR_CAP)
                    xin_ref[k, at, :] = rows_p[piece]
                    dr_ref[k, at, :] = (grads_p[piece] * gates[k]).astype(BF16)
                    weight[k, at, :] = gates[k]
                return 0

            lax.fori_loop(0, PAIRS, pick, 0)

        def work(h, _):
            at = pl.ds(pl.multiple_of(h * half, half), half)
            x = xin_ref[e, at, :]
            dr = dr_ref[e, at, :]
            gate = dot(x, wg_ref[0])
            up = dot(x, wu_ref[0])
            sig = jax.nn.sigmoid(gate)
            silu = gate * sig
            act = (silu * up).astype(BF16)
            act_ref[0, at, :] = act
            d_act = dot(dr, wd_ref[0], NT)
            d_gate = (d_act * up * sig * (1.0 + gate * (1.0 - sig))).astype(BF16)
            d_up = (d_act * silu).astype(BF16)
            dg_ref[0, at, :] = d_gate
            du_ref[0, at, :] = d_up
            y = (dot(act, wd_ref[0]) * weight[e, at, :]).astype(BF16)
            dch = (dot(d_gate, wg_ref[0], NT) + dot(d_up, wu_ref[0], NT)).astype(BF16)
            place_at = pl.ds(pl.multiple_of(e * PAIR_CAP, PAIR_CAP), PAIR_CAP)
            for k in range(2):
                piece = slice(k * PAIR_CAP, (k + 1) * PAIR_CAP)
                made[2 * h + k, place_at, :] = y[piece]
                back[2 * h + k, place_at, :] = dch[piece]
            return 0

        lax.fori_loop(0, 2, work, 0)

        @pl.when(e == LOCAL - 1)
        def _():
            lane_id = lax.broadcasted_iota(jnp.int32, (PAIR_ROWS, PAIR_SLOTS), 1).astype(F32)

            def give(p, _):
                meta_p = mt_ref[p]
                chosen = jnp.zeros((PAIR_ROWS, PAIR_SLOTS), F32)
                for k in range(LOCAL):
                    spot = meta_p[:, k : k + 1]
                    lane = jnp.where(spot < 0.0, -1.0, spot + float(k * PAIR_CAP))
                    chosen = chosen + jnp.where(lane_id == lane, 1.0, 0.0)
                chosen = chosen.astype(BF16)
                dx_ref[p] = dot(chosen, back[p]).astype(BF16)
                out_ref[p] = dot(chosen, made[p]).astype(BF16)
                return 0

            lax.fori_loop(0, PAIRS, give, 0)

    def fixed(*shape):
        return pl.BlockSpec(shape, lambda e: (0,) * len(shape), pipeline_mode=pl.Buffered(1))

    def each(*shape):
        return pl.BlockSpec((1,) + shape, lambda e: (e, 0, 0))

    return compute_call(
        body,
        "experts",
        [
            jax.ShapeDtypeStruct((LOCAL, SLOTS, WIDTH), BF16),
            jax.ShapeDtypeStruct((LOCAL, SLOTS, WIDTH), BF16),
            jax.ShapeDtypeStruct((LOCAL, SLOTS, FF), BF16),
            jax.ShapeDtypeStruct((LOCAL, SLOTS, FF), BF16),
            jax.ShapeDtypeStruct((LOCAL, SLOTS, FF), BF16),
            jax.ShapeDtypeStruct((PAIRS, PAIR_ROWS, WIDTH), BF16),
            jax.ShapeDtypeStruct((PAIRS, PAIR_ROWS, WIDTH), BF16),
        ],
        [rows, grads, meta, meta_t, w_gate, w_up, w_down],
        vmem=60,
        grid=(LOCAL,),
        in_specs=[
            fixed(PAIRS, PAIR_ROWS, WIDTH),
            fixed(PAIRS, PAIR_ROWS, WIDTH),
            fixed(PAIRS, 8, PAIR_ROWS),
            fixed(PAIRS, PAIR_ROWS, 8),
            each(WIDTH, FF),
            each(WIDTH, FF),
            each(FF, WIDTH),
        ],
        out_specs=[
            fixed(LOCAL, SLOTS, WIDTH),
            fixed(LOCAL, SLOTS, WIDTH),
            each(SLOTS, FF),
            each(SLOTS, FF),
            each(SLOTS, FF),
            fixed(PAIRS, PAIR_ROWS, WIDTH),
            fixed(PAIRS, PAIR_ROWS, WIDTH),
        ],
        scratch_shapes=[
            pltpu.VMEM((PAIRS, PAIR_SLOTS, WIDTH), BF16),
            pltpu.VMEM((PAIRS, PAIR_SLOTS, WIDTH), BF16),
            pltpu.VMEM((LOCAL, SLOTS, 1), F32),
        ],
    )


def expert_grads(rows, d_rows, act, d_gate, d_up):
    def body(x_ref, dr_ref, a_ref, dg_ref, du_ref, gg_ref, gu_ref, gd_ref):
        def wide(r, _):
            x = x_ref[0, :, pl.ds(pl.multiple_of(r * 256, 256), 256)]
            for d_ref, o_ref in ((dg_ref, gg_ref), (du_ref, gu_ref)):
                grad = dot(x, d_ref[0], TN).astype(BF16)
                for k in range(4):
                    o_ref[k % 2, 2 * r + k // 2, 0] = grad[k * 64 : (k + 1) * 64]
            return 0

        lax.fori_loop(0, 4, wide, 0)

        def tall(r, _):
            a = a_ref[0, :, pl.ds(pl.multiple_of(r * 256, 256), 256)]
            grad = dot(a, dr_ref[0], TN).astype(BF16)
            for k in range(8):
                gd_ref[k % 2, 4 * r + k // 2, 0] = grad[k * 32 : (k + 1) * 32]
            return 0

        lax.fori_loop(0, 2, tall, 0)

    def each(*shape):
        return pl.BlockSpec((1,) + shape, lambda e: (e, 0, 0))

    def cut(*shape):
        return pl.BlockSpec((2, CHIPS, 1) + shape, lambda e: (0, 0, e, 0, 0))

    return compute_call(
        body,
        "expert_grads",
        [
            jax.ShapeDtypeStruct((2, CHIPS, LOCAL, 64, FF), BF16),
            jax.ShapeDtypeStruct((2, CHIPS, LOCAL, 64, FF), BF16),
            jax.ShapeDtypeStruct((2, CHIPS, LOCAL, 32, WIDTH), BF16),
        ],
        [rows, d_rows, act, d_gate, d_up],
        grid=(LOCAL,),
        in_specs=[each(SLOTS, WIDTH), each(SLOTS, WIDTH)] + [each(SLOTS, FF)] * 3,
        out_specs=[cut(64, FF), cut(64, FF), cut(32, WIDTH)],
    )


def norm_back(values, total_squares, width, weighted, mask=None):
    scale = row_scale(total_squares, width)
    inner = jnp.sum(weighted * values, axis=1, keepdims=True) * (1.0 / width)
    return scale * weighted - values * (scale * scale * scale) * inner, scale


def back_to_branch(d_parts, resid, cotangent, gains, w_out):
    def body(p_ref, r_ref, c_ref, g_ref, w_ref, dr_ref, db_ref, da_ref, gg_ref):
        incoming = p_ref[0].astype(F32)
        for s in range(1, EXP):
            incoming = incoming + p_ref[s].astype(F32)
        resid_v = r_ref[...]
        squares = jnp.sum(resid_v * resid_v, axis=1, keepdims=True)
        d_norm, scale = norm_back(resid_v, squares, WIDTH, incoming * g_ref[3:4, :])
        gg_ref[...] = jnp.sum(incoming * resid_v * scale, axis=0, keepdims=True)
        d_resid = c_ref[...].astype(F32) + d_norm
        dr_ref[...] = d_resid
        d_branch = d_resid.astype(BF16)
        db_ref[...] = d_branch
        da_ref[...] = dot(d_branch, w_ref[...], NT).astype(BF16)

    return compute_call(
        body,
        "back_to_branch",
        [
            jax.ShapeDtypeStruct((ROWS, WIDTH), F32),
            jax.ShapeDtypeStruct((ROWS, WIDTH), BF16),
            jax.ShapeDtypeStruct((ROWS, WIDTH), BF16),
            jax.ShapeDtypeStruct((1, WIDTH), F32),
        ],
        [d_parts, resid, cotangent, gains, w_out],
    )


def back_to_input(dq, dkv, q_lin, kv_lin, tokens, d_resid, w_q, w_kv, gains, tables):
    def body(
        dq_ref, dkv_ref, q_ref, kv_ref, t_ref, r_ref, wq_ref, wkv_ref, g_ref, tab_ref,
        dql_ref, dkl_ref, di_ref, gg_ref, e_q, e_kv,
    ):
        keys = key_lanes()
        sums = [jnp.zeros((ROWS, 128), F32) for _ in range(4)]
        for c in range(CHIPS):
            at = slice(c * 128, (c + 1) * 128)
            q = q_ref[:, at]
            e = turn(dq_ref[:, at].astype(F32), tab_ref[0], -tab_ref[1], -tab_ref[2])
            e_q[:, at] = e
            sums[0] = sums[0] + q * q
            sums[1] = sums[1] + e * q * g_ref[1:2, at]
            kv = kv_ref[:, at]
            both = dkv_ref[0, :, at].astype(F32) + dkv_ref[1, :, at].astype(F32)
            e = turn(both, tab_ref[3], -tab_ref[4], -tab_ref[5])
            e_kv[:, at] = e
            sums[2] = sums[2] + jnp.where(keys, kv * kv, 0.0)
            sums[3] = sums[3] + jnp.where(keys, e * kv * g_ref[2:3, at], 0.0)
        qq, qe, kk, ke = [jnp.sum(s, axis=1, keepdims=True) for s in sums]
        q_scale, k_scale = row_scale(qq, WIDTH), row_scale(kk, WIDTH // 2)
        q_cut = q_scale * q_scale * q_scale * qe * (1.0 / WIDTH)
        k_cut = k_scale * k_scale * k_scale * ke * (2.0 / WIDTH)
        k_cut = jnp.where(keys, k_cut, 0.0)
        kv_scale = jnp.where(keys, k_scale, 1.0)
        for c in range(CHIPS):
            at = slice(c * 128, (c + 1) * 128)
            q, e = q_ref[:, at], e_q[:, at]
            gg_ref[1:2, at] = jnp.sum(e * q * q_scale, axis=0, keepdims=True)
            dql_ref[:, at] = (q_scale * (e * g_ref[1:2, at]) - q * q_cut).astype(BF16)
            kv, e = kv_ref[:, at], e_kv[:, at]
            gg_ref[2:3, at] = jnp.sum(e * kv * kv_scale, axis=0, keepdims=True)
            dkl_ref[:, at] = (kv_scale * (e * g_ref[2:3, at]) - kv * k_cut).astype(BF16)
        d_normed = dot(dql_ref[...], wq_ref[...], NT) + dot(dkl_ref[...], wkv_ref[...], NT)
        d_normed = d_normed.astype(BF16).astype(F32)
        x = t_ref[...].astype(F32)
        squares = jnp.sum(x * x, axis=1, keepdims=True)
        d_norm, scale = norm_back(x, squares, WIDTH, d_normed * g_ref[0:1, :])
        gg_ref[0:1, :] = jnp.sum(d_normed * x * scale, axis=0, keepdims=True)
        di_ref[...] = r_ref[...] + d_norm

    return compute_call(
        body,
        "back_to_input",
        [
            jax.ShapeDtypeStruct((ROWS, WIDTH), BF16),
            jax.ShapeDtypeStruct((ROWS, WIDTH), BF16),
            jax.ShapeDtypeStruct((ROWS, WIDTH), F32),
            jax.ShapeDtypeStruct((3, WIDTH), F32),
        ],
        [dq, dkv, q_lin, kv_lin, tokens, d_resid, w_q, w_kv, gains, tables],
        scratch_shapes=[pltpu.VMEM((ROWS, WIDTH), F32)] * 2,
    )


def dense_grads(normed, d_q, d_kv, attended, d_branch, gain_rows):
    def body(n_ref, dq_ref, dkv_ref, a_ref, db_ref, g_ref, o_ref):
        def part(r, _):
            at = pl.ds(pl.multiple_of(r * 256, 256), 256)
            n, a = n_ref[:, at], a_ref[:, at]
            for w, (left, right) in enumerate(((n, dq_ref), (n, dkv_ref), (a, db_ref))):
                grad = dot(left, right[...], TN).astype(BF16)
                for k in range(4):
                    o_ref[2 * r + k // 2, k % 2, w * 64 : (w + 1) * 64, :] = grad[k * 64 : (k + 1) * 64]
            return 0

        lax.fori_loop(0, 4, part, 0)
        for e in range(EXP):
            o_ref[e, 0, 192:208, :] = g_ref[e]
            o_ref[e, 1, 192:208, :] = jnp.zeros((16, WIDTH), BF16)

    return compute_call(
        body,
        "dense_grads",
        [jax.ShapeDtypeStruct((EXP, 2, 208, WIDTH), BF16)],
        [normed, d_q, d_kv, attended, d_branch, gain_rows],
    )[0]


def sum_blocks(blocks):
    return jnp.sum(blocks.astype(F32), axis=0)


def per_device(
    tokens,
    cotangent,
    lengths,
    deal_perm,
    routes,
    gate_logits,
    norm_attn,
    norm_query,
    norm_key,
    norm_ffn,
    w_query,
    w_key,
    w_value,
    w_out,
    w_gate,
    w_up,
    w_down,
):
    ctx_index = lax.axis_index("ctx")
    core = lax.rem(ctx_index, 2)
    tokens, cotangent = tokens[0], cotangent[0]

    pieces = jnp.arange(CTX, dtype=jnp.int32)[:, None] * CTX + deal_perm[0]
    positions = (pieces[:, :, None] * 12 + jnp.arange(12, dtype=jnp.int32)).reshape(CTX, ROWS)
    ends = jnp.cumsum(lengths[0])
    starts = ends - lengths[0]
    inside = positions[:, :, None] >= starts
    row_start = jnp.max(jnp.where(inside, starts, 0), axis=2)
    own = lambda a: lax.dynamic_index_in_dim(a, ctx_index, 0, keepdims=False)
    offsets = own(positions - row_start).astype(F32)
    inverse_freq = ROPE_BASE ** (-jnp.arange(32).astype(F32) * 2.0 / 64)
    angles = offsets[:, None] * inverse_freq[None, :]
    cosine, sine = jnp.cos(angles), jnp.sin(angles)
    zero, one = jnp.zeros_like(cosine), jnp.ones_like(cosine)
    tables = jnp.stack(
        [
            jnp.concatenate(parts, axis=1)
            for parts in (
                [cosine] * 4,
                [-sine, zero, -sine, zero],
                [zero, sine, zero, sine],
                [cosine, cosine, one, one],
                [-sine, zero, zero, zero],
                [zero, sine, zero, zero],
            )
        ]
    )
    paired = lambda a: lax.dynamic_index_in_dim(a.reshape(CHIPS, 2, ROWS), core, 1, keepdims=False)
    query_pos, query_start = paired(positions), paired(row_start)
    key_pos = positions.reshape(CHIPS, CHUNK)
    first_chunk = jnp.min(query_start, axis=1) // CHUNK

    heads_of = lambda w: w.reshape(128, KV_HEADS, 64)
    kv_shard = jnp.concatenate([heads_of(w_key), heads_of(w_value)], axis=2).reshape(128, WIDTH)
    gain_shard = jnp.zeros((8, 128), F32)
    gain_shard = gain_shard.at[0].set(norm_attn.astype(F32)).at[1].set(norm_query.astype(F32))
    gain_shard = gain_shard.at[2].set(jnp.concatenate([norm_key.astype(F32), jnp.ones((64,), F32)]))
    gain_shard = gain_shard.at[3].set(norm_ffn.astype(F32))
    w_both, gain_all = gather_weights(jnp.stack([w_query, kv_shard]), gain_shard)
    w_q, w_kv = w_both[0].reshape(WIDTH, WIDTH), w_both[1].reshape(WIDTH, WIDTH)
    gains = gain_all.transpose(1, 0, 2).reshape(8, WIDTH)

    w_o = lax.all_gather(w_out, "exp", axis=0, tiled=True)
    grads_all = lax.all_gather(cotangent, "exp", axis=0, tiled=True)

    normed, q_lin, kv_lin, q_send, kv_send, meta = project(
        tokens, w_q, w_kv, gains, tables, routes[0].T, gate_logits[0].T
    )
    q_all, kv_all, meta_all = spread_heads(q_send, kv_send, meta)
    kv_all = kv_all.reshape(KEYS, 128)
    out_low, out_wide, log_total = attend(
        q_all, kv_all, key_pos[:, None, :], query_pos[:, :, None], query_start[:, :, None], first_chunk
    )
    attended = collect_heads(out_low)
    resid, ffn_rows = finish_attention(attended, w_o, tokens, gains)
    rows_all = gather_rows(ffn_rows)

    shift = jnp.array([0.0, float(CAP)], F32)[None, None, :, None]
    spots = meta_all[:, :LOCAL].reshape(PAIRS, 2, LOCAL, ROWS).transpose(0, 2, 1, 3)
    spots = jnp.where(spots < 0.0, -1.0, spots + shift).reshape(PAIRS, LOCAL, PAIR_ROWS)
    weights = meta_all[:, LOCAL:].reshape(PAIRS, 2, LOCAL, ROWS).transpose(0, 2, 1, 3)
    pair_meta = jnp.concatenate([spots, weights.reshape(PAIRS, LOCAL, PAIR_ROWS)], axis=1)
    rows_in, d_rows, act, d_gate, d_up, out_parts, d_parts = experts(
        rows_all.reshape(PAIRS, PAIR_ROWS, WIDTH),
        grads_all.reshape(PAIRS, PAIR_ROWS, WIDTH),
        pair_meta,
        pair_meta.transpose(0, 2, 1),
        w_gate,
        w_up,
        w_down,
    )
    d_parts = trade_exp(d_parts.reshape(EXP, ROWS, WIDTH), 8)
    out_parts = lax.all_to_all(
        out_parts.reshape(EXP, ROWS, WIDTH), "exp", split_axis=0, concat_axis=0, tiled=True
    )
    layer_out = (resid + sum_blocks(out_parts)).astype(BF16)

    pieces_w = expert_grads(rows_in, d_rows, act, d_gate, d_up)
    groups = [[2 * c + k for c in range(CHIPS)] for k in range(2)]
    swap = [(k, k ^ 1) for k in range(CTX)]
    summed_w = []
    for piece in pieces_w:
        mine = lax.dynamic_index_in_dim(piece, core, 0, keepdims=False)
        other = lax.ppermute(
            lax.dynamic_index_in_dim(piece, 1 - core, 0, keepdims=False), "ctx", swap
        )
        joint = (mine.astype(F32) + other.astype(F32)).astype(BF16)
        summed_w.append(
            sum_blocks(
                lax.all_to_all(
                    joint, "ctx", split_axis=0, concat_axis=0, tiled=True, axis_index_groups=groups
                )
            )
        )

    d_resid, d_branch, d_attended, ffn_gain_grad = back_to_branch(
        d_parts, resid, cotangent, gains, w_o
    )
    d_out = spread_grads(d_attended)
    dq_all, dkv_all = attend_back(
        q_all,
        kv_all,
        d_out,
        out_wide,
        log_total,
        key_pos[:, :, None],
        query_pos[:, None, :],
        query_start[:, None, :],
        first_chunk,
    )
    dq, dkv = collect_grads(dq_all, dkv_all.reshape(CTX, ROWS, 128))
    d_q_lin, d_kv_lin, input_grad, gain_grads = back_to_input(
        dq, dkv, q_lin, kv_lin, tokens, d_resid, w_q, w_kv, gains, tables
    )
    gain_rows = jnp.concatenate([gain_grads, ffn_gain_grad], axis=0).astype(BF16)
    gain_rows = gain_rows.reshape(4, EXP, 128).transpose(1, 0, 2).reshape(EXP, 1, 512)
    gain_rows = jnp.pad(gain_rows, ((0, 0), (0, 15), (0, 512)))
    parts = dense_grads(normed, d_q_lin, d_kv_lin, attended, d_branch, gain_rows)
    other = swap_cores(parts)
    mine = lax.dynamic_index_in_dim(parts, core, 1, keepdims=False)
    joint = (mine.astype(F32) + other.astype(F32)).astype(BF16)
    joint = sum_blocks(trade_exp(joint, 11)).astype(BF16)
    joint = sum_blocks(trade_chips(joint)).astype(BF16)
    full = share_all(joint).astype(F32)
    dense = full[:, :192].reshape(2, 3, 64, WIDTH).transpose(1, 0, 2, 3).reshape(3, 128, WIDTH)
    kv_grad = dense[1].reshape(128, KV_HEADS, 2, 64)
    gain_out = full[0, 192, :512].reshape(4, 128)
    return (
        layer_out[None],
        input_grad[None],
        dense[0],
        kv_grad[:, :, 0].reshape(128, 512),
        kv_grad[:, :, 1].reshape(128, 512),
        dense[2],
        gain_out[0],
        gain_out[1],
        gain_out[2, :64],
        gain_out[3],
        summed_w[0],
        summed_w[1],
        summed_w[2],
    )


def solution(mesh):
    in_specs = (
        P("exp", "ctx", None),
        P("exp", "ctx", None),
        P("exp", None),
        P("exp", None, None),
        P("exp", "ctx", None),
        P("exp", "ctx", None),
        P("exp"),
        P("exp"),
        P("exp"),
        P("exp"),
        P("exp", None),
        P("exp", None),
        P("exp", None),
        P("exp", None),
        P("exp", None, None),
        P("exp", None, None),
        P("exp", None, None),
    )
    out_specs = (
        P("exp", "ctx", None),
        P("exp", "ctx", None),
        P("exp", None),
        P("exp", None),
        P("exp", None),
        P("exp", None),
        P("exp"),
        P("exp"),
        P("exp"),
        P("exp"),
        P("exp", "ctx", None),
        P("exp", "ctx", None),
        P("exp", "ctx", None),
    )
    return jax.shard_map(
        per_device, mesh=mesh, in_specs=in_specs, out_specs=out_specs, check_vma=False
    )
```

time: 1460 us -> 612 us (0.42)
  waiting for transfers between devices: 769 us -> 41.6 us
  Pallas kernels: 0 us -> 429 us
  blocking collectives: 189 us -> 0 us
  matrix products: 186 us -> 0 us
  other arithmetic: 115 us -> 37.8 us
  local copies, waits for them, and re-layouts: 125 us -> 62.5 us
  starting transfers between devices: 54.3 us -> 24.7 us
    pallas_call x0 -> x20, Pallas kernels: none -> 429 us  [the longest x11 308 us: comm_call(): pl.pallas_call(body, name=name, out_shape=outs, in_specs=[ANY_SPEC] * len...]
    reduce_scatter x7 -> x0, waiting for transfers between devices: 329 us -> none  [the longest x1 81.6 us: per_device(): lax.psum_scatter(full_grads[1].astype(jnp.bfloat16), 'ctx', scatter_dimen...]
    dot_general x27 -> x0, matrix products: 186 us -> none  [the longest x1 28.8 us: per_device(): jnp.einsum('qgsd,kgd->gsqk', d_attended_heads, value_heads, preferred_ele...]
    psum x1 -> x0, waiting for transfers between devices: 142 us -> none  [per_device(): lax.psum(shard_grads[0].astype(jnp.bfloat16), 'ctx').astype(jnp.float32)]
    all_gather x6 -> x2, waiting for transfers between devices: 120 us -> 0.02 us  [the longest x1 0.02 us: per_device(): grads_all = lax.all_gather(cotangent, 'exp', axis=0, tiled=True)]
    all_gather x3 -> x0, blocking collectives: 106 us -> none  [the longest x1 76.4 us: per_device(): lax.all_gather(norm_ffn, 'exp', axis=0, tiled=True)]
    all_to_all x7 -> x4, waiting for transfers between devices: 132 us -> 38.9 us  [the longest x3 32.5 us: per_device(): lax.all_to_all(joint, 'ctx', split_axis=0, concat_axis=0, tiled=True, axi...]
    unnamed x18 -> x2, waiting for transfers between devices: 45.7 us -> 1.38 us
  transfers between devices with their start and end apart: 23 -> 9, of which waited for: 16 -> 4; matrix products, arithmetic and copies ran while one was open for 22% -> 10% of each run, Pallas kernels for 0% -> 64%
where the time goes in v1:
time: 612 us; the launch traced here: 611 us
  Pallas kernels  429 us (70%)
  local copies, waits for them, and re-layouts  62.5 us (10%)
  waiting for transfers between devices  41.6 us (7%)
  other arithmetic  37.8 us (6%)
  starting transfers between devices  24.7 us (4%)
  between operations  14.9 us (2%)
    pallas_call x11, Pallas kernels, comm_call(): pl.pallas_call(body, name=name, out_shape=outs, in_specs=[ANY_SPEC] * len...  308 us
    pallas_call x7, Pallas kernels, compute_call(): pl.pallas_call(body, name=name, out_shape=outs, compiler_params=pltpu.Com...  77.8 us
    unnamed x128, local copies, waits for them, and re-layouts  37.9 us
    all_to_all x3, waiting for transfers between devices, per_device(): lax.all_to_all(joint, 'ctx', split_axis=0, concat_axis=0, tiled=True, axi...  32.5 us
    pallas_call x1, Pallas kernels, attend_back(): pl.pallas_call(body, name='attend_back', out_shape=[jax.ShapeDtypeStruct(...  26.6 us
    pallas_call x1, Pallas kernels, attend(): pl.pallas_call(body, name='attend', out_shape=[jax.ShapeDtypeStruct((CHIP...  16.6 us
    convert_element_type x4, other arithmetic, per_device(): joint = (mine.astype(F32) + other.astype(F32)).astype(BF16)  16.3 us
    all_to_all x3, starting transfers between devices, per_device(): lax.all_to_all(joint, 'ctx', split_axis=0, concat_axis=0, tiled=True, axi...  15.7 us
  transfers between devices with their start and end apart: 9, of which 4 were waited for; matrix products, arithmetic and copies ran while one was open for 10% of the time, Pallas kernels for 64%

profile of v1, /device:TPU:1, one launch (start us, length us, event | category | flops | bytes accessed | tf_op | source)
XLA Modules:
  0.0 610.8 jit_solution(4379940838030011125)
XLA Ops:
  16.9 44.2 %gather_weights.1 = (bf16[2,8,128,1024]{3,2,1,0:T(8,128)(2,1)}, f32[8,8,128]{2,1,0:T(8,128)}) custom-call(bf16[2,128,1024]{2,1,0:T(8,128)(2,1)} %pad_maximum_fusion.x_ref, f32[8,128]{1,0:T(8,128)} %copy-done.55), custom_call_target="tpu_custom_call" | custom-call | tf_op jit(solution)/shard_map/gather_weights/pallas_call | solution.py:46
  75.5 43.4 %spread_heads.1 = (bf16[8,192,128]{2,1,0:T(8,128)(2,1)}, bf16[16,192,128]{2,1,0:T(8,128)(2,1)}, f32[8,8,192]{2,1,0:T(8,128)}) custom-call(bf16[8,192,128]{2,1,0:T(8,128)(2,1)} %copy-done.40, bf16[8,192,128]{2,1,0:T(8,128)(2,1)} %copy-done.41, f32[8,8,192]{2,1,0:T(8,128)} %copy-done.42), custom_call_target="tpu_custom_call" | custom-call | tf_op jit(solution)/shard_map/spread_heads/pallas_call | solution.py:46
  122.1 16.6 %attend.1 = (bf16[8,192,128]{2,1,0:T(8,128)(2,1)S(1)}, f32[8,192,128]{2,1,0:T(8,128)S(1)}, f32[8,192,128]{2,1,0:T(8,128)S(1)}) custom-call(s32[8]{0:T(128)S(1)} %and_select_fusion.first_ref, bf16[8,192,128]{2,1,0:T(8,128)(2,1)S(1)} %copy-done.14, bf16[3072,128]{1,0:T(8,128)(2,1)S(1)} %bitcast.129, s32[8,1,384]{2,1,0:T(1,128)S(1)} %add.159.kp_ref, ...), custom_call_target="tpu_custom_call" | custom-call | tf_op jit(solution)/shard_map/attend/pallas_call | solution.py:512
  141.3 10.4 %collect_heads.1.a_ref = bf16[192,1024]{1,0:T(8,128)(2,1)} custom-call(bf16[8,192,128]{2,1,0:T(8,128)(2,1)} %copy-done.37), custom_call_target="tpu_custom_call" | custom-call | tf_op jit(solution)/shard_map/collect_heads/pallas_call | solution.py:46
  157.3 28.3 %gather_rows.1 = bf16[8,192,1024]{2,1,0:T(8,128)(2,1)} custom-call(bf16[192,1024]{1,0:T(8,128)(2,1)} %copy-done.36), custom_call_target="tpu_custom_call" | custom-call | tf_op jit(solution)/shard_map/gather_rows/pallas_call | solution.py:46
  185.7 40.1 %experts.1 = (bf16[4,576,1024]{2,1,0:T(8,128)(2,1)}, bf16[4,576,1024]{2,1,0:T(8,128)(2,1)}, bf16[4,576,512]{2,1,0:T(8,128)(2,1)}, bf16[4,576,512]{2,1,0:T(8,128)...) custom-call(bf16[4,384,1024]{2,1,0:T(8,128)(2,1)} %bitcast.141, ...), custom_call_target="tpu_custom_call" | custom-call | tf_op jit(solution)/shard_map/experts/pallas_call | solution.py:377
  225.8 4.7 all-to-all-start
  233.8 18.2 %expert_grads.1 = (bf16[2,8,4,64,512]{4,3,2,1,0:T(8,128)(2,1)}, bf16[2,8,4,64,512]{4,3,2,1,0:T(8,128)(2,1)}, bf16[2,8,4,32,1024]{4,3,2,1,0:T(8,128)(2,1)}) custom-call(bf16[4,576,1024]{2,1,0:T(8,128)(2,1)} %get-tuple-element.129.x_ref, bf16[4,576,1024]{2,1,0:T(8,128)(2,1)} %get-tuple-element.130.dr_ref, bf16[4,576,512]{2,1,0:T(8,128)(2,1)S(1)} %copy-done.12, ...), custom_call_target="tpu_custom_call" | custom-call | tf_op jit(solution)/shard_map/expert_grads/pallas_call | solution.py:377
  262.2 6.3 %all-to-all-done = bf16[8,192,1024]{2,1,0:T(8,128)(2,1)} async-done(((bf16[8,192,1024]{2,1,0:T(8,128)(2,1)}), bf16[8,192,1024]{2,1,0:T(8,128)(2,1)}, u32[]{:S(2)}, u32[]{:S(2)}) %all-to-all-start) | async-done | bytes 3145760 | tf_op jit(solution)/shard_map/all_to_all | solution.py:1024
  268.6 5.6 all-to-all-start.1
  282.4 20.3 %all-to-all-done.1 = bf16[8,4,64,512]{3,2,1,0:T(8,128)(2,1)S(1)} async-done(((bf16[8,4,64,512]{3,2,1,0:T(8,128)(2,1)}), bf16[8,4,64,512]{3,2,1,0:T(8,128)(2,1)S(1)}, u32[]{:S(2)}, u32[]{:S(2)}) %all-to-all-start.1) | async-done | bytes 2097184 | tf_op jit(solution)/shard_map/all_to_all | solution.py:1041
  308.7 62.3 %trade_exp.2.p_ref = bf16[8,192,1024]{2,1,0:T(8,128)(2,1)} custom-call(bf16[8,192,1024]{2,1,0:T(8,128)(2,1)} %bitcast.145), custom_call_target="tpu_custom_call" | custom-call | tf_op jit(solution)/shard_map/trade_exp/pallas_call | solution.py:46
  377.8 10.6 %spread_grads.1.do_ref = bf16[8,192,128]{2,1,0:T(8,128)(2,1)} custom-call(bf16[192,1024]{1,0:T(8,128)(2,1)} %copy-done.38), custom_call_target="tpu_custom_call" | custom-call | tf_op jit(solution)/shard_map/spread_grads/pallas_call | solution.py:46
  395.2 26.6 %attend_back.1 = (bf16[8,192,128]{2,1,0:T(8,128)(2,1)S(1)}, bf16[3072,128]{1,0:T(8,128)(2,1)S(1)}) custom-call(s32[8]{0:T(128)S(1)} %and_select_fusion.first_ref, bf16[8,192,128]{2,1,0:T(8,128)(2,1)S(1)} %copy-done.15, bf16[3072,128]{1,0:T(8,128)(2,1)S(1)} %bitcast.130, bf16[8,192,128]{2,1,0:T(8,128)(2,1)S(1)} %copy-done.17, f32[8,192,128]{2,1,0:T(8,128)S(1)} %copy-done.23, ...), custom_call_target="tpu_custom_call" | custom-call | tf_op jit(solution)/shard_map/attend_back/pallas_call | solution.py:601
  423.4 21.4 %collect_grads.1 = (bf16[192,1024]{1,0:T(8,128)(2,1)}, bf16[2,192,1024]{2,1,0:T(8,128)(2,1)}) custom-call(bf16[8,192,128]{2,1,0:T(8,128)(2,1)} %copy-done.39, bf16[16,192,128]{2,1,0:T(8,128)(2,1)} %bitcast.132), custom_call_target="tpu_custom_call" | custom-call | tf_op jit(solution)/shard_map/collect_grads/pallas_call | solution.py:46
  449.3 6.0 back_to_input.1
  455.4 5.5 dense_grads.1.x_ref
  460.9 7.1 %swap_cores.1 = bf16[8,208,1024]{2,1,0:T(8,128)(2,1)} custom-call(bf16[8,2,208,1024]{3,2,1,0:T(8,128)(2,1)} %dense_grads.1.x_ref), custom_call_target="tpu_custom_call" | custom-call | tf_op jit(solution)/shard_map/swap_cores/pallas_call | solution.py:46
  468.0 6.6 %fusion.x_ref = bf16[8,208,1024]{2,1,0:T(8,128)(2,1)} fusion(bf16[8,208,1024]{2,1,0:T(8,128)(2,1)} %swap_cores.1, bf16[8,2,208,1024]{3,2,1,0:T(8,128)(2,1)} %dense_grads.1.x_ref, s32[]{:T(128)S(6)} %select_n.38), kind=kLoop, calls=%fused_computation.1 | loop fusion | flops 6815744 | bytes 10223620 | tf_op jit(solution)/shard_map/convert_element_type | solution.py:1072
  474.6 56.3 %trade_exp.3 = bf16[8,208,1024]{2,1,0:T(8,128)(2,1)} custom-call(bf16[8,208,1024]{2,1,0:T(8,128)(2,1)} %fusion.x_ref), custom_call_target="tpu_custom_call" | custom-call | tf_op jit(solution)/shard_map/trade_exp/pallas_call | solution.py:46
  534.3 10.8 %trade_chips.1 = bf16[8,208,128]{2,1,0:T(8,128)(2,1)} custom-call(bf16[208,1024]{1,0:T(8,128)(2,1)} %reduce_sum.61.x_ref), custom_call_target="tpu_custom_call" | custom-call | tf_op jit(solution)/shard_map/trade_chips/pallas_call | solution.py:46
  546.8 13.6 %share_all.1 = bf16[2,208,1024]{2,1,0:T(8,128)(2,1)} custom-call(bf16[208,128]{1,0:T(8,128)(2,1)} %reduce_sum.62.x_ref), custom_call_target="tpu_custom_call" | custom-call | tf_op jit(solution)/shard_map/share_all/pallas_call | solution.py:46
  566.7 5.7 all-to-all-start.3
  589.0 12.2 %all-to-all-done.3 = bf16[8,4,32,1024]{3,2,1,0:T(8,128)(2,1)} async-done(((bf16[8,4,32,1024]{3,2,1,0:T(8,128)(2,1)}), bf16[8,4,32,1024]{3,2,1,0:T(8,128)(2,1)}, u32[]{:S(2)}, u32[]{:S(2)}) %all-to-all-start.3) | async-done | bytes 2097184 | tf_op jit(solution)/shard_map/all_to_all | solution.py:1041
  (225 shorter events, 113.2 us)
Async XLA Ops:
  7.2 8.7 %copy-start.57 = (bf16[128]{0:T(256)(128)(2,1)S(1)}, bf16[128]{0:T(256)(128)(2,1)}, u32[]{:S(2)}) copy-start(bf16[128]{0:T(256)(128)(2,1)} %param.32) | copy-start | bytes 772
  7.2 8.7 %copy-start.58 = (bf16[128]{0:T(256)(128)(2,1)S(1)}, bf16[128]{0:T(256)(128)(2,1)}, u32[]{:S(2)}) copy-start(bf16[128]{0:T(256)(128)(2,1)} %param.33) | copy-start | bytes 772
  7.2 8.7 %copy-start.59 = (bf16[64]{0:T(256)(128)(2,1)S(1)}, bf16[64]{0:T(256)(128)(2,1)}, u32[]{:S(2)}) copy-start(bf16[64]{0:T(256)(128)(2,1)} %param.34) | copy-start | bytes 388
  7.2 8.8 %copy-start.60 = (bf16[128]{0:T(256)(128)(2,1)S(1)}, bf16[128]{0:T(256)(128)(2,1)}, u32[]{:S(2)}) copy-start(bf16[128]{0:T(256)(128)(2,1)} %param.35) | copy-start | bytes 772
  7.2 8.8 %copy-start.53 = (bf16[128,1024]{1,0:T(8,128)(2,1)S(1)}, bf16[128,1024]{1,0:T(8,128)(2,1)}, u32[]{:S(2)}) copy-start(bf16[128,1024]{1,0:T(8,128)(2,1)} %param.36) | copy-start | bytes 786436
  7.2 146.0 %all-gather.4.cloned.1.call-start = ((), (), s32[]{:S(2)}) async-start(), calls=%async_computation.4 | async-start | bytes 2359296 | tf_op jit(solution)/shard_map/all_gather | solution.py:994
  8.0 177.7 %all-gather.6.cloned.1.call-start = ((), (), s32[]{:S(2)}) async-start(), calls=%async_computation.5 | async-start | bytes 3538944 | tf_op jit(solution)/shard_map/all_gather | solution.py:995
  66.7 72.0 %copy-start = (bf16[1,8,128,1024]{3,2,1,0:T(8,128)(2,1)}, bf16[1,8,128,1024]{3,2,1,0:T(8,128)(2,1)S(1)}, u32[]{:S(2)}) copy-start(bf16[1,8,128,1024]{3,2,1,0:T(8,128)(2,1)S(1)} %get-tuple-element.182) | copy-start | bytes 6291460
  75.5 76.4 %copy-start.56 = (f32[2]{0:T(128)S(1)}, f32[2]{0:T(128)}, u32[]{:S(2)}) copy-start(f32[2]{0:T(128)} %constant.201.clone) | copy-start | bytes 28
  122.1 29.6 %copy-start.54 = (f32[8,8,192]{2,1,0:T(8,128)S(1)}, f32[8,8,192]{2,1,0:T(8,128)}, u32[]{:S(2)}) copy-start(f32[8,8,192]{2,1,0:T(8,128)} %get-tuple-element.109) | copy-start | bytes 147460
  152.1 33.6 %copy-start.52 = (f32[4,8,384]{2,1,0:T(8,128)}, f32[4,8,384]{2,1,0:T(8,128)S(1)}, u32[]{:S(2)}) copy-start(f32[4,8,384]{2,1,0:T(8,128)S(1)} %pad_maximum_fusion.4.m_ref) | copy-start | bytes 147460
  225.8 42.8 %all-to-all-start = ((bf16[8,192,1024]{2,1,0:T(8,128)(2,1)}), bf16[8,192,1024]{2,1,0:T(8,128)(2,1)}, u32[]{:S(2)}, u32[]{:S(2)}) async-start(bf16[8,192,1024]{2,1,0:T(8,128)(2,1)} %bitcast.146), calls=%async_computation | async-start | bytes 6291456 | tf_op jit(solution)/shard_map/all_to_all | solution.py:1024
  253.9 6.1 %copy-start.51 = (bf16[2,8,4,64,512]{4,3,2,1,0:T(8,128)(2,1)S(1)}, bf16[2,8,4,64,512]{4,3,2,1,0:T(8,128)(2,1)}, u32[]{:S(2)}) copy-start(bf16[2,8,4,64,512]{4,3,2,1,0:T(8,128)(2,1)} %get-tuple-element.134) | copy-start | bytes 12582916
  253.9 6.1 %collective-permute-start = (bf16[8,4,64,512]{3,2,1,0:T(8,128)(2,1)S(1)}, bf16[8,4,64,512]{3,2,1,0:T(8,128)(2,1)S(1)}, u32[]{:S(2)}, u32[]{:S(2)}) collective-permute-start(bf16[8,4,64,512]{3,2,1,0:T(8,128)(2,1)S(1)} %dynamic-slice_bitcast_fusion.2), channel_id=1, source_target_pairs={{0,8},{8,0},{16,24},{24,16},{32,40},{40,32},{48,56},{56,48},{64,72... | collective-permute-start | bytes 6291464 | tf_op jit(solution)/shard_map/ppermute | solution.py:1035
  257.9 20.8 %collective-permute-start.1 = (bf16[8,4,64,512]{3,2,1,0:T(8,128)(2,1)}, bf16[8,4,64,512]{3,2,1,0:T(8,128)(2,1)}, u32[]{:S(2)}, u32[]{:S(2)}) collective-permute-start(bf16[8,4,64,512]{3,2,1,0:T(8,128)(2,1)} %dynamic-slice_bitcast_fusion.1), channel_id=1, source_target_pairs={{0,8},{8,0},{16,24},{24,16},{32,40},{40,32},{48,56},{56,48},{64,72... | collective-permute-start | bytes 6291464 | tf_op jit(solution)/shard_map/ppermute | solution.py:1035
  268.6 34.1 %all-to-all-start.1 = ((bf16[8,4,64,512]{3,2,1,0:T(8,128)(2,1)}), bf16[8,4,64,512]{3,2,1,0:T(8,128)(2,1)S(1)}, u32[]{:S(2)}, u32[]{:S(2)}) async-start(bf16[8,4,64,512]{3,2,1,0:T(8,128)(2,1)} %fusion.3), calls=%async_computation.1 | async-start | bytes 4194304 | tf_op jit(solution)/shard_map/all_to_all | solution.py:1041
  277.5 284.5 %collective-permute-start.2 = (bf16[8,4,32,1024]{3,2,1,0:T(8,128)(2,1)}, bf16[8,4,32,1024]{3,2,1,0:T(8,128)(2,1)}, u32[]{:S(2)}, u32[]{:S(2)}) collective-permute-start(bf16[8,4,32,1024]{3,2,1,0:T(8,128)(2,1)} %dynamic-slice_bitcast_fusion), channel_id=1, source_target_pairs={{0,8},{8,0},{16,24},{24,16},{32,40},{40,32},{48,56},{56,48},{64,72... | collective-permute-start | bytes 6291464 | tf_op jit(solution)/shard_map/ppermute | solution.py:1035
  302.7 264.0 %all-to-all-start.2 = ((bf16[8,4,64,512]{3,2,1,0:T(8,128)(2,1)}), bf16[8,4,64,512]{3,2,1,0:T(8,128)(2,1)}, u32[]{:S(2)}, u32[]{:S(2)}) async-start(bf16[8,4,64,512]{3,2,1,0:T(8,128)(2,1)} %fusion.2), calls=%async_computation.2 | async-start | bytes 4194304 | tf_op jit(solution)/shard_map/all_to_all | solution.py:1041
  308.7 62.3 %copy-start.2 = (bf16[1024,1024]{1,0:T(8,128)(2,1)S(1)}, bf16[1024,1024]{1,0:T(8,128)(2,1)}, u32[]{:S(2)}) copy-start(bf16[1024,1024]{1,0:T(8,128)(2,1)} %all-gather.4.cloned.1.call-done.w_ref) | copy-start | bytes 6291460
  377.8 67.1 %copy-start.11 = (f32[6,192,128]{2,1,0:T(8,128)S(1)}, f32[6,192,128]{2,1,0:T(8,128)}, u32[]{:S(2)}) copy-start(f32[6,192,128]{2,1,0:T(8,128)} %copy-done.10) | copy-start | bytes 1769476
  395.2 49.7 %copy-start.19 = (f32[192,1024]{1,0:T(8,128)S(1)}, f32[192,1024]{1,0:T(8,128)}, u32[]{:S(2)}) copy-start(f32[192,1024]{1,0:T(8,128)} %copy-done.18) | copy-start | bytes 2359300
  449.3 6.1 copy-start.34
  566.7 6.9 %copy-start.45 = (bf16[2,208,1024]{2,1,0:T(8,128)(2,1)S(1)}, bf16[2,208,1024]{2,1,0:T(8,128)(2,1)}, u32[]{:S(2)}) copy-start(bf16[2,208,1024]{2,1,0:T(8,128)(2,1)} %share_all.1) | copy-start | bytes 2555908
  566.7 34.5 %all-to-all-start.3 = ((bf16[8,4,32,1024]{3,2,1,0:T(8,128)(2,1)}), bf16[8,4,32,1024]{3,2,1,0:T(8,128)(2,1)}, u32[]{:S(2)}, u32[]{:S(2)}) async-start(bf16[8,4,32,1024]{3,2,1,0:T(8,128)(2,1)} %fusion.1), calls=%async_computation.3 | async-start | bytes 4194304 | tf_op jit(solution)/shard_map/all_to_all | solution.py:1041
  (46 other events, 92.1 us)
Sparse Core Ops, SparseCore 0:
  9.7 51.5 all-gather.3
  63.0 50.5 all-gather.5

commit v2 on v1

v2 whole, which is shorter than its diff:
```python
import jax
import jax.numpy as jnp
from jax import lax
from jax.experimental import pallas as pl
from jax.experimental.pallas import tpu as pltpu
from jax.sharding import PartitionSpec as P

HEADS = 16
KV_HEADS = 8
EPSILON = 1e-05
ROPE_BASE = 10000.0
MASKED = -1e30

MESH = pl.DeviceIdType.MESH
CTX = 16
EXP = 8
CHIPS = 8
ROWS = 192
WIDTH = 1024
FF = 512
LOCAL = 4
CAP = 72
PAIRS = EXP // 2
PAIR_ROWS = 2 * ROWS
PAIR_CAP = 2 * CAP
SLOTS = EXP * CAP
PAIR_SLOTS = LOCAL * PAIR_CAP
KEYS = CTX * ROWS
CHUNK = 2 * ROWS
MIB = 1 << 20

ANY_SPEC = pl.BlockSpec(memory_space=pl.ANY)
F32 = jnp.float32
BF16 = jnp.bfloat16


def dot(a, b, dims=((1,), (0,))):
    return lax.dot_general(a, b, (dims, ((), ())), preferred_element_type=F32)


NT = ((1,), (1,))
TN = ((0,), (0,))


def comm_call(body, name, collective_id, outs, ins, copies, in_specs=None):
    return pl.pallas_call(
        body,
        name=name,
        out_shape=outs,
        in_specs=in_specs or [ANY_SPEC] * len(ins),
        out_specs=[ANY_SPEC] * len(outs),
        scratch_shapes=[
            pltpu.SemaphoreType.DMA((copies,)),
            pltpu.SemaphoreType.DMA((copies,)),
            pltpu.SemaphoreType.DMA((8,)),
        ],
        compiler_params=pltpu.CompilerParams(
            collective_id=collective_id, has_side_effects=True, vmem_limit_bytes=60 * MIB
        ),
    )(*ins)


class Copier:
    def __init__(self, send_sem, recv_sem, local_sem):
        self.send_sem, self.recv_sem, self.local_sem = send_sem, recv_sem, local_sem
        self.remote, self.local = [], []

    def send(self, src, dst, axis, index):
        at = len(self.remote)
        copy = pltpu.make_async_remote_copy(
            src_ref=src,
            dst_ref=dst,
            send_sem=self.send_sem.at[at],
            recv_sem=self.recv_sem.at[at],
            device_id={axis: index},
            device_id_type=MESH,
        )
        copy.start()
        self.remote.append([copy, False])
        return at

    def keep(self, src, dst):
        copy = pltpu.make_async_copy(src, dst, self.local_sem.at[len(self.local)])
        copy.start()
        self.local.append([copy, False])
        return len(self.local) - 1

    def arrived(self, at):
        self.remote[at][0].wait_recv()
        self.remote[at][1] = True

    def kept(self, at):
        self.local[at][0].wait()
        self.local[at][1] = True

    def finish(self):
        for copy, seen in self.remote:
            if not seen:
                copy.wait_recv()
        for copy, _ in self.remote:
            copy.wait_send()
        for copy, seen in self.local:
            if not seen:
                copy.wait()


def meet(partners):
    barrier = pltpu.get_barrier_semaphore()
    for axis, index in partners:
        pl.semaphore_signal(barrier, inc=1, device_id={axis: index}, device_id_type=MESH)
    pl.semaphore_wait(barrier, len(partners))


def place():
    ctx = lax.axis_index("ctx")
    core = lax.rem(ctx, 2)
    return ctx, ctx // 2, core, ctx + 1 - 2 * core


def ring_of(me):
    half, spot = me // 4, lax.rem(me, 4)
    over = (1 - half) * 4
    turns = [lax.rem(spot + d, 4) for d in (0, 1, 3, 2)]
    return tuple([half * 4 + t for t in turns] + [over + t for t in turns])


def relay(copier, own, slot, rows, ring, reach, landed=lambda partner: None):
    me, right, left, far, over, over_right, over_left, over_far = ring
    half = rows // 2
    low, high = pl.ds(0, half), pl.ds(half, half)

    def send(src, dst, partner):
        return copier.send(src, dst, *reach(partner))

    to_over = send(own, slot(me), over)
    to_right = send(own, slot(me), right)
    to_left = send(own, slot(me), left)
    yield
    copier.arrived(to_right)
    far_r = send(slot(left).at[low], slot(left).at[low], right)
    landed(left)
    copier.arrived(to_left)
    far_l = send(slot(right).at[high], slot(right).at[high], left)
    landed(right)
    yield
    copier.arrived(to_over)
    over_r = send(slot(over), slot(over), right)
    over_l = send(slot(over), slot(over), left)
    landed(over)
    yield
    copier.arrived(far_r)
    copier.arrived(far_l)
    landed(far)
    yield
    copier.arrived(over_r)
    far_r = send(slot(over_left).at[low], slot(over_left).at[low], right)
    landed(over_left)
    copier.arrived(over_l)
    far_l = send(slot(over_right).at[high], slot(over_right).at[high], left)
    landed(over_right)
    yield
    copier.arrived(far_r)
    copier.arrived(far_l)
    landed(over_far)


def side_by_side(*relays):
    for _ in zip(*relays):
        pass
    for one in relays:
        for _ in one:
            pass


def gather_inputs(tokens, weights, gains):
    half = weights.shape[0] // 2

    def body(t_ref, w_ref, g_ref, to_ref, wo_ref, go_ref, send_sem, recv_sem, local_sem):
        _, chip, core, sibling = place()
        me = lax.axis_index("exp")
        chips, exps = ring_of(chip), ring_of(me)
        to_chip = lambda p: ("ctx", 2 * p + core)
        to_exp = lambda p: ("exp", p)
        copier = Copier(send_sem, recv_sem, local_sem)
        meet([to_chip(chips[k]) for k in (1, 2, 4)] + [to_exp(p) for p in exps[1:]] + [("ctx", sibling)])
        part = pl.ds(pl.multiple_of(core * half, half), half)
        slot = lambda s: wo_ref.at[s, part]
        both = (
            relay(copier, t_ref, lambda s: to_ref.at[s], ROWS, chips, to_chip),
            relay(
                copier,
                w_ref.at[part],
                slot,
                half,
                exps,
                to_exp,
                lambda s: copier.send(slot(s), slot(s), "ctx", sibling),
            ),
        )
        for one in both:
            next(one)
        copier.keep(t_ref, to_ref.at[chip])
        copier.keep(w_ref, wo_ref.at[me])
        copier.keep(g_ref, go_ref.at[me])
        for p in exps[1:]:
            copier.send(g_ref, go_ref.at[me], *to_exp(p))
        side_by_side(*both)
        copier.finish()

    vmem = pl.BlockSpec(memory_space=pltpu.VMEM)
    return comm_call(
        body,
        "gather_inputs",
        1,
        [
            jax.ShapeDtypeStruct((CHIPS, ROWS, WIDTH), BF16),
            jax.ShapeDtypeStruct((EXP,) + weights.shape, BF16),
            jax.ShapeDtypeStruct((EXP, 8, 128), F32),
        ],
        [tokens, weights, gains],
        32,
        in_specs=[vmem] * 3,
    )


def gather_rows(rows, meta):
    def body(x_ref, m_ref, o_ref, mo_ref, send_sem, recv_sem, local_sem):
        ring = ring_of(lax.axis_index("exp"))
        me = ring[0]
        to_exp = lambda p: ("exp", p)
        copier = Copier(send_sem, recv_sem, local_sem)
        meet([to_exp(p) for p in ring[1:]])
        copier.keep(x_ref, o_ref.at[me])
        copier.keep(m_ref.at[me], mo_ref.at[me])
        for p in ring[1:]:
            copier.send(m_ref.at[p], mo_ref.at[me], *to_exp(p))
        side_by_side(relay(copier, x_ref, lambda s: o_ref.at[s], rows.shape[0], ring, to_exp))
        copier.finish()

    return comm_call(
        body,
        "gather_rows",
        2,
        [
            jax.ShapeDtypeStruct((EXP,) + rows.shape, rows.dtype),
            jax.ShapeDtypeStruct(meta.shape, F32),
        ],
        [rows, meta],
        16,
        in_specs=[pl.BlockSpec(memory_space=pltpu.VMEM)] * 2,
    )


def share_totals(totals, collective_id):
    def body(x_ref, o_ref, send_sem, recv_sem, local_sem):
        _, chip, core, _ = place()
        chips = [lax.rem(chip + d, CHIPS) for d in range(1, CHIPS)]
        copier = Copier(send_sem, recv_sem, local_sem)
        meet([("ctx", 2 * p + core) for p in chips])
        for p in chips:
            copier.send(x_ref, o_ref.at[chip], "ctx", 2 * p + core)
        copier.keep(x_ref, o_ref.at[chip])
        copier.finish()

    return comm_call(
        body,
        "share_totals",
        collective_id,
        [jax.ShapeDtypeStruct((CHIPS,) + totals.shape, F32)],
        [totals],
        7,
    )[0]


def pair_keys(kv):
    def body(x_ref, o_ref, send_sem, recv_sem, local_sem):
        _, _, core, sibling = place()
        copier = Copier(send_sem, recv_sem, local_sem)
        meet([("ctx", sibling)])
        copier.send(x_ref, o_ref.at[:, core], "ctx", sibling)
        copier.keep(x_ref, o_ref.at[:, core])
        copier.finish()

    return comm_call(
        body, "pair_keys", 12, [jax.ShapeDtypeStruct((CHIPS, 2, ROWS, 128), BF16)], [kv], 1,
        in_specs=[pl.BlockSpec(memory_space=pltpu.VMEM)],
    )[0]


def pair_grads(dkv):
    def body(x_ref, o_ref, send_sem, recv_sem, local_sem):
        _, _, _, sibling = place()
        copier = Copier(send_sem, recv_sem, local_sem)
        meet([("ctx", sibling)])
        copier.send(x_ref, o_ref, "ctx", sibling)
        copier.finish()

    return comm_call(
        body, "pair_grads", 13, [jax.ShapeDtypeStruct((CHIPS, ROWS, 128), BF16)], [dkv], 1
    )[0]


def lanes(index):
    return pl.ds(pl.multiple_of(index * 128, 128), 128)


def collect_heads(blocks):
    def body(x_ref, o_ref, send_sem, recv_sem, local_sem):
        _, chip, core, _ = place()
        chips = [lax.rem(chip + d, CHIPS) for d in range(1, CHIPS)]
        copier = Copier(send_sem, recv_sem, local_sem)
        meet([("ctx", 2 * p + core) for p in chips])
        for p in chips:
            copier.send(x_ref.at[p], o_ref.at[:, lanes(chip)], "ctx", 2 * p + core)
        copier.keep(x_ref.at[chip], o_ref.at[:, lanes(chip)])
        copier.finish()

    return comm_call(
        body, "collect_heads", 4, [jax.ShapeDtypeStruct((ROWS, WIDTH), BF16)], [blocks], 7
    )[0]


def spread_grads(rows):
    def body(x_ref, o_ref, send_sem, recv_sem, local_sem):
        _, chip, core, _ = place()
        chips = [lax.rem(chip + d, CHIPS) for d in range(1, CHIPS)]
        copier = Copier(send_sem, recv_sem, local_sem)
        meet([("ctx", 2 * p + core) for p in chips])
        for p in chips:
            copier.send(x_ref.at[:, lanes(p)], o_ref.at[chip], "ctx", 2 * p + core)
        copier.keep(x_ref.at[:, lanes(chip)], o_ref.at[chip])
        copier.finish()

    return comm_call(
        body, "spread_grads", 5, [jax.ShapeDtypeStruct((CHIPS, ROWS, 128), BF16)], [rows], 7
    )[0]


def settle_grads(d_q, d_kv, w_parts, out_part, layer_part):
    def body(
        q_ref, kv_ref, w_ref, a_ref, l_ref, qo_ref, kvo_ref, wo_ref, ao_ref, lo_ref,
        got, joint, traded, done, a_got, a_half, a_other, a_done, send_sem, recv_sem, local_sem,
    ):
        ctx, chip, core, sibling = place()
        me = lax.axis_index("exp")
        chips = [lax.rem(chip + d, CHIPS) for d in range(1, CHIPS)]
        exps = [lax.rem(me + d, EXP) for d in range(1, EXP)]
        others = [lax.rem(ctx + d, CTX) for d in range(1, CTX)]
        copier = Copier(send_sem, recv_sem, local_sem)
        meet([("ctx", p) for p in others] + [("exp", p) for p in exps])
        swapped = copier.send(w_ref.at[1 - core], got, "ctx", sibling)
        spread = [copier.send(a_ref.at[:, lanes(p)], a_got.at[chip], "ctx", 2 * p + core) for p in chips]
        for p in chips:
            copier.send(q_ref.at[p], qo_ref.at[:, lanes(chip)], "ctx", 2 * p + core)
            copier.send(kv_ref.at[p], kvo_ref.at[:, lanes(chip)], "ctx", 2 * p + core)
        copier.keep(q_ref.at[chip], qo_ref.at[:, lanes(chip)])
        copier.keep(kv_ref.at[chip], kvo_ref.at[:, lanes(chip)])
        copier.send(l_ref, lo_ref, "exp", lax.rem(me + 4, EXP))
        copier.arrived(swapped)
        both = w_ref[core].astype(F32) + got[...].astype(F32)
        joint[...] = both.astype(BF16).reshape(EXP, 128, 128)
        trades = [copier.send(joint.at[p], traded.at[me], "exp", p) for p in exps]
        traded[me] = joint[me]
        for at in spread:
            copier.arrived(at)
        a_got[chip] = a_ref[:, lanes(chip)]
        total = a_got[0].astype(F32)
        for c in range(1, CHIPS):
            total = total + a_got[c].astype(F32)
        a_half[...] = total.astype(BF16)
        halves = copier.send(a_half, a_other, "ctx", sibling)
        for at in trades:
            copier.arrived(at)
        total = traded[0].astype(F32)
        for e in range(1, EXP):
            total = total + traded[e].astype(F32)
        done[...] = total.astype(BF16)
        for p in others:
            copier.send(done, wo_ref.at[core, :, lanes(chip)], "ctx", p)
        copier.keep(done, wo_ref.at[core, :, lanes(chip)])
        copier.arrived(halves)
        a_done[...] = (a_half[...].astype(F32) + a_other[...].astype(F32)).astype(BF16)
        for p in chips:
            copier.send(a_done, ao_ref.at[:, lanes(chip)], "ctx", 2 * p + core)
        copier.keep(a_done, ao_ref.at[:, lanes(chip)])
        copier.finish()

    vmem = pl.BlockSpec(memory_space=pltpu.VMEM)
    tile = pltpu.VMEM((128, 128), BF16)
    return pl.pallas_call(
        body,
        name="settle_grads",
        out_shape=[
            jax.ShapeDtypeStruct((ROWS, WIDTH), BF16),
            jax.ShapeDtypeStruct((ROWS, WIDTH), BF16),
            jax.ShapeDtypeStruct((2, 128, WIDTH), BF16),
            jax.ShapeDtypeStruct((128, WIDTH), BF16),
            jax.ShapeDtypeStruct((ROWS, WIDTH), BF16),
        ],
        in_specs=[ANY_SPEC, ANY_SPEC, vmem, vmem, ANY_SPEC],
        out_specs=[ANY_SPEC] * 5,
        scratch_shapes=[
            pltpu.VMEM((WIDTH, 128), BF16),
            pltpu.VMEM((EXP, 128, 128), BF16),
            pltpu.VMEM((EXP, 128, 128), BF16),
            tile,
            pltpu.VMEM((CHIPS, 128, 128), BF16),
            tile,
            tile,
            tile,
            pltpu.SemaphoreType.DMA((53,)),
            pltpu.SemaphoreType.DMA((53,)),
            pltpu.SemaphoreType.DMA((8,)),
        ],
        compiler_params=pltpu.CompilerParams(
            collective_id=6, has_side_effects=True, vmem_limit_bytes=60 * MIB
        ),
    )(d_q, d_kv, w_parts, out_part, layer_part)


def sum_gains(parts):
    def body(x_ref, o_ref, traded, mine, shared, send_sem, recv_sem, local_sem):
        ctx, _, _, _ = place()
        me = lax.axis_index("exp")
        exps = [lax.rem(me + d, EXP) for d in range(1, EXP)]
        others = [lax.rem(ctx + d, CTX) for d in range(1, CTX)]
        copier = Copier(send_sem, recv_sem, local_sem)
        meet([("ctx", p) for p in others] + [("exp", p) for p in exps])
        trades = [copier.send(x_ref.at[p], traded.at[me], "exp", p) for p in exps]
        traded[me] = x_ref[me]
        for at in trades:
            copier.arrived(at)
        total = traded[0]
        for e in range(1, EXP):
            total = total + traded[e]
        mine[...] = total
        shares = [copier.send(mine, shared.at[ctx], "ctx", p) for p in others]
        shared[ctx] = total
        for at in shares:
            copier.arrived(at)
        total = shared[0]
        for c in range(1, CTX):
            total = total + shared[c]
        o_ref[...] = total
        copier.finish()

    vmem = pl.BlockSpec(memory_space=pltpu.VMEM)
    return pl.pallas_call(
        body,
        name="sum_gains",
        out_shape=jax.ShapeDtypeStruct((8, 128), F32),
        in_specs=[vmem],
        out_specs=vmem,
        scratch_shapes=[
            pltpu.VMEM((EXP, 8, 128), F32),
            pltpu.VMEM((8, 128), F32),
            pltpu.VMEM((CTX, 8, 128), F32),
            pltpu.SemaphoreType.DMA((22,)),
            pltpu.SemaphoreType.DMA((22,)),
            pltpu.SemaphoreType.DMA((8,)),
        ],
        compiler_params=pltpu.CompilerParams(
            collective_id=7, has_side_effects=True, vmem_limit_bytes=60 * MIB
        ),
    )(parts)


def settle_experts(rows, d_rows, act, d_gate, d_up, d_parts, layer_parts):
    def body(
        x_ref, r_ref, a_ref, g_ref, u_ref, p_ref, l_ref, gate_out, up_out, down_out, dx_out, keep_out, give_out,
        x_v, r_v, a_v, g_v, u_v, gate, up, down, gate_o, up_o, down_o, gate_a, down_a, up_b, down_b,
        gate_c, down_c, up_d, down_d, mine, from_x, to_z, from_z, layer_mine, layer_from, send_sem, recv_sem, local_sem,
    ):
        _, chip, core, sibling = place()
        me = lax.axis_index("exp")
        zl, x = me // 4, lax.rem(me, 4)
        zh, y = chip // 4, lax.rem(chip, 4)
        at_ctx = lambda z, yy: ("ctx", z * 8 + yy * 2 + core)
        over = at_ctx(1 - zh, y)
        columns = [lax.rem(y + d, 4) for d in (1, 3, 2)]
        spots = [lax.rem(x + d, 4) for d in (1, 3, 2)]
        copier = Copier(send_sem, recv_sem, local_sem)
        loads = []
        for e in range(LOCAL):
            pairs = ((x_ref, x_v), (r_ref, r_v), (a_ref, a_v), (g_ref, g_v), (u_ref, u_v))
            loads.append([copier.keep(src.at[e], dst.at[e]) for src, dst in pairs])
        own_part = copier.keep(p_ref.at[:, x], mine)
        own_layer = copier.keep(l_ref.at[:, x], layer_mine)
        meet(
            [("ctx", sibling), over]
            + [at_ctx(zh, c) for c in columns]
            + [("exp", zl * 4 + p) for p in spots]
            + [("exp", (1 - zl) * 4 + x)]
        )
        x_stage = [copier.send(p_ref.at[:, p], from_x.at[x], "exp", zl * 4 + p) for p in spots]

        def work(e):
            for at in loads[e]:
                copier.kept(at)

            def wide(r, _):
                rows_r = x_v[e, :, pl.ds(pl.multiple_of(r * 256, 256), 256)]
                for d_v, o_v in ((g_v, gate), (u_v, up)):
                    grad = dot(rows_r, d_v[e], TN).astype(BF16)
                    for k in range(4):
                        o_v[k % 2, r // 2, 2 * lax.rem(r, 2) + k // 2, e] = grad[k * 64 : (k + 1) * 64]
                return 0

            lax.fori_loop(0, 4, wide, 0)

            def tall(r, _):
                act_r = a_v[e, :, pl.ds(pl.multiple_of(r * 256, 256), 256)]
                grad = dot(act_r, r_v[e], TN).astype(BF16)
                for k in range(8):
                    down[k % 2, r, k // 2, e] = grad[k * 32 : (k + 1) * 32]
                return 0

            lax.fori_loop(0, 2, tall, 0)
            return [
                copier.send(full.at[1 - core, :, :, e], other.at[:, :, e], "ctx", sibling)
                for full, other in ((gate, gate_o), (up, up_o), (down, down_o))
            ]

        first_a, first_b = [], []

        def join(e, swaps):
            for at in swaps:
                copier.arrived(at)

            def add(c, _):
                z, yy = c // 4, lax.rem(c, 4)
                for full, other in ((gate, gate_o), (up, up_o), (down, down_o)):
                    both = full[core, z, yy, e].astype(F32) + other[z, yy, e].astype(F32)
                    full[core, z, yy, e] = both.astype(BF16)
                return 0

            lax.fori_loop(0, CHIPS, add, 0)
            first_a.append(copier.send(gate.at[core, 1 - zh, :, e], gate_a.at[:, e], *over))
            if e < 2:
                first_a.append(copier.send(down.at[core, 1 - zh, :, e], down_a.at[:, e], *over))
            for c in columns:
                to = at_ctx(zh, c)
                first_b.append(copier.send(up.at[core, :, c, e], up_b.at[y, :, e], *to))
                if e >= 2:
                    first_b.append(copier.send(down.at[core, :, c, e], down_b.at[y, :, e - 2], *to))

        swaps = work(0)
        for e in range(1, LOCAL):
            later = work(e)
            join(e - 1, swaps)
            swaps = later
        join(LOCAL - 1, swaps)

        copier.kept(own_part)
        for at in x_stage:
            copier.arrived(at)
        layer_stage = [copier.send(l_ref.at[:, p], layer_from.at[x], "exp", zl * 4 + p) for p in spots]
        sources = [lax.rem(x + d, 4) for d in (1, 2, 3)]

        def gather_x(r, _):
            at = pl.ds(pl.multiple_of(r * 48, 16), 48)
            keep, give = mine[zl, at, :].astype(F32), mine[1 - zl, at, :].astype(F32)
            for p in sources:
                keep = keep + from_x[p, zl, at, :].astype(F32)
                give = give + from_x[p, 1 - zl, at, :].astype(F32)
            dx_out[at, :] = keep
            to_z[at, :] = give.astype(BF16)
            return 0

        lax.fori_loop(0, 4, gather_x, 0)
        z_stage = copier.send(to_z, from_z, "exp", (1 - zl) * 4 + x)

        for at in first_a:
            copier.arrived(at)

        def sum_a(c, _):
            for e in range(LOCAL):
                both = gate[core, zh, c, e].astype(F32) + gate_a[c, e].astype(F32)
                gate[core, zh, c, e] = both.astype(BF16)
            for e in range(2):
                both = down[core, zh, c, e].astype(F32) + down_a[c, e].astype(F32)
                down[core, zh, c, e] = both.astype(BF16)
            return 0

        lax.fori_loop(0, 4, sum_a, 0)
        second_a = []
        for c in columns:
            to = at_ctx(zh, c)
            second_a.append(copier.send(gate.at[core, zh, c], gate_c.at[y], *to))
            second_a.append(copier.send(down.at[core, zh, c, pl.ds(0, 2)], down_c.at[y], *to))

        for at in first_b:
            copier.arrived(at)
        others = [lax.rem(y + d, 4) for d in (1, 2, 3)]

        def sum_b(e, _):
            for z in range(2):
                total = up[core, z, y, e].astype(F32)
                for c in others:
                    total = total + up_b[c, z, e].astype(F32)
                up[core, z, y, e] = total.astype(BF16)
            return 0

        lax.fori_loop(0, LOCAL, sum_b, 0)

        def sum_b_down(e, _):
            for z in range(2):
                total = down[core, z, y, e + 2].astype(F32)
                for c in others:
                    total = total + down_b[c, z, e].astype(F32)
                down[core, z, y, e + 2] = total.astype(BF16)
            return 0

        lax.fori_loop(0, 2, sum_b_down, 0)
        second_b = [
            copier.send(up.at[core, 1 - zh, y], up_d, *over),
            copier.send(down.at[core, 1 - zh, y, pl.ds(2, 2)], down_d, *over),
        ]

        copier.arrived(z_stage)

        def gather_z(r, _):
            at = pl.ds(pl.multiple_of(r * 48, 16), 48)
            dx_out[at, :] += from_z[at, :].astype(F32)
            return 0

        lax.fori_loop(0, 4, gather_z, 0)
        for at in second_a + second_b:
            copier.arrived(at)

        def final(e, _):
            total = gate[core, zh, y, e].astype(F32)
            for c in others:
                total = total + gate_c[c, e].astype(F32)
            gate_out[e] = total
            up_out[e] = up[core, zh, y, e].astype(F32) + up_d[e].astype(F32)
            return 0

        lax.fori_loop(0, LOCAL, final, 0)
        for e in range(2):
            total = down[core, zh, y, e].astype(F32)
            for c in others:
                total = total + down_c[c, e].astype(F32)
            down_out[e] = total
            down_out[e + 2] = down[core, zh, y, e + 2].astype(F32) + down_d[e].astype(F32)
        copier.kept(own_layer)
        for at in layer_stage:
            copier.arrived(at)

        def gather_layer(r, _):
            at = pl.ds(pl.multiple_of(r * 48, 16), 48)
            keep, give = layer_mine[zl, at, :].astype(F32), layer_mine[1 - zl, at, :].astype(F32)
            for p in sources:
                keep = keep + layer_from[p, zl, at, :].astype(F32)
                give = give + layer_from[p, 1 - zl, at, :].astype(F32)
            keep_out[at, :] = keep
            give_out[at, :] = give.astype(BF16)
            return 0

        lax.fori_loop(0, 4, gather_layer, 0)
        copier.finish()

    vmem = pl.BlockSpec(memory_space=pltpu.VMEM)
    buf = lambda *shape: pltpu.VMEM(shape, BF16)
    wide, tall = (64, FF), (32, WIDTH)
    return pl.pallas_call(
        body,
        name="settle_experts",
        out_shape=[
            jax.ShapeDtypeStruct((LOCAL,) + wide, F32),
            jax.ShapeDtypeStruct((LOCAL,) + wide, F32),
            jax.ShapeDtypeStruct((LOCAL,) + tall, F32),
            jax.ShapeDtypeStruct((ROWS, WIDTH), F32),
            jax.ShapeDtypeStruct((ROWS, WIDTH), F32),
            jax.ShapeDtypeStruct((ROWS, WIDTH), BF16),
        ],
        in_specs=[ANY_SPEC] * 7,
        out_specs=[vmem] * 6,
        scratch_shapes=[
            buf(LOCAL, SLOTS, WIDTH),
            buf(LOCAL, SLOTS, WIDTH),
            buf(LOCAL, SLOTS, FF),
            buf(LOCAL, SLOTS, FF),
            buf(LOCAL, SLOTS, FF),
            buf(2, 2, 4, LOCAL, *wide),
            buf(2, 2, 4, LOCAL, *wide),
            buf(2, 2, 4, LOCAL, *tall),
            buf(2, 4, LOCAL, *wide),
            buf(2, 4, LOCAL, *wide),
            buf(2, 4, LOCAL, *tall),
            buf(4, LOCAL, *wide),
            buf(4, 2, *tall),
            buf(4, 2, LOCAL, *wide),
            buf(4, 2, 2, *tall),
            buf(4, LOCAL, *wide),
            buf(4, 2, *tall),
            buf(LOCAL, *wide),
            buf(2, *tall),
            buf(2, ROWS, WIDTH),
            buf(4, 2, ROWS, WIDTH),
            buf(ROWS, WIDTH),
            buf(ROWS, WIDTH),
            buf(2, ROWS, WIDTH),
            buf(4, 2, ROWS, WIDTH),
            pltpu.SemaphoreType.DMA((51,)),
            pltpu.SemaphoreType.DMA((51,)),
            pltpu.SemaphoreType.DMA((24,)),
        ],
        compiler_params=pltpu.CompilerParams(
            collective_id=8, has_side_effects=True, vmem_limit_bytes=62 * MIB
        ),
    )(rows, d_rows, act, d_gate, d_up, d_parts, layer_parts)


def compute_call(body, name, outs, ins, vmem=60, **kw):
    return pl.pallas_call(
        body,
        name=name,
        out_shape=outs,
        compiler_params=pltpu.CompilerParams(vmem_limit_bytes=vmem * MIB),
        **kw,
    )(*ins)


def row_scale(total, width):
    return lax.rsqrt(total * (1.0 / width) + EPSILON)


def key_lanes():
    return lax.broadcasted_iota(jnp.int32, (1, 128), 1) < 64


def turn(values, cosine, sine):
    first = lax.rem(lax.broadcasted_iota(jnp.int32, (1, 128), 1), 64) < 32
    return values * cosine + jnp.where(first, -pltpu.roll(values, 96, 1), pltpu.roll(values, 32, 1)) * sine


def across(select, values):
    return lax.dot_general(
        select, values, (NT, ((), ())), precision=lax.Precision.HIGHEST, preferred_element_type=F32
    )


def both_totals(left, right):
    row_id = lax.broadcasted_iota(jnp.int32, (8, 128), 0)
    ones = jnp.where(row_id == 0, 1.0, 0.0)
    keys = jnp.where((row_id == 1) & key_lanes(), 1.0, 0.0)
    return (across(ones, left) + across(keys, right))[0:2, :]


def down_rows(values, row, width=128):
    chosen = lax.broadcasted_iota(jnp.int32, (2, width), 0) == row
    return lax.dot_general(
        values,
        jnp.where(chosen, 1.0, 0.0),
        (TN, ((), ())),
        precision=lax.Precision.HIGHEST,
        preferred_element_type=F32,
    )


def own_chip():
    return lax.axis_index("ctx") // 2


def project(rows, weights, gains, chip):
    step = 2 * ROWS

    def body(c_ref, x_ref, wq_ref, wk_ref, wv_ref, g_ref, n_ref, q_ref, kv_ref, s_ref, w_own):
        @pl.when(pl.program_id(0) == 0)
        def _():
            odd = lax.rem(c_ref[0], 2) == 1
            wk, wv = wk_ref[...].astype(F32), wv_ref[...].astype(F32)
            wk = jnp.where(odd, pltpu.roll(wk, 64, 1), wk)
            wv = jnp.where(odd, wv, pltpu.roll(wv, 64, 1))
            w_own[:, 0:128] = wq_ref[...]
            w_own[:, 128:256] = jnp.where(key_lanes(), wk, wv).astype(BF16)

        x = x_ref[...].astype(F32)
        scale = row_scale(jnp.sum(x * x, axis=1, keepdims=True), WIDTH)
        normed = (x * scale * g_ref[0:1, :]).astype(BF16)
        n_ref[...] = normed
        both = dot(normed, w_own[...])
        q, kv = both[:, 0:128], both[:, 128:256]
        q_ref[...] = q
        kv_ref[...] = kv
        for k in range(2):
            at = slice(k * ROWS, (k + 1) * ROWS)
            s_ref[k] = both_totals(q[at] * q[at], kv[at] * kv[at])

    def each(*shape):
        return pl.BlockSpec((step,) + shape, lambda i, c: (i, 0))

    return pl.pallas_call(
        body,
        name="project",
        out_shape=[
            jax.ShapeDtypeStruct((CHIPS * ROWS, WIDTH), BF16),
            jax.ShapeDtypeStruct((CHIPS * ROWS, 128), F32),
            jax.ShapeDtypeStruct((CHIPS * ROWS, 128), F32),
            jax.ShapeDtypeStruct((CHIPS, 2, ROWS), F32),
        ],
        grid_spec=pltpu.PrefetchScalarGridSpec(
            num_scalar_prefetch=1,
            grid=(CHIPS // 2,),
            in_specs=[
                each(WIDTH),
                pl.BlockSpec((WIDTH, 128), lambda i, c: (0, c[0])),
                pl.BlockSpec((WIDTH, 128), lambda i, c: (0, 8 + c[0] // 2)),
                pl.BlockSpec((WIDTH, 128), lambda i, c: (0, 12 + c[0] // 2)),
                pl.BlockSpec((8, WIDTH), lambda i, c: (0, 0)),
            ],
            out_specs=[
                each(WIDTH),
                each(128),
                each(128),
                pl.BlockSpec((2, 2, ROWS), lambda i, c: (i, 0, 0)),
            ],
            scratch_shapes=[pltpu.VMEM((WIDTH, 256), BF16)],
        ),
        compiler_params=pltpu.CompilerParams(vmem_limit_bytes=60 * MIB),
    )(chip, rows, weights, weights, weights, gains)


def turn_heads(q_lin, kv_lin, totals, places, gains):
    def body(q_ref, kv_ref, t_ref, p_ref, g_ref, qo_ref, kvo_ref, s_ref, c_ref, n_ref):
        gain = g_ref[own_chip()]
        keys = key_lanes()
        lane = lax.broadcasted_iota(jnp.int32, (1, 128), 1)
        freq = jnp.exp(lax.rem(lane, 32).astype(F32) * (-2.0 / 64 * 9.210340371976184))
        shift = jnp.where(keys, 0.0, 1.5707963267948966)

        def one(i, _):
            place_i = p_ref[i]
            offset = down_rows(place_i, 0) - down_rows(place_i, 1)
            mixed = jnp.cos(offset * freq - shift)
            other = pltpu.roll(mixed, 64, 1)
            cos, sin = jnp.where(keys, mixed, other), jnp.where(keys, other, mixed)
            c_ref[i] = cos
            n_ref[i] = sin
            squares = t_ref[0, i]
            for c in range(1, CHIPS):
                squares = squares + t_ref[c, i]
            s_ref[i] = squares
            q = q_ref[i] * row_scale(down_rows(squares, 0), WIDTH) * gain[1:2, :]
            q = turn(q, cos, sin).astype(BF16).astype(F32)
            qo_ref[i] = (q * 0.125).astype(BF16)
            scale = jnp.where(keys, row_scale(down_rows(squares, 1), WIDTH // 2), 1.0)
            kv = kv_ref[i] * scale * gain[2:3, :]
            kvo_ref[i] = turn(kv, jnp.where(keys, cos, 1.0), jnp.where(keys, sin, 0.0)).astype(BF16)
            return 0

        lax.fori_loop(0, CHIPS, one, 0)

    return compute_call(
        body,
        "turn_heads",
        [jax.ShapeDtypeStruct((CHIPS, ROWS, 128), BF16)] * 2
        + [jax.ShapeDtypeStruct((CHIPS, 2, ROWS), F32)]
        + [jax.ShapeDtypeStruct((CHIPS, ROWS, 128), F32)] * 2,
        [q_lin, kv_lin, totals, places, gains],
    )


def route(routes_t, logits_t):
    def body(r_ref, l_ref, m_ref):
        logits = l_ref[...]
        raised = jnp.exp(logits - jnp.max(logits, axis=0, keepdims=True))
        gates = raised / jnp.sum(raised, axis=0, keepdims=True)
        experts = lax.broadcasted_iota(jnp.int32, (32, ROWS), 0)
        member = jnp.zeros((32, ROWS), F32)
        weight = jnp.zeros((32, ROWS), F32)
        for c in range(8):
            hit = r_ref[c : c + 1, :] == experts
            member = member + jnp.where(hit, 1.0, 0.0)
            weight = weight + jnp.where(hit, gates[c : c + 1, :], 0.0)
        before = lax.broadcasted_iota(jnp.int32, (ROWS, ROWS), 0) < lax.broadcasted_iota(
            jnp.int32, (ROWS, ROWS), 1
        )
        rank = dot(member.astype(BF16), jnp.where(before, 1.0, 0.0).astype(BF16))
        spot = jnp.where(member > 0.5, rank, -1.0)
        for e in range(EXP):
            m_ref[e, 0:4, :] = spot[e * 4 : e * 4 + 4, :]
            m_ref[e, 4:8, :] = weight[e * 4 : e * 4 + 4, :]

    return compute_call(
        body, "route", [jax.ShapeDtypeStruct((EXP, 8, ROWS), F32)], [routes_t, logits_t]
    )[0]


def split_kv(kv_ref, klo, khi, vlo, vhi):
    low = key_lanes()
    both = kv_ref[...].astype(F32)
    other = pltpu.roll(both, 64, 1)
    if klo is not None:
        klo[...] = jnp.where(low, both, 0.0).astype(BF16)
        khi[...] = jnp.where(low, 0.0, other).astype(BF16)
    vlo[...] = jnp.where(low, other, 0.0).astype(BF16)
    vhi[...] = jnp.where(low, 0.0, both).astype(BF16)


def attend(q, kv, key_pos, places, first_chunk):
    def body(first_ref, q_ref, kv_ref, kp_ref, p_ref, o_ref, of_ref, l_ref, klo, khi, vlo, vhi):
        i = pl.program_id(0)

        @pl.when(i == 0)
        def _():
            split_kv(kv_ref, klo, khi, vlo, vhi)

        q_block = q_ref[0]
        at_row, start_row = [
            jnp.concatenate([down_rows(p_ref[0], k)] * (CHUNK // 128), axis=1) for k in range(2)
        ]
        low = key_lanes()

        def step(p, carry):
            m0, m1, l0, l1, acc = carry
            rows = pl.ds(pl.multiple_of(p * CHUNK, CHUNK), CHUNK)
            at_key = kp_ref[p]
            seen = (at_key >= start_row) & (at_key <= at_row)
            s0 = jnp.where(seen, dot(q_block, klo[rows, :], NT), MASKED)
            s1 = jnp.where(seen, dot(q_block, khi[rows, :], NT), MASKED)
            n0 = jnp.maximum(m0, jnp.max(s0, axis=1, keepdims=True))
            n1 = jnp.maximum(m1, jnp.max(s1, axis=1, keepdims=True))
            p0 = jnp.exp(s0 - n0)
            p1 = jnp.exp(s1 - n1)
            a0 = jnp.exp(m0 - n0)
            a1 = jnp.exp(m1 - n1)
            l0 = l0 * a0 + jnp.sum(p0, axis=1, keepdims=True)
            l1 = l1 * a1 + jnp.sum(p1, axis=1, keepdims=True)
            acc = acc * jnp.where(low, a0, a1)
            acc = acc + dot(p0.astype(BF16), vlo[rows, :]) + dot(p1.astype(BF16), vhi[rows, :])
            return n0, n1, l0, l1, acc

        top = jnp.full((ROWS, 1), MASKED, F32)
        none = jnp.zeros((ROWS, 1), F32)
        m0, m1, l0, l1, acc = lax.fori_loop(
            first_ref[i], i + 1, step, (top, top, none, none, jnp.zeros((ROWS, 128), F32))
        )
        out = acc / jnp.where(low, l0, l1)
        of_ref[0] = out
        o_ref[0] = out.astype(BF16)
        l_ref[0] = jnp.where(low, m0 + jnp.log(l0), m1 + jnp.log(l1))

    def block(*shape):
        return pl.BlockSpec((1,) + shape, lambda i, first: (i, 0, 0))

    return pl.pallas_call(
        body,
        name="attend",
        out_shape=[
            jax.ShapeDtypeStruct((CHIPS, ROWS, 128), BF16),
            jax.ShapeDtypeStruct((CHIPS, ROWS, 128), F32),
            jax.ShapeDtypeStruct((CHIPS, ROWS, 128), F32),
        ],
        grid_spec=pltpu.PrefetchScalarGridSpec(
            num_scalar_prefetch=1,
            grid=(CHIPS,),
            in_specs=[
                block(ROWS, 128),
                pl.BlockSpec((KEYS, 128), lambda i, first: (0, 0)),
                pl.BlockSpec((CHIPS, 1, CHUNK), lambda i, first: (0, 0, 0)),
                block(2, ROWS),
            ],
            out_specs=[block(ROWS, 128)] * 3,
            scratch_shapes=[pltpu.VMEM((KEYS, 128), BF16)] * 4,
        ),
        compiler_params=pltpu.CompilerParams(vmem_limit_bytes=60 * MIB),
    )(first_chunk, q, kv, key_pos, places)


def attend_back(q, kv, d_out, out, log_total, key_pos, places, first_chunk):
    def body(
        first_ref, q_ref, kv_ref, do_ref, o_ref, l_ref, kp_ref, p_ref,
        dq_ref, mine_ref, other_ref, klo, khi, vlo, vhi, acc, key_at,
    ):
        i = pl.program_id(0)

        @pl.when(i == 0)
        def _():
            split_kv(kv_ref, klo, khi, vlo, vhi)
            acc[...] = jnp.zeros_like(acc)

            def place_keys(p, _):
                both = jnp.concatenate([kp_ref[p], kp_ref[p]], axis=0)
                key_at[pl.ds(pl.multiple_of(p * CHUNK, CHUNK), CHUNK), :] = down_rows(both, 0, ROWS)
                return 0

            lax.fori_loop(0, CHIPS, place_keys, 0)

        low = key_lanes()
        q_block, do_block = q_ref[0], do_ref[0]
        do_wide, q_wide = do_block.astype(F32), q_block.astype(F32)
        q_turned, do_turned = pltpu.roll(q_wide, 64, 1), pltpu.roll(do_wide, 64, 1)
        right = jnp.concatenate(
            [
                jnp.where(low, q_wide, 0.0).astype(BF16),
                jnp.where(low, q_turned, 0.0).astype(BF16),
                jnp.where(low, 0.0, do_turned).astype(BF16),
                jnp.where(low, 0.0, do_wide).astype(BF16),
            ],
            axis=0,
        )
        row_id = lax.broadcasted_iota(jnp.int32, (8, 128), 0)
        lane_id = lax.broadcasted_iota(jnp.int32, (8, 128), 1)
        halves = jnp.where(lane_id // 64 == row_id, 1.0, 0.0)
        picks = jnp.where(lane_id == 64 * row_id, 1.0, 0.0)

        delta = across(halves, do_wide * o_ref[0])
        total = across(picks, l_ref[0])
        at_row, start_row = p_ref[0, 0:1, :], p_ref[0, 1:2, :]

        def step(p, dq):
            rows = pl.ds(pl.multiple_of(p * CHUNK, CHUNK), CHUNK)
            at_key = key_at[rows, :]
            seen = (at_key >= start_row) & (at_key <= at_row)
            k0, k1 = klo[rows, :], khi[rows, :]
            s0 = jnp.where(seen, dot(k0, q_block, NT), MASKED)
            s1 = jnp.where(seen, dot(k1, q_block, NT), MASKED)
            p0 = jnp.exp(s0 - total[0:1, :])
            p1 = jnp.exp(s1 - total[1:2, :])
            d0 = (p0 * (dot(vlo[rows, :], do_block, NT) - delta[0:1, :])).astype(BF16)
            d1 = (p1 * (dot(vhi[rows, :], do_block, NT) - delta[1:2, :])).astype(BF16)
            left = jnp.concatenate([d0, d1, p0.astype(BF16), p1.astype(BF16)], axis=1)
            acc[rows, :] += dot(left, right)
            return dq + dot(d0, k0, TN) + dot(d1, k1, TN)

        dq = lax.fori_loop(first_ref[i], i + 1, step, jnp.zeros((ROWS, 128), F32))
        dq_ref[0] = dq * 0.125

        @pl.when(i == CHIPS - 1)
        def _():
            core = lax.rem(lax.axis_index("ctx"), 2)

            def part(s, _):
                mine = pl.ds(pl.multiple_of((2 * s + core) * ROWS, ROWS), ROWS)
                other = pl.ds(pl.multiple_of((2 * s + 1 - core) * ROWS, ROWS), ROWS)
                mine_ref[s] = acc[mine, :]
                other_ref[s] = acc[other, :].astype(BF16)
                return 0

            lax.fori_loop(0, CHIPS, part, 0)

    def block(*shape):
        return pl.BlockSpec((1,) + shape, lambda i, first: (i, 0, 0))

    whole = pl.BlockSpec((KEYS, 128), lambda i, first: (0, 0))
    return pl.pallas_call(
        body,
        name="attend_back",
        out_shape=[
            jax.ShapeDtypeStruct((CHIPS, ROWS, 128), F32),
            jax.ShapeDtypeStruct((CHIPS, ROWS, 128), F32),
            jax.ShapeDtypeStruct((CHIPS, ROWS, 128), BF16),
        ],
        grid_spec=pltpu.PrefetchScalarGridSpec(
            num_scalar_prefetch=1,
            grid=(CHIPS,),
            in_specs=[
                block(ROWS, 128),
                whole,
                block(ROWS, 128),
                block(ROWS, 128),
                block(ROWS, 128),
                pl.BlockSpec((CHIPS, 1, CHUNK), lambda i, first: (0, 0, 0)),
                block(2, ROWS),
            ],
            out_specs=[block(ROWS, 128)] + [pl.BlockSpec((CHIPS, ROWS, 128), lambda i, first: (0, 0, 0))] * 2,
            scratch_shapes=[pltpu.VMEM((KEYS, 128), BF16)] * 4
            + [pltpu.VMEM((KEYS, 128), F32), pltpu.VMEM((KEYS, ROWS), F32)],
        ),
        compiler_params=pltpu.CompilerParams(vmem_limit_bytes=60 * MIB),
    )(first_chunk, q, kv, d_out, out, log_total, key_pos, places)


def whole(*shape):
    return pl.BlockSpec(shape, lambda i: (0,) * len(shape))


def columns(block, width=WIDTH):
    return pl.BlockSpec((WIDTH, width), lambda i: (0, block))


def finish_attention(attended, w_out, tokens, gains):
    def body(a_ref, w_ref, t_ref, g_ref, r_ref, f_ref):
        branch = dot(a_ref[...], w_ref[...]).astype(BF16).astype(F32)
        resid = t_ref[...].astype(F32) + branch
        r_ref[...] = resid
        scale = row_scale(jnp.sum(resid * resid, axis=1, keepdims=True), WIDTH)
        f_ref[...] = (resid * scale * g_ref[3:4, :]).astype(BF16)

    return compute_call(
        body,
        "finish_attention",
        [jax.ShapeDtypeStruct((ROWS, WIDTH), F32), jax.ShapeDtypeStruct((ROWS, WIDTH), BF16)],
        [attended, w_out, tokens, gains],
        grid=(1,),
        in_specs=[whole(ROWS, WIDTH), columns(2), whole(ROWS, WIDTH), whole(8, WIDTH)],
        out_specs=[whole(ROWS, WIDTH)] * 2,
    )


def experts(rows, grads, meta, meta_t, w_gate, w_up, w_down):
    half = SLOTS // 2

    def body(
        x_ref, g_ref, m_ref, mt_ref, wg_ref, wu_ref, wd_ref,
        xin_ref, dr_ref, act_ref, dg_ref, du_ref, out_ref, dx_ref,
        made, back, weight,
    ):
        e = pl.program_id(0)

        @pl.when(e == 0)
        def _():
            slot_id = lax.broadcasted_iota(jnp.int32, (PAIR_CAP, PAIR_ROWS), 0).astype(F32)

            def pick(p, _):
                meta_p = m_ref[p]
                parts, gates = [], []
                for k in range(LOCAL):
                    hit = slot_id == meta_p[k : k + 1, :]
                    parts.append(jnp.where(hit, 1.0, 0.0).astype(BF16))
                    gates.append(
                        jnp.sum(jnp.where(hit, meta_p[4 + k : 5 + k, :], 0.0), axis=1, keepdims=True)
                    )
                chosen = jnp.concatenate(parts, axis=0)
                rows_p = dot(chosen, x_ref[p]).astype(BF16)
                grads_p = dot(chosen, g_ref[p])
                at = pl.ds(pl.multiple_of(p * PAIR_CAP, PAIR_CAP), PAIR_CAP)
                for k in range(LOCAL):
                    piece = slice(k * PAIR_CAP, (k + 1) * PAIR_CAP)
                    xin_ref[k, at, :] = rows_p[piece]
                    dr_ref[k, at, :] = (grads_p[piece] * gates[k]).astype(BF16)
                    weight[k, at, :] = gates[k]
                return 0

            lax.fori_loop(0, PAIRS, pick, 0)

        def work(h, _):
            at = pl.ds(pl.multiple_of(h * half, half), half)
            x = xin_ref[e, at, :]
            dr = dr_ref[e, at, :]
            gate = dot(x, wg_ref[0])
            up = dot(x, wu_ref[0])
            sig = jax.nn.sigmoid(gate)
            silu = gate * sig
            act = (silu * up).astype(BF16)
            act_ref[0, at, :] = act
            d_act = dot(dr, wd_ref[0], NT)
            d_gate = (d_act * up * sig * (1.0 + gate * (1.0 - sig))).astype(BF16)
            d_up = (d_act * silu).astype(BF16)
            dg_ref[0, at, :] = d_gate
            du_ref[0, at, :] = d_up
            y = (dot(act, wd_ref[0]) * weight[e, at, :]).astype(BF16)
            dch = (dot(d_gate, wg_ref[0], NT) + dot(d_up, wu_ref[0], NT)).astype(BF16)
            place_at = pl.ds(pl.multiple_of(e * PAIR_CAP, PAIR_CAP), PAIR_CAP)
            for k in range(2):
                piece = slice(k * PAIR_CAP, (k + 1) * PAIR_CAP)
                made[2 * h + k, place_at, :] = y[piece]
                back[2 * h + k, place_at, :] = dch[piece]
            return 0

        lax.fori_loop(0, 2, work, 0)

        @pl.when(e == LOCAL - 1)
        def _():
            lane_id = lax.broadcasted_iota(jnp.int32, (PAIR_ROWS, PAIR_SLOTS), 1).astype(F32)

            def give(p, _):
                meta_p = mt_ref[p]
                chosen = jnp.zeros((PAIR_ROWS, PAIR_SLOTS), F32)
                for k in range(LOCAL):
                    spot = meta_p[:, k : k + 1]
                    lane = jnp.where(spot < 0.0, -1.0, spot + float(k * PAIR_CAP))
                    chosen = chosen + jnp.where(lane_id == lane, 1.0, 0.0)
                chosen = chosen.astype(BF16)
                dx_ref[p] = dot(chosen, back[p]).astype(BF16)
                out_ref[p] = dot(chosen, made[p]).astype(BF16)
                return 0

            lax.fori_loop(0, PAIRS, give, 0)

    def fixed(*shape):
        return pl.BlockSpec(shape, lambda e: (0,) * len(shape), pipeline_mode=pl.Buffered(1))

    def each(*shape):
        return pl.BlockSpec((1,) + shape, lambda e: (e, 0, 0))

    return compute_call(
        body,
        "experts",
        [
            jax.ShapeDtypeStruct((LOCAL, SLOTS, WIDTH), BF16),
            jax.ShapeDtypeStruct((LOCAL, SLOTS, WIDTH), BF16),
            jax.ShapeDtypeStruct((LOCAL, SLOTS, FF), BF16),
            jax.ShapeDtypeStruct((LOCAL, SLOTS, FF), BF16),
            jax.ShapeDtypeStruct((LOCAL, SLOTS, FF), BF16),
            jax.ShapeDtypeStruct((PAIRS, PAIR_ROWS, WIDTH), BF16),
            jax.ShapeDtypeStruct((PAIRS, PAIR_ROWS, WIDTH), BF16),
        ],
        [rows, grads, meta, meta_t, w_gate, w_up, w_down],
        vmem=60,
        grid=(LOCAL,),
        in_specs=[
            fixed(PAIRS, PAIR_ROWS, WIDTH),
            fixed(PAIRS, PAIR_ROWS, WIDTH),
            fixed(PAIRS, 8, PAIR_ROWS),
            fixed(PAIRS, PAIR_ROWS, 8),
            each(WIDTH, FF),
            each(WIDTH, FF),
            each(FF, WIDTH),
        ],
        out_specs=[
            fixed(LOCAL, SLOTS, WIDTH),
            fixed(LOCAL, SLOTS, WIDTH),
            each(SLOTS, FF),
            each(SLOTS, FF),
            each(SLOTS, FF),
            fixed(PAIRS, PAIR_ROWS, WIDTH),
            fixed(PAIRS, PAIR_ROWS, WIDTH),
        ],
        scratch_shapes=[
            pltpu.VMEM((PAIRS, PAIR_SLOTS, WIDTH), BF16),
            pltpu.VMEM((PAIRS, PAIR_SLOTS, WIDTH), BF16),
            pltpu.VMEM((LOCAL, SLOTS, 1), F32),
        ],
    )


def norm_back(values, total_squares, width, weighted, mask=None):
    scale = row_scale(total_squares, width)
    inner = jnp.sum(weighted * values, axis=1, keepdims=True) * (1.0 / width)
    return scale * weighted - values * (scale * scale * scale) * inner, scale


def back_to_branch(d_ffn, resid, cotangent, gains, w_out):
    def body(p_ref, r_ref, c_ref, g_ref, w_ref, dr_ref, db_ref, da_ref, gg_ref):
        incoming = p_ref[...]
        resid_v = r_ref[...]
        squares = jnp.sum(resid_v * resid_v, axis=1, keepdims=True)
        d_norm, scale = norm_back(resid_v, squares, WIDTH, incoming * g_ref[3:4, :])
        gg_ref[...] = jnp.sum(incoming * resid_v * scale, axis=0, keepdims=True)
        d_resid = c_ref[...].astype(F32) + d_norm
        dr_ref[...] = d_resid
        d_branch = d_resid.astype(BF16)
        db_ref[...] = d_branch
        da_ref[...] = dot(d_branch, w_ref[...], NT).astype(BF16)

    return compute_call(
        body,
        "back_to_branch",
        [
            jax.ShapeDtypeStruct((ROWS, WIDTH), F32),
            jax.ShapeDtypeStruct((ROWS, WIDTH), BF16),
            jax.ShapeDtypeStruct((ROWS, WIDTH), BF16),
            jax.ShapeDtypeStruct((1, WIDTH), F32),
        ],
        [d_ffn, resid, cotangent, gains, w_out],
        grid=(1,),
        in_specs=[whole(ROWS, WIDTH)] * 3 + [whole(8, WIDTH), columns(2)],
        out_specs=[whole(ROWS, WIDTH)] * 3 + [whole(1, WIDTH)],
    )


def out_grads(attended, d_branch):
    def body(a_ref, d_ref, o_ref):
        def part(r, _):
            at = pl.ds(pl.multiple_of(r * 256, 256), 256)
            o_ref[at, :] = dot(a_ref[:, at], d_ref[...], TN).astype(BF16)
            return 0

        lax.fori_loop(0, 4, part, 0)

    return compute_call(
        body, "out_grads", [jax.ShapeDtypeStruct((WIDTH, WIDTH), BF16)], [attended, d_branch]
    )[0]


def unturn_heads(dq, dkv, dkv_other, q_lin, kv_lin, gains, cosine, sine):
    def body(dq_ref, dk_ref, do_ref, q_ref, kv_ref, g_ref, c_ref, n_ref, eq_ref, ek_ref, s_ref):
        gain = g_ref[own_chip()]
        keys = key_lanes()

        def one(i, _):
            cos, sin = c_ref[i], -n_ref[i]
            e_q = turn(dq_ref[i], cos, sin)
            eq_ref[i] = e_q
            both = dk_ref[i] + do_ref[i].astype(F32)
            e_kv = turn(both, jnp.where(keys, cos, 1.0), jnp.where(keys, sin, 0.0))
            ek_ref[i] = e_kv
            s_ref[i] = both_totals(e_q * gain[1:2, :] * q_ref[i], e_kv * gain[2:3, :] * kv_ref[i])
            return 0

        lax.fori_loop(0, CHIPS, one, 0)

    return compute_call(
        body,
        "unturn_heads",
        [jax.ShapeDtypeStruct((CHIPS, ROWS, 128), F32)] * 2 + [jax.ShapeDtypeStruct((CHIPS, 2, ROWS), F32)],
        [dq, dkv, dkv_other, q_lin, kv_lin, gains, cosine, sine],
    )


def head_grads(e_q, e_kv, inner, squares, q_lin, kv_lin, normed, gains):
    def body(eq_ref, ek_ref, i_ref, s_ref, q_ref, kv_ref, n_ref, g_ref, dq_ref, dk_ref, w_ref, gg_ref):
        gain = g_ref[own_chip()]
        keys = key_lanes()

        def one(i, carry):
            q_sum, kv_sum = carry
            inner = i_ref[0, i]
            for c in range(1, CHIPS):
                inner = inner + i_ref[c, i]
            q_scale = row_scale(down_rows(s_ref[i], 0), WIDTH)
            k_scale = row_scale(down_rows(s_ref[i], 1), WIDTH // 2)
            q_cut = q_scale * q_scale * q_scale * down_rows(inner, 0) * (1.0 / WIDTH)
            k_cut = k_scale * k_scale * k_scale * down_rows(inner, 1) * (2.0 / WIDTH)
            kv_scale = jnp.where(keys, k_scale, 1.0)
            k_cut = jnp.where(keys, k_cut, 0.0)
            q, e = q_ref[i], eq_ref[i]
            dq_ref[i] = (q_scale * (e * gain[1:2, :]) - q * q_cut).astype(BF16)
            q_sum = q_sum + jnp.sum(e * q * q_scale, axis=0, keepdims=True)
            kv, e = kv_ref[i], ek_ref[i]
            dk_ref[i] = (kv_scale * (e * gain[2:3, :]) - kv * k_cut).astype(BF16)
            kv_sum = kv_sum + jnp.sum(e * kv * kv_scale, axis=0, keepdims=True)
            return q_sum, kv_sum

        none = jnp.zeros((1, 128), F32)
        q_sum, kv_sum = lax.fori_loop(0, CHIPS, one, (none, none))
        gg_ref[...] = jnp.concatenate([q_sum, kv_sum], axis=0)
        d_q = dq_ref[...].reshape(CHIPS * ROWS, 128)
        d_kv = dk_ref[...].reshape(CHIPS * ROWS, 128)

        def part(r, _):
            at = pl.ds(pl.multiple_of(r * 256, 256), 256)
            n = n_ref[:, at]
            w_ref[0, at, :] = dot(n, d_q, TN).astype(BF16)
            w_ref[1, at, :] = dot(n, d_kv, TN).astype(BF16)
            return 0

        lax.fori_loop(0, 4, part, 0)

    return compute_call(
        body,
        "head_grads",
        [jax.ShapeDtypeStruct((CHIPS, ROWS, 128), BF16)] * 2
        + [jax.ShapeDtypeStruct((2, WIDTH, 128), BF16), jax.ShapeDtypeStruct((2, 128), F32)],
        [e_q, e_kv, inner, squares, q_lin, kv_lin, normed, gains],
    )


def apart(pieces):
    first, second = pieces
    keys = key_lanes()
    return (
        jnp.where(keys, first, pltpu.roll(second, 64, 1)),
        jnp.where(keys, pltpu.roll(first, 64, 1), second),
    )


def back_to_input(d_q, d_kv, tokens, d_resid, weights, gains):
    def body(dq_ref, dkv_ref, t_ref, r_ref, w_ref, g_ref, di_ref, gg_ref):
        keys, values = [], []
        for c in range(4):
            k, v = apart([dkv_ref[:, (2 * c + j) * 128 : (2 * c + j + 1) * 128].astype(F32) for j in range(2)])
            keys.append(k.astype(BF16))
            values.append(v.astype(BF16))
        left = jnp.concatenate([dq_ref[...]] + keys + values, axis=1)
        d_normed = dot(left, w_ref[...], NT)
        d_normed = d_normed.astype(BF16).astype(F32)
        x = t_ref[...].astype(F32)
        squares = jnp.sum(x * x, axis=1, keepdims=True)
        d_norm, scale = norm_back(x, squares, WIDTH, d_normed * g_ref[0:1, :])
        gg_ref[...] = jnp.sum(d_normed * x * scale, axis=0, keepdims=True)
        di_ref[...] = r_ref[...] + d_norm

    return compute_call(
        body,
        "back_to_input",
        [jax.ShapeDtypeStruct((ROWS, WIDTH), F32), jax.ShapeDtypeStruct((1, WIDTH), F32)],
        [d_q, d_kv, tokens, d_resid, weights, gains],
        grid=(1,),
        in_specs=[whole(ROWS, WIDTH)] * 4 + [columns(0, 2 * WIDTH), whole(8, WIDTH)],
        out_specs=[whole(ROWS, WIDTH), whole(1, WIDTH)],
    )


def deliver(resid, layer_keep, layer_got, dense, out_grad, gain_sums, expert_sums):
    def body(r_ref, k_ref, g_ref, d_ref, o_ref, s_ref, eg_ref, eu_ref, ed_ref, lo, wq, wk, wv, wo, ga, gq, gk, gf, eg, eu, ed):
        lo[...] = (r_ref[...] + k_ref[...] + g_ref[...].astype(F32)).astype(BF16)
        wq[...] = d_ref[0].astype(F32)
        for c in range(4):
            k, v = apart([d_ref[1, :, (2 * c + j) * 128 : (2 * c + j + 1) * 128].astype(F32) for j in range(2)])
            wk[:, c * 128 : (c + 1) * 128] = k
            wv[:, c * 128 : (c + 1) * 128] = v
        wo[...] = o_ref[...].astype(F32)
        ga[...] = s_ref[0:1, :]
        gq[...] = s_ref[1:2, :]
        gk[...] = s_ref[2:3, 0:64]
        gf[...] = s_ref[3:4, :]
        eg[...] = eg_ref[...]
        eu[...] = eu_ref[...]
        ed[...] = ed_ref[...]

    return compute_call(
        body,
        "deliver",
        [
            jax.ShapeDtypeStruct((ROWS, WIDTH), BF16),
            jax.ShapeDtypeStruct((128, WIDTH), F32),
            jax.ShapeDtypeStruct((128, 512), F32),
            jax.ShapeDtypeStruct((128, 512), F32),
            jax.ShapeDtypeStruct((128, WIDTH), F32),
            jax.ShapeDtypeStruct((1, 128), F32),
            jax.ShapeDtypeStruct((1, 128), F32),
            jax.ShapeDtypeStruct((1, 64), F32),
            jax.ShapeDtypeStruct((1, 128), F32),
        ]
        + [jax.ShapeDtypeStruct(a.shape, F32) for a in expert_sums],
        [resid, layer_keep, layer_got, dense, out_grad, gain_sums, *expert_sums],
    )


def sum_blocks(blocks):
    return jnp.sum(blocks.astype(F32), axis=0)


def per_device(
    tokens,
    cotangent,
    lengths,
    deal_perm,
    routes,
    gate_logits,
    norm_attn,
    norm_query,
    norm_key,
    norm_ffn,
    w_query,
    w_key,
    w_value,
    w_out,
    w_gate,
    w_up,
    w_down,
):
    ctx_index = lax.axis_index("ctx")
    core, chip = lax.rem(ctx_index, 2), ctx_index // 2
    tokens, cotangent = tokens[0], cotangent[0]

    weights = jnp.concatenate([w_query, w_key, w_value, w_out], axis=1)
    gain_shard = jnp.stack(
        [
            norm_attn.astype(F32),
            norm_query.astype(F32),
            jnp.concatenate([norm_key.astype(F32), jnp.ones((64,), F32)]),
            norm_ffn.astype(F32),
        ]
        + [jnp.zeros((128,), F32)] * 4
    )
    rows_group, weights, gain_all = gather_inputs(tokens, weights, gain_shard)
    weights = weights.reshape(WIDTH, 3 * WIDTH)
    gains = gain_all.transpose(1, 0, 2).reshape(8, WIDTH)

    pieces = jnp.arange(CTX, dtype=jnp.int32)[:, None] * CTX + deal_perm[0]
    positions = (pieces[:, :, None] * 12 + jnp.arange(12, dtype=jnp.int32)).reshape(CTX, ROWS)
    ends = jnp.cumsum(lengths[0])
    starts = ends - lengths[0]
    row_start = jnp.zeros_like(positions)
    for k in range(1, starts.shape[0]):
        row_start = jnp.where(positions >= starts[k], starts[k], row_start)
    paired = lambda a: lax.dynamic_index_in_dim(a.reshape(CHIPS, 2, ROWS), core, 1, keepdims=False)
    query_pos, query_start = paired(positions), paired(row_start)
    places = jnp.stack([query_pos, query_start], axis=1).astype(F32)
    key_pos = positions.reshape(CHIPS, 1, CHUNK).astype(F32)
    first_chunk = jnp.min(query_start, axis=1) // CHUNK

    normed, q_lin, kv_lin, totals = project(
        rows_group.reshape(CHIPS * ROWS, WIDTH), weights, gains, chip.reshape(1)
    )
    q_lin, kv_lin = q_lin.reshape(CHIPS, ROWS, 128), kv_lin.reshape(CHIPS, ROWS, 128)
    totals, cotangent_late = lax.optimization_barrier((share_totals(totals, 3), cotangent))
    grads_all = lax.all_gather(cotangent_late, "exp", axis=0, tiled=True)
    q_all, kv_half, squares, cosine, sine = turn_heads(q_lin, kv_lin, totals, places, gain_all)
    kv_all = pair_keys(kv_half).reshape(KEYS, 128)
    out_low, out_wide, log_total = attend(q_all, kv_all, key_pos, places, first_chunk)
    attended = collect_heads(out_low)
    resid, ffn_rows = finish_attention(attended, weights, tokens, gains)
    rows_all, meta_all = gather_rows(ffn_rows, route(routes[0].T, gate_logits[0].T))

    shift = jnp.array([0.0, float(CAP)], F32)[None, None, :, None]
    spots = meta_all[:, :LOCAL].reshape(PAIRS, 2, LOCAL, ROWS).transpose(0, 2, 1, 3)
    spots = jnp.where(spots < 0.0, -1.0, spots + shift).reshape(PAIRS, LOCAL, PAIR_ROWS)
    gates = meta_all[:, LOCAL:].reshape(PAIRS, 2, LOCAL, ROWS).transpose(0, 2, 1, 3)
    pair_meta = jnp.concatenate([spots, gates.reshape(PAIRS, LOCAL, PAIR_ROWS)], axis=1)
    rows_in, d_rows, act, d_gate, d_up, out_parts, d_parts = experts(
        rows_all.reshape(PAIRS, PAIR_ROWS, WIDTH),
        grads_all.reshape(PAIRS, PAIR_ROWS, WIDTH),
        pair_meta,
        pair_meta.transpose(0, 2, 1),
        w_gate,
        w_up,
        w_down,
    )
    gate_grad, up_grad, down_grad, d_ffn, layer_keep, layer_give = settle_experts(
        rows_in,
        d_rows,
        act,
        d_gate,
        d_up,
        d_parts.reshape(2, 4, ROWS, WIDTH),
        out_parts.reshape(2, 4, ROWS, WIDTH),
    )
    d_resid, d_branch, d_attended, ffn_gain_grad = back_to_branch(
        d_ffn, resid, cotangent, gains, weights
    )
    d_out = spread_grads(d_attended)
    out_part = lax.psum_scatter(
        out_grads(attended, d_branch), "exp", scatter_dimension=0, tiled=True
    )
    dq, dkv_mine, dkv_other = attend_back(
        q_all, kv_all, d_out, out_wide, log_total, key_pos, places, first_chunk
    )
    e_q, e_kv, inner = unturn_heads(
        dq, dkv_mine, pair_grads(dkv_other), q_lin, kv_lin, gain_all, cosine, sine
    )
    inner = share_totals(inner, 9)
    d_q_heads, d_kv_heads, w_parts, head_gains = head_grads(
        e_q, e_kv, inner, squares, q_lin, kv_lin, normed, gain_all
    )
    d_q, d_kv, dense, out_grad, layer_got = settle_grads(
        d_q_heads, d_kv_heads, w_parts, out_part, layer_give
    )
    input_grad, attn_gain_grad = back_to_input(d_q, d_kv, tokens, d_resid, weights, gains)
    here = (jnp.arange(EXP) == chip)[:, None, None]
    gain_sums = sum_gains(
        jnp.concatenate(
            [
                attn_gain_grad.reshape(EXP, 1, 128),
                jnp.where(here, head_gains[None], 0.0),
                ffn_gain_grad.reshape(EXP, 1, 128),
                jnp.zeros((EXP, 4, 128), F32),
            ],
            axis=1,
        )
    )
    outs = deliver(
        resid, layer_keep, layer_got, dense, out_grad, gain_sums, (gate_grad, up_grad, down_grad)
    )
    return (
        outs[0][None],
        input_grad[None],
        *outs[1:5],
        *[g.reshape(-1) for g in outs[5:9]],
        *outs[9:],
    )


def solution(mesh):
    in_specs = (
        P("exp", "ctx", None),
        P("exp", "ctx", None),
        P("exp", None),
        P("exp", None, None),
        P("exp", "ctx", None),
        P("exp", "ctx", None),
        P("exp"),
        P("exp"),
        P("exp"),
        P("exp"),
        P("exp", None),
        P("exp", None),
        P("exp", None),
        P("exp", None),
        P("exp", None, None),
        P("exp", None, None),
        P("exp", None, None),
    )
    out_specs = (
        P("exp", "ctx", None),
        P("exp", "ctx", None),
        P("exp", None),
        P("exp", None),
        P("exp", None),
        P("exp", None),
        P("exp"),
        P("exp"),
        P("exp"),
        P("exp"),
        P("exp", "ctx", None),
        P("exp", "ctx", None),
        P("exp", "ctx", None),
    )
    return jax.shard_map(
        per_device, mesh=mesh, in_specs=in_specs, out_specs=out_specs, check_vma=False
    )
```

time: 612 us -> 443 us (0.72)
  local copies, waits for them, and re-layouts: 62.5 us -> 4.68 us
  waiting for transfers between devices: 41.6 us -> 0.05 us
  other arithmetic: 37.8 us -> 9.36 us
  starting transfers between devices: 24.7 us -> 0.08 us
  Pallas kernels: 429 us -> 416 us
    all_to_all x4 -> x0, waiting for transfers between devices: 38.9 us -> none  [the longest x3 32.5 us: per_device(): lax.all_to_all(joint, 'ctx', split_axis=0, concat_axis=0, tiled=True, axi...]
    unnamed x128 -> x10, local copies, waits for them, and re-layouts: 37.9 us -> 0.03 us
    pallas_call x11 -> x12, Pallas kernels: 308 us -> 272 us  [the longest x8 122 us: comm_call(): pl.pallas_call(body, name=name, out_shape=outs, in_specs=in_specs or [ANY...]
    all_to_all x4 -> x0, starting transfers between devices: 20.3 us -> none  [the longest x3 15.7 us: per_device(): lax.all_to_all(joint, 'ctx', split_axis=0, concat_axis=0, tiled=True, axi...]
    convert_element_type x6 -> x2, other arithmetic: 17.7 us -> 0.73 us  [the longest x1 0.63 us: per_device(): places = jnp.stack([query_pos, query_start], axis=1).astype(F32)]
    reduce_sum x6 -> x0, other arithmetic: 14.4 us -> none  [sum_blocks(): return jnp.sum(blocks.astype(F32), axis=0)]
    pallas_call x7 -> x10, Pallas kernels: 77.8 us -> 90.7 us  [compute_call(): pl.pallas_call(body, name=name, out_shape=outs, compiler_params=pltpu.Com...]
    squeeze x5 -> x0, local copies, waits for them, and re-layouts: 8.58 us -> none  [the longest x3 6.85 us: per_device(): lax.dynamic_index_in_dim(piece, 1 - core, 0, keepdims=False)]
  transfers between devices with their start and end apart: 9 -> 2, of which waited for: 4 -> 0; matrix products, arithmetic and copies ran while one was open for 10% -> 2% of each run, Pallas kernels for 64% -> 35%
where the time goes in v2:
time: 443 us; the launch traced here: 444 us
  Pallas kernels  416 us (94%)
  between operations  14.3 us (3%)
  other arithmetic  9.36 us (2%)
  local copies, waits for them, and re-layouts  4.68 us (1%)
    pallas_call x8, Pallas kernels, comm_call(): pl.pallas_call(body, name=name, out_shape=outs, in_specs=in_specs or [ANY...  122 us
    pallas_call x10, Pallas kernels, compute_call(): pl.pallas_call(body, name=name, out_shape=outs, compiler_params=pltpu.Com...  90.7 us
    pallas_call x1, Pallas kernels, settle_experts(): pl.pallas_call(body, name='settle_experts', out_shape=[jax.ShapeDtypeStru...  77.7 us
    pallas_call x1, Pallas kernels, settle_grads(): pl.pallas_call(body, name='settle_grads', out_shape=[jax.ShapeDtypeStruct...  41.6 us
    pallas_call x1, Pallas kernels, attend_back(): pl.pallas_call(body, name='attend_back', out_shape=[jax.ShapeDtypeStruct(...  32.7 us
    pallas_call x1, Pallas kernels, sum_gains(): pl.pallas_call(body, name='sum_gains', out_shape=jax.ShapeDtypeStruct((8,...  24.3 us
    pallas_call x1, Pallas kernels, attend(): pl.pallas_call(body, name='attend', out_shape=[jax.ShapeDtypeStruct((CHIP...  20.1 us
  transfers between devices with their start and end apart: 2, of which 0 were waited for; matrix products, arithmetic and copies ran while one was open for 2% of the time, Pallas kernels for 35%

profile of v2, /device:TPU:1, one launch (start us, length us, event | category | flops | bytes accessed | tf_op | source)
XLA Modules:
  0.0 444.3 jit_solution(7493548961627617183)
XLA Ops:
  11.3 43.6 %gather_inputs.1 = (bf16[8,192,1024]{2,1,0:T(8,128)(2,1)}, bf16[8,128,3072]{2,1,0:T(8,128)(2,1)}, f32[8,8,128]{2,1,0:T(8,128)}) custom-call(bf16[192,1024]{1,0:T(8,128)(2,1)} %bitcast.74, bf16[128,3072]{1,0:T(8,128)(2,1)} %pad_maximum_fusion.w_ref, f32[8,128]{1,0:T(8,128)} %stack.44.g_ref), custom_call_target="tpu_custom_call" | custom-call | tf_op jit(solution)/shard_map/gather_inputs/pallas_call | solution.py:46
  55.0 7.0 %project.1 = (bf16[1536,1024]{1,0:T(8,128)(2,1)}, f32[1536,128]{1,0:T(8,128)}, f32[1536,128]{1,0:T(8,128)}, f32[8,2,192]{2,1,0:T(2,128)}) custom-call(s32[1]{0:T(128)} %bitcast.7.c_ref, bf16[1536,1024]{1,0:T(8,128)(2,1)} %bitcast.78, bf16[1024,3072]{1,0:T(8,128)(2,1)} %bitcast.60, bf16[1024,3072]{1,0:T(8,128)(2,1)} %bitcast.61, bf16[1024,3072]{1,0:T(8,128)(2,1)} %bitcast.62, ...), custom_call_target="tpu_custom_call" | custom-call | tf_op jit(solution)/shard_map/project/pallas_call | solution.py:794
  62.0 8.7 %share_totals.2.t_ref = f32[8,8,2,192]{3,2,1,0:T(2,128)} custom-call(f32[8,2,192]{2,1,0:T(2,128)} %get-tuple-element.85.x_ref), custom_call_target="tpu_custom_call" | custom-call | tf_op jit(solution)/shard_map/share_totals/pallas_call | solution.py:46
  72.0 2.2 fusion.1
  74.8 9.6 %turn_heads.1 = (bf16[8,192,128]{2,1,0:T(8,128)(2,1)}, bf16[8,192,128]{2,1,0:T(8,128)(2,1)}, f32[8,2,192]{2,1,0:T(2,128)}, f32[8,192,128]{2,1,0:T(8,128)}, f32[8,192,128]{2,1,0:T(8,128)}) custom-call(f32[8,192,128]{2,1,0:T(8,128)} %bitcast.66, f32[8,192,128]{2,1,0:T(8,128)} %bitcast.69, f32[8,8,2,192]{3,2,1,0:T(2,128)} %share_totals.2.t_ref, ...), custom_call_target="tpu_custom_call" | custom-call | tf_op jit(solution)/shard_map/turn_heads/pallas_call | solution.py:716
  84.4 3.4 pair_keys.1
  89.2 20.1 %attend.1 = (bf16[8,192,128]{2,1,0:T(8,128)(2,1)}, f32[8,192,128]{2,1,0:T(8,128)}, f32[8,192,128]{2,1,0:T(8,128)}) custom-call(s32[8]{0:T(128)} %and_select_fusion.first_ref, bf16[8,192,128]{2,1,0:T(8,128)(2,1)} %get-tuple-element.87.q_ref, bf16[3072,128]{1,0:T(8,128)(2,1)} %bitcast.72, f32[8,1,384]{2,1,0:T(1,128)} %convert_element_type.15.kp_ref, ...), custom_call_target="tpu_custom_call" | custom-call | tf_op jit(solution)/shard_map/attend/pallas_call | solution.py:948
  109.3 11.1 %collect_heads.1.a_ref = bf16[192,1024]{1,0:T(8,128)(2,1)} custom-call(bf16[8,192,128]{2,1,0:T(8,128)(2,1)} %get-tuple-element.89.x_ref), custom_call_target="tpu_custom_call" | custom-call | tf_op jit(solution)/shard_map/collect_heads/pallas_call | solution.py:46
  120.4 3.4 finish_attention.1
  125.3 29.1 %gather_rows.1 = (bf16[8,192,1024]{2,1,0:T(8,128)(2,1)}, f32[8,8,192]{2,1,0:T(8,128)}) custom-call(bf16[192,1024]{1,0:T(8,128)(2,1)} %get-tuple-element.91.x_ref, f32[8,8,192]{2,1,0:T(8,128)} %route.1.m_ref), custom_call_target="tpu_custom_call" | custom-call | tf_op jit(solution)/shard_map/gather_rows/pallas_call | solution.py:46
  156.9 40.3 %experts.1 = (bf16[4,576,1024]{2,1,0:T(8,128)(2,1)}, bf16[4,576,1024]{2,1,0:T(8,128)(2,1)}, bf16[4,576,512]{2,1,0:T(8,128)(2,1)}, bf16[4,576,512]{2,1,0:T(8,128)...) custom-call(bf16[4,384,1024]{2,1,0:T(8,128)(2,1)} %bitcast.80, ...), custom_call_target="tpu_custom_call" | custom-call | tf_op jit(solution)/shard_map/experts/pallas_call | solution.py:716
  197.2 77.7 %settle_experts.1 = (f32[4,64,512]{2,1,0:T(8,128)}, f32[4,64,512]{2,1,0:T(8,128)}, f32[4,32,1024]{2,1,0:T(8,128)}, f32[192,1024]{1,0:T(8,128)}, f32[192,1024]{1,0:T(8,128)}, /*index=5*/bf16[192,1024]{1,0:T(8,128)(2,1)}) custom-call(bf16[4,576,1024]{2,1,0:T(8,128)(2,1)} %get-tuple-element.95.x_ref, bf16[4,576,1024]{2,1,0:T(8,128)(2,1)} %get-tuple-element.96.r_ref, ...), custom_call_target="tpu_custom_call" | custom-call | tf_op jit(solution)/shard_map/settle_experts/pallas_call | solution.py:666
  275.0 4.1 back_to_branch.1
  279.1 3.8 out_grads.1
  283.0 8.6 %spread_grads.1.do_ref = bf16[8,192,128]{2,1,0:T(8,128)(2,1)} custom-call(bf16[192,1024]{1,0:T(8,128)(2,1)} %get-tuple-element.104.x_ref), custom_call_target="tpu_custom_call" | custom-call | tf_op jit(solution)/shard_map/spread_grads/pallas_call | solution.py:46
  291.6 32.7 %attend_back.1 = (f32[8,192,128]{2,1,0:T(8,128)}, f32[8,192,128]{2,1,0:T(8,128)}, bf16[8,192,128]{2,1,0:T(8,128)(2,1)}) custom-call(s32[8]{0:T(128)} %and_select_fusion.first_ref, bf16[8,192,128]{2,1,0:T(8,128)(2,1)} %get-tuple-element.87.q_ref, bf16[3072,128]{1,0:T(8,128)(2,1)} %bitcast.73, bf16[8,192,128]{2,1,0:T(8,128)(2,1)} %spread_grads.1.do_ref, ...), custom_call_target="tpu_custom_call" | custom-call | tf_op jit(solution)/shard_map/attend_back/pallas_call | solution.py:1048
  324.3 9.5 %pair_grads.1.do_ref = bf16[8,192,128]{2,1,0:T(8,128)(2,1)} custom-call(bf16[8,192,128]{2,1,0:T(8,128)(2,1)} %get-tuple-element.109.x_ref), custom_call_target="tpu_custom_call" | custom-call | tf_op jit(solution)/shard_map/pair_grads/pallas_call | solution.py:46
  333.8 7.7 %unturn_heads.1 = (f32[8,192,128]{2,1,0:T(8,128)}, f32[8,192,128]{2,1,0:T(8,128)}, f32[8,2,192]{2,1,0:T(2,128)}) custom-call(f32[8,192,128]{2,1,0:T(8,128)} %get-tuple-element.107.dq_ref, f32[8,192,128]{2,1,0:T(8,128)} %get-tuple-element.108.dk_ref, bf16[8,192,128]{2,1,0:T(8,128)(2,1)} %pair_grads.1.do_ref, f32[8,192,128]{2,1,0:T(8,128)} %bitcast.67, ...), custom_call_target="tpu_custom_call" | custom-call | tf_op jit(solution)/shard_map/unturn_heads/pallas_call | solution.py:716
  341.4 7.5 %share_totals.3.i_ref = f32[8,8,2,192]{3,2,1,0:T(2,128)} custom-call(f32[8,2,192]{2,1,0:T(2,128)} %get-tuple-element.114.x_ref), custom_call_target="tpu_custom_call" | custom-call | tf_op jit(solution)/shard_map/share_totals/pallas_call | solution.py:46
  349.0 10.7 %head_grads.1 = (bf16[8,192,128]{2,1,0:T(8,128)(2,1)}, bf16[8,192,128]{2,1,0:T(8,128)(2,1)}, bf16[2,1024,128]{2,1,0:T(8,128)(2,1)}, f32[2,128]{1,0:T(2,128)}) custom-call(f32[8,192,128]{2,1,0:T(8,128)} %get-tuple-element.112.eq_ref, f32[8,192,128]{2,1,0:T(8,128)} %get-tuple-element.113.ek_ref, f32[8,8,2,192]{3,2,1,0:T(2,128)} %share_totals.3.i_ref, ...), custom_call_target="tpu_custom_call" | custom-call | tf_op jit(solution)/shard_map/head_grads/pallas_call | solution.py:716
  360.5 41.6 %settle_grads.1 = (bf16[192,1024]{1,0:T(8,128)(2,1)}, bf16[192,1024]{1,0:T(8,128)(2,1)}, bf16[2,128,1024]{2,1,0:T(8,128)(2,1)}, bf16[128,1024]{1,0:T(8,128)(2,1)}, bf16[192,1024]{1,0:T(8,128)(2,1)}) custom-call(bf16[8,192,128]{2,1,0:T(8,128)(2,1)} %get-tuple-element.117.q_ref, bf16[8,192,128]{2,1,0:T(8,128)(2,1)} %get-tuple-element.118.kv_ref, ...), custom_call_target="tpu_custom_call" | custom-call | tf_op jit(solution)/shard_map/settle_grads/pallas_call | solution.py:390
  402.1 5.5 %back_to_input.1 = (f32[192,1024]{1,0:T(8,128)}, f32[1,1024]{1,0:T(1,128)}) custom-call(bf16[192,1024]{1,0:T(8,128)(2,1)} %get-tuple-element.125.dq_ref, bf16[192,1024]{1,0:T(8,128)(2,1)} %get-tuple-element.126.dkv_ref, bf16[192,1024]{1,0:T(8,128)(2,1)} %bitcast.76, f32[192,1024]{1,0:T(8,128)} %get-tuple-element.127.r_ref, bf16[1024,3072]{1,0:T(8,128)(2,1)} %bitcast.65, ...), custom_call_target="tpu_custom_call" | custom-call | tf_op jit(solution)/shard_map/back_to_input/pallas_call | solution.py:716
  408.9 24.3 %sum_gains.1.s_ref = f32[8,128]{1,0:T(8,128)} custom-call(f32[8,8,128]{2,1,0:T(8,128)} %maximum_maximum_fusion.x_ref), custom_call_target="tpu_custom_call" | custom-call | tf_op jit(solution)/shard_map/sum_gains/pallas_call | solution.py:448
  433.3 4.1 deliver.1
  (49 shorter events, 13.5 us)
Async XLA Ops:
  7.2 149.7 %all-gather.2.cloned.1.call-start = ((), (), s32[]{:S(2)}) async-start(), calls=%async_computation.1 | async-start | bytes 3538944 | tf_op jit(solution)/shard_map/all_gather | solution.py:1483
  54.9 15.8 %copy-start.4 = (s32[1,4]{1,0:T(1,128)S(1)}, s32[1,4]{1,0:T(1,128)}, u32[]{:S(2)}) copy-start(s32[1,4]{1,0:T(1,128)} %param.20) | copy-start | bytes 52
  55.0 16.0 %copy-start.1 = (s32[1,16,16]{2,1,0:T(8,128)S(1)}, s32[1,16,16]{2,1,0:T(8,128)}, u32[]{:S(2)}) copy-start(s32[1,16,16]{2,1,0:T(8,128)} %param.21) | copy-start | bytes 3076
  70.7 289.7 %reduce-scatter.2.cloned.1.call-start = ((), (), s32[]{:S(2)}) async-start(), calls=%async_computation.2 | async-start | bytes 2359296 | tf_op jit(solution)/shard_map/reduce_scatter | solution.py:1518
  120.4 35.1 %copy-start.3 = (f32[2]{0:T(128)S(1)}, f32[2]{0:T(128)}, u32[]{:S(2)}) copy-start(f32[2]{0:T(128)} %constant.57.clone) | copy-start | bytes 28
  155.7 1.2 copy-start
  402.1 5.5 %copy-start.2 = (f32[1,1024]{1,0:T(1,128)S(1)}, f32[1,1024]{1,0:T(1,128)}, u32[]{:S(2)}) copy-start(f32[1,1024]{1,0:T(1,128)} %get-tuple-element.130) | copy-start | bytes 12292
Sparse Core Ops, SparseCore 0:
  70.8 41.2 all-gather.1
  283.0 39.5 reduce-scatter.1

commit v3 on v2

v3 whole, which is shorter than its diff:
```python
import jax
import jax.numpy as jnp
from jax import lax
from jax.experimental import pallas as pl
from jax.experimental.pallas import tpu as pltpu
from jax.sharding import PartitionSpec as P

HEADS = 16
KV_HEADS = 8
EPSILON = 1e-05
ROPE_BASE = 10000.0
MASKED = -1e30

MESH = pl.DeviceIdType.MESH
CTX = 16
EXP = 8
CHIPS = 8
ROWS = 192
WIDTH = 1024
FF = 512
LOCAL = 4
CAP = 72
PAIRS = EXP // 2
PAIR_ROWS = 2 * ROWS
PAIR_CAP = 2 * CAP
SLOTS = EXP * CAP
PAIR_SLOTS = LOCAL * PAIR_CAP
KEYS = CTX * ROWS
CHUNK = 2 * ROWS
MIB = 1 << 20
FAR_FIRST = (6, 2, 5, 7, 4, 1, 3)

ANY_SPEC = pl.BlockSpec(memory_space=pl.ANY)
F32 = jnp.float32
BF16 = jnp.bfloat16


def dot(a, b, dims=((1,), (0,))):
    return lax.dot_general(a, b, (dims, ((), ())), preferred_element_type=F32)


NT = ((1,), (1,))
TN = ((0,), (0,))


def comm_call(body, name, collective_id, outs, ins, copies, in_specs=None):
    return pl.pallas_call(
        body,
        name=name,
        out_shape=outs,
        in_specs=in_specs or [ANY_SPEC] * len(ins),
        out_specs=[ANY_SPEC] * len(outs),
        scratch_shapes=[
            pltpu.SemaphoreType.DMA((copies,)),
            pltpu.SemaphoreType.DMA((copies,)),
            pltpu.SemaphoreType.DMA((8,)),
        ],
        compiler_params=pltpu.CompilerParams(
            collective_id=collective_id, has_side_effects=True, vmem_limit_bytes=60 * MIB
        ),
    )(*ins)


class Copier:
    def __init__(self, send_sem, recv_sem, local_sem):
        self.send_sem, self.recv_sem, self.local_sem = send_sem, recv_sem, local_sem
        self.remote, self.local = [], []

    def send(self, src, dst, axis, index):
        at = len(self.remote)
        copy = pltpu.make_async_remote_copy(
            src_ref=src,
            dst_ref=dst,
            send_sem=self.send_sem.at[at],
            recv_sem=self.recv_sem.at[at],
            device_id={axis: index},
            device_id_type=MESH,
        )
        copy.start()
        self.remote.append([copy, False])
        return at

    def keep(self, src, dst):
        copy = pltpu.make_async_copy(src, dst, self.local_sem.at[len(self.local)])
        copy.start()
        self.local.append([copy, False])
        return len(self.local) - 1

    def arrived(self, at):
        self.remote[at][0].wait_recv()
        self.remote[at][1] = True

    def kept(self, at):
        self.local[at][0].wait()
        self.local[at][1] = True

    def finish(self):
        for copy, seen in self.remote:
            if not seen:
                copy.wait_recv()
        for copy, _ in self.remote:
            copy.wait_send()
        for copy, seen in self.local:
            if not seen:
                copy.wait()


def meet(partners):
    barrier = pltpu.get_barrier_semaphore()
    for axis, index in partners:
        pl.semaphore_signal(barrier, inc=1, device_id={axis: index}, device_id_type=MESH)
    pl.semaphore_wait(barrier, len(partners))


def place():
    ctx = lax.axis_index("ctx")
    core = lax.rem(ctx, 2)
    return ctx, ctx // 2, core, ctx + 1 - 2 * core


def ring_of(me):
    half, spot = me // 4, lax.rem(me, 4)
    over = (1 - half) * 4
    turns = [lax.rem(spot + d, 4) for d in (0, 1, 3, 2)]
    return tuple([half * 4 + t for t in turns] + [over + t for t in turns])


def relay(copier, own, slot, rows, ring, reach, landed=lambda partner: None):
    me, right, left, far, over, over_right, over_left, over_far = ring
    half = rows // 2
    low, high = pl.ds(0, half), pl.ds(half, half)

    def send(block, to, part, partner):
        return copier.send(block.at[part], slot(to).at[part], *reach(partner))

    def on(of, part, partner):
        return send(slot(of), of, part, partner)

    over_low = send(own, me, low, over)
    over_high = send(own, me, high, over)
    yield
    right_low = send(own, me, low, right)
    left_high = send(own, me, high, left)
    right_high = send(own, me, high, right)
    left_low = send(own, me, low, left)
    yield
    copier.arrived(right_low)
    far_right = on(left, low, right)
    copier.arrived(left_high)
    far_left = on(right, high, left)
    yield
    copier.arrived(over_low)
    next_right_low = on(over, low, right)
    next_left_low = on(over, low, left)
    copier.arrived(over_high)
    next_left_high = on(over, high, left)
    next_right_high = on(over, high, right)
    landed(over)
    yield
    copier.arrived(right_high)
    landed(left)
    copier.arrived(left_low)
    landed(right)
    yield
    copier.arrived(far_right)
    copier.arrived(far_left)
    landed(far)
    yield
    copier.arrived(next_right_low)
    far_right = on(over_left, low, right)
    copier.arrived(next_left_high)
    far_left = on(over_right, high, left)
    copier.arrived(next_right_high)
    landed(over_left)
    copier.arrived(next_left_low)
    landed(over_right)
    yield
    copier.arrived(far_right)
    copier.arrived(far_left)
    landed(over_far)


def side_by_side(*relays):
    for _ in zip(*relays):
        pass
    for one in relays:
        for _ in one:
            pass


def gather_rows(rows, meta):
    def body(x_ref, m_ref, o_ref, mo_ref, send_sem, recv_sem, local_sem):
        ring = ring_of(lax.axis_index("exp"))
        me = ring[0]
        to_exp = lambda p: ("exp", p)
        copier = Copier(send_sem, recv_sem, local_sem)
        meet([to_exp(p) for p in ring[1:]])
        copier.keep(x_ref, o_ref.at[me])
        copier.keep(m_ref.at[me], mo_ref.at[me])
        for p in ring[1:]:
            copier.send(m_ref.at[p], mo_ref.at[me], *to_exp(p))
        side_by_side(relay(copier, x_ref, lambda s: o_ref.at[s], rows.shape[0], ring, to_exp))
        copier.finish()

    return comm_call(
        body,
        "gather_rows",
        2,
        [
            jax.ShapeDtypeStruct((EXP,) + rows.shape, rows.dtype),
            jax.ShapeDtypeStruct(meta.shape, F32),
        ],
        [rows, meta],
        21,
        in_specs=[pl.BlockSpec(memory_space=pltpu.VMEM)] * 2,
    )


def lanes(index):
    return pl.ds(pl.multiple_of(index * 128, 128), 128)


def collect_heads(blocks):
    def body(x_ref, o_ref, send_sem, recv_sem, local_sem):
        _, chip, core, _ = place()
        chips = [lax.rem(chip + d, CHIPS) for d in FAR_FIRST]
        copier = Copier(send_sem, recv_sem, local_sem)
        meet([("ctx", 2 * p + core) for p in chips])
        for p in chips:
            copier.send(x_ref.at[p], o_ref.at[:, lanes(chip)], "ctx", 2 * p + core)
        copier.keep(x_ref.at[chip], o_ref.at[:, lanes(chip)])
        copier.finish()

    return comm_call(
        body, "collect_heads", 4, [jax.ShapeDtypeStruct((ROWS, WIDTH), BF16)], [blocks], 7
    )[0]


def spread_grads(rows):
    def body(x_ref, o_ref, send_sem, recv_sem, local_sem):
        _, chip, core, _ = place()
        chips = [lax.rem(chip + d, CHIPS) for d in FAR_FIRST]
        copier = Copier(send_sem, recv_sem, local_sem)
        meet([("ctx", 2 * p + core) for p in chips])
        for p in chips:
            copier.send(x_ref.at[:, lanes(p)], o_ref.at[chip], "ctx", 2 * p + core)
        copier.keep(x_ref.at[:, lanes(chip)], o_ref.at[chip])
        copier.finish()

    return comm_call(
        body, "spread_grads", 5, [jax.ShapeDtypeStruct((CHIPS, ROWS, 128), BF16)], [rows], 7
    )[0]


def settle_experts(rows, d_rows, act, d_gate, d_up, d_parts, layer_parts):
    def body(
        x_ref, r_ref, a_ref, g_ref, u_ref, p_ref, l_ref, gate_out, up_out, down_a_out, down_b_out, dx_out, keep_out, give_out,
        x_v, r_v, a_v, g_v, u_v, gate, up, down, gate_o, up_o, down_o, gate_a, down_a, up_b, down_b,
        to_z, from_z, d_own, d_right, d_left, d_low, d_high, d_from, l_own, l_right, l_left, l_low, l_high, l_from, send_sem, recv_sem, local_sem,
    ):
        _, chip, core, sibling = place()
        me = lax.axis_index("exp")
        zl, x = me // 4, lax.rem(me, 4)
        zh, y = chip // 4, lax.rem(chip, 4)
        at_ctx = lambda z, yy: ("ctx", z * 8 + yy * 2 + core)
        over = at_ctx(1 - zh, y)
        columns = [lax.rem(y + d, 4) for d in (1, 3, 2)]
        right, left, far = [lax.rem(x + d, 4) for d in (1, 3, 2)]
        at_exp = lambda p: ("exp", zl * 4 + p)
        low, high = pl.ds(0, ROWS // 2), pl.ds(ROWS // 2, ROWS // 2)
        copier = Copier(send_sem, recv_sem, local_sem)
        loads = []
        for e in range(LOCAL):
            pairs = ((x_ref, x_v), (r_ref, r_v), (a_ref, a_v), (g_ref, g_v), (u_ref, u_v))
            loads.append([copier.keep(src.at[e], dst.at[e]) for src, dst in pairs])
        parts = (p_ref, d_own, d_right, d_left, d_low, d_high, d_from)
        layers = (l_ref, l_own, l_right, l_left, l_low, l_high, l_from)

        def fetch(src, own, to_right, to_left, *_):
            return [
                copier.keep(src.at[:, x], own),
                copier.keep(src.at[:, right, low], to_right),
                copier.keep(src.at[:, left, high], to_left),
            ]

        part_loads, layer_loads = fetch(*parts), fetch(*layers)
        meet(
            [("ctx", sibling), over]
            + [at_ctx(zh, c) for c in columns]
            + [at_exp(right), at_exp(left)]
            + [("exp", (1 - zl) * 4 + x)]
        )

        def set_out(src, own, to_right, to_left, in_low, in_high, arrived):
            return [
                copier.send(src.at[:, far, low], in_low, *at_exp(right)),
                copier.send(src.at[:, far, high], in_high, *at_exp(left)),
                copier.send(src.at[:, right, high], arrived.at[0, :, high], *at_exp(right)),
                copier.send(src.at[:, left, low], arrived.at[1, :, low], *at_exp(left)),
            ]

        def pass_on(stage, loads_of, src, own, to_right, to_left, in_low, in_high, arrived):
            for at in loads_of:
                copier.kept(at)
            for at in stage[:2]:
                copier.arrived(at)

            def add(r, _):
                at = pl.ds(pl.multiple_of(r * 48, 16), 48)
                for z in range(2):
                    for mine, other in ((to_right, in_low), (to_left, in_high)):
                        mine[z, at, :] = (mine[z, at, :].astype(F32) + other[z, at, :].astype(F32)).astype(BF16)
                return 0

            lax.fori_loop(0, 2, add, 0)
            return stage[2:] + [
                copier.send(to_right, arrived.at[0, :, low], *at_exp(right)),
                copier.send(to_left, arrived.at[1, :, high], *at_exp(left)),
            ]

        part_stage = set_out(*parts)

        def work(e):
            for at in loads[e]:
                copier.kept(at)

            def wide(r, _):
                rows_r = x_v[e, :, pl.ds(pl.multiple_of(r * 256, 256), 256)]
                for d_v, o_v in ((g_v, gate), (u_v, up)):
                    grad = dot(rows_r, d_v[e], TN).astype(BF16)
                    for k in range(4):
                        o_v[k % 2, r // 2, 2 * lax.rem(r, 2) + k // 2, e] = grad[k * 64 : (k + 1) * 64]
                return 0

            lax.fori_loop(0, 4, wide, 0)

            def tall(r, _):
                act_r = a_v[e, :, pl.ds(pl.multiple_of(r * 256, 256), 256)]
                grad = dot(act_r, r_v[e], TN).astype(BF16)
                for k in range(8):
                    down[k % 2, r, k // 2, e] = grad[k * 32 : (k + 1) * 32]
                return 0

            lax.fori_loop(0, 2, tall, 0)
            return [
                copier.send(full.at[1 - core, :, :, e], other.at[:, :, e], "ctx", sibling)
                for full, other in ((gate, gate_o), (up, up_o), (down, down_o))
            ]

        first_a, first_b = [], []

        def join(e, swaps):
            for at in swaps:
                copier.arrived(at)

            def add(c, _):
                z, yy = c // 4, lax.rem(c, 4)
                for full, other in ((gate, gate_o), (up, up_o), (down, down_o)):
                    both = full[core, z, yy, e].astype(F32) + other[z, yy, e].astype(F32)
                    full[core, z, yy, e] = both.astype(BF16)
                return 0

            lax.fori_loop(0, CHIPS, add, 0)
            first_a.append(copier.send(gate.at[core, 1 - zh, :, e], gate_a.at[:, e], *over))
            if e < 2:
                first_a.append(copier.send(down.at[core, 1 - zh, :, e], down_a.at[:, e], *over))
            for c in columns:
                to = at_ctx(zh, c)
                first_b.append(copier.send(up.at[core, :, c, e], up_b.at[y, :, e], *to))
                if e >= 2:
                    first_b.append(copier.send(down.at[core, :, c, e], down_b.at[y, :, e - 2], *to))

        swaps = work(0)
        later = work(1)
        join(0, swaps)
        part_stage = pass_on(part_stage, part_loads, *parts)
        layer_stage = set_out(*layers)
        swaps = later
        later = work(2)
        join(1, swaps)
        swaps = later
        later = work(3)
        join(2, swaps)
        join(3, later)

        def sum_up(stage, own, arrived, keep_ref, give_ref):
            for at in stage:
                copier.arrived(at)

            def add(r, _):
                at = pl.ds(pl.multiple_of(r * 48, 16), 48)
                keep, give = [
                    own[z, at, :].astype(F32) + arrived[0, z, at, :].astype(F32) + arrived[1, z, at, :].astype(F32)
                    for z in (zl, 1 - zl)
                ]
                keep_ref[at, :] = keep
                give_ref[at, :] = give.astype(BF16)
                return 0

            lax.fori_loop(0, 4, add, 0)

        sum_up(part_stage, d_own, d_from, dx_out, to_z)
        z_stage = copier.send(to_z, from_z, "exp", (1 - zl) * 4 + x)
        layer_stage = pass_on(layer_stage, layer_loads, *layers)

        for at in first_a:
            copier.arrived(at)

        def sum_a(c, _):
            for e in range(LOCAL):
                both = gate[core, zh, c, e].astype(F32) + gate_a[c, e].astype(F32)
                gate_out[c, e] = both.astype(BF16)
            for e in range(2):
                both = down[core, zh, c, e].astype(F32) + down_a[c, e].astype(F32)
                down_a_out[c, e] = both.astype(BF16)
            return 0

        lax.fori_loop(0, 4, sum_a, 0)

        for at in first_b:
            copier.arrived(at)
        others = [lax.rem(y + d, 4) for d in (1, 2, 3)]

        def sum_b(e, _):
            for z in range(2):
                total = up[core, z, y, e].astype(F32)
                for c in others:
                    total = total + up_b[c, z, e].astype(F32)
                up_out[z, e] = total.astype(BF16)
            return 0

        lax.fori_loop(0, LOCAL, sum_b, 0)

        def sum_b_down(e, _):
            for z in range(2):
                total = down[core, z, y, e + 2].astype(F32)
                for c in others:
                    total = total + down_b[c, z, e].astype(F32)
                down_b_out[z, e] = total.astype(BF16)
            return 0

        lax.fori_loop(0, 2, sum_b_down, 0)
        copier.arrived(z_stage)

        def gather_z(r, _):
            at = pl.ds(pl.multiple_of(r * 48, 16), 48)
            dx_out[at, :] += from_z[at, :].astype(F32)
            return 0

        lax.fori_loop(0, 4, gather_z, 0)
        sum_up(layer_stage, l_own, l_from, keep_out, give_out)
        copier.finish()

    vmem = pl.BlockSpec(memory_space=pltpu.VMEM)
    buf = lambda *shape: pltpu.VMEM(shape, BF16)
    wide, tall = (64, FF), (32, WIDTH)
    return pl.pallas_call(
        body,
        name="settle_experts",
        out_shape=[
            jax.ShapeDtypeStruct((4, LOCAL) + wide, BF16),
            jax.ShapeDtypeStruct((2, LOCAL) + wide, BF16),
            jax.ShapeDtypeStruct((4, 2) + tall, BF16),
            jax.ShapeDtypeStruct((2, 2) + tall, BF16),
            jax.ShapeDtypeStruct((ROWS, WIDTH), F32),
            jax.ShapeDtypeStruct((ROWS, WIDTH), F32),
            jax.ShapeDtypeStruct((ROWS, WIDTH), BF16),
        ],
        in_specs=[ANY_SPEC] * 7,
        out_specs=[vmem] * 7,
        scratch_shapes=[
            buf(LOCAL, SLOTS, WIDTH),
            buf(LOCAL, SLOTS, WIDTH),
            buf(LOCAL, SLOTS, FF),
            buf(LOCAL, SLOTS, FF),
            buf(LOCAL, SLOTS, FF),
            buf(2, 2, 4, LOCAL, *wide),
            buf(2, 2, 4, LOCAL, *wide),
            buf(2, 2, 4, LOCAL, *tall),
            buf(2, 4, LOCAL, *wide),
            buf(2, 4, LOCAL, *wide),
            buf(2, 4, LOCAL, *tall),
            buf(4, LOCAL, *wide),
            buf(4, 2, *tall),
            buf(4, 2, LOCAL, *wide),
            buf(4, 2, 2, *tall),
            buf(ROWS, WIDTH),
            buf(ROWS, WIDTH),
        ]
        + [
            buf(2, ROWS, WIDTH),
            buf(2, ROWS // 2, WIDTH),
            buf(2, ROWS // 2, WIDTH),
            buf(2, ROWS // 2, WIDTH),
            buf(2, ROWS // 2, WIDTH),
            buf(2, 2, ROWS, WIDTH),
        ]
        * 2
        + [
            pltpu.SemaphoreType.DMA((49,)),
            pltpu.SemaphoreType.DMA((49,)),
            pltpu.SemaphoreType.DMA((28,)),
        ],
        compiler_params=pltpu.CompilerParams(
            collective_id=8, has_side_effects=True, vmem_limit_bytes=62 * MIB
        ),
    )(rows, d_rows, act, d_gate, d_up, d_parts, layer_parts)


def compute_call(body, name, outs, ins, vmem=60, **kw):
    return pl.pallas_call(
        body,
        name=name,
        out_shape=outs,
        compiler_params=pltpu.CompilerParams(vmem_limit_bytes=vmem * MIB),
        **kw,
    )(*ins)


def row_scale(total, width):
    return lax.rsqrt(total * (1.0 / width) + EPSILON)


def key_lanes():
    return lax.broadcasted_iota(jnp.int32, (1, 128), 1) < 64


def turn(values, cosine, sine):
    first = lax.rem(lax.broadcasted_iota(jnp.int32, (1, 128), 1), 64) < 32
    return values * cosine + jnp.where(first, -pltpu.roll(values, 96, 1), pltpu.roll(values, 32, 1)) * sine


def across(select, values):
    return lax.dot_general(
        select, values, (NT, ((), ())), precision=lax.Precision.HIGHEST, preferred_element_type=F32
    )


def both_totals(left, right):
    row_id = lax.broadcasted_iota(jnp.int32, (8, 128), 0)
    ones = jnp.where(row_id == 0, 1.0, 0.0)
    keys = jnp.where((row_id == 1) & key_lanes(), 1.0, 0.0)
    return (across(ones, left) + across(keys, right))[0:2, :]


def down_rows(values, row, width=128):
    chosen = lax.broadcasted_iota(jnp.int32, (2, width), 0) == row
    return lax.dot_general(
        values,
        jnp.where(chosen, 1.0, 0.0),
        (TN, ((), ())),
        precision=lax.Precision.HIGHEST,
        preferred_element_type=F32,
    )


def own_chip():
    return lax.axis_index("ctx") // 2


def route(routes_t, logits_t):
    def body(r_ref, l_ref, m_ref):
        logits = l_ref[...]
        raised = jnp.exp(logits - jnp.max(logits, axis=0, keepdims=True))
        gates = raised / jnp.sum(raised, axis=0, keepdims=True)
        experts = lax.broadcasted_iota(jnp.int32, (32, ROWS), 0)
        member = jnp.zeros((32, ROWS), F32)
        weight = jnp.zeros((32, ROWS), F32)
        for c in range(8):
            hit = r_ref[c : c + 1, :] == experts
            member = member + jnp.where(hit, 1.0, 0.0)
            weight = weight + jnp.where(hit, gates[c : c + 1, :], 0.0)
        before = lax.broadcasted_iota(jnp.int32, (ROWS, ROWS), 0) < lax.broadcasted_iota(
            jnp.int32, (ROWS, ROWS), 1
        )
        rank = dot(member.astype(BF16), jnp.where(before, 1.0, 0.0).astype(BF16))
        spot = jnp.where(member > 0.5, rank, -1.0)
        for e in range(EXP):
            m_ref[e, 0:4, :] = spot[e * 4 : e * 4 + 4, :]
            m_ref[e, 4:8, :] = weight[e * 4 : e * 4 + 4, :]

    return compute_call(
        body, "route", [jax.ShapeDtypeStruct((EXP, 8, ROWS), F32)], [routes_t, logits_t]
    )[0]


def split_kv(kv_ref, klo, khi, vlo, vhi):
    low = key_lanes()
    both = kv_ref[...].astype(F32)
    other = pltpu.roll(both, 64, 1)
    if klo is not None:
        klo[...] = jnp.where(low, both, 0.0).astype(BF16)
        khi[...] = jnp.where(low, 0.0, other).astype(BF16)
    vlo[...] = jnp.where(low, other, 0.0).astype(BF16)
    vhi[...] = jnp.where(low, 0.0, both).astype(BF16)


def attend(q, kv, key_pos, places, first_chunk):
    def body(first_ref, q_ref, kv_ref, kp_ref, p_ref, o_ref, of_ref, l_ref, klo, khi, vlo, vhi):
        i = pl.program_id(0)

        @pl.when(i == 0)
        def _():
            split_kv(kv_ref, klo, khi, vlo, vhi)

        q_block = q_ref[0]
        at_row, start_row = [
            jnp.concatenate([down_rows(p_ref[0], k)] * (CHUNK // 128), axis=1) for k in range(2)
        ]
        low = key_lanes()

        def step(p, carry):
            m0, m1, l0, l1, acc = carry
            rows = pl.ds(pl.multiple_of(p * CHUNK, CHUNK), CHUNK)
            at_key = kp_ref[p]
            seen = (at_key >= start_row) & (at_key <= at_row)
            s0 = jnp.where(seen, dot(q_block, klo[rows, :], NT), MASKED)
            s1 = jnp.where(seen, dot(q_block, khi[rows, :], NT), MASKED)
            n0 = jnp.maximum(m0, jnp.max(s0, axis=1, keepdims=True))
            n1 = jnp.maximum(m1, jnp.max(s1, axis=1, keepdims=True))
            p0 = jnp.exp(s0 - n0)
            p1 = jnp.exp(s1 - n1)
            a0 = jnp.exp(m0 - n0)
            a1 = jnp.exp(m1 - n1)
            l0 = l0 * a0 + jnp.sum(p0, axis=1, keepdims=True)
            l1 = l1 * a1 + jnp.sum(p1, axis=1, keepdims=True)
            acc = acc * jnp.where(low, a0, a1)
            acc = acc + dot(p0.astype(BF16), vlo[rows, :]) + dot(p1.astype(BF16), vhi[rows, :])
            return n0, n1, l0, l1, acc

        top = jnp.full((ROWS, 1), MASKED, F32)
        none = jnp.zeros((ROWS, 1), F32)
        m0, m1, l0, l1, acc = lax.fori_loop(
            first_ref[i], i + 1, step, (top, top, none, none, jnp.zeros((ROWS, 128), F32))
        )
        out = acc / jnp.where(low, l0, l1)
        of_ref[0] = out
        o_ref[0] = out.astype(BF16)
        l_ref[0] = jnp.where(low, m0 + jnp.log(l0), m1 + jnp.log(l1))

    def block(*shape):
        return pl.BlockSpec((1,) + shape, lambda i, first: (i, 0, 0))

    return pl.pallas_call(
        body,
        name="attend",
        out_shape=[
            jax.ShapeDtypeStruct((CHIPS, ROWS, 128), BF16),
            jax.ShapeDtypeStruct((CHIPS, ROWS, 128), F32),
            jax.ShapeDtypeStruct((CHIPS, ROWS, 128), F32),
        ],
        grid_spec=pltpu.PrefetchScalarGridSpec(
            num_scalar_prefetch=1,
            grid=(CHIPS,),
            in_specs=[
                block(ROWS, 128),
                pl.BlockSpec((KEYS, 128), lambda i, first: (0, 0)),
                pl.BlockSpec((CHIPS, 1, CHUNK), lambda i, first: (0, 0, 0)),
                block(2, ROWS),
            ],
            out_specs=[block(ROWS, 128)] * 3,
            scratch_shapes=[pltpu.VMEM((KEYS, 128), BF16)] * 4,
        ),
        compiler_params=pltpu.CompilerParams(vmem_limit_bytes=60 * MIB),
    )(first_chunk, q, kv, key_pos, places)


def attend_back(q, kv, d_out, out, log_total, key_pos, places, first_chunk):
    def body(
        first_ref, q_ref, kv_ref, do_ref, o_ref, l_ref, kp_ref, p_ref,
        dq_ref, mine_ref, other_ref, klo, khi, vlo, vhi, acc, key_at,
    ):
        i = pl.program_id(0)

        @pl.when(i == 0)
        def _():
            split_kv(kv_ref, klo, khi, vlo, vhi)
            acc[...] = jnp.zeros_like(acc)

            def place_keys(p, _):
                both = jnp.concatenate([kp_ref[p], kp_ref[p]], axis=0)
                key_at[pl.ds(pl.multiple_of(p * CHUNK, CHUNK), CHUNK), :] = down_rows(both, 0, ROWS)
                return 0

            lax.fori_loop(0, CHIPS, place_keys, 0)

        low = key_lanes()
        q_block, do_block = q_ref[0], do_ref[0]
        do_wide, q_wide = do_block.astype(F32), q_block.astype(F32)
        q_turned, do_turned = pltpu.roll(q_wide, 64, 1), pltpu.roll(do_wide, 64, 1)
        right = jnp.concatenate(
            [
                jnp.where(low, q_wide, 0.0).astype(BF16),
                jnp.where(low, q_turned, 0.0).astype(BF16),
                jnp.where(low, 0.0, do_turned).astype(BF16),
                jnp.where(low, 0.0, do_wide).astype(BF16),
            ],
            axis=0,
        )
        row_id = lax.broadcasted_iota(jnp.int32, (8, 128), 0)
        lane_id = lax.broadcasted_iota(jnp.int32, (8, 128), 1)
        halves = jnp.where(lane_id // 64 == row_id, 1.0, 0.0)
        picks = jnp.where(lane_id == 64 * row_id, 1.0, 0.0)

        delta = across(halves, do_wide * o_ref[0])
        total = across(picks, l_ref[0])
        at_row, start_row = p_ref[0, 0:1, :], p_ref[0, 1:2, :]

        def step(p, dq):
            rows = pl.ds(pl.multiple_of(p * CHUNK, CHUNK), CHUNK)
            at_key = key_at[rows, :]
            seen = (at_key >= start_row) & (at_key <= at_row)
            k0, k1 = klo[rows, :], khi[rows, :]
            s0 = jnp.where(seen, dot(k0, q_block, NT), MASKED)
            s1 = jnp.where(seen, dot(k1, q_block, NT), MASKED)
            p0 = jnp.exp(s0 - total[0:1, :])
            p1 = jnp.exp(s1 - total[1:2, :])
            d0 = (p0 * (dot(vlo[rows, :], do_block, NT) - delta[0:1, :])).astype(BF16)
            d1 = (p1 * (dot(vhi[rows, :], do_block, NT) - delta[1:2, :])).astype(BF16)
            left = jnp.concatenate([d0, d1, p0.astype(BF16), p1.astype(BF16)], axis=1)
            acc[rows, :] += dot(left, right)
            return dq + dot(d0, k0, TN) + dot(d1, k1, TN)

        dq = lax.fori_loop(first_ref[i], i + 1, step, jnp.zeros((ROWS, 128), F32))
        dq_ref[0] = dq * 0.125

        @pl.when(i == CHIPS - 1)
        def _():
            core = lax.rem(lax.axis_index("ctx"), 2)

            def part(s, _):
                mine = pl.ds(pl.multiple_of((2 * s + core) * ROWS, ROWS), ROWS)
                other = pl.ds(pl.multiple_of((2 * s + 1 - core) * ROWS, ROWS), ROWS)
                mine_ref[s] = acc[mine, :]
                other_ref[s] = acc[other, :].astype(BF16)
                return 0

            lax.fori_loop(0, CHIPS, part, 0)

    def block(*shape):
        return pl.BlockSpec((1,) + shape, lambda i, first: (i, 0, 0))

    whole = pl.BlockSpec((KEYS, 128), lambda i, first: (0, 0))
    return pl.pallas_call(
        body,
        name="attend_back",
        out_shape=[
            jax.ShapeDtypeStruct((CHIPS, ROWS, 128), F32),
            jax.ShapeDtypeStruct((CHIPS, ROWS, 128), F32),
            jax.ShapeDtypeStruct((CHIPS, ROWS, 128), BF16),
        ],
        grid_spec=pltpu.PrefetchScalarGridSpec(
            num_scalar_prefetch=1,
            grid=(CHIPS,),
            in_specs=[
                block(ROWS, 128),
                whole,
                block(ROWS, 128),
                block(ROWS, 128),
                block(ROWS, 128),
                pl.BlockSpec((CHIPS, 1, CHUNK), lambda i, first: (0, 0, 0)),
                block(2, ROWS),
            ],
            out_specs=[block(ROWS, 128)] + [pl.BlockSpec((CHIPS, ROWS, 128), lambda i, first: (0, 0, 0))] * 2,
            scratch_shapes=[pltpu.VMEM((KEYS, 128), BF16)] * 4
            + [pltpu.VMEM((KEYS, 128), F32), pltpu.VMEM((KEYS, ROWS), F32)],
        ),
        compiler_params=pltpu.CompilerParams(vmem_limit_bytes=60 * MIB),
    )(first_chunk, q, kv, d_out, out, log_total, key_pos, places)


def whole(*shape):
    return pl.BlockSpec(shape, lambda i: (0,) * len(shape))


def columns(block, width=WIDTH):
    return pl.BlockSpec((WIDTH, width), lambda i: (0, block))


def finish_attention(attended, w_out, tokens, gains):
    def body(a_ref, w_ref, t_ref, g_ref, r_ref, f_ref):
        branch = dot(a_ref[...], w_ref[...]).astype(BF16).astype(F32)
        resid = t_ref[...].astype(F32) + branch
        r_ref[...] = resid
        scale = row_scale(jnp.sum(resid * resid, axis=1, keepdims=True), WIDTH)
        f_ref[...] = (resid * scale * g_ref[3:4, :]).astype(BF16)

    return compute_call(
        body,
        "finish_attention",
        [jax.ShapeDtypeStruct((ROWS, WIDTH), F32), jax.ShapeDtypeStruct((ROWS, WIDTH), BF16)],
        [attended, w_out, tokens, gains],
        grid=(1,),
        in_specs=[whole(ROWS, WIDTH), whole(WIDTH, WIDTH), whole(ROWS, WIDTH), whole(8, WIDTH)],
        out_specs=[whole(ROWS, WIDTH)] * 2,
    )


def experts(rows, grads, meta, meta_t, w_gate, w_up, w_down):
    half = SLOTS // 2

    def body(
        x_ref, g_ref, m_ref, mt_ref, wg_ref, wu_ref, wd_ref,
        xin_ref, dr_ref, act_ref, dg_ref, du_ref, out_ref, dx_ref,
        made, back, weight,
    ):
        e = pl.program_id(0)

        @pl.when(e == 0)
        def _():
            slot_id = lax.broadcasted_iota(jnp.int32, (PAIR_CAP, PAIR_ROWS), 0).astype(F32)

            def pick(p, _):
                meta_p = m_ref[p]
                parts, gates = [], []
                for k in range(LOCAL):
                    hit = slot_id == meta_p[k : k + 1, :]
                    parts.append(jnp.where(hit, 1.0, 0.0).astype(BF16))
                    gates.append(
                        jnp.sum(jnp.where(hit, meta_p[4 + k : 5 + k, :], 0.0), axis=1, keepdims=True)
                    )
                chosen = jnp.concatenate(parts, axis=0)
                rows_p = dot(chosen, x_ref[p]).astype(BF16)
                grads_p = dot(chosen, g_ref[p])
                at = pl.ds(pl.multiple_of(p * PAIR_CAP, PAIR_CAP), PAIR_CAP)
                for k in range(LOCAL):
                    piece = slice(k * PAIR_CAP, (k + 1) * PAIR_CAP)
                    xin_ref[k, at, :] = rows_p[piece]
                    dr_ref[k, at, :] = (grads_p[piece] * gates[k]).astype(BF16)
                    weight[k, at, :] = gates[k]
                return 0

            lax.fori_loop(0, PAIRS, pick, 0)

        def work(h, _):
            at = pl.ds(pl.multiple_of(h * half, half), half)
            x = xin_ref[e, at, :]
            dr = dr_ref[e, at, :]
            gate = dot(x, wg_ref[0])
            up = dot(x, wu_ref[0])
            sig = jax.nn.sigmoid(gate)
            silu = gate * sig
            act = (silu * up).astype(BF16)
            act_ref[0, at, :] = act
            d_act = dot(dr, wd_ref[0], NT)
            d_gate = (d_act * up * sig * (1.0 + gate * (1.0 - sig))).astype(BF16)
            d_up = (d_act * silu).astype(BF16)
            dg_ref[0, at, :] = d_gate
            du_ref[0, at, :] = d_up
            y = (dot(act, wd_ref[0]) * weight[e, at, :]).astype(BF16)
            dch = (dot(d_gate, wg_ref[0], NT) + dot(d_up, wu_ref[0], NT)).astype(BF16)
            place_at = pl.ds(pl.multiple_of(e * PAIR_CAP, PAIR_CAP), PAIR_CAP)
            for k in range(2):
                piece = slice(k * PAIR_CAP, (k + 1) * PAIR_CAP)
                made[2 * h + k, place_at, :] = y[piece]
                back[2 * h + k, place_at, :] = dch[piece]
            return 0

        lax.fori_loop(0, 2, work, 0)

        @pl.when(e == LOCAL - 1)
        def _():
            lane_id = lax.broadcasted_iota(jnp.int32, (PAIR_ROWS, PAIR_SLOTS), 1).astype(F32)

            def give(p, _):
                meta_p = mt_ref[p]
                chosen = jnp.zeros((PAIR_ROWS, PAIR_SLOTS), F32)
                for k in range(LOCAL):
                    spot = meta_p[:, k : k + 1]
                    lane = jnp.where(spot < 0.0, -1.0, spot + float(k * PAIR_CAP))
                    chosen = chosen + jnp.where(lane_id == lane, 1.0, 0.0)
                chosen = chosen.astype(BF16)
                dx_ref[p] = dot(chosen, back[p]).astype(BF16)
                out_ref[p] = dot(chosen, made[p]).astype(BF16)
                return 0

            lax.fori_loop(0, PAIRS, give, 0)

    def fixed(*shape):
        return pl.BlockSpec(shape, lambda e: (0,) * len(shape), pipeline_mode=pl.Buffered(1))

    def each(*shape):
        return pl.BlockSpec((1,) + shape, lambda e: (e, 0, 0))

    return compute_call(
        body,
        "experts",
        [
            jax.ShapeDtypeStruct((LOCAL, SLOTS, WIDTH), BF16),
            jax.ShapeDtypeStruct((LOCAL, SLOTS, WIDTH), BF16),
            jax.ShapeDtypeStruct((LOCAL, SLOTS, FF), BF16),
            jax.ShapeDtypeStruct((LOCAL, SLOTS, FF), BF16),
            jax.ShapeDtypeStruct((LOCAL, SLOTS, FF), BF16),
            jax.ShapeDtypeStruct((PAIRS, PAIR_ROWS, WIDTH), BF16),
            jax.ShapeDtypeStruct((PAIRS, PAIR_ROWS, WIDTH), BF16),
        ],
        [rows, grads, meta, meta_t, w_gate, w_up, w_down],
        vmem=60,
        grid=(LOCAL,),
        in_specs=[
            fixed(PAIRS, PAIR_ROWS, WIDTH),
            fixed(PAIRS, PAIR_ROWS, WIDTH),
            fixed(PAIRS, 8, PAIR_ROWS),
            fixed(PAIRS, PAIR_ROWS, 8),
            each(WIDTH, FF),
            each(WIDTH, FF),
            each(FF, WIDTH),
        ],
        out_specs=[
            fixed(LOCAL, SLOTS, WIDTH),
            fixed(LOCAL, SLOTS, WIDTH),
            each(SLOTS, FF),
            each(SLOTS, FF),
            each(SLOTS, FF),
            fixed(PAIRS, PAIR_ROWS, WIDTH),
            fixed(PAIRS, PAIR_ROWS, WIDTH),
        ],
        scratch_shapes=[
            pltpu.VMEM((PAIRS, PAIR_SLOTS, WIDTH), BF16),
            pltpu.VMEM((PAIRS, PAIR_SLOTS, WIDTH), BF16),
            pltpu.VMEM((LOCAL, SLOTS, 1), F32),
        ],
    )


def norm_back(values, total_squares, width, weighted, mask=None):
    scale = row_scale(total_squares, width)
    inner = jnp.sum(weighted * values, axis=1, keepdims=True) * (1.0 / width)
    return scale * weighted - values * (scale * scale * scale) * inner, scale


def back_to_branch(d_ffn, resid, cotangent, gains, w_out):
    def body(p_ref, r_ref, c_ref, g_ref, w_ref, dr_ref, db_ref, da_ref, gg_ref):
        incoming = p_ref[...]
        resid_v = r_ref[...]
        squares = jnp.sum(resid_v * resid_v, axis=1, keepdims=True)
        d_norm, scale = norm_back(resid_v, squares, WIDTH, incoming * g_ref[3:4, :])
        gg_ref[...] = jnp.sum(incoming * resid_v * scale, axis=0, keepdims=True)
        d_resid = c_ref[...].astype(F32) + d_norm
        dr_ref[...] = d_resid
        d_branch = d_resid.astype(BF16)
        db_ref[...] = d_branch
        da_ref[...] = dot(d_branch, w_ref[...], NT).astype(BF16)

    return compute_call(
        body,
        "back_to_branch",
        [
            jax.ShapeDtypeStruct((ROWS, WIDTH), F32),
            jax.ShapeDtypeStruct((ROWS, WIDTH), BF16),
            jax.ShapeDtypeStruct((ROWS, WIDTH), BF16),
            jax.ShapeDtypeStruct((1, WIDTH), F32),
        ],
        [d_ffn, resid, cotangent, gains, w_out],
        grid=(1,),
        in_specs=[whole(ROWS, WIDTH)] * 3 + [whole(8, WIDTH), whole(WIDTH, WIDTH)],
        out_specs=[whole(ROWS, WIDTH)] * 3 + [whole(1, WIDTH)],
    )


def out_grads(attended, d_branch):
    def body(a_ref, d_ref, o_ref):
        def part(r, _):
            at = pl.ds(pl.multiple_of(r * 256, 256), 256)
            o_ref[at, :] = dot(a_ref[:, at], d_ref[...], TN).astype(BF16)
            return 0

        lax.fori_loop(0, 4, part, 0)

    return compute_call(
        body, "out_grads", [jax.ShapeDtypeStruct((WIDTH, WIDTH), BF16)], [attended, d_branch]
    )[0]


def deliver(resid, layer_keep, layer_got, dense, out_grad, gain_sums, input_grad, expert_sums):
    def body(
        r_ref, k_ref, g_ref, d_ref, o_ref, s_ref, i_ref, eg_ref, eu_ref, ed_ref,
        lo, wq, wk, wv, wo, ga, gq, gk, gf, di, eg, eu, ed,
    ):
        lo[...] = (r_ref[...] + k_ref[...] + g_ref[...].astype(F32)).astype(BF16)
        wq[...] = d_ref[0].astype(F32)
        for c in range(4):
            k, v = apart([d_ref[1, :, (2 * c + j) * 128 : (2 * c + j + 1) * 128].astype(F32) for j in range(2)])
            wk[:, c * 128 : (c + 1) * 128] = k
            wv[:, c * 128 : (c + 1) * 128] = v
        wo[...] = o_ref[...].astype(F32)
        ga[...] = s_ref[0:1, :]
        gq[...] = s_ref[1:2, :]
        gk[...] = s_ref[2:3, 0:64]
        gf[...] = s_ref[3:4, :]
        di[...] = i_ref[...]
        eg[...] = eg_ref[...]
        eu[...] = eu_ref[...]
        ed[...] = ed_ref[...]

    return compute_call(
        body,
        "deliver",
        [
            jax.ShapeDtypeStruct((ROWS, WIDTH), BF16),
            jax.ShapeDtypeStruct((128, WIDTH), F32),
            jax.ShapeDtypeStruct((128, 512), F32),
            jax.ShapeDtypeStruct((128, 512), F32),
            jax.ShapeDtypeStruct((128, WIDTH), F32),
            jax.ShapeDtypeStruct((1, 128), F32),
            jax.ShapeDtypeStruct((1, 128), F32),
            jax.ShapeDtypeStruct((1, 64), F32),
            jax.ShapeDtypeStruct((1, 128), F32),
            jax.ShapeDtypeStruct((ROWS, WIDTH), F32),
        ]
        + [jax.ShapeDtypeStruct(a.shape, F32) for a in expert_sums],
        [resid, layer_keep, layer_got, dense, out_grad, gain_sums, input_grad, *expert_sums],
    )


def cosine_of_turns(turns):
    part = turns - jnp.floor(turns + 0.5)
    square = part * part * 39.47841760435743
    total = jnp.full_like(square, -1.0 / 6402373705728000.0)
    for n in (20922789888000.0, -87178291200.0, 479001600.0, -3628800.0, 40320.0, -720.0, 24.0, -2.0, 1.0):
        total = total * square + 1.0 / n
    return total


def front(tokens, cotangent, dense, norms, perm, lengths):
    half = 64

    def body(
        t_ref, cot_ref, wq_ref, wk_ref, wv_ref, wd_ref, na_ref, nq_ref, nk_ref, nf_ref, perm_ref, len_ref,
        wo_ref, go_ref, n_ref, ql_ref, kl_ref, s_ref, c_ref, sn_ref, p_ref, q_ref, kv_ref, co_ref,
        g_ref, w_mine, rows, normed, gains_v, w_own, totals, totals_all, kv_half, send_sem, recv_sem, local_sem,
    ):
        _, chip, core, sibling = place()
        me = lax.axis_index("exp")
        chips, exps = ring_of(chip), ring_of(me)
        twins = [lax.rem(chip + d, CHIPS) for d in (2, 6, 4, 1, 3, 5, 7)]
        to_chip = lambda p: ("ctx", 2 * p + core)
        to_exp = lambda p: ("exp", p)
        copier = Copier(send_sem, recv_sem, local_sem)
        keys = key_lanes()
        odd = lax.rem(chip, 2) == 1
        wk, wv = wk_ref[:, lanes(chip // 2)].astype(F32), wv_ref[:, lanes(chip // 2)].astype(F32)
        wk = jnp.where(odd, pltpu.roll(wk, 64, 1), wk)
        wv = jnp.where(odd, wv, pltpu.roll(wv, 64, 1))
        w_mine[:, 0:128] = wq_ref[:, lanes(chip)]
        w_mine[:, 128:256] = jnp.where(keys, wk, wv).astype(BF16)
        g_ref[...] = jnp.ones((8, 128), F32)
        g_ref[0:1, :] = na_ref[...].astype(F32)
        g_ref[1:2, :] = nq_ref[...].astype(F32)
        g_ref[2:3, 0:64] = nk_ref[...].astype(F32)
        g_ref[3:4, :] = nf_ref[...].astype(F32)
        meet([to_chip(p) for p in twins] + [to_exp(p) for p in exps[1:]] + [("ctx", sibling)])
        gain_sends = [copier.send(g_ref, gains_v.at[me], *to_exp(p)) for p in exps[1:]]
        part = pl.ds(pl.multiple_of(core * half, half), half)
        slot = lambda s: wo_ref.at[s, part]
        handed = []

        def norm(block, s):
            x = block.astype(F32)
            scale = row_scale(jnp.sum(x * x, axis=1, keepdims=True), WIDTH)
            for e in range(EXP):
                at = slice(e * 128, (e + 1) * 128)
                normed[s, :, at] = (x[:, at] * scale * gains_v[e, 0:1, :]).astype(BF16)

        projected = []

        def project(s):
            both = dot(normed[s], w_own[...].reshape(WIDTH, 256))
            q, kv = both[:, 0:128], both[:, 128:256]
            ql_ref[s] = q
            kl_ref[s] = kv
            totals[s] = both_totals(q * q, kv * kv)

        def landed(s):
            norm(rows[s], s)
            projected.append(s)

        main = relay(copier, t_ref, lambda s: rows.at[s], ROWS, chips, to_chip, landed)
        extra = relay(copier, cot_ref, lambda s: co_ref.at[s], ROWS, exps, to_exp)
        dense = relay(
            copier,
            wd_ref.at[part],
            slot,
            half,
            exps,
            to_exp,
            lambda s: handed.append(copier.send(slot(s), slot(s), "ctx", sibling)),
        )
        next(main)
        next(main)
        next(dense)
        next(dense)
        copier.keep(wd_ref, wo_ref.at[me])
        copier.keep(cot_ref, co_ref.at[me])
        w_own[me] = w_mine[...]
        gains_v[me] = g_ref[...]

        row = lax.broadcasted_iota(jnp.int32, (CTX, ROWS), 1)
        piece = jnp.where(row // 12 == lax.broadcasted_iota(jnp.int32, (CTX, ROWS), 0), 1.0, 0.0)
        dealt = dot(perm_ref[...].astype(F32).astype(BF16), piece.astype(BF16))
        source = lax.broadcasted_iota(jnp.int32, (CTX, ROWS), 0)
        position = (source * CTX).astype(F32) + dealt
        position = position * 12.0 + lax.rem(row, 12).astype(F32)
        begin = jnp.zeros((CTX, ROWS), F32)
        ends = jnp.zeros((1, 1), F32)
        for k in range(3):
            ends = ends + len_ref[0:1, k : k + 1].astype(F32)
            begin = jnp.where(position >= ends, ends, begin)
        for i in range(CHIPS):
            mine = [jnp.where(core == 0, v[2 * i : 2 * i + 1], v[2 * i + 1 : 2 * i + 2]) for v in (position, begin)]
            p_ref[i] = jnp.concatenate(mine, axis=0)

        def angles(i, _):
            keys = key_lanes()
            lane = lax.broadcasted_iota(jnp.int32, (1, 128), 1)
            freq = jnp.exp(lax.rem(lane, 32).astype(F32) * (-2.0 / 64 * 9.210340371976184))
            place_i = p_ref[i]
            offset = down_rows(place_i, 0) - down_rows(place_i, 1)
            mixed = cosine_of_turns(offset * (freq * 0.15915494309189535) - jnp.where(keys, 0.0, 0.25))
            other = pltpu.roll(mixed, 64, 1)
            c_ref[i] = jnp.where(keys, mixed, other)
            sn_ref[i] = jnp.where(keys, other, mixed)
            return 0

        lax.fori_loop(0, CHIPS, angles, 0)
        for at in gain_sends:
            copier.arrived(at)
        go_ref[...] = gains_v[...]
        norm(t_ref[...], chip)
        projected.append(chip)
        next(main)
        next(dense)
        next(main)
        own_sends = [copier.send(w_mine, w_own.at[me], *to_exp(p)) for p in exps[1:]]
        next(extra)
        next(extra)
        next(dense)
        next(main)
        next(main)
        next(dense)
        for at in own_sends:
            copier.arrived(at)
        for s in projected:
            project(s)
        projected.clear()
        next(extra)
        next(extra)
        next(main)
        next(dense)
        for s in projected:
            project(s)
        projected.clear()
        side_by_side(main)
        for s in projected:
            project(s)
        shares = [copier.send(totals, totals_all.at[chip], *to_chip(p)) for p in twins]
        totals_all[chip] = totals[...]
        side_by_side(dense)
        copier.keep(normed, n_ref)
        for _ in range(3):
            next(extra)
        for at in shares:
            copier.arrived(at)

        def turn_one(i, _):
            squares = totals_all[0, i]
            for c in range(1, CHIPS):
                squares = squares + totals_all[c, i]
            s_ref[i] = squares
            cos, sin = c_ref[i], sn_ref[i]
            gain = gains_v[chip]
            q = ql_ref[i] * row_scale(down_rows(squares, 0), WIDTH) * gain[1:2, :]
            q = turn(q, cos, sin).astype(BF16).astype(F32)
            q_ref[i] = (q * 0.125).astype(BF16)
            scale = jnp.where(keys, row_scale(down_rows(squares, 1), WIDTH // 2), 1.0)
            kv = kl_ref[i] * scale * gain[2:3, :]
            kv_half[i] = turn(kv, jnp.where(keys, cos, 1.0), jnp.where(keys, sin, 0.0)).astype(BF16)
            return 0

        lax.fori_loop(0, CHIPS, turn_one, 0)
        copier.send(kv_half, kv_ref.at[:, core], "ctx", sibling)
        copier.keep(kv_half, kv_ref.at[:, core])
        side_by_side(extra)
        copier.finish()

    vmem = pl.BlockSpec(memory_space=pltpu.VMEM)
    wide = jax.ShapeDtypeStruct((CHIPS, ROWS, 128), F32)
    return pl.pallas_call(
        body,
        name="front",
        out_shape=[
            jax.ShapeDtypeStruct((EXP, 128, WIDTH), BF16),
            jax.ShapeDtypeStruct((EXP, 8, 128), F32),
            jax.ShapeDtypeStruct((CHIPS, ROWS, WIDTH), BF16),
            wide,
            wide,
            jax.ShapeDtypeStruct((CHIPS, 2, ROWS), F32),
            wide,
            wide,
            jax.ShapeDtypeStruct((CHIPS, 2, ROWS), F32),
            jax.ShapeDtypeStruct((CHIPS, ROWS, 128), BF16),
            jax.ShapeDtypeStruct((CHIPS, 2, ROWS, 128), BF16),
            jax.ShapeDtypeStruct((EXP, ROWS, WIDTH), BF16),
        ],
        in_specs=[vmem] * 12,
        out_specs=[ANY_SPEC, vmem, ANY_SPEC] + [vmem] * 7 + [ANY_SPEC] * 2,
        scratch_shapes=[
            pltpu.VMEM((8, 128), F32),
            pltpu.VMEM((128, 256), BF16),
            pltpu.VMEM((CHIPS, ROWS, WIDTH), BF16),
            pltpu.VMEM((CHIPS, ROWS, WIDTH), BF16),
            pltpu.VMEM((EXP, 8, 128), F32),
            pltpu.VMEM((EXP, 128, 256), BF16),
            pltpu.VMEM((CHIPS, 2, ROWS), F32),
            pltpu.VMEM((CHIPS, CHIPS, 2, ROWS), F32),
            pltpu.VMEM((CHIPS, ROWS, 128), BF16),
            pltpu.SemaphoreType.DMA((71,)),
            pltpu.SemaphoreType.DMA((71,)),
            pltpu.SemaphoreType.DMA((8,)),
        ],
        compiler_params=pltpu.CompilerParams(
            collective_id=1, has_side_effects=True, vmem_limit_bytes=60 * MIB
        ),
    )(tokens, cotangent, *dense, *norms, perm, lengths)


def apart(pieces):
    first, second = pieces
    keys = key_lanes()
    return (
        jnp.where(keys, first, pltpu.roll(second, 64, 1)),
        jnp.where(keys, pltpu.roll(first, 64, 1), second),
    )


def tail(
    dq, dkv_mine, dkv_other, q_lin, kv_lin, cosine, sine, squares, gains, normed, out_part, layer_part,
    weights, tokens, d_resid, ffn_gain, gate_part, up_part, down_a, down_b,
):
    def body(
        dq_ref, dm_ref, do_ref, ql_ref, kl_ref, c_ref, sn_ref, s_ref, g_ref, n_ref, op_ref, lp_ref,
        w_ref, t_ref, r_ref, fg_ref, gp_ref, up_ref, da_ref, db_ref,
        eg_ref, eu_ref, ed_ref, di_ref, dense_ref, og_ref, lo_ref, gs_ref,
        dq_v, dm_v, ql_v, kl_v, c_v, sn_v, n_v, w_v, t_v, r_v,
        got, e_q, e_kv, totals, totals_all, d_lin, home, w_give, w_keep, w_got, joint, traded, done,
        o_keep, o_got, o_traded, o_half, a_got, a_done, packet, packets, mine, shared, gate_c, down_c, up_d, down_d, send_sem, recv_sem, local_sem,
    ):
        ctx, chip, core, sibling = place()
        me = lax.axis_index("exp")
        twins = [lax.rem(chip + d, CHIPS) for d in (2, 6, 4, 1, 3, 5, 7)]
        exps = [lax.rem(me + d, EXP) for d in range(1, EXP)]
        others = [lax.rem(ctx + d, CTX) for d in range(1, CTX)]
        to_chip = lambda p: ("ctx", 2 * p + core)
        copier = Copier(send_sem, recv_sem, local_sem)
        heads = [
            copier.keep(src, dst)
            for src, dst in ((dq_ref, dq_v), (c_ref, c_v), (sn_ref, sn_v), (ql_ref, ql_v), (kl_ref, kl_v), (dm_ref, dm_v))
        ]
        late = [
            copier.keep(src, dst)
            for src, dst in ((n_ref, n_v), (w_ref, w_v), (t_ref, t_v), (r_ref, r_v))
        ]
        o_load = copier.keep(op_ref.at[:, core], o_keep)
        meet([("ctx", p) for p in others] + [("exp", p) for p in exps])
        swapped = copier.send(do_ref, got, "ctx", sibling)
        o_swap = copier.send(op_ref.at[:, 1 - core], o_got, "ctx", sibling)
        keys = key_lanes()
        gain = g_ref[chip]
        for at in heads:
            copier.kept(at)

        def unturn_q(i, _):
            e_q[i] = turn(dq_v[i], c_v[i], -sn_v[i])
            return 0

        lax.fori_loop(0, CHIPS, unturn_q, 0)
        copier.arrived(swapped)

        def unturn_kv(i, carry):
            q_sum, kv_sum = carry
            cos, sin = jnp.where(keys, c_v[i], 1.0), jnp.where(keys, -sn_v[i], 0.0)
            e = turn(dm_v[i] + got[i].astype(F32), cos, sin)
            e_kv[i] = e
            q_part, kv_part = e_q[i] * ql_v[i], e * kl_v[i]
            totals[i] = both_totals(q_part * gain[1:2, :], kv_part * gain[2:3, :])
            q_scale = row_scale(down_rows(s_ref[i], 0), WIDTH)
            k_scale = row_scale(down_rows(s_ref[i], 1), WIDTH // 2)
            q_sum = q_sum + jnp.sum(q_part * q_scale, axis=0, keepdims=True)
            kv_sum = kv_sum + jnp.sum(kv_part * jnp.where(keys, k_scale, 1.0), axis=0, keepdims=True)
            return q_sum, kv_sum

        none = jnp.zeros((1, 128), F32)
        q_sum, kv_sum = lax.fori_loop(0, CHIPS, unturn_kv, (none, none))
        shares = [copier.send(totals, totals_all.at[chip], *to_chip(p)) for p in twins]
        totals_all[chip] = totals[...]
        copier.kept(o_load)
        copier.arrived(o_swap)

        def add_cores(e, _):
            o_keep[e] = (o_keep[e].astype(F32) + o_got[e].astype(F32)).astype(BF16)
            return 0

        lax.fori_loop(0, EXP, add_cores, 0)
        o_trades = [copier.send(o_keep.at[p], o_traded.at[me], "exp", p) for p in exps]
        for at in shares:
            copier.arrived(at)

        def gradient(i):
            inner = totals_all[0, i]
            for c in range(1, CHIPS):
                inner = inner + totals_all[c, i]
            squares_i = s_ref[i]
            q_scale = row_scale(down_rows(squares_i, 0), WIDTH)
            k_scale = row_scale(down_rows(squares_i, 1), WIDTH // 2)
            q_cut = q_scale * q_scale * q_scale * down_rows(inner, 0) * (1.0 / WIDTH)
            k_cut = k_scale * k_scale * k_scale * down_rows(inner, 1) * (2.0 / WIDTH)
            d_lin[0, i] = (q_scale * (e_q[i] * gain[1:2, :]) - ql_v[i] * q_cut).astype(BF16)
            kv_scale = jnp.where(keys, k_scale, 1.0)
            k_cut = jnp.where(keys, k_cut, 0.0)
            d_lin[1, i] = (kv_scale * (e_kv[i] * gain[2:3, :]) - kl_v[i] * k_cut).astype(BF16)

        homeward = []
        for p in twins:
            gradient(p)
            for k in range(2):
                homeward.append(copier.send(d_lin.at[k, p], home.at[k, :, lanes(chip)], *to_chip(p)))
        zh, y = chip // 4, lax.rem(chip, 4)
        second = []
        for d in (1, 3, 2):
            c = lax.rem(y + d, 4)
            second.append(copier.send(gp_ref.at[c], gate_c.at[y], *to_chip(zh * 4 + c)))
            second.append(copier.send(da_ref.at[c], down_c.at[y], *to_chip(zh * 4 + c)))
        second.append(copier.send(up_ref.at[1 - zh], up_d, *to_chip((1 - zh) * 4 + y)))
        second.append(copier.send(db_ref.at[1 - zh], down_d, *to_chip((1 - zh) * 4 + y)))
        gradient(chip)
        for k in range(2):
            home[k, :, lanes(chip)] = d_lin[k, chip]
        for at in late:
            copier.kept(at)

        def columns_grad(half, out):
            d = d_lin[half].reshape(CHIPS * ROWS, 128)

            def part(r, _):
                n = n_v[:, :, pl.ds(pl.multiple_of(r * 256, 256), 256)].reshape(CHIPS * ROWS, 256)
                out[pl.ds(pl.multiple_of(r * 256, 256), 256), :] = dot(n, d, TN).astype(BF16)
                return 0

            lax.fori_loop(0, 4, part, 0)

        for at in o_trades:
            copier.arrived(at)
        o_traded[me] = o_keep[me]
        total = o_traded[0].astype(F32)
        for e in range(1, EXP):
            total = total + o_traded[e].astype(F32)
        o_half[...] = total.astype(BF16)
        spread = [copier.send(o_half.at[:, lanes(p)], a_got.at[chip], *to_chip(p)) for p in twins]
        a_got[chip] = o_half[:, lanes(chip)]
        columns_grad(1 - core, w_give)
        w_swap = copier.send(w_give, w_got, "ctx", sibling)
        columns_grad(core, w_keep)
        copier.arrived(w_swap)
        both = w_keep[...].astype(F32) + w_got[...].astype(F32)
        joint[...] = both.astype(BF16).reshape(EXP, 128, 128)
        trades = [copier.send(joint.at[p], traded.at[me], "exp", p) for p in exps]
        traded[me] = joint[me]
        for at in spread:
            copier.arrived(at)
        total = a_got[0].astype(F32)
        for c in range(1, CHIPS):
            total = total + a_got[c].astype(F32)
        a_done[...] = total.astype(BF16)

        for at in homeward:
            copier.arrived(at)
        k_parts, v_parts = [], []
        for c in range(4):
            k, v = apart([home[1, :, (2 * c + j) * 128 : (2 * c + j + 1) * 128].astype(F32) for j in range(2)])
            k_parts.append(k.astype(BF16))
            v_parts.append(v.astype(BF16))
        left = jnp.concatenate([home[0]] + k_parts + v_parts, axis=1)
        x = t_v[...].astype(F32)
        scale = row_scale(jnp.sum(x * x, axis=1, keepdims=True), WIDTH)
        inner = jnp.zeros((ROWS, 1), F32)
        pieces = []
        for e in range(EXP):
            at = slice(e * 128, (e + 1) * 128)
            d_normed = dot(left, w_v[e], NT).astype(BF16).astype(F32)
            packet[e] = jnp.zeros((8, 128), F32)
            packet[e, 0:1, :] = jnp.sum(d_normed * x[:, at] * scale, axis=0, keepdims=True)
            packet[e, 3:4, :] = fg_ref[:, at]
            weighted = d_normed * g_ref[e, 0:1, :]
            inner = inner + jnp.sum(weighted * x[:, at], axis=1, keepdims=True)
            pieces.append(weighted)
        packet[chip, 1:2, :] = q_sum
        packet[chip, 2:3, :] = kv_sum
        gain_trades = [copier.send(packet.at[p], packets.at[me], "exp", p) for p in exps]
        packets[me] = packet[me]

        for at in trades:
            copier.arrived(at)
        total = traded[0].astype(F32)
        for e in range(1, EXP):
            total = total + traded[e].astype(F32)
        done[...] = total.astype(BF16)
        spot = dense_ref.at[core, :, lanes(chip)]
        w_shares = [copier.send(done, spot, *to_chip(p)) for p in twins]
        copier.send(done, spot, "ctx", sibling)
        copier.keep(done, spot)
        half = pl.ds(pl.multiple_of(core * 64, 64), 64)
        a_shares = [copier.send(a_done, og_ref.at[half, lanes(chip)], *to_chip(p)) for p in twins]
        copier.send(a_done, og_ref.at[half, lanes(chip)], "ctx", sibling)
        copier.keep(a_done, og_ref.at[half, lanes(chip)])
        copier.send(lp_ref, lo_ref, "exp", lax.rem(me + 4, EXP))

        for at in gain_trades:
            copier.arrived(at)
        total = packets[0]
        for e in range(1, EXP):
            total = total + packets[e]
        mine[...] = total
        gain_shares = [copier.send(mine, shared.at[ctx], "ctx", p) for p in others]
        shared[ctx] = total

        inner = inner * (1.0 / WIDTH)
        cut = scale * scale * scale * inner
        for e in range(EXP):
            at = slice(e * 128, (e + 1) * 128)
            di_ref[:, at] = r_v[:, at] + scale * pieces[e] - x[:, at] * cut
        for at in second:
            copier.arrived(at)
        columns = [lax.rem(y + d, 4) for d in (1, 2, 3)]

        def add_experts(e, _):
            total = gp_ref[y, e].astype(F32)
            for c in columns:
                total = total + gate_c[c, e].astype(F32)
            eg_ref[e] = total
            eu_ref[e] = up_ref[zh, e].astype(F32) + up_d[e].astype(F32)
            return 0

        lax.fori_loop(0, LOCAL, add_experts, 0)
        for e in range(2):
            total = da_ref[y, e].astype(F32)
            for c in columns:
                total = total + down_c[c, e].astype(F32)
            ed_ref[e] = total
            ed_ref[e + 2] = db_ref[zh, e].astype(F32) + down_d[e].astype(F32)
        for d, at in zip((2, 6, 4, 1, 3, 5, 7), w_shares):
            copier.arrived(at)
            got_at = dense_ref.at[core, :, lanes(lax.rem(chip + CHIPS - d, CHIPS))]
            copier.send(got_at, got_at, "ctx", sibling)
        for d, at in zip((2, 6, 4, 1, 3, 5, 7), a_shares):
            copier.arrived(at)
            got_at = og_ref.at[half, lanes(lax.rem(chip + CHIPS - d, CHIPS))]
            copier.send(got_at, got_at, "ctx", sibling)
        for at in gain_shares:
            copier.arrived(at)
        total = shared[0]
        for c in range(1, CTX):
            total = total + shared[c]
        gs_ref[...] = total
        copier.finish()

    vmem = pl.BlockSpec(memory_space=pltpu.VMEM)
    block = (CHIPS, ROWS, 128)
    tile = pltpu.VMEM((128, 128), BF16)
    return pl.pallas_call(
        body,
        name="tail",
        out_shape=[
            jax.ShapeDtypeStruct((LOCAL, 64, FF), F32),
            jax.ShapeDtypeStruct((LOCAL, 64, FF), F32),
            jax.ShapeDtypeStruct((LOCAL, 32, WIDTH), F32),
            jax.ShapeDtypeStruct((ROWS, WIDTH), F32),
            jax.ShapeDtypeStruct((2, 128, WIDTH), BF16),
            jax.ShapeDtypeStruct((128, WIDTH), BF16),
            jax.ShapeDtypeStruct((ROWS, WIDTH), BF16),
            jax.ShapeDtypeStruct((8, 128), F32),
        ],
        in_specs=[ANY_SPEC] * 7 + [vmem] * 2 + [ANY_SPEC] * 6 + [vmem] * 5,
        out_specs=[vmem] * 4 + [ANY_SPEC] * 3 + [vmem],
        scratch_shapes=[
            pltpu.VMEM(block, F32),
            pltpu.VMEM(block, F32),
            pltpu.VMEM(block, F32),
            pltpu.VMEM(block, F32),
            pltpu.VMEM(block, F32),
            pltpu.VMEM(block, F32),
            pltpu.VMEM((CHIPS, ROWS, WIDTH), BF16),
            pltpu.VMEM((EXP, 128, 2 * WIDTH), BF16),
            pltpu.VMEM((ROWS, WIDTH), BF16),
            pltpu.VMEM((ROWS, WIDTH), F32),
            pltpu.VMEM(block, BF16),
            pltpu.VMEM(block, F32),
            pltpu.VMEM(block, F32),
            pltpu.VMEM((CHIPS, 2, ROWS), F32),
            pltpu.VMEM((CHIPS, CHIPS, 2, ROWS), F32),
            pltpu.VMEM((2,) + block, BF16),
            pltpu.VMEM((2, ROWS, WIDTH), BF16),
            pltpu.VMEM((WIDTH, 128), BF16),
            pltpu.VMEM((WIDTH, 128), BF16),
            pltpu.VMEM((WIDTH, 128), BF16),
            pltpu.VMEM((EXP, 128, 128), BF16),
            pltpu.VMEM((EXP, 128, 128), BF16),
            tile,
            pltpu.VMEM((EXP, 64, WIDTH), BF16),
            pltpu.VMEM((EXP, 64, WIDTH), BF16),
            pltpu.VMEM((EXP, 64, WIDTH), BF16),
            pltpu.VMEM((64, WIDTH), BF16),
            pltpu.VMEM((CHIPS, 64, 128), BF16),
            pltpu.VMEM((64, 128), BF16),
            pltpu.VMEM((EXP, 8, 128), F32),
            pltpu.VMEM((EXP, 8, 128), F32),
            pltpu.VMEM((8, 128), F32),
            pltpu.VMEM((CTX, 8, 128), F32),
            pltpu.VMEM((4, LOCAL, 64, FF), BF16),
            pltpu.VMEM((4, 2, 32, WIDTH), BF16),
            pltpu.VMEM((LOCAL, 64, FF), BF16),
            pltpu.VMEM((2, 32, WIDTH), BF16),
            pltpu.SemaphoreType.DMA((106,)),
            pltpu.SemaphoreType.DMA((106,)),
            pltpu.SemaphoreType.DMA((14,)),
        ],
        compiler_params=pltpu.CompilerParams(
            collective_id=6, has_side_effects=True, vmem_limit_bytes=60 * MIB
        ),
    )(
        dq, dkv_mine, dkv_other, q_lin, kv_lin, cosine, sine, squares, gains, normed, out_part, layer_part,
        weights, tokens, d_resid, ffn_gain, gate_part, up_part, down_a, down_b,
    )


def sum_blocks(blocks):
    return jnp.sum(blocks.astype(F32), axis=0)


def per_device(
    tokens,
    cotangent,
    lengths,
    deal_perm,
    routes,
    gate_logits,
    norm_attn,
    norm_query,
    norm_key,
    norm_ffn,
    w_query,
    w_key,
    w_value,
    w_out,
    w_gate,
    w_up,
    w_down,
):
    tokens, cotangent = tokens[0], cotangent[0]

    row = lambda v: v.reshape(1, -1)
    (
        w_o, gain_all, normed, q_lin, kv_lin, squares, cosine, sine, places, q_all, kv_all, grads_all,
    ) = front(
        tokens,
        cotangent,
        (w_query, w_key, w_value, w_out),
        (row(norm_attn), row(norm_query), row(norm_key), row(norm_ffn)),
        deal_perm[0],
        lengths,
    )

    pieces = jnp.arange(CTX, dtype=jnp.int32)[:, None] * CTX + deal_perm[0]
    positions = (pieces[:, :, None] * 12 + jnp.arange(12, dtype=jnp.int32)).reshape(CTX, ROWS)
    key_pos = positions.reshape(CHIPS, 1, CHUNK).astype(F32)
    first_chunk = jnp.min(places[:, 1], axis=1).astype(jnp.int32) // CHUNK
    gains = gain_all.transpose(1, 0, 2).reshape(8, WIDTH)
    w_o = w_o.reshape(WIDTH, WIDTH)
    kv_all = kv_all.reshape(KEYS, 128)
    out_low, out_wide, log_total = attend(q_all, kv_all, key_pos, places, first_chunk)
    attended = collect_heads(out_low)
    resid, ffn_rows = finish_attention(attended, w_o, tokens, gains)
    rows_all, meta_all = gather_rows(ffn_rows, route(routes[0].T, gate_logits[0].T))

    rows_all, dense_late = lax.optimization_barrier(
        (rows_all, jnp.concatenate([w_query, w_key, w_value], axis=1))
    )
    dense_late = lax.all_gather(dense_late, "exp", axis=0, tiled=True)

    shift = jnp.array([0.0, float(CAP)], F32)[None, None, :, None]
    spots = meta_all[:, :LOCAL].reshape(PAIRS, 2, LOCAL, ROWS).transpose(0, 2, 1, 3)
    spots = jnp.where(spots < 0.0, -1.0, spots + shift).reshape(PAIRS, LOCAL, PAIR_ROWS)
    gates = meta_all[:, LOCAL:].reshape(PAIRS, 2, LOCAL, ROWS).transpose(0, 2, 1, 3)
    pair_meta = jnp.concatenate([spots, gates.reshape(PAIRS, LOCAL, PAIR_ROWS)], axis=1)
    rows_in, d_rows, act, d_gate, d_up, out_parts, d_parts = experts(
        rows_all.reshape(PAIRS, PAIR_ROWS, WIDTH),
        grads_all.reshape(PAIRS, PAIR_ROWS, WIDTH),
        pair_meta,
        pair_meta.transpose(0, 2, 1),
        w_gate,
        w_up,
        w_down,
    )
    gate_part, up_part, down_a, down_b, d_ffn, layer_keep, layer_give = settle_experts(
        rows_in,
        d_rows,
        act,
        d_gate,
        d_up,
        d_parts.reshape(2, 4, ROWS, WIDTH),
        out_parts.reshape(2, 4, ROWS, WIDTH),
    )
    d_resid, d_branch, d_attended, ffn_gain_grad = back_to_branch(
        d_ffn, resid, cotangent, gains, w_o
    )
    d_out = spread_grads(d_attended)
    out_part = out_grads(attended, d_branch).reshape(EXP, 2, 64, WIDTH)
    dq, dkv_mine, dkv_other = attend_back(
        q_all, kv_all, d_out, out_wide, log_total, key_pos, places, first_chunk
    )
    gate_grad, up_grad, down_grad, input_grad, dense, out_grad, layer_got, gain_sums = tail(
        dq,
        dkv_mine,
        dkv_other,
        q_lin,
        kv_lin,
        cosine,
        sine,
        squares,
        gain_all,
        normed,
        out_part,
        layer_give,
        dense_late.reshape(EXP, 128, 2 * WIDTH),
        tokens,
        d_resid,
        ffn_gain_grad,
        gate_part,
        up_part,
        down_a,
        down_b,
    )
    outs = deliver(
        resid,
        layer_keep,
        layer_got,
        dense,
        out_grad,
        gain_sums,
        input_grad,
        (gate_grad, up_grad, down_grad),
    )
    return (
        outs[0][None],
        outs[9][None],
        *outs[1:5],
        *[g.reshape(-1) for g in outs[5:9]],
        *outs[10:],
    )


def solution(mesh):
    in_specs = (
        P("exp", "ctx", None),
        P("exp", "ctx", None),
        P("exp", None),
        P("exp", None, None),
        P("exp", "ctx", None),
        P("exp", "ctx", None),
        P("exp"),
        P("exp"),
        P("exp"),
        P("exp"),
        P("exp", None),
        P("exp", None),
        P("exp", None),
        P("exp", None),
        P("exp", None, None),
        P("exp", None, None),
        P("exp", None, None),
    )
    out_specs = (
        P("exp", "ctx", None),
        P("exp", "ctx", None),
        P("exp", None),
        P("exp", None),
        P("exp", None),
        P("exp", None),
        P("exp"),
        P("exp"),
        P("exp"),
        P("exp"),
        P("exp", "ctx", None),
        P("exp", "ctx", None),
        P("exp", "ctx", None),
    )
    return jax.shard_map(
        per_device, mesh=mesh, in_specs=in_specs, out_specs=out_specs, check_vma=False
    )
```

time: 443 us -> 391 us (0.88); the launches traced: 444 us -> 386 us
  Pallas kernels: 416 us -> 365 us
  other arithmetic: 9.36 us -> 4.27 us
    pallas_call x3 -> x2, Pallas kernels: 72.9 us -> 143 us  [the longest x1 80.4 us: tail(): pl.pallas_call(body, name='tail', out_shape=[jax.ShapeDtypeStruct((LOCAL,...]
    pallas_call x8 -> x3, Pallas kernels: 122 us -> 55.6 us  [comm_call(): pl.pallas_call(body, name=name, out_shape=outs, in_specs=in_specs or [ANY...]
    pallas_call x10 -> x6, Pallas kernels: 90.7 us -> 58 us  [compute_call(): pl.pallas_call(body, name=name, out_shape=outs, compiler_params=pltpu.Com...]
    pallas_call x1, Pallas kernels: 77.7 us -> 62.5 us  [settle_experts(): pl.pallas_call(body, name='settle_experts', out_shape=[jax.ShapeDtypeStru...]
  transfers between devices with their start and end apart: 2 -> 1, of which waited for: 0 -> 0; matrix products, arithmetic and copies ran while one was open for 2% -> 1% of each run, Pallas kernels for 35% -> 39%
where the time goes in v3:
time: 391 us; the launch traced here: 386 us
  Pallas kernels  365 us (93%)
  between operations  14.2 us (4%)
  other arithmetic  4.27 us (1%)
    pallas_call x1, Pallas kernels, tail(): pl.pallas_call(body, name='tail', out_shape=[jax.ShapeDtypeStruct((LOCAL,...  80.4 us
    pallas_call x1, Pallas kernels, settle_experts(): pl.pallas_call(body, name='settle_experts', out_shape=[jax.ShapeDtypeStru...  62.5 us
    pallas_call x1, Pallas kernels, front(): pl.pallas_call(body, name='front', out_shape=[jax.ShapeDtypeStruct((EXP,...  62.3 us
    pallas_call x6, Pallas kernels, compute_call(): pl.pallas_call(body, name=name, out_shape=outs, compiler_params=pltpu.Com...  58 us
    pallas_call x3, Pallas kernels, comm_call(): pl.pallas_call(body, name=name, out_shape=outs, in_specs=in_specs or [ANY...  55.6 us
    pallas_call x1, Pallas kernels, attend_back(): pl.pallas_call(body, name='attend_back', out_shape=[jax.ShapeDtypeStruct(...  28.3 us
    pallas_call x1, Pallas kernels, attend(): pl.pallas_call(body, name='attend', out_shape=[jax.ShapeDtypeStruct((CHIP...  17.5 us
  transfers between devices with their start and end apart: 1, of which 0 were waited for; matrix products, arithmetic and copies ran while one was open for 1% of the time, Pallas kernels for 39%

profile of v3, /device:TPU:1, one launch (start us, length us, event | category | flops | bytes accessed | tf_op | source)
XLA Modules:
  0.0 386.3 jit_solution(17178973855593797527)
XLA Ops:
  7.2 1.9 pad_maximum_fusion
  9.2 62.3 %front.1 = (bf16[8,128,1024]{2,1,0:T(8,128)(2,1)}, f32[8,8,128]{2,1,0:T(8,128)}, bf16[8,192,1024]{2,1,0:T(8,128)(2,1)}, f32[8,192,128]{2,1,0:T(8,128)}, f32[8,19...) custom-call(bf16[192,1024]{1,0:T(8,128)(2,1)} %bitcast.42, ...), custom_call_target="tpu_custom_call" | custom-call | tf_op jit(solution)/shard_map/front/pallas_call | solution.py:1188
  71.5 0.9 slice_reduce_fusion
  72.4 0.5 and_select_fusion.first_ref
  72.9 0.8 add_multiply_fusion
  73.7 0.1 add_convert_fusion
  73.8 0.7 convert_element_type.11.kp_ref
  74.5 17.5 %attend.1 = (bf16[8,192,128]{2,1,0:T(8,128)(2,1)}, f32[8,192,128]{2,1,0:T(8,128)}, f32[8,192,128]{2,1,0:T(8,128)}) custom-call(s32[8]{0:T(128)} %and_select_fusion.first_ref, bf16[8,192,128]{2,1,0:T(8,128)(2,1)} %get-tuple-element.77.q_ref, bf16[3072,128]{1,0:T(8,128)(2,1)} %bitcast.46, f32[8,1,384]{2,1,0:T(1,128)} %convert_element_type.11.kp_ref, ...), custom_call_target="tpu_custom_call" | custom-call | tf_op jit(solution)/shard_map/attend/pallas_call | solution.py:644
  92.0 9.3 %collect_heads.1.a_ref = bf16[192,1024]{1,0:T(8,128)(2,1)} custom-call(bf16[8,192,128]{2,1,0:T(8,128)(2,1)} %get-tuple-element.79.x_ref), custom_call_target="tpu_custom_call" | custom-call | tf_op jit(solution)/shard_map/collect_heads/pallas_call | solution.py:47
  101.3 1.5 route.1.m_ref
  102.9 3.4 finish_attention.1
  106.2 35.1 %gather_rows.1 = (bf16[8,192,1024]{2,1,0:T(8,128)(2,1)}, f32[8,8,192]{2,1,0:T(8,128)}) custom-call(bf16[192,1024]{1,0:T(8,128)(2,1)} %get-tuple-element.83.x_ref, f32[8,8,192]{2,1,0:T(8,128)} %route.1.m_ref), custom_call_target="tpu_custom_call" | custom-call | tf_op jit(solution)/shard_map/gather_rows/pallas_call | solution.py:47
  141.4 0.9 fusion
  142.4 0.1 reshape.154
  142.6 0.1 reshape.152
  142.7 1.2 copy.44
  143.9 40.6 %experts.1 = (bf16[4,576,1024]{2,1,0:T(8,128)(2,1)}, bf16[4,576,1024]{2,1,0:T(8,128)(2,1)}, bf16[4,576,512]{2,1,0:T(8,128)(2,1)}, bf16[4,576,512]{2,1,0:T(8,128)...) custom-call(bf16[4,384,1024]{2,1,0:T(8,128)(2,1)} %bitcast.49, ...), custom_call_target="tpu_custom_call" | custom-call | tf_op jit(solution)/shard_map/experts/pallas_call | solution.py:511
  184.5 62.5 %settle_experts.1 = (bf16[4,4,64,512]{3,2,1,0:T(8,128)(2,1)}, bf16[2,4,64,512]{3,2,1,0:T(8,128)(2,1)}, bf16[4,2,32,1024]{3,2,1,0:T(8,128)(2,1)}, bf16[2,2,32,102...) custom-call(bf16[4,576,1024]{2,1,0:T(8,128)(2,1)} %get-tuple-element.88.x_ref, ...), custom_call_target="tpu_custom_call" | custom-call | tf_op jit(solution)/shard_map/settle_experts/pallas_call | solution.py:457
  247.0 4.1 %back_to_branch.1 = (f32[192,1024]{1,0:T(8,128)}, bf16[192,1024]{1,0:T(8,128)(2,1)}, bf16[192,1024]{1,0:T(8,128)(2,1)}, f32[1,1024]{1,0:T(1,128)}) custom-call(f32[192,1024]{1,0:T(8,128)} %get-tuple-element.96.p_ref, f32[192,1024]{1,0:T(8,128)} %get-tuple-element.82.r_ref, bf16[192,1024]{1,0:T(8,128)(2,1)} %bitcast.53, f32[8,1024]{1,0:T(8,128)} %bitcast.55, ...), custom_call_target="tpu_custom_call" | custom-call | tf_op jit(solution)/shard_map/back_to_branch/pallas_call | solution.py:511
  251.1 11.2 %spread_grads.1.do_ref = bf16[8,192,128]{2,1,0:T(8,128)(2,1)} custom-call(bf16[192,1024]{1,0:T(8,128)(2,1)} %get-tuple-element.97.x_ref), custom_call_target="tpu_custom_call" | custom-call | tf_op jit(solution)/shard_map/spread_grads/pallas_call | solution.py:47
  262.3 3.8 out_grads.1
  266.0 28.3 %attend_back.1 = (f32[8,192,128]{2,1,0:T(8,128)}, f32[8,192,128]{2,1,0:T(8,128)}, bf16[8,192,128]{2,1,0:T(8,128)(2,1)}) custom-call(s32[8]{0:T(128)} %and_select_fusion.first_ref, bf16[8,192,128]{2,1,0:T(8,128)(2,1)} %get-tuple-element.77.q_ref, bf16[3072,128]{1,0:T(8,128)(2,1)} %bitcast.47, bf16[8,192,128]{2,1,0:T(8,128)(2,1)} %spread_grads.1.do_ref, ...), custom_call_target="tpu_custom_call" | custom-call | tf_op jit(solution)/shard_map/attend_back/pallas_call | solution.py:744
  294.4 80.4 %tail.1 = (f32[4,64,512]{2,1,0:T(8,128)}, f32[4,64,512]{2,1,0:T(8,128)}, f32[4,32,1024]{2,1,0:T(8,128)}, f32[192,1024]{1,0:T(8,128)}, bf16[2,128,1024]{2,1,0:T(8...) custom-call(f32[8,192,128]{2,1,0:T(8,128)} %get-tuple-element.100.dq_ref, ...), custom_call_target="tpu_custom_call" | custom-call | tf_op jit(solution)/shard_map/tail/pallas_call | solution.py:1469
  374.8 4.7 %deliver.1 = (bf16[192,1024]{1,0:T(8,128)(2,1)}, f32[128,1024]{1,0:T(8,128)}, f32[128,512]{1,0:T(8,128)}, f32[128,512]{1,0:T(8,128)}, f32[128,1024]{1,0:T(8,128)...) custom-call(f32[192,1024]{1,0:T(8,128)} %get-tuple-element.82.r_ref,, ...), custom_call_target="tpu_custom_call" | custom-call | tf_op jit(solution)/shard_map/deliver/pallas_call | solution.py:511
  (12 shorter events, 0.2 us)
Async XLA Ops:
  7.2 287.2 %all-gather.2.cloned.1.call-start = ((), (), s32[]{:S(2)}) async-start(), calls=%async_computation | async-start | bytes 4718592 | tf_op jit(solution)/shard_map/all_gather | solution.py:1587
  74.5 68.0 %copy-start.1 = (f32[2]{0:T(128)S(1)}, f32[2]{0:T(128)}, u32[]{:S(2)}) copy-start(f32[2]{0:T(128)} %constant.23.clone) | copy-start | bytes 28
  142.7 1.2 copy-start
Sparse Core Ops, SparseCore 0:
  141.5 54.9 all-gather.1

commit v4 on v3

--- a/solution.py
+++ b/solution.py
@@ -188,73 +188,99 @@
             pass
 
 
-def gather_rows(rows, meta):
-    def body(x_ref, m_ref, o_ref, mo_ref, send_sem, recv_sem, local_sem):
+def lanes(index):
+    return pl.ds(pl.multiple_of(index * 128, 128), 128)
+
+
+def join_heads(blocks, w_out, tokens, gains, routes_t, logits_t):
+    def body(
+        x_ref, w_ref, t_ref, g_ref, r_ref, l_ref,
+        a_ref, res_ref, o_ref, mo_ref, w_v, ffn, m_v, send_sem, recv_sem, local_sem,
+    ):
+        _, chip, core, _ = place()
         ring = ring_of(lax.axis_index("exp"))
         me = ring[0]
+        twins = [lax.rem(chip + d, CHIPS) for d in FAR_FIRST]
+        to_chip = lambda p: ("ctx", 2 * p + core)
         to_exp = lambda p: ("exp", p)
         copier = Copier(send_sem, recv_sem, local_sem)
-        meet([to_exp(p) for p in ring[1:]])
-        copier.keep(x_ref, o_ref.at[me])
-        copier.keep(m_ref.at[me], mo_ref.at[me])
+        load = copier.keep(w_ref, w_v)
+        meet([to_chip(p) for p in twins] + [to_exp(p) for p in ring[1:]])
+        arrivals = [copier.send(x_ref.at[p], a_ref.at[:, lanes(chip)], *to_chip(p)) for p in twins]
+        own = copier.keep(x_ref.at[chip], a_ref.at[:, lanes(chip)])
+
+        logits = l_ref[...]
+        raised = jnp.exp(logits - jnp.max(logits, axis=0, keepdims=True))
+        gates = raised / jnp.sum(raised, axis=0, keepdims=True)
+        experts = lax.broadcasted_iota(jnp.int32, (32, ROWS), 0)
+        member = jnp.zeros((32, ROWS), F32)
+        weight = jnp.zeros((32, ROWS), F32)
+        for c in range(8):
+            hit = r_ref[c : c + 1, :] == experts
+            member = member + jnp.where(hit, 1.0, 0.0)
+            weight = weight + jnp.where(hit, gates[c : c + 1, :], 0.0)
+        before = lax.broadcasted_iota(jnp.int32, (ROWS, ROWS), 0) < lax.broadcasted_iota(
+            jnp.int32, (ROWS, ROWS), 1
+        )
+        rank = dot(member.astype(BF16), jnp.where(before, 1.0, 0.0).astype(BF16))
+        spot = jnp.where(member > 0.5, rank, -1.0)
+        for e in range(EXP):
+            m_v[e, 0:4, :] = spot[e * 4 : e * 4 + 4, :]
+            m_v[e, 4:8, :] = weight[e * 4 : e * 4 + 4, :]
         for p in ring[1:]:
-            copier.send(m_ref.at[p], mo_ref.at[me], *to_exp(p))
-        side_by_side(relay(copier, x_ref, lambda s: o_ref.at[s], rows.shape[0], ring, to_exp))
+            copier.send(m_v.at[p], mo_ref.at[me], *to_exp(p))
+        copier.keep(m_v.at[me], mo_ref.at[me])
+
+        copier.kept(load)
+        copier.kept(own)
+        for at in arrivals:
+            copier.arrived(at)
+        branch = dot(a_ref[...], w_v[...]).astype(BF16).astype(F32)
+        resid = t_ref[...].astype(F32) + branch
+        res_ref[...] = resid
+        scale = row_scale(jnp.sum(resid * resid, axis=1, keepdims=True), WIDTH)
+        for e in range(EXP):
+            at = slice(e * 128, (e + 1) * 128)
+            ffn[:, at] = (resid[:, at] * scale * g_ref[e, 3:4, :]).astype(BF16)
+        rows_out = relay(copier, ffn, lambda s: o_ref.at[s], ROWS, ring, to_exp)
+        next(rows_out)
+        next(rows_out)
+        copier.keep(ffn, o_ref.at[me])
+        side_by_side(rows_out)
         copier.finish()
 
-    return comm_call(
+    vmem = pl.BlockSpec(memory_space=pltpu.VMEM)
+    return pl.pallas_call(
         body,
-        "gather_rows",
-        2,
-        [
-            jax.ShapeDtypeStruct((EXP,) + rows.shape, rows.dtype),
-            jax.ShapeDtypeStruct(meta.shape, F32),
+        name="join_heads",
+        out_shape=[
+            jax.ShapeDtypeStruct((ROWS, WIDTH), BF16),
+            jax.ShapeDtypeStruct((ROWS, WIDTH), F32),
+            jax.ShapeDtypeStruct((EXP, ROWS, WIDTH), BF16),
+            jax.ShapeDtypeStruct((EXP, 8, ROWS), F32),
         ],
-        [rows, meta],
-        21,
-        in_specs=[pl.BlockSpec(memory_space=pltpu.VMEM)] * 2,
-    )
-
-
-def lanes(index):
-    return pl.ds(pl.multiple_of(index * 128, 128), 128)
-
-
-def collect_heads(blocks):
-    def body(x_ref, o_ref, send_sem, recv_sem, local_sem):
-        _, chip, core, _ = place()
-        chips = [lax.rem(chip + d, CHIPS) for d in FAR_FIRST]
-        copier = Copier(send_sem, recv_sem, local_sem)
-        meet([("ctx", 2 * p + core) for p in chips])
-        for p in chips:
-            copier.send(x_ref.at[p], o_ref.at[:, lanes(chip)], "ctx", 2 * p + core)
-        copier.keep(x_ref.at[chip], o_ref.at[:, lanes(chip)])
-        copier.finish()
-
-    return comm_call(
-        body, "collect_heads", 4, [jax.ShapeDtypeStruct((ROWS, WIDTH), BF16)], [blocks], 7
-    )[0]
-
-
-def spread_grads(rows):
-    def body(x_ref, o_ref, send_sem, recv_sem, local_sem):
-        _, chip, core, _ = place()
-        chips = [lax.rem(chip + d, CHIPS) for d in FAR_FIRST]
-        copier = Copier(send_sem, recv_sem, local_sem)
-        meet([("ctx", 2 * p + core) for p in chips])
-        for p in chips:
-            copier.send(x_ref.at[:, lanes(p)], o_ref.at[chip], "ctx", 2 * p + core)
-        copier.keep(x_ref.at[:, lanes(chip)], o_ref.at[chip])
-        copier.finish()
-
-    return comm_call(
-        body, "spread_grads", 5, [jax.ShapeDtypeStruct((CHIPS, ROWS, 128), BF16)], [rows], 7
-    )[0]
-
-
-def settle_experts(rows, d_rows, act, d_gate, d_up, d_parts, layer_parts):
+        in_specs=[ANY_SPEC] * 2 + [vmem] * 4,
+        out_specs=[vmem, vmem, ANY_SPEC, ANY_SPEC],
+        scratch_shapes=[
+            pltpu.VMEM((WIDTH, WIDTH), BF16),
+            pltpu.VMEM((ROWS, WIDTH), BF16),
+            pltpu.VMEM((EXP, 8, ROWS), F32),
+            pltpu.SemaphoreType.DMA((28,)),
+            pltpu.SemaphoreType.DMA((28,)),
+            pltpu.SemaphoreType.DMA((8,)),
+        ],
+        compiler_params=pltpu.CompilerParams(
+            collective_id=2, has_side_effects=True, vmem_limit_bytes=60 * MIB
+        ),
+    )(blocks, w_out, tokens, gains, routes_t, logits_t)
+
+
+def settle_experts(
+    rows, d_rows, act, d_gate, d_up, d_parts, layer_parts, resid, cotangent, gains, w_out
+):
     def body(
-        x_ref, r_ref, a_ref, g_ref, u_ref, p_ref, l_ref, gate_out, up_out, down_a_out, down_b_out, dx_out, keep_out, give_out,
+        x_ref, r_ref, a_ref, g_ref, u_ref, p_ref, l_ref, res_ref, cot_ref, gain_ref, w_ref,
+        gate_out, up_out, down_a_out, down_b_out, dr_out, db_out, gg_out, do_out, keep_out, give_out, dx_out, d_att,
         x_v, r_v, a_v, g_v, u_v, gate, up, down, gate_o, up_o, down_o, gate_a, down_a, up_b, down_b,
         to_z, from_z, d_own, d_right, d_left, d_low, d_high, d_from, l_own, l_right, l_left, l_low, l_high, l_from, send_sem, recv_sem, local_sem,
     ):
@@ -265,6 +291,7 @@
         at_ctx = lambda z, yy: ("ctx", z * 8 + yy * 2 + core)
         over = at_ctx(1 - zh, y)
         columns = [lax.rem(y + d, 4) for d in (1, 3, 2)]
+        twins = [lax.rem(chip + d, CHIPS) for d in FAR_FIRST]
         right, left, far = [lax.rem(x + d, 4) for d in (1, 3, 2)]
         at_exp = lambda p: ("exp", zl * 4 + p)
         low, high = pl.ds(0, ROWS // 2), pl.ds(ROWS // 2, ROWS // 2)
@@ -285,8 +312,8 @@
 
         part_loads, layer_loads = fetch(*parts), fetch(*layers)
         meet(
-            [("ctx", sibling), over]
-            + [at_ctx(zh, c) for c in columns]
+            [("ctx", sibling)]
+            + [("ctx", 2 * p + core) for p in twins]
             + [at_exp(right), at_exp(left)]
             + [("exp", (1 - zl) * 4 + x)]
         )
@@ -380,6 +407,7 @@
         join(1, swaps)
         swaps = later
         later = work(3)
+        w_loads = [copier.keep(w_ref.at[pl.ds(k * FF, FF)], r_v.at[k, pl.ds(0, FF)]) for k in range(2)]
         join(2, swaps)
         join(3, later)
 
@@ -403,6 +431,30 @@
         z_stage = copier.send(to_z, from_z, "exp", (1 - zl) * 4 + x)
         layer_stage = pass_on(layer_stage, layer_loads, *layers)
 
+        copier.arrived(z_stage)
+        incoming = dx_out[...] + from_z[...].astype(F32)
+        resid_v = res_ref[...]
+        scale = row_scale(jnp.sum(resid_v * resid_v, axis=1, keepdims=True), WIDTH)
+        inner = jnp.zeros((ROWS, 1), F32)
+        for e in range(EXP):
+            at = slice(e * 128, (e + 1) * 128)
+            product = incoming[:, at] * resid_v[:, at]
+            gg_out[:, at] = jnp.sum(product * scale, axis=0, keepdims=True)
+            inner = inner + jnp.sum(product * gain_ref[e, 3:4, :], axis=1, keepdims=True)
+        cut = scale * scale * scale * inner * (1.0 / WIDTH)
+        for e in range(EXP):
+            at = slice(e * 128, (e + 1) * 128)
+            d_norm = scale * (incoming[:, at] * gain_ref[e, 3:4, :]) - resid_v[:, at] * cut
+            d_resid = cot_ref[:, at].astype(F32) + d_norm
+            dr_out[:, at] = d_resid
+            db_out[:, at] = d_resid.astype(BF16)
+        for at in w_loads:
+            copier.kept(at)
+        for k in range(2):
+            d_att[:, k * FF : (k + 1) * FF] = dot(db_out[...], r_v[k, 0:FF, :], NT).astype(BF16)
+        for p in twins:
+            copier.send(d_att.at[:, lanes(p)], do_out.at[chip], "ctx", 2 * p + core)
+        copier.keep(d_att.at[:, lanes(chip)], do_out.at[chip])
         for at in first_a:
             copier.arrived(at)
 
@@ -440,14 +492,6 @@
             return 0
 
         lax.fori_loop(0, 2, sum_b_down, 0)
-        copier.arrived(z_stage)
-
-        def gather_z(r, _):
-            at = pl.ds(pl.multiple_of(r * 48, 16), 48)
-            dx_out[at, :] += from_z[at, :].astype(F32)
-            return 0
-
-        lax.fori_loop(0, 4, gather_z, 0)
         sum_up(layer_stage, l_own, l_from, keep_out, give_out)
         copier.finish()
 
@@ -463,12 +507,17 @@
             jax.ShapeDtypeStruct((4, 2) + tall, BF16),
             jax.ShapeDtypeStruct((2, 2) + tall, BF16),
             jax.ShapeDtypeStruct((ROWS, WIDTH), F32),
+            jax.ShapeDtypeStruct((ROWS, WIDTH), BF16),
+            jax.ShapeDtypeStruct((1, WIDTH), F32),
+            jax.ShapeDtypeStruct((CHIPS, ROWS, 128), BF16),
             jax.ShapeDtypeStruct((ROWS, WIDTH), F32),
             jax.ShapeDtypeStruct((ROWS, WIDTH), BF16),
         ],
-        in_specs=[ANY_SPEC] * 7,
-        out_specs=[vmem] * 7,
+        in_specs=[ANY_SPEC] * 7 + [vmem] * 3 + [ANY_SPEC],
+        out_specs=[vmem] * 7 + [ANY_SPEC] + [vmem] * 2,
         scratch_shapes=[
+            pltpu.VMEM((ROWS, WIDTH), F32),
+            buf(ROWS, WIDTH),
             buf(LOCAL, SLOTS, WIDTH),
             buf(LOCAL, SLOTS, WIDTH),
             buf(LOCAL, SLOTS, FF),
@@ -497,14 +546,14 @@
         ]
         * 2
         + [
-            pltpu.SemaphoreType.DMA((49,)),
-            pltpu.SemaphoreType.DMA((49,)),
-            pltpu.SemaphoreType.DMA((28,)),
+            pltpu.SemaphoreType.DMA((56,)),
+            pltpu.SemaphoreType.DMA((56,)),
+            pltpu.SemaphoreType.DMA((32,)),
         ],
         compiler_params=pltpu.CompilerParams(
-            collective_id=8, has_side_effects=True, vmem_limit_bytes=62 * MIB
+            collective_id=8, has_side_effects=True, vmem_limit_bytes=63 * MIB
         ),
-    )(rows, d_rows, act, d_gate, d_up, d_parts, layer_parts)
+    )(rows, d_rows, act, d_gate, d_up, d_parts, layer_parts, resid, cotangent, gains, w_out)
 
 
 def compute_call(body, name, outs, ins, vmem=60, **kw):
@@ -558,189 +607,167 @@
     return lax.axis_index("ctx") // 2
 
 
-def route(routes_t, logits_t):
-    def body(r_ref, l_ref, m_ref):
-        logits = l_ref[...]
-        raised = jnp.exp(logits - jnp.max(logits, axis=0, keepdims=True))
-        gates = raised / jnp.sum(raised, axis=0, keepdims=True)
-        experts = lax.broadcasted_iota(jnp.int32, (32, ROWS), 0)
-        member = jnp.zeros((32, ROWS), F32)
-        weight = jnp.zeros((32, ROWS), F32)
-        for c in range(8):
-            hit = r_ref[c : c + 1, :] == experts
-            member = member + jnp.where(hit, 1.0, 0.0)
-            weight = weight + jnp.where(hit, gates[c : c + 1, :], 0.0)
-        before = lax.broadcasted_iota(jnp.int32, (ROWS, ROWS), 0) < lax.broadcasted_iota(
-            jnp.int32, (ROWS, ROWS), 1
-        )
-        rank = dot(member.astype(BF16), jnp.where(before, 1.0, 0.0).astype(BF16))
-        spot = jnp.where(member > 0.5, rank, -1.0)
-        for e in range(EXP):
-            m_ref[e, 0:4, :] = spot[e * 4 : e * 4 + 4, :]
-            m_ref[e, 4:8, :] = weight[e * 4 : e * 4 + 4, :]
-
-    return compute_call(
-        body, "route", [jax.ShapeDtypeStruct((EXP, 8, ROWS), F32)], [routes_t, logits_t]
-    )[0]
-
-
-def split_kv(kv_ref, klo, khi, vlo, vhi):
-    low = key_lanes()
-    both = kv_ref[...].astype(F32)
-    other = pltpu.roll(both, 64, 1)
-    if klo is not None:
-        klo[...] = jnp.where(low, both, 0.0).astype(BF16)
-        khi[...] = jnp.where(low, 0.0, other).astype(BF16)
-    vlo[...] = jnp.where(low, other, 0.0).astype(BF16)
-    vhi[...] = jnp.where(low, 0.0, both).astype(BF16)
-
-
-def attend(q, kv, key_pos, places, first_chunk):
-    def body(first_ref, q_ref, kv_ref, kp_ref, p_ref, o_ref, of_ref, l_ref, klo, khi, vlo, vhi):
-        i = pl.program_id(0)
-
-        @pl.when(i == 0)
-        def _():
-            split_kv(kv_ref, klo, khi, vlo, vhi)
-
-        q_block = q_ref[0]
-        at_row, start_row = [
-            jnp.concatenate([down_rows(p_ref[0], k)] * (CHUNK // 128), axis=1) for k in range(2)
-        ]
+def key_columns(row):
+    upper = jnp.floor(row * (1.0 / 64.0))
+    parts = jnp.concatenate([upper, row - 64.0 * upper], axis=0).astype(BF16)
+    scale = jnp.where(lax.broadcasted_iota(jnp.int32, (2, 128), 0) == 0, 64.0, 1.0).astype(BF16)
+    return dot(parts, scale, TN)
+
+
+def pair_rows(places_i):
+    return [jnp.concatenate([places_i[k : k + 1, :]] * 2, axis=1) for k in range(2)]
+
+
+def attend(q, kv, key_pos, places, chunks):
+    def body(at_ref, q_ref, kv_ref, kp_ref, p_ref, o_ref, ot_ref, l_ref, keys, values, key_at):
         low = key_lanes()
 
-        def step(p, carry):
-            m0, m1, l0, l1, acc = carry
+        def place_keys(p, _):
             rows = pl.ds(pl.multiple_of(p * CHUNK, CHUNK), CHUNK)
-            at_key = kp_ref[p]
-            seen = (at_key >= start_row) & (at_key <= at_row)
-            s0 = jnp.where(seen, dot(q_block, klo[rows, :], NT), MASKED)
-            s1 = jnp.where(seen, dot(q_block, khi[rows, :], NT), MASKED)
-            n0 = jnp.maximum(m0, jnp.max(s0, axis=1, keepdims=True))
-            n1 = jnp.maximum(m1, jnp.max(s1, axis=1, keepdims=True))
-            p0 = jnp.exp(s0 - n0)
-            p1 = jnp.exp(s1 - n1)
-            a0 = jnp.exp(m0 - n0)
-            a1 = jnp.exp(m1 - n1)
-            l0 = l0 * a0 + jnp.sum(p0, axis=1, keepdims=True)
-            l1 = l1 * a1 + jnp.sum(p1, axis=1, keepdims=True)
-            acc = acc * jnp.where(low, a0, a1)
-            acc = acc + dot(p0.astype(BF16), vlo[rows, :]) + dot(p1.astype(BF16), vhi[rows, :])
-            return n0, n1, l0, l1, acc
-
-        top = jnp.full((ROWS, 1), MASKED, F32)
-        none = jnp.zeros((ROWS, 1), F32)
-        m0, m1, l0, l1, acc = lax.fori_loop(
-            first_ref[i], i + 1, step, (top, top, none, none, jnp.zeros((ROWS, 128), F32))
-        )
-        out = acc / jnp.where(low, l0, l1)
-        of_ref[0] = out
-        o_ref[0] = out.astype(BF16)
-        l_ref[0] = jnp.where(low, m0 + jnp.log(l0), m1 + jnp.log(l1))
-
-    def block(*shape):
-        return pl.BlockSpec((1,) + shape, lambda i, first: (i, 0, 0))
-
+            both = kv_ref[rows, :].astype(F32)
+            keys[rows, :] = jnp.where(low, both, 0.0).astype(BF16)
+            values[:, rows] = jnp.where(low, pltpu.roll(both, 64, 1), 0.0).T.astype(BF16)
+            key_at[rows, :] = key_columns(kp_ref[p])
+            return 0
+
+        lax.fori_loop(0, CHIPS, place_keys, 0)
+
+        def block(i, _):
+            wide = q_ref[i].astype(F32)
+            stacked = jnp.concatenate([wide, pltpu.roll(wide, 64, 1)], axis=0).astype(BF16)
+            at_row, start_row = pair_rows(p_ref[i])
+
+            def step(masked, diagonal, p, carry):
+                top, total, acc = carry
+                rows = pl.ds(pl.multiple_of(p * CHUNK, CHUNK), CHUNK)
+                scores = dot(keys[rows, :], stacked, NT)
+                if masked:
+                    at_key = jnp.concatenate([key_at[rows, :]] * (CHUNK // 128), axis=1)
+                    seen = at_key >= start_row
+                    if diagonal:
+                        seen = seen & (at_key <= at_row)
+                    scores = jnp.where(seen, scores, MASKED)
+                new_top = jnp.maximum(top, jnp.max(scores, axis=0, keepdims=True))
+                probs = jnp.exp(scores - new_top)
+                scale = jnp.exp(top - new_top)
+                total = total * scale + jnp.sum(probs, axis=0, keepdims=True)
+                acc = acc * scale + dot(values[:, rows], probs.astype(BF16))
+                return new_top, total, acc
+
+            def masked_step(p, carry):
+                return step(True, False, p, carry)
+
+            def plain_step(p, carry):
+                return step(False, False, p, carry)
+
+            none = jnp.zeros((1, 2 * ROWS), F32)
+            carry = (none + MASKED, none, jnp.zeros((128, 2 * ROWS), F32))
+            carry = lax.fori_loop(at_ref[0, i], at_ref[1, i], masked_step, carry)
+            carry = lax.fori_loop(at_ref[1, i], i, plain_step, carry)
+            top, total, acc = step(True, True, i, carry)
+            turned = acc[0:64, :] / total
+            ot_ref[i] = turned
+            l_ref[i] = top + jnp.log(total)
+            out = jnp.concatenate([turned, turned], axis=0).T
+            o_ref[i] = jnp.where(low, out[:ROWS], out[ROWS:]).astype(BF16)
+            return 0
+
+        lax.fori_loop(0, CHIPS, block, 0)
+
+    vmem = pl.BlockSpec(memory_space=pltpu.VMEM)
     return pl.pallas_call(
         body,
         name="attend",
         out_shape=[
             jax.ShapeDtypeStruct((CHIPS, ROWS, 128), BF16),
-            jax.ShapeDtypeStruct((CHIPS, ROWS, 128), F32),
-            jax.ShapeDtypeStruct((CHIPS, ROWS, 128), F32),
+            jax.ShapeDtypeStruct((CHIPS, 64, 2 * ROWS), F32),
+            jax.ShapeDtypeStruct((CHIPS, 1, 2 * ROWS), F32),
         ],
-        grid_spec=pltpu.PrefetchScalarGridSpec(
-            num_scalar_prefetch=1,
-            grid=(CHIPS,),
-            in_specs=[
-                block(ROWS, 128),
-                pl.BlockSpec((KEYS, 128), lambda i, first: (0, 0)),
-                pl.BlockSpec((CHIPS, 1, CHUNK), lambda i, first: (0, 0, 0)),
-                block(2, ROWS),
-            ],
-            out_specs=[block(ROWS, 128)] * 3,
-            scratch_shapes=[pltpu.VMEM((KEYS, 128), BF16)] * 4,
-        ),
+        in_specs=[pl.BlockSpec(memory_space=pltpu.SMEM)] + [vmem] * 4,
+        out_specs=[vmem] * 3,
+        scratch_shapes=[
+            pltpu.VMEM((KEYS, 128), BF16),
+            pltpu.VMEM((128, KEYS), BF16),
+            pltpu.VMEM((KEYS, 128), F32),
+        ],
         compiler_params=pltpu.CompilerParams(vmem_limit_bytes=60 * MIB),
-    )(first_chunk, q, kv, key_pos, places)
-
-
-def attend_back(q, kv, d_out, out, log_total, key_pos, places, first_chunk):
+    )(chunks, q, kv, key_pos, places)
+
+
+def attend_back(q, kv, d_out, out_turned, log_total, key_pos, places, chunks):
     def body(
-        first_ref, q_ref, kv_ref, do_ref, o_ref, l_ref, kp_ref, p_ref,
-        dq_ref, mine_ref, other_ref, klo, khi, vlo, vhi, acc, key_at,
+        at_ref, q_ref, kv_ref, do_ref, ot_ref, l_ref, kp_ref, p_ref,
+        dq_ref, mine_ref, other_ref, keys, values, acc, key_at, keys_t,
     ):
-        i = pl.program_id(0)
-
-        @pl.when(i == 0)
-        def _():
-            split_kv(kv_ref, klo, khi, vlo, vhi)
-            acc[...] = jnp.zeros_like(acc)
-
-            def place_keys(p, _):
-                both = jnp.concatenate([kp_ref[p], kp_ref[p]], axis=0)
-                key_at[pl.ds(pl.multiple_of(p * CHUNK, CHUNK), CHUNK), :] = down_rows(both, 0, ROWS)
-                return 0
-
-            lax.fori_loop(0, CHIPS, place_keys, 0)
-
         low = key_lanes()
-        q_block, do_block = q_ref[0], do_ref[0]
-        do_wide, q_wide = do_block.astype(F32), q_block.astype(F32)
-        q_turned, do_turned = pltpu.roll(q_wide, 64, 1), pltpu.roll(do_wide, 64, 1)
-        right = jnp.concatenate(
-            [
-                jnp.where(low, q_wide, 0.0).astype(BF16),
-                jnp.where(low, q_turned, 0.0).astype(BF16),
-                jnp.where(low, 0.0, do_turned).astype(BF16),
-                jnp.where(low, 0.0, do_wide).astype(BF16),
-            ],
-            axis=0,
-        )
-        row_id = lax.broadcasted_iota(jnp.int32, (8, 128), 0)
-        lane_id = lax.broadcasted_iota(jnp.int32, (8, 128), 1)
-        halves = jnp.where(lane_id // 64 == row_id, 1.0, 0.0)
-        picks = jnp.where(lane_id == 64 * row_id, 1.0, 0.0)
-
-        delta = across(halves, do_wide * o_ref[0])
-        total = across(picks, l_ref[0])
-        at_row, start_row = p_ref[0, 0:1, :], p_ref[0, 1:2, :]
-
-        def step(p, dq):
+
+        def place_keys(p, _):
             rows = pl.ds(pl.multiple_of(p * CHUNK, CHUNK), CHUNK)
-            at_key = key_at[rows, :]
-            seen = (at_key >= start_row) & (at_key <= at_row)
-            k0, k1 = klo[rows, :], khi[rows, :]
-            s0 = jnp.where(seen, dot(k0, q_block, NT), MASKED)
-            s1 = jnp.where(seen, dot(k1, q_block, NT), MASKED)
-            p0 = jnp.exp(s0 - total[0:1, :])
-            p1 = jnp.exp(s1 - total[1:2, :])
-            d0 = (p0 * (dot(vlo[rows, :], do_block, NT) - delta[0:1, :])).astype(BF16)
-            d1 = (p1 * (dot(vhi[rows, :], do_block, NT) - delta[1:2, :])).astype(BF16)
-            left = jnp.concatenate([d0, d1, p0.astype(BF16), p1.astype(BF16)], axis=1)
-            acc[rows, :] += dot(left, right)
-            return dq + dot(d0, k0, TN) + dot(d1, k1, TN)
-
-        dq = lax.fori_loop(first_ref[i], i + 1, step, jnp.zeros((ROWS, 128), F32))
-        dq_ref[0] = dq * 0.125
-
-        @pl.when(i == CHIPS - 1)
-        def _():
-            core = lax.rem(lax.axis_index("ctx"), 2)
-
-            def part(s, _):
-                mine = pl.ds(pl.multiple_of((2 * s + core) * ROWS, ROWS), ROWS)
-                other = pl.ds(pl.multiple_of((2 * s + 1 - core) * ROWS, ROWS), ROWS)
-                mine_ref[s] = acc[mine, :]
-                other_ref[s] = acc[other, :].astype(BF16)
-                return 0
-
-            lax.fori_loop(0, CHIPS, part, 0)
-
-    def block(*shape):
-        return pl.BlockSpec((1,) + shape, lambda i, first: (i, 0, 0))
-
-    whole = pl.BlockSpec((KEYS, 128), lambda i, first: (0, 0))
+            both = kv_ref[rows, :].astype(F32)
+            own_keys = jnp.where(low, both, 0.0)
+            keys[rows, :] = own_keys.astype(BF16)
+            keys_t[:, rows] = own_keys.T.astype(BF16)
+            values[rows, :] = jnp.where(low, pltpu.roll(both, 64, 1), 0.0).astype(BF16)
+            key_at[rows, :] = key_columns(kp_ref[p])
+            acc[rows, :] = jnp.zeros((CHUNK, 128), F32)
+            return 0
+
+        lax.fori_loop(0, CHIPS, place_keys, 0)
+
+        def block(i, _):
+            q_wide, do_wide = q_ref[i].astype(F32), do_ref[i].astype(F32)
+            q_turned, do_turned = pltpu.roll(q_wide, 64, 1), pltpu.roll(do_wide, 64, 1)
+            q_rows = jnp.concatenate([q_wide, q_turned], axis=0)
+            do_rows = jnp.concatenate([do_wide, do_turned], axis=0)
+            do_high = jnp.concatenate([do_turned, do_wide], axis=0)
+            right = [jnp.where(low, q_rows, 0.0), jnp.where(low, 0.0, do_high)]
+            right = jnp.concatenate(right, axis=0).astype(BF16)
+            q_rows = q_rows.astype(BF16)
+            delta = jnp.sum(do_rows.T[0:64, :] * ot_ref[i], axis=0, keepdims=True)
+            do_rows = do_rows.astype(BF16)
+            total = l_ref[i]
+            at_row, start_row = pair_rows(p_ref[i])
+
+            def step(masked, diagonal, p, dq):
+                rows = pl.ds(pl.multiple_of(p * CHUNK, CHUNK), CHUNK)
+                scores = dot(keys[rows, :], q_rows, NT)
+                if masked:
+                    at_key = jnp.concatenate([key_at[rows, :]] * (CHUNK // 128), axis=1)
+                    seen = at_key >= start_row
+                    if diagonal:
+                        seen = seen & (at_key <= at_row)
+                    scores = jnp.where(seen, scores, MASKED)
+                probs = jnp.exp(scores - total)
+                d_scores = (probs * (dot(values[rows, :], do_rows, NT) - delta)).astype(BF16)
+                acc[rows, :] += dot(jnp.concatenate([d_scores, probs.astype(BF16)], axis=1), right)
+                return dq + dot(keys_t[:, rows], d_scores)
+
+            def masked_step(p, dq):
+                return step(True, False, p, dq)
+
+            def plain_step(p, dq):
+                return step(False, False, p, dq)
+
+            dq = jnp.zeros((128, 2 * ROWS), F32)
+            dq = lax.fori_loop(at_ref[0, i], at_ref[1, i], masked_step, dq)
+            dq = lax.fori_loop(at_ref[1, i], i, plain_step, dq)
+            dq = step(True, True, i, dq).T * 0.125
+            dq_ref[i] = jnp.where(low, dq[:ROWS], pltpu.roll(dq[ROWS:], 64, 1))
+            return 0
+
+        lax.fori_loop(0, CHIPS, block, 0)
+        core = lax.rem(lax.axis_index("ctx"), 2)
+
+        def part(s, _):
+            mine = pl.ds(pl.multiple_of((2 * s + core) * ROWS, ROWS), ROWS)
+            other = pl.ds(pl.multiple_of((2 * s + 1 - core) * ROWS, ROWS), ROWS)
+            mine_ref[s] = acc[mine, :]
+            other_ref[s] = acc[other, :].astype(BF16)
+            return 0
+
+        lax.fori_loop(0, CHIPS, part, 0)
+
+    vmem = pl.BlockSpec(memory_space=pltpu.VMEM)
     return pl.pallas_call(
         body,
         name="attend_back",
@@ -749,51 +776,17 @@
             jax.ShapeDtypeStruct((CHIPS, ROWS, 128), F32),
             jax.ShapeDtypeStruct((CHIPS, ROWS, 128), BF16),
         ],
-        grid_spec=pltpu.PrefetchScalarGridSpec(
-            num_scalar_prefetch=1,
-            grid=(CHIPS,),
-            in_specs=[
-                block(ROWS, 128),
-                whole,
-                block(ROWS, 128),
-                block(ROWS, 128),
-                block(ROWS, 128),
-                pl.BlockSpec((CHIPS, 1, CHUNK), lambda i, first: (0, 0, 0)),
-                block(2, ROWS),
-            ],
-            out_specs=[block(ROWS, 128)] + [pl.BlockSpec((CHIPS, ROWS, 128), lambda i, first: (0, 0, 0))] * 2,
-            scratch_shapes=[pltpu.VMEM((KEYS, 128), BF16)] * 4
-            + [pltpu.VMEM((KEYS, 128), F32), pltpu.VMEM((KEYS, ROWS), F32)],
-        ),
+        in_specs=[pl.BlockSpec(memory_space=pltpu.SMEM)] + [vmem] * 7,
+        out_specs=[vmem] * 3,
+        scratch_shapes=[
+            pltpu.VMEM((KEYS, 128), BF16),
+            pltpu.VMEM((KEYS, 128), BF16),
+            pltpu.VMEM((KEYS, 128), F32),
+            pltpu.VMEM((KEYS, 128), F32),
+            pltpu.VMEM((128, KEYS), BF16),
+        ],
         compiler_params=pltpu.CompilerParams(vmem_limit_bytes=60 * MIB),
-    )(first_chunk, q, kv, d_out, out, log_total, key_pos, places)
-
-
-def whole(*shape):
-    return pl.BlockSpec(shape, lambda i: (0,) * len(shape))
-
-
-def columns(block, width=WIDTH):
-    return pl.BlockSpec((WIDTH, width), lambda i: (0, block))
-
-
-def finish_attention(attended, w_out, tokens, gains):
-    def body(a_ref, w_ref, t_ref, g_ref, r_ref, f_ref):
-        branch = dot(a_ref[...], w_ref[...]).astype(BF16).astype(F32)
-        resid = t_ref[...].astype(F32) + branch
-        r_ref[...] = resid
-        scale = row_scale(jnp.sum(resid * resid, axis=1, keepdims=True), WIDTH)
-        f_ref[...] = (resid * scale * g_ref[3:4, :]).astype(BF16)
-
-    return compute_call(
-        body,
-        "finish_attention",
-        [jax.ShapeDtypeStruct((ROWS, WIDTH), F32), jax.ShapeDtypeStruct((ROWS, WIDTH), BF16)],
-        [attended, w_out, tokens, gains],
-        grid=(1,),
-        in_specs=[whole(ROWS, WIDTH), whole(WIDTH, WIDTH), whole(ROWS, WIDTH), whole(8, WIDTH)],
-        out_specs=[whole(ROWS, WIDTH)] * 2,
-    )
+    )(chunks, q, kv, d_out, out_turned, log_total, key_pos, places)
 
 
 def experts(rows, grads, meta, meta_t, w_gate, w_up, w_down):
@@ -927,35 +920,6 @@
     scale = row_scale(total_squares, width)
     inner = jnp.sum(weighted * values, axis=1, keepdims=True) * (1.0 / width)
     return scale * weighted - values * (scale * scale * scale) * inner, scale
-
-
-def back_to_branch(d_ffn, resid, cotangent, gains, w_out):
-    def body(p_ref, r_ref, c_ref, g_ref, w_ref, dr_ref, db_ref, da_ref, gg_ref):
-        incoming = p_ref[...]
-        resid_v = r_ref[...]
-        squares = jnp.sum(resid_v * resid_v, axis=1, keepdims=True)
-        d_norm, scale = norm_back(resid_v, squares, WIDTH, incoming * g_ref[3:4, :])
-        gg_ref[...] = jnp.sum(incoming * resid_v * scale, axis=0, keepdims=True)
-        d_resid = c_ref[...].astype(F32) + d_norm
-        dr_ref[...] = d_resid
-        d_branch = d_resid.astype(BF16)
-        db_ref[...] = d_branch
-        da_ref[...] = dot(d_branch, w_ref[...], NT).astype(BF16)
-
-    return compute_call(
-        body,
-        "back_to_branch",
-        [
-            jax.ShapeDtypeStruct((ROWS, WIDTH), F32),
-            jax.ShapeDtypeStruct((ROWS, WIDTH), BF16),
-            jax.ShapeDtypeStruct((ROWS, WIDTH), BF16),
-            jax.ShapeDtypeStruct((1, WIDTH), F32),
-        ],
-        [d_ffn, resid, cotangent, gains, w_out],
-        grid=(1,),
-        in_specs=[whole(ROWS, WIDTH)] * 3 + [whole(8, WIDTH), whole(WIDTH, WIDTH)],
-        out_specs=[whole(ROWS, WIDTH)] * 3 + [whole(1, WIDTH)],
-    )
 
 
 def out_grads(attended, d_branch):
@@ -1243,7 +1207,7 @@
         eg_ref, eu_ref, ed_ref, di_ref, dense_ref, og_ref, lo_ref, gs_ref,
         dq_v, dm_v, ql_v, kl_v, c_v, sn_v, n_v, w_v, t_v, r_v,
         got, e_q, e_kv, totals, totals_all, d_lin, home, w_give, w_keep, w_got, joint, traded, done,
-        o_keep, o_got, o_traded, o_half, a_got, a_done, packet, packets, mine, shared, gate_c, down_c, up_d, down_d, send_sem, recv_sem, local_sem,
+        o_keep, o_got, o_traded, o_pair, o_half, o_full, a_got, a_done, packet, packets, mine, shared, gate_c, down_c, up_d, down_d, send_sem, recv_sem, local_sem,
     ):
         ctx, chip, core, sibling = place()
         me = lax.axis_index("exp")
@@ -1264,6 +1228,7 @@
         meet([("ctx", p) for p in others] + [("exp", p) for p in exps])
         swapped = copier.send(do_ref, got, "ctx", sibling)
         o_swap = copier.send(op_ref.at[:, 1 - core], o_got, "ctx", sibling)
+        copier.send(lp_ref, lo_ref, "exp", lax.rem(me + 4, EXP))
         keys = key_lanes()
         gain = g_ref[chip]
         for at in heads:
@@ -1301,7 +1266,12 @@
             return 0
 
         lax.fori_loop(0, EXP, add_cores, 0)
-        o_trades = [copier.send(o_keep.at[p], o_traded.at[me], "exp", p) for p in exps]
+        zl, x = me // 4, lax.rem(me, 4)
+        o_trades = []
+        for d in (2, 1, 3):
+            p = lax.rem(x + d, 4)
+            for z in range(2):
+                o_trades.append(copier.send(o_keep.at[z * 4 + p], o_traded.at[x, z], "exp", zl * 4 + p))
         for at in shares:
             copier.arrived(at)
 
@@ -1348,15 +1318,6 @@
 
             lax.fori_loop(0, 4, part, 0)
 
-        for at in o_trades:
-            copier.arrived(at)
-        o_traded[me] = o_keep[me]
-        total = o_traded[0].astype(F32)
-        for e in range(1, EXP):
-            total = total + o_traded[e].astype(F32)
-        o_half[...] = total.astype(BF16)
-        spread = [copier.send(o_half.at[:, lanes(p)], a_got.at[chip], *to_chip(p)) for p in twins]
-        a_got[chip] = o_half[:, lanes(chip)]
         columns_grad(1 - core, w_give)
         w_swap = copier.send(w_give, w_got, "ctx", sibling)
         columns_grad(core, w_keep)
@@ -1365,12 +1326,15 @@
         joint[...] = both.astype(BF16).reshape(EXP, 128, 128)
         trades = [copier.send(joint.at[p], traded.at[me], "exp", p) for p in exps]
         traded[me] = joint[me]
-        for at in spread:
+        for at in o_trades:
             copier.arrived(at)
-        total = a_got[0].astype(F32)
-        for c in range(1, CHIPS):
-            total = total + a_got[c].astype(F32)
-        a_done[...] = total.astype(BF16)
+        keep, give = o_keep[zl * 4 + x].astype(F32), o_keep[(1 - zl) * 4 + x].astype(F32)
+        for d in (1, 2, 3):
+            p = lax.rem(x + d, 4)
+            keep = keep + o_traded[p, zl].astype(F32)
+            give = give + o_traded[p, 1 - zl].astype(F32)
+        o_half[...] = give.astype(BF16)
+        o_pairs = copier.send(o_half, o_pair, "exp", (1 - zl) * 4 + x)
 
         for at in homeward:
             copier.arrived(at)
@@ -1393,6 +1357,10 @@
             weighted = d_normed * g_ref[e, 0:1, :]
             inner = inner + jnp.sum(weighted * x[:, at], axis=1, keepdims=True)
             pieces.append(weighted)
+        copier.arrived(o_pairs)
+        o_full[...] = (keep + o_pair[...].astype(F32)).astype(BF16)
+        spread = [copier.send(o_full.at[:, lanes(p)], a_got.at[chip], *to_chip(p)) for p in twins]
+        a_got[chip] = o_full[:, lanes(chip)]
         packet[chip, 1:2, :] = q_sum
         packet[chip, 2:3, :] = kv_sum
         gain_trades = [copier.send(packet.at[p], packets.at[me], "exp", p) for p in exps]
@@ -1408,11 +1376,6 @@
         w_shares = [copier.send(done, spot, *to_chip(p)) for p in twins]
         copier.send(done, spot, "ctx", sibling)
         copier.keep(done, spot)
-        half = pl.ds(pl.multiple_of(core * 64, 64), 64)
-        a_shares = [copier.send(a_done, og_ref.at[half, lanes(chip)], *to_chip(p)) for p in twins]
-        copier.send(a_done, og_ref.at[half, lanes(chip)], "ctx", sibling)
-        copier.keep(a_done, og_ref.at[half, lanes(chip)])
-        copier.send(lp_ref, lo_ref, "exp", lax.rem(me + 4, EXP))
 
         for at in gain_trades:
             copier.arrived(at)
@@ -1423,6 +1386,16 @@
         gain_shares = [copier.send(mine, shared.at[ctx], "ctx", p) for p in others]
         shared[ctx] = total
 
+        for at in spread:
+            copier.arrived(at)
+        total = a_got[0].astype(F32)
+        for c in range(1, CHIPS):
+            total = total + a_got[c].astype(F32)
+        a_done[...] = total.astype(BF16)
+        half = pl.ds(pl.multiple_of(core * 64, 64), 64)
+        a_shares = [copier.send(a_done, og_ref.at[half, lanes(chip)], *to_chip(p)) for p in twins]
+        copier.send(a_done, og_ref.at[half, lanes(chip)], "ctx", sibling)
+        copier.keep(a_done, og_ref.at[half, lanes(chip)])
         inner = inner * (1.0 / WIDTH)
         cut = scale * scale * scale * inner
         for e in range(EXP):
@@ -1507,7 +1480,9 @@
             tile,
             pltpu.VMEM((EXP, 64, WIDTH), BF16),
             pltpu.VMEM((EXP, 64, WIDTH), BF16),
-            pltpu.VMEM((EXP, 64, WIDTH), BF16),
+            pltpu.VMEM((4, 2, 64, WIDTH), BF16),
+            pltpu.VMEM((64, WIDTH), BF16),
+            pltpu.VMEM((64, WIDTH), BF16),
             pltpu.VMEM((64, WIDTH), BF16),
             pltpu.VMEM((CHIPS, 64, 128), BF16),
             pltpu.VMEM((64, 128), BF16),
@@ -1572,14 +1547,17 @@
     pieces = jnp.arange(CTX, dtype=jnp.int32)[:, None] * CTX + deal_perm[0]
     positions = (pieces[:, :, None] * 12 + jnp.arange(12, dtype=jnp.int32)).reshape(CTX, ROWS)
     key_pos = positions.reshape(CHIPS, 1, CHUNK).astype(F32)
-    first_chunk = jnp.min(places[:, 1], axis=1).astype(jnp.int32) // CHUNK
-    gains = gain_all.transpose(1, 0, 2).reshape(8, WIDTH)
+    starts = places[:, 1].astype(jnp.int32)
+    whole_from = (jnp.max(starts, axis=1) + CHUNK - 1) // CHUNK
+    chunks = jnp.stack(
+        [jnp.min(starts, axis=1) // CHUNK, jnp.minimum(whole_from, jnp.arange(CHIPS, dtype=jnp.int32))]
+    )
     w_o = w_o.reshape(WIDTH, WIDTH)
     kv_all = kv_all.reshape(KEYS, 128)
-    out_low, out_wide, log_total = attend(q_all, kv_all, key_pos, places, first_chunk)
-    attended = collect_heads(out_low)
-    resid, ffn_rows = finish_attention(attended, w_o, tokens, gains)
-    rows_all, meta_all = gather_rows(ffn_rows, route(routes[0].T, gate_logits[0].T))
+    out_low, out_wide, log_total = attend(q_all, kv_all, key_pos, places, chunks)
+    attended, resid, rows_all, meta_all = join_heads(
+        out_low, w_o, tokens, gain_all, routes[0].T, gate_logits[0].T
+    )
 
     rows_all, dense_late = lax.optimization_barrier(
         (rows_all, jnp.concatenate([w_query, w_key, w_value], axis=1))
@@ -1600,7 +1578,9 @@
         w_up,
         w_down,
     )
-    gate_part, up_part, down_a, down_b, d_ffn, layer_keep, layer_give = settle_experts(
+    (
+        gate_part, up_part, down_a, down_b, d_resid, d_branch, ffn_gain_grad, d_out, layer_keep, layer_give,
+    ) = settle_experts(
         rows_in,
         d_rows,
         act,
@@ -1608,14 +1588,14 @@
         d_up,
         d_parts.reshape(2, 4, ROWS, WIDTH),
         out_parts.reshape(2, 4, ROWS, WIDTH),
-    )
-    d_resid, d_branch, d_attended, ffn_gain_grad = back_to_branch(
-        d_ffn, resid, cotangent, gains, w_o
-    )
-    d_out = spread_grads(d_attended)
+        resid,
+        cotangent,
+        gain_all,
+        w_o,
+    )
     out_part = out_grads(attended, d_branch).reshape(EXP, 2, 64, WIDTH)
     dq, dkv_mine, dkv_other = attend_back(
-        q_all, kv_all, d_out, out_wide, log_total, key_pos, places, first_chunk
+        q_all, kv_all, d_out, out_wide, log_total, key_pos, places, chunks
     )
     gate_grad, up_grad, down_grad, input_grad, dense, out_grad, layer_got, gain_sums = tail(
         dq,

time: 391 us -> 349 us (0.89)
  Pallas kernels: 365 us -> 325 us
    pallas_call x1, Pallas kernels: 80.4 us -> 66.3 us  [tail(): pl.pallas_call(body, name='tail', out_shape=[jax.ShapeDtypeStruct((LOCAL,...]
    pallas_call x3 -> x1, Pallas kernels: 55.6 us -> 42.5 us  [join_heads(): pl.pallas_call(body, name='join_heads', out_shape=[jax.ShapeDtypeStruct((...]
    pallas_call x6 -> x3, Pallas kernels: 58 us -> 49 us  [compute_call(): pl.pallas_call(body, name=name, out_shape=outs, compiler_params=pltpu.Com...]
    pallas_call x1, Pallas kernels: 28.3 us -> 19.7 us  [attend_back(): pl.pallas_call(body, name='attend_back', out_shape=[jax.ShapeDtypeStruct(...]
    pallas_call x1, Pallas kernels: 62.5 us -> 69.2 us  [settle_experts(): pl.pallas_call(body, name='settle_experts', out_shape=[jax.ShapeDtypeStru...]
  transfers between devices with their start and end apart: 1 -> 1, of which waited for: 0 -> 0; matrix products, arithmetic and copies ran while one was open for 1% -> 1% of each run, Pallas kernels for 39% -> 38%
where the time goes in v4:
time: 349 us; the launch traced here: 347 us
  Pallas kernels  325 us (93%)
  between operations  14.1 us (4%)
  other arithmetic  4.57 us (1%)
    pallas_call x1, Pallas kernels, settle_experts(): pl.pallas_call(body, name='settle_experts', out_shape=[jax.ShapeDtypeStru...  69.2 us
    pallas_call x1, Pallas kernels, tail(): pl.pallas_call(body, name='tail', out_shape=[jax.ShapeDtypeStruct((LOCAL,...  66.3 us
    pallas_call x1, Pallas kernels, front(): pl.pallas_call(body, name='front', out_shape=[jax.ShapeDtypeStruct((EXP,...  62.4 us
    pallas_call x3, Pallas kernels, compute_call(): pl.pallas_call(body, name=name, out_shape=outs, compiler_params=pltpu.Com...  49 us
    pallas_call x1, Pallas kernels, join_heads(): pl.pallas_call(body, name='join_heads', out_shape=[jax.ShapeDtypeStruct((...  42.5 us
    pallas_call x1, Pallas kernels, attend_back(): pl.pallas_call(body, name='attend_back', out_shape=[jax.ShapeDtypeStruct(...  19.7 us
    pallas_call x1, Pallas kernels, attend(): pl.pallas_call(body, name='attend', out_shape=[jax.ShapeDtypeStruct((CHIP...  15.9 us
  transfers between devices with their start and end apart: 1, of which 0 were waited for; matrix products, arithmetic and copies ran while one was open for 1% of the time, Pallas kernels for 38%

profile of v4, /device:TPU:1, one launch (start us, length us, event | category | flops | bytes accessed | tf_op | source)
XLA Modules:
  0.0 346.9 jit_solution(17924495252478566056)
XLA Ops:
  7.2 0.0 all-gather.2.cloned.1.call-start
  7.2 1.9 pad_maximum_fusion
  9.2 62.4 %front.1 = (bf16[8,128,1024]{2,1,0:T(8,128)(2,1)}, f32[8,8,128]{2,1,0:T(8,128)}, bf16[8,192,1024]{2,1,0:T(8,128)(2,1)}, f32[8,192,128]{2,1,0:T(8,128)}, f32[8,19...) custom-call(bf16[192,1024]{1,0:T(8,128)(2,1)} %bitcast.51, ...), custom_call_target="tpu_custom_call" | custom-call | tf_op jit(solution)/shard_map/front/pallas_call | solution.py:1152
  71.5 1.1 convert_reduce_fusion.1
  72.6 0.8 add_multiply_fusion
  73.4 0.1 add_convert_fusion
  73.5 0.7 convert_element_type.12.kp_ref
  74.3 0.6 pad_add_fusion.at_ref
  74.8 15.9 %attend.1 = (bf16[8,192,128]{2,1,0:T(8,128)(2,1)}, f32[8,64,384]{2,1,0:T(8,128)}, f32[8,1,384]{2,1,0:T(1,128)}) custom-call(s32[2,8]{1,0:T(2,128)} %pad_add_fusion.at_ref, bf16[8,192,128]{2,1,0:T(8,128)(2,1)} %get-tuple-element.76.q_ref, bf16[3072,128]{1,0:T(8,128)(2,1)} %bitcast.57, f32[8,1,384]{2,1,0:T(1,128)} %convert_element_type.12.kp_ref, ...), custom_call_target="tpu_custom_call" | custom-call | tf_op jit(solution)/shard_map/attend/pallas_call | solution.py:678
  90.7 42.5 %join_heads.1 = (bf16[192,1024]{1,0:T(8,128)(2,1)}, f32[192,1024]{1,0:T(8,128)}, bf16[8,192,1024]{2,1,0:T(8,128)(2,1)}, f32[8,8,192]{2,1,0:T(8,128)}) custom-call(bf16[8,192,128]{2,1,0:T(8,128)(2,1)} %get-tuple-element.78.x_ref, bf16[1024,1024]{1,0:T(8,128)(2,1)} %bitcast.47, bf16[192,1024]{1,0:T(8,128)(2,1)} %bitcast.52, ...), custom_call_target="tpu_custom_call" | custom-call | tf_op jit(solution)/shard_map/join_heads/pallas_call | solution.py:253
  133.3 0.0 all-gather.2.cloned.1.call-update
  133.3 0.9 fusion
  134.2 0.0 copy-done.1
  134.2 0.1 select_bitcast_fusion
  134.3 0.1 reshape.237
  134.5 0.1 reshape.239
  134.6 0.0 copy-start
  134.6 1.2 copy.44
  135.8 40.6 %experts.1 = (bf16[4,576,1024]{2,1,0:T(8,128)(2,1)}, bf16[4,576,1024]{2,1,0:T(8,128)(2,1)}, bf16[4,576,512]{2,1,0:T(8,128)(2,1)}, bf16[4,576,512]{2,1,0:T(8,128)...) custom-call(bf16[4,384,1024]{2,1,0:T(8,128)(2,1)} %bitcast.60, ...), custom_call_target="tpu_custom_call" | custom-call | tf_op jit(solution)/shard_map/experts/pallas_call | solution.py:560
  176.4 69.2 %settle_experts.1 = (bf16[4,4,64,512]{3,2,1,0:T(8,128)(2,1)}, bf16[2,4,64,512]{3,2,1,0:T(8,128)(2,1)}, bf16[4,2,32,1024]{3,2,1,0:T(8,128)(2,1)}, bf16[2,2,32,102...) custom-call(bf16[4,576,1024]{2,1,0:T(8,128)(2,1)} %get-tuple-element, ...), custom_call_target="tpu_custom_call" | custom-call | tf_op jit(solution)/shard_map/settle_experts/pallas_call | solution.py:501
  245.6 3.8 %out_grads.1 = bf16[1024,1024]{1,0:T(8,128)(2,1)} custom-call(bf16[192,1024]{1,0:T(8,128)(2,1)} %get-tuple-element.106.a_ref, bf16[192,1024]{1,0:T(8,128)(2,1)} %get-tuple-element.107.d_ref), custom_call_target="tpu_custom_call" | custom-call | tf_op jit(solution)/shard_map/out_grads/pallas_call | solution.py:560
  249.4 19.7 %attend_back.1 = (f32[8,192,128]{2,1,0:T(8,128)}, f32[8,192,128]{2,1,0:T(8,128)}, bf16[8,192,128]{2,1,0:T(8,128)(2,1)}) custom-call(s32[2,8]{1,0:T(2,128)} %pad_add_fusion.at_ref, bf16[8,192,128]{2,1,0:T(8,128)(2,1)} %get-tuple-element.76.q_ref, bf16[3072,128]{1,0:T(8,128)(2,1)} %bitcast.58, bf16[8,192,128]{2,1,0:T(8,128)(2,1)} %get-tuple-element.94.do_ref, ...), custom_call_target="tpu_custom_call" | custom-call | tf_op jit(solution)/shard_map/attend_back/pallas_call | solution.py:771
  269.1 66.3 %tail.1 = (f32[4,64,512]{2,1,0:T(8,128)}, f32[4,64,512]{2,1,0:T(8,128)}, f32[4,32,1024]{2,1,0:T(8,128)}, f32[192,1024]{1,0:T(8,128)}, bf16[2,128,1024]{2,1,0:T(8...) custom-call(f32[8,192,128]{2,1,0:T(8,128)} %get-tuple-element.97.dq_ref, ...), custom_call_target="tpu_custom_call" | custom-call | tf_op jit(solution)/shard_map/tail/pallas_call | solution.py:1442
  335.3 4.7 %deliver.1 = (bf16[192,1024]{1,0:T(8,128)(2,1)}, f32[128,1024]{1,0:T(8,128)}, f32[128,512]{1,0:T(8,128)}, f32[128,512]{1,0:T(8,128)}, f32[128,1024]{1,0:T(8,128)...) custom-call(f32[192,1024]{1,0:T(8,128)} %get-tuple-element.81.res_re, ...), custom_call_target="tpu_custom_call" | custom-call | tf_op jit(solution)/shard_map/deliver/pallas_call | solution.py:560
  (8 shorter events, 0.1 us)
Async XLA Ops:
  7.2 261.9 %all-gather.2.cloned.1.call-start = ((), (), s32[]{:S(2)}) async-start(), calls=%async_computation | async-start | bytes 4718592 | tf_op jit(solution)/shard_map/all_gather | solution.py:1565
  9.2 125.1 %copy-start.1 = (f32[2]{0:T(128)S(1)}, f32[2]{0:T(128)}, u32[]{:S(2)}) copy-start(f32[2]{0:T(128)} %constant.33.clone) | copy-start | bytes 28
  134.6 1.2 copy-start
Sparse Core Ops, SparseCore 0:
  133.4 55.0 all-gather.1

commit v5 on v4

--- a/solution.py
+++ b/solution.py
@@ -618,7 +618,17 @@
     return [jnp.concatenate([places_i[k : k + 1, :]] * 2, axis=1) for k in range(2)]
 
 
-def attend(q, kv, key_pos, places, chunks):
+def block_chunks(len_ref, i):
+    first_row = (2 * i + lax.rem(lax.axis_index("ctx"), 2)) * ROWS
+    first, last, end = 0, 0, 0
+    for k in range(3):
+        end = end + len_ref[0, k]
+        first = jnp.where(first_row >= end, end, first)
+        last = jnp.where(first_row + ROWS - 1 >= end, end, last)
+    return first // CHUNK, jnp.minimum((last + CHUNK - 1) // CHUNK, i)
+
+
+def attend(q, kv, key_pos, places, lengths):
     def body(at_ref, q_ref, kv_ref, kp_ref, p_ref, o_ref, ot_ref, l_ref, keys, values, key_at):
         low = key_lanes()
 
@@ -662,8 +672,9 @@
 
             none = jnp.zeros((1, 2 * ROWS), F32)
             carry = (none + MASKED, none, jnp.zeros((128, 2 * ROWS), F32))
-            carry = lax.fori_loop(at_ref[0, i], at_ref[1, i], masked_step, carry)
-            carry = lax.fori_loop(at_ref[1, i], i, plain_step, carry)
+            first, plain = block_chunks(at_ref, i)
+            carry = lax.fori_loop(first, plain, masked_step, carry)
+            carry = lax.fori_loop(plain, i, plain_step, carry)
             top, total, acc = step(True, True, i, carry)
             turned = acc[0:64, :] / total
             ot_ref[i] = turned
@@ -691,227 +702,162 @@
             pltpu.VMEM((KEYS, 128), F32),
         ],
         compiler_params=pltpu.CompilerParams(vmem_limit_bytes=60 * MIB),
-    )(chunks, q, kv, key_pos, places)
-
-
-def attend_back(q, kv, d_out, out_turned, log_total, key_pos, places, chunks):
+    )(lengths, q, kv, key_pos, places)
+
+
+def experts(rows, grads, meta, w_gate, w_up, w_down):
+    half = SLOTS // 2
+
     def body(
-        at_ref, q_ref, kv_ref, do_ref, ot_ref, l_ref, kp_ref, p_ref,
-        dq_ref, mine_ref, other_ref, keys, values, acc, key_at, keys_t,
+        x_ref, g_ref, m_ref, wg_ref, wu_ref, wd_ref,
+        xin_ref, dr_ref, act_ref, dg_ref, du_ref, out_ref, dx_ref,
+        x, g, wg, wu, wd, xin, dr, act, dg, du, out, dx, made, back, weight, sems,
     ):
-        low = key_lanes()
-
-        def place_keys(p, _):
-            rows = pl.ds(pl.multiple_of(p * CHUNK, CHUNK), CHUNK)
-            both = kv_ref[rows, :].astype(F32)
-            own_keys = jnp.where(low, both, 0.0)
-            keys[rows, :] = own_keys.astype(BF16)
-            keys_t[:, rows] = own_keys.T.astype(BF16)
-            values[rows, :] = jnp.where(low, pltpu.roll(both, 64, 1), 0.0).astype(BF16)
-            key_at[rows, :] = key_columns(kp_ref[p])
-            acc[rows, :] = jnp.zeros((CHUNK, 128), F32)
+        def pair_in(p):
+            at = pl.ds(2 * p, 2)
+            return [pltpu.make_async_copy(a.at[at], b.at[at], sems.at[0, p]) for a, b in ((x_ref, x), (g_ref, g))]
+
+        def weights_in(e):
+            pairs = ((wg_ref, wg), (wu_ref, wu), (wd_ref, wd))
+            return [pltpu.make_async_copy(a.at[e], b.at[e], sems.at[1, e]) for a, b in pairs]
+
+        def rows_out(e):
+            return [pltpu.make_async_copy(a.at[e], b.at[e], sems.at[2, e]) for a, b in ((xin, xin_ref), (dr, dr_ref))]
+
+        def acts_out(e):
+            pairs = ((act, act_ref), (dg, dg_ref), (du, du_ref))
+            return [pltpu.make_async_copy(a.at[e], b.at[e], sems.at[3, e]) for a, b in pairs]
+
+        def pair_out(p):
+            at = pl.ds(2 * p, 2)
+            return [pltpu.make_async_copy(a.at[at], b.at[at], sems.at[4, p]) for a, b in ((dx, dx_ref), (out, out_ref))]
+
+        def start(copies):
+            for copy in copies:
+                copy.start()
+
+        def wait(copies):
+            for copy in copies:
+                copy.wait()
+
+        for p in range(PAIRS):
+            start(pair_in(p))
+        for e in range(LOCAL):
+            start(weights_in(e))
+
+        def pair_meta(p):
+            first, second = m_ref[2 * p], m_ref[2 * p + 1]
+            slots = jnp.where(second[:LOCAL] < 0.0, -1.0, second[:LOCAL] + float(CAP))
+            return jnp.concatenate([first, jnp.concatenate([slots, second[LOCAL:]], axis=0)], axis=1)
+
+        slot_id = lax.broadcasted_iota(jnp.int32, (PAIR_CAP, PAIR_ROWS), 0).astype(F32)
+
+        def pick(p, _):
+            wait(pair_in(p))
+            meta_p = pair_meta(p)
+            parts, gates = [], []
+            for k in range(LOCAL):
+                hit = slot_id == meta_p[k : k + 1, :]
+                parts.append(jnp.where(hit, 1.0, 0.0).astype(BF16))
+                gates.append(jnp.sum(jnp.where(hit, meta_p[4 + k : 5 + k, :], 0.0), axis=1, keepdims=True))
+            chosen = jnp.concatenate(parts, axis=0)
+            at_pair = pl.ds(2 * p, 2)
+            rows_p = dot(chosen, x[at_pair].reshape(PAIR_ROWS, WIDTH)).astype(BF16)
+            grads_p = dot(chosen, g[at_pair].reshape(PAIR_ROWS, WIDTH))
+            at = pl.ds(pl.multiple_of(p * PAIR_CAP, PAIR_CAP), PAIR_CAP)
+            for k in range(LOCAL):
+                piece = slice(k * PAIR_CAP, (k + 1) * PAIR_CAP)
+                xin[k, at, :] = rows_p[piece]
+                dr[k, at, :] = (grads_p[piece] * gates[k]).astype(BF16)
+                weight[k, at, :] = gates[k]
             return 0
 
-        lax.fori_loop(0, CHIPS, place_keys, 0)
-
-        def block(i, _):
-            q_wide, do_wide = q_ref[i].astype(F32), do_ref[i].astype(F32)
-            q_turned, do_turned = pltpu.roll(q_wide, 64, 1), pltpu.roll(do_wide, 64, 1)
-            q_rows = jnp.concatenate([q_wide, q_turned], axis=0)
-            do_rows = jnp.concatenate([do_wide, do_turned], axis=0)
-            do_high = jnp.concatenate([do_turned, do_wide], axis=0)
-            right = [jnp.where(low, q_rows, 0.0), jnp.where(low, 0.0, do_high)]
-            right = jnp.concatenate(right, axis=0).astype(BF16)
-            q_rows = q_rows.astype(BF16)
-            delta = jnp.sum(do_rows.T[0:64, :] * ot_ref[i], axis=0, keepdims=True)
-            do_rows = do_rows.astype(BF16)
-            total = l_ref[i]
-            at_row, start_row = pair_rows(p_ref[i])
-
-            def step(masked, diagonal, p, dq):
-                rows = pl.ds(pl.multiple_of(p * CHUNK, CHUNK), CHUNK)
-                scores = dot(keys[rows, :], q_rows, NT)
-                if masked:
-                    at_key = jnp.concatenate([key_at[rows, :]] * (CHUNK // 128), axis=1)
-                    seen = at_key >= start_row
-                    if diagonal:
-                        seen = seen & (at_key <= at_row)
-                    scores = jnp.where(seen, scores, MASKED)
-                probs = jnp.exp(scores - total)
-                d_scores = (probs * (dot(values[rows, :], do_rows, NT) - delta)).astype(BF16)
-                acc[rows, :] += dot(jnp.concatenate([d_scores, probs.astype(BF16)], axis=1), right)
-                return dq + dot(keys_t[:, rows], d_scores)
-
-            def masked_step(p, dq):
-                return step(True, False, p, dq)
-
-            def plain_step(p, dq):
-                return step(False, False, p, dq)
-
-            dq = jnp.zeros((128, 2 * ROWS), F32)
-            dq = lax.fori_loop(at_ref[0, i], at_ref[1, i], masked_step, dq)
-            dq = lax.fori_loop(at_ref[1, i], i, plain_step, dq)
-            dq = step(True, True, i, dq).T * 0.125
-            dq_ref[i] = jnp.where(low, dq[:ROWS], pltpu.roll(dq[ROWS:], 64, 1))
+        lax.fori_loop(0, PAIRS, pick, 0)
+        for e in range(LOCAL):
+            start(rows_out(e))
+
+        def expert(e, _):
+            wait(weights_in(e))
+
+            def work(h, _):
+                at = pl.ds(pl.multiple_of(h * half, half), half)
+                x_h, dr_h = xin[e, at, :], dr[e, at, :]
+                gate = dot(x_h, wg[e])
+                up = dot(x_h, wu[e])
+                sig = jax.nn.sigmoid(gate)
+                silu = gate * sig
+                act_h = (silu * up).astype(BF16)
+                act[e, at, :] = act_h
+                d_act = dot(dr_h, wd[e], NT)
+                d_gate = (d_act * up * sig * (1.0 + gate * (1.0 - sig))).astype(BF16)
+                d_up = (d_act * silu).astype(BF16)
+                dg[e, at, :] = d_gate
+                du[e, at, :] = d_up
+                y = (dot(act_h, wd[e]) * weight[e, at, :]).astype(BF16)
+                dch = (dot(d_gate, wg[e], NT) + dot(d_up, wu[e], NT)).astype(BF16)
+                place_at = pl.ds(pl.multiple_of(e * PAIR_CAP, PAIR_CAP), PAIR_CAP)
+                for k in range(2):
+                    piece = slice(k * PAIR_CAP, (k + 1) * PAIR_CAP)
+                    made[2 * h + k, place_at, :] = y[piece]
+                    back[2 * h + k, place_at, :] = dch[piece]
+                return 0
+
+            lax.fori_loop(0, 2, work, 0)
+            start(acts_out(e))
             return 0
 
-        lax.fori_loop(0, CHIPS, block, 0)
-        core = lax.rem(lax.axis_index("ctx"), 2)
-
-        def part(s, _):
-            mine = pl.ds(pl.multiple_of((2 * s + core) * ROWS, ROWS), ROWS)
-            other = pl.ds(pl.multiple_of((2 * s + 1 - core) * ROWS, ROWS), ROWS)
-            mine_ref[s] = acc[mine, :]
-            other_ref[s] = acc[other, :].astype(BF16)
+        lax.fori_loop(0, LOCAL, expert, 0)
+        lane_id = lax.broadcasted_iota(jnp.int32, (PAIR_ROWS, PAIR_SLOTS), 1).astype(F32)
+
+        def give(p, _):
+            turned = jnp.concatenate([pair_meta(p), jnp.zeros((120, PAIR_ROWS), F32)], axis=0).T
+            chosen = jnp.zeros((PAIR_ROWS, PAIR_SLOTS), F32)
+            for k in range(LOCAL):
+                spot = turned[:, k : k + 1]
+                lane = jnp.where(spot < 0.0, -1.0, spot + float(k * PAIR_CAP))
+                chosen = chosen + jnp.where(lane_id == lane, 1.0, 0.0)
+            chosen = chosen.astype(BF16)
+            at_pair = pl.ds(2 * p, 2)
+            dx[at_pair] = dot(chosen, back[p]).astype(BF16).reshape(2, ROWS, WIDTH)
+            out[at_pair] = dot(chosen, made[p]).astype(BF16).reshape(2, ROWS, WIDTH)
+            start(pair_out(p))
             return 0
 
-        lax.fori_loop(0, CHIPS, part, 0)
+        lax.fori_loop(0, PAIRS, give, 0)
+        for e in range(LOCAL):
+            wait(rows_out(e))
+            wait(acts_out(e))
+        for p in range(PAIRS):
+            wait(pair_out(p))
 
     vmem = pl.BlockSpec(memory_space=pltpu.VMEM)
-    return pl.pallas_call(
-        body,
-        name="attend_back",
-        out_shape=[
-            jax.ShapeDtypeStruct((CHIPS, ROWS, 128), F32),
-            jax.ShapeDtypeStruct((CHIPS, ROWS, 128), F32),
-            jax.ShapeDtypeStruct((CHIPS, ROWS, 128), BF16),
-        ],
-        in_specs=[pl.BlockSpec(memory_space=pltpu.SMEM)] + [vmem] * 7,
-        out_specs=[vmem] * 3,
-        scratch_shapes=[
-            pltpu.VMEM((KEYS, 128), BF16),
-            pltpu.VMEM((KEYS, 128), BF16),
-            pltpu.VMEM((KEYS, 128), F32),
-            pltpu.VMEM((KEYS, 128), F32),
-            pltpu.VMEM((128, KEYS), BF16),
-        ],
-        compiler_params=pltpu.CompilerParams(vmem_limit_bytes=60 * MIB),
-    )(chunks, q, kv, d_out, out_turned, log_total, key_pos, places)
-
-
-def experts(rows, grads, meta, meta_t, w_gate, w_up, w_down):
-    half = SLOTS // 2
-
-    def body(
-        x_ref, g_ref, m_ref, mt_ref, wg_ref, wu_ref, wd_ref,
-        xin_ref, dr_ref, act_ref, dg_ref, du_ref, out_ref, dx_ref,
-        made, back, weight,
-    ):
-        e = pl.program_id(0)
-
-        @pl.when(e == 0)
-        def _():
-            slot_id = lax.broadcasted_iota(jnp.int32, (PAIR_CAP, PAIR_ROWS), 0).astype(F32)
-
-            def pick(p, _):
-                meta_p = m_ref[p]
-                parts, gates = [], []
-                for k in range(LOCAL):
-                    hit = slot_id == meta_p[k : k + 1, :]
-                    parts.append(jnp.where(hit, 1.0, 0.0).astype(BF16))
-                    gates.append(
-                        jnp.sum(jnp.where(hit, meta_p[4 + k : 5 + k, :], 0.0), axis=1, keepdims=True)
-                    )
-                chosen = jnp.concatenate(parts, axis=0)
-                rows_p = dot(chosen, x_ref[p]).astype(BF16)
-                grads_p = dot(chosen, g_ref[p])
-                at = pl.ds(pl.multiple_of(p * PAIR_CAP, PAIR_CAP), PAIR_CAP)
-                for k in range(LOCAL):
-                    piece = slice(k * PAIR_CAP, (k + 1) * PAIR_CAP)
-                    xin_ref[k, at, :] = rows_p[piece]
-                    dr_ref[k, at, :] = (grads_p[piece] * gates[k]).astype(BF16)
-                    weight[k, at, :] = gates[k]
-                return 0
-
-            lax.fori_loop(0, PAIRS, pick, 0)
-
-        def work(h, _):
-            at = pl.ds(pl.multiple_of(h * half, half), half)
-            x = xin_ref[e, at, :]
-            dr = dr_ref[e, at, :]
-            gate = dot(x, wg_ref[0])
-            up = dot(x, wu_ref[0])
-            sig = jax.nn.sigmoid(gate)
-            silu = gate * sig
-            act = (silu * up).astype(BF16)
-            act_ref[0, at, :] = act
-            d_act = dot(dr, wd_ref[0], NT)
-            d_gate = (d_act * up * sig * (1.0 + gate * (1.0 - sig))).astype(BF16)
-            d_up = (d_act * silu).astype(BF16)
-            dg_ref[0, at, :] = d_gate
-            du_ref[0, at, :] = d_up
-            y = (dot(act, wd_ref[0]) * weight[e, at, :]).astype(BF16)
-            dch = (dot(d_gate, wg_ref[0], NT) + dot(d_up, wu_ref[0], NT)).astype(BF16)
-            place_at = pl.ds(pl.multiple_of(e * PAIR_CAP, PAIR_CAP), PAIR_CAP)
-            for k in range(2):
-                piece = slice(k * PAIR_CAP, (k + 1) * PAIR_CAP)
-                made[2 * h + k, place_at, :] = y[piece]
-                back[2 * h + k, place_at, :] = dch[piece]
-            return 0
-
-        lax.fori_loop(0, 2, work, 0)
-
-        @pl.when(e == LOCAL - 1)
-        def _():
-            lane_id = lax.broadcasted_iota(jnp.int32, (PAIR_ROWS, PAIR_SLOTS), 1).astype(F32)
-
-            def give(p, _):
-                meta_p = mt_ref[p]
-                chosen = jnp.zeros((PAIR_ROWS, PAIR_SLOTS), F32)
-                for k in range(LOCAL):
-                    spot = meta_p[:, k : k + 1]
-                    lane = jnp.where(spot < 0.0, -1.0, spot + float(k * PAIR_CAP))
-                    chosen = chosen + jnp.where(lane_id == lane, 1.0, 0.0)
-                chosen = chosen.astype(BF16)
-                dx_ref[p] = dot(chosen, back[p]).astype(BF16)
-                out_ref[p] = dot(chosen, made[p]).astype(BF16)
-                return 0
-
-            lax.fori_loop(0, PAIRS, give, 0)
-
-    def fixed(*shape):
-        return pl.BlockSpec(shape, lambda e: (0,) * len(shape), pipeline_mode=pl.Buffered(1))
-
-    def each(*shape):
-        return pl.BlockSpec((1,) + shape, lambda e: (e, 0, 0))
-
+    buf = lambda *shape: pltpu.VMEM(shape, BF16)
+    wide, narrow, source = (LOCAL, SLOTS, WIDTH), (LOCAL, SLOTS, FF), (EXP, ROWS, WIDTH)
     return compute_call(
         body,
         "experts",
-        [
-            jax.ShapeDtypeStruct((LOCAL, SLOTS, WIDTH), BF16),
-            jax.ShapeDtypeStruct((LOCAL, SLOTS, WIDTH), BF16),
-            jax.ShapeDtypeStruct((LOCAL, SLOTS, FF), BF16),
-            jax.ShapeDtypeStruct((LOCAL, SLOTS, FF), BF16),
-            jax.ShapeDtypeStruct((LOCAL, SLOTS, FF), BF16),
-            jax.ShapeDtypeStruct((PAIRS, PAIR_ROWS, WIDTH), BF16),
-            jax.ShapeDtypeStruct((PAIRS, PAIR_ROWS, WIDTH), BF16),
-        ],
-        [rows, grads, meta, meta_t, w_gate, w_up, w_down],
-        vmem=60,
-        grid=(LOCAL,),
-        in_specs=[
-            fixed(PAIRS, PAIR_ROWS, WIDTH),
-            fixed(PAIRS, PAIR_ROWS, WIDTH),
-            fixed(PAIRS, 8, PAIR_ROWS),
-            fixed(PAIRS, PAIR_ROWS, 8),
-            each(WIDTH, FF),
-            each(WIDTH, FF),
-            each(FF, WIDTH),
-        ],
-        out_specs=[
-            fixed(LOCAL, SLOTS, WIDTH),
-            fixed(LOCAL, SLOTS, WIDTH),
-            each(SLOTS, FF),
-            each(SLOTS, FF),
-            each(SLOTS, FF),
-            fixed(PAIRS, PAIR_ROWS, WIDTH),
-            fixed(PAIRS, PAIR_ROWS, WIDTH),
-        ],
+        [jax.ShapeDtypeStruct(shape, BF16) for shape in (wide, wide, narrow, narrow, narrow, source, source)],
+        [rows, grads, meta, w_gate, w_up, w_down],
+        vmem=63,
+        in_specs=[ANY_SPEC, ANY_SPEC, vmem] + [ANY_SPEC] * 3,
+        out_specs=[ANY_SPEC] * 7,
         scratch_shapes=[
-            pltpu.VMEM((PAIRS, PAIR_SLOTS, WIDTH), BF16),
-            pltpu.VMEM((PAIRS, PAIR_SLOTS, WIDTH), BF16),
+            buf(*source),
+            buf(*source),
+            buf(LOCAL, WIDTH, FF),
+            buf(LOCAL, WIDTH, FF),
+            buf(LOCAL, FF, WIDTH),
+            buf(*wide),
+            buf(*wide),
+            buf(*narrow),
+            buf(*narrow),
+            buf(*narrow),
+            buf(*source),
+            buf(*source),
+            buf(PAIRS, PAIR_SLOTS, WIDTH),
+            buf(PAIRS, PAIR_SLOTS, WIDTH),
             pltpu.VMEM((LOCAL, SLOTS, 1), F32),
+            pltpu.SemaphoreType.DMA((5, 4)),
         ],
     )
 
@@ -920,20 +866,6 @@
     scale = row_scale(total_squares, width)
     inner = jnp.sum(weighted * values, axis=1, keepdims=True) * (1.0 / width)
     return scale * weighted - values * (scale * scale * scale) * inner, scale
-
-
-def out_grads(attended, d_branch):
-    def body(a_ref, d_ref, o_ref):
-        def part(r, _):
-            at = pl.ds(pl.multiple_of(r * 256, 256), 256)
-            o_ref[at, :] = dot(a_ref[:, at], d_ref[...], TN).astype(BF16)
-            return 0
-
-        lax.fori_loop(0, 4, part, 0)
-
-    return compute_call(
-        body, "out_grads", [jax.ShapeDtypeStruct((WIDTH, WIDTH), BF16)], [attended, d_branch]
-    )[0]
 
 
 def deliver(resid, layer_keep, layer_got, dense, out_grad, gain_sums, input_grad, expert_sums):
@@ -991,7 +923,7 @@
 
     def body(
         t_ref, cot_ref, wq_ref, wk_ref, wv_ref, wd_ref, na_ref, nq_ref, nk_ref, nf_ref, perm_ref, len_ref,
-        wo_ref, go_ref, n_ref, ql_ref, kl_ref, s_ref, c_ref, sn_ref, p_ref, q_ref, kv_ref, co_ref,
+        wo_ref, go_ref, n_ref, ql_ref, kl_ref, s_ref, c_ref, sn_ref, p_ref, kp_ref, q_ref, kv_ref, co_ref,
         g_ref, w_mine, rows, normed, gains_v, w_own, totals, totals_all, kv_half, send_sem, recv_sem, local_sem,
     ):
         _, chip, core, sibling = place()
@@ -1073,6 +1005,7 @@
         for i in range(CHIPS):
             mine = [jnp.where(core == 0, v[2 * i : 2 * i + 1], v[2 * i + 1 : 2 * i + 2]) for v in (position, begin)]
             p_ref[i] = jnp.concatenate(mine, axis=0)
+            kp_ref[i] = jnp.concatenate([position[2 * i : 2 * i + 1], position[2 * i + 1 : 2 * i + 2]], axis=1)
 
         def angles(i, _):
             keys = key_lanes()
@@ -1162,12 +1095,13 @@
             wide,
             wide,
             jax.ShapeDtypeStruct((CHIPS, 2, ROWS), F32),
+            jax.ShapeDtypeStruct((CHIPS, 1, CHUNK), F32),
             jax.ShapeDtypeStruct((CHIPS, ROWS, 128), BF16),
             jax.ShapeDtypeStruct((CHIPS, 2, ROWS, 128), BF16),
             jax.ShapeDtypeStruct((EXP, ROWS, WIDTH), BF16),
         ],
         in_specs=[vmem] * 12,
-        out_specs=[ANY_SPEC, vmem, ANY_SPEC] + [vmem] * 7 + [ANY_SPEC] * 2,
+        out_specs=[ANY_SPEC, vmem, ANY_SPEC] + [vmem] * 8 + [ANY_SPEC] * 2,
         scratch_shapes=[
             pltpu.VMEM((8, 128), F32),
             pltpu.VMEM((128, 256), BF16),
@@ -1198,16 +1132,16 @@
 
 
 def tail(
-    dq, dkv_mine, dkv_other, q_lin, kv_lin, cosine, sine, squares, gains, normed, out_part, layer_part,
-    weights, tokens, d_resid, ffn_gain, gate_part, up_part, down_a, down_b,
+    q, kv, d_out, out_turned, log_total, key_pos, places, q_lin, kv_lin, cosine, sine, squares, gains, normed, attended, d_branch, layer_part,
+    w_query, w_key, w_value, tokens, d_resid, ffn_gain, gate_part, up_part, down_a, down_b,
 ):
     def body(
-        dq_ref, dm_ref, do_ref, ql_ref, kl_ref, c_ref, sn_ref, s_ref, g_ref, n_ref, op_ref, lp_ref,
-        w_ref, t_ref, r_ref, fg_ref, gp_ref, up_ref, da_ref, db_ref,
+        q_ref, kv_ref, do_ref, ot_ref, l_ref, kp_ref, p_ref, ql_ref, kl_ref, c_ref, sn_ref, s_ref, g_ref, n_ref, at_ref, br_ref, lp_ref,
+        wq_ref, wk_ref, wv_ref, t_ref, r_ref, fg_ref, gp_ref, up_ref, da_ref, db_ref,
         eg_ref, eu_ref, ed_ref, di_ref, dense_ref, og_ref, lo_ref, gs_ref,
-        dq_v, dm_v, ql_v, kl_v, c_v, sn_v, n_v, w_v, t_v, r_v,
+        keys_v, values, acc, key_at, keys_t, dq_v, other_v, w_mine, ql_v, kl_v, c_v, sn_v, n_v, w_v, t_v, r_v,
         got, e_q, e_kv, totals, totals_all, d_lin, home, w_give, w_keep, w_got, joint, traded, done,
-        o_keep, o_got, o_traded, o_pair, o_half, o_full, a_got, a_done, packet, packets, mine, shared, gate_c, down_c, up_d, down_d, send_sem, recv_sem, local_sem,
+        o_both, o_keep, o_got, o_traded, o_pair, o_half, o_full, a_got, a_done, packet, packets, mine, shared, gate_c, down_c, up_d, down_d, send_sem, recv_sem, local_sem,
     ):
         ctx, chip, core, sibling = place()
         me = lax.axis_index("exp")
@@ -1218,17 +1152,142 @@
         copier = Copier(send_sem, recv_sem, local_sem)
         heads = [
             copier.keep(src, dst)
-            for src, dst in ((dq_ref, dq_v), (c_ref, c_v), (sn_ref, sn_v), (ql_ref, ql_v), (kl_ref, kl_v), (dm_ref, dm_v))
+            for src, dst in ((c_ref, c_v), (sn_ref, sn_v), (ql_ref, ql_v), (kl_ref, kl_v))
         ]
         late = [
             copier.keep(src, dst)
-            for src, dst in ((n_ref, n_v), (w_ref, w_v), (t_ref, t_v), (r_ref, r_v))
+            for src, dst in ((n_ref, n_v),  (t_ref, t_v), (r_ref, r_v))
         ]
-        o_load = copier.keep(op_ref.at[:, core], o_keep)
+        w_mine[:, 0:1024] = wq_ref[...]
+        w_mine[:, 1024:1536] = wk_ref[...]
+        w_mine[:, 1536:2048] = wv_ref[...]
+        w_v[me] = w_mine[...]
+        w_part = pl.ds(pl.multiple_of(core * 64, 64), 64)
+        w_slot = lambda s: w_v.at[s, w_part]
+        handed = []
+        weights = relay(
+            copier,
+            w_mine.at[w_part],
+            w_slot,
+            64,
+            ring_of(me),
+            lambda p: ("exp", p),
+            lambda s: handed.append(copier.send(w_slot(s), w_slot(s), "ctx", sibling)),
+        )
         meet([("ctx", p) for p in others] + [("exp", p) for p in exps])
-        swapped = copier.send(do_ref, got, "ctx", sibling)
-        o_swap = copier.send(op_ref.at[:, 1 - core], o_got, "ctx", sibling)
+        next(weights)
+        next(weights)
         copier.send(lp_ref, lo_ref, "exp", lax.rem(me + 4, EXP))
+        zh, y = chip // 4, lax.rem(chip, 4)
+        second = []
+        for d in (1, 3, 2):
+            c = lax.rem(y + d, 4)
+            second.append(copier.send(gp_ref.at[c], gate_c.at[y], *to_chip(zh * 4 + c)))
+            second.append(copier.send(da_ref.at[c], down_c.at[y], *to_chip(zh * 4 + c)))
+        second.append(copier.send(up_ref.at[1 - zh], up_d, *to_chip((1 - zh) * 4 + y)))
+        second.append(copier.send(db_ref.at[1 - zh], down_d, *to_chip((1 - zh) * 4 + y)))
+
+        def out_grad(r, _):
+            grad = dot(at_ref[:, pl.ds(pl.multiple_of(r * 256, 256), 256)], br_ref[...], TN).astype(BF16)
+            for k in range(2):
+                for c in range(2):
+                    o_both[c, 2 * r + k] = grad[(2 * k + c) * 64 : (2 * k + c + 1) * 64]
+            return 0
+
+        lax.fori_loop(0, 4, out_grad, 0)
+        o_swap = copier.send(o_both.at[1 - core], o_got, "ctx", sibling)
+        low = key_lanes()
+
+        def place_keys(p, _):
+            rows = pl.ds(pl.multiple_of(p * CHUNK, CHUNK), CHUNK)
+            both = kv_ref[rows, :].astype(F32)
+            own_keys = jnp.where(low, both, 0.0)
+            keys_v[rows, :] = own_keys.astype(BF16)
+            keys_t[:, rows] = own_keys.T.astype(BF16)
+            values[rows, :] = jnp.where(low, pltpu.roll(both, 64, 1), 0.0).astype(BF16)
+            key_at[rows, :] = key_columns(kp_ref[p])
+            acc[rows, :] = jnp.zeros((CHUNK, 128), F32)
+            return 0
+
+        lax.fori_loop(0, CHIPS, place_keys, 0)
+
+        def attend_block(i, _):
+            q_wide, do_wide = q_ref[i].astype(F32), do_ref[i].astype(F32)
+            q_turned, do_turned = pltpu.roll(q_wide, 64, 1), pltpu.roll(do_wide, 64, 1)
+            q_rows = jnp.concatenate([q_wide, q_turned], axis=0)
+            do_rows = jnp.concatenate([do_wide, do_turned], axis=0)
+            do_high = jnp.concatenate([do_turned, do_wide], axis=0)
+            right = [jnp.where(low, q_rows, 0.0), jnp.where(low, 0.0, do_high)]
+            right = jnp.concatenate(right, axis=0).astype(BF16)
+            q_rows = q_rows.astype(BF16)
+            delta = jnp.sum(do_rows.T[0:64, :] * ot_ref[i], axis=0, keepdims=True)
+            do_rows = do_rows.astype(BF16)
+            total = l_ref[i]
+            at_row, start_row = pair_rows(p_ref[i])
+
+            def step(diagonal, p, dq):
+                rows = pl.ds(pl.multiple_of(p * CHUNK, CHUNK), CHUNK)
+                scores = dot(keys_v[rows, :], q_rows, NT)
+                at_key = jnp.concatenate([key_at[rows, :]] * (CHUNK // 128), axis=1)
+                seen = at_key >= start_row
+                if diagonal:
+                    seen = seen & (at_key <= at_row)
+                probs = jnp.exp(jnp.where(seen, scores, MASKED) - total)
+                d_scores = (probs * (dot(values[rows, :], do_rows, NT) - delta)).astype(BF16)
+                acc[rows, :] += dot(jnp.concatenate([d_scores, probs.astype(BF16)], axis=1), right)
+                return dq + dot(keys_t[:, rows], d_scores)
+
+            dq = lax.fori_loop(0, i, lambda p, dq: step(False, p, dq), jnp.zeros((128, 2 * ROWS), F32))
+            dq = step(True, i, dq).T * 0.125
+            dq_v[i] = jnp.where(low, dq[:ROWS], pltpu.roll(dq[ROWS:], 64, 1))
+            return 0
+
+        lax.fori_loop(0, 4, attend_block, 0)
+        next(weights)
+        next(weights)
+        copier.arrived(o_swap)
+
+        def add_cores(e, _):
+            o_keep[e] = (o_both[core, e].astype(F32) + o_got[e].astype(F32)).astype(BF16)
+            return 0
+
+        lax.fori_loop(0, EXP, add_cores, 0)
+        zl, x = me // 4, lax.rem(me, 4)
+        o_trades = []
+        for d in (2, 1, 3):
+            p = lax.rem(x + d, 4)
+            for z in range(2):
+                o_trades.append(copier.send(o_keep.at[z * 4 + p], o_traded.at[x, z], "exp", zl * 4 + p))
+        lax.fori_loop(4, 6, attend_block, 0)
+        next(weights)
+        next(weights)
+        lax.fori_loop(6, 7, attend_block, 0)
+        next(weights)
+        for at in o_trades:
+            copier.arrived(at)
+        keep, give = o_keep[zl * 4 + x].astype(F32), o_keep[(1 - zl) * 4 + x].astype(F32)
+        for d in (1, 2, 3):
+            p = lax.rem(x + d, 4)
+            keep = keep + o_traded[p, zl].astype(F32)
+            give = give + o_traded[p, 1 - zl].astype(F32)
+        o_half[...] = give.astype(BF16)
+        o_full[...] = keep.astype(BF16)
+        o_pairs = copier.send(o_half, o_pair, "exp", (1 - zl) * 4 + x)
+        lax.fori_loop(7, CHIPS, attend_block, 0)
+
+        side_by_side(weights)
+
+        def give_other(s, _):
+            other = pl.ds(pl.multiple_of((2 * s + 1 - core) * ROWS, ROWS), ROWS)
+            other_v[s] = acc[other, :].astype(BF16)
+            return 0
+
+        lax.fori_loop(0, CHIPS, give_other, 0)
+        swapped = copier.send(other_v, got, "ctx", sibling)
+        copier.arrived(o_pairs)
+        o_full[...] = (o_full[...].astype(F32) + o_pair[...].astype(F32)).astype(BF16)
+        spread = [copier.send(o_full.at[:, lanes(p)], a_got.at[chip], *to_chip(p)) for p in twins]
+        a_got[chip] = o_full[:, lanes(chip)]
         keys = key_lanes()
         gain = g_ref[chip]
         for at in heads:
@@ -1244,7 +1303,8 @@
         def unturn_kv(i, carry):
             q_sum, kv_sum = carry
             cos, sin = jnp.where(keys, c_v[i], 1.0), jnp.where(keys, -sn_v[i], 0.0)
-            e = turn(dm_v[i] + got[i].astype(F32), cos, sin)
+            mine_rows = pl.ds(pl.multiple_of((2 * i + core) * ROWS, ROWS), ROWS)
+            e = turn(acc[mine_rows, :] + got[i].astype(F32), cos, sin)
             e_kv[i] = e
             q_part, kv_part = e_q[i] * ql_v[i], e * kl_v[i]
             totals[i] = both_totals(q_part * gain[1:2, :], kv_part * gain[2:3, :])
@@ -1258,20 +1318,16 @@
         q_sum, kv_sum = lax.fori_loop(0, CHIPS, unturn_kv, (none, none))
         shares = [copier.send(totals, totals_all.at[chip], *to_chip(p)) for p in twins]
         totals_all[chip] = totals[...]
-        copier.kept(o_load)
-        copier.arrived(o_swap)
-
-        def add_cores(e, _):
-            o_keep[e] = (o_keep[e].astype(F32) + o_got[e].astype(F32)).astype(BF16)
-            return 0
-
-        lax.fori_loop(0, EXP, add_cores, 0)
-        zl, x = me // 4, lax.rem(me, 4)
-        o_trades = []
-        for d in (2, 1, 3):
-            p = lax.rem(x + d, 4)
-            for z in range(2):
-                o_trades.append(copier.send(o_keep.at[z * 4 + p], o_traded.at[x, z], "exp", zl * 4 + p))
+        for at in spread:
+            copier.arrived(at)
+        total = a_got[0].astype(F32)
+        for c in range(1, CHIPS):
+            total = total + a_got[c].astype(F32)
+        a_done[...] = total.astype(BF16)
+        half = pl.ds(pl.multiple_of(core * 64, 64), 64)
+        a_shares = [copier.send(a_done, og_ref.at[half, lanes(chip)], *to_chip(p)) for p in twins]
+        copier.send(a_done, og_ref.at[half, lanes(chip)], "ctx", sibling)
+        copier.keep(a_done, og_ref.at[half, lanes(chip)])
         for at in shares:
             copier.arrived(at)
 
@@ -1294,14 +1350,6 @@
             gradient(p)
             for k in range(2):
                 homeward.append(copier.send(d_lin.at[k, p], home.at[k, :, lanes(chip)], *to_chip(p)))
-        zh, y = chip // 4, lax.rem(chip, 4)
-        second = []
-        for d in (1, 3, 2):
-            c = lax.rem(y + d, 4)
-            second.append(copier.send(gp_ref.at[c], gate_c.at[y], *to_chip(zh * 4 + c)))
-            second.append(copier.send(da_ref.at[c], down_c.at[y], *to_chip(zh * 4 + c)))
-        second.append(copier.send(up_ref.at[1 - zh], up_d, *to_chip((1 - zh) * 4 + y)))
-        second.append(copier.send(db_ref.at[1 - zh], down_d, *to_chip((1 - zh) * 4 + y)))
         gradient(chip)
         for k in range(2):
             home[k, :, lanes(chip)] = d_lin[k, chip]
@@ -1326,17 +1374,8 @@
         joint[...] = both.astype(BF16).reshape(EXP, 128, 128)
         trades = [copier.send(joint.at[p], traded.at[me], "exp", p) for p in exps]
         traded[me] = joint[me]
-        for at in o_trades:
-            copier.arrived(at)
-        keep, give = o_keep[zl * 4 + x].astype(F32), o_keep[(1 - zl) * 4 + x].astype(F32)
-        for d in (1, 2, 3):
-            p = lax.rem(x + d, 4)
-            keep = keep + o_traded[p, zl].astype(F32)
-            give = give + o_traded[p, 1 - zl].astype(F32)
-        o_half[...] = give.astype(BF16)
-        o_pairs = copier.send(o_half, o_pair, "exp", (1 - zl) * 4 + x)
-
-        for at in homeward:
+
+        for at in homeward + handed:
             copier.arrived(at)
         k_parts, v_parts = [], []
         for c in range(4):
@@ -1357,10 +1396,6 @@
             weighted = d_normed * g_ref[e, 0:1, :]
             inner = inner + jnp.sum(weighted * x[:, at], axis=1, keepdims=True)
             pieces.append(weighted)
-        copier.arrived(o_pairs)
-        o_full[...] = (keep + o_pair[...].astype(F32)).astype(BF16)
-        spread = [copier.send(o_full.at[:, lanes(p)], a_got.at[chip], *to_chip(p)) for p in twins]
-        a_got[chip] = o_full[:, lanes(chip)]
         packet[chip, 1:2, :] = q_sum
         packet[chip, 2:3, :] = kv_sum
         gain_trades = [copier.send(packet.at[p], packets.at[me], "exp", p) for p in exps]
@@ -1386,16 +1421,6 @@
         gain_shares = [copier.send(mine, shared.at[ctx], "ctx", p) for p in others]
         shared[ctx] = total
 
-        for at in spread:
-            copier.arrived(at)
-        total = a_got[0].astype(F32)
-        for c in range(1, CHIPS):
-            total = total + a_got[c].astype(F32)
-        a_done[...] = total.astype(BF16)
-        half = pl.ds(pl.multiple_of(core * 64, 64), 64)
-        a_shares = [copier.send(a_done, og_ref.at[half, lanes(chip)], *to_chip(p)) for p in twins]
-        copier.send(a_done, og_ref.at[half, lanes(chip)], "ctx", sibling)
-        copier.keep(a_done, og_ref.at[half, lanes(chip)])
         inner = inner * (1.0 / WIDTH)
         cut = scale * scale * scale * inner
         for e in range(EXP):
@@ -1452,11 +1477,17 @@
             jax.ShapeDtypeStruct((ROWS, WIDTH), BF16),
             jax.ShapeDtypeStruct((8, 128), F32),
         ],
-        in_specs=[ANY_SPEC] * 7 + [vmem] * 2 + [ANY_SPEC] * 6 + [vmem] * 5,
+        in_specs=[vmem] * 7 + [ANY_SPEC] * 4 + [vmem] * 2 + [ANY_SPEC] + [vmem] * 2 + [ANY_SPEC] + [vmem] * 3 + [ANY_SPEC] * 2 + [vmem] * 5,
         out_specs=[vmem] * 4 + [ANY_SPEC] * 3 + [vmem],
         scratch_shapes=[
+            pltpu.VMEM((KEYS, 128), BF16),
+            pltpu.VMEM((KEYS, 128), BF16),
+            pltpu.VMEM((KEYS, 128), F32),
+            pltpu.VMEM((KEYS, 128), F32),
+            pltpu.VMEM((128, KEYS), BF16),
             pltpu.VMEM(block, F32),
-            pltpu.VMEM(block, F32),
+            pltpu.VMEM(block, BF16),
+            pltpu.VMEM((128, 2 * WIDTH), BF16),
             pltpu.VMEM(block, F32),
             pltpu.VMEM(block, F32),
             pltpu.VMEM(block, F32),
@@ -1478,6 +1509,7 @@
             pltpu.VMEM((EXP, 128, 128), BF16),
             pltpu.VMEM((EXP, 128, 128), BF16),
             tile,
+            pltpu.VMEM((2, EXP, 64, WIDTH), BF16),
             pltpu.VMEM((EXP, 64, WIDTH), BF16),
             pltpu.VMEM((EXP, 64, WIDTH), BF16),
             pltpu.VMEM((4, 2, 64, WIDTH), BF16),
@@ -1494,16 +1526,16 @@
             pltpu.VMEM((4, 2, 32, WIDTH), BF16),
             pltpu.VMEM((LOCAL, 64, FF), BF16),
             pltpu.VMEM((2, 32, WIDTH), BF16),
-            pltpu.SemaphoreType.DMA((106,)),
-            pltpu.SemaphoreType.DMA((106,)),
-            pltpu.SemaphoreType.DMA((14,)),
+            pltpu.SemaphoreType.DMA((127,)),
+            pltpu.SemaphoreType.DMA((127,)),
+            pltpu.SemaphoreType.DMA((15,)),
         ],
         compiler_params=pltpu.CompilerParams(
             collective_id=6, has_side_effects=True, vmem_limit_bytes=60 * MIB
         ),
     )(
-        dq, dkv_mine, dkv_other, q_lin, kv_lin, cosine, sine, squares, gains, normed, out_part, layer_part,
-        weights, tokens, d_resid, ffn_gain, gate_part, up_part, down_a, down_b,
+        q, kv, d_out, out_turned, log_total, key_pos, places, q_lin, kv_lin, cosine, sine, squares, gains, normed, attended, d_branch, layer_part,
+        w_query, w_key, w_value, tokens, d_resid, ffn_gain, gate_part, up_part, down_a, down_b,
     )
 
 
@@ -1534,7 +1566,7 @@
 
     row = lambda v: v.reshape(1, -1)
     (
-        w_o, gain_all, normed, q_lin, kv_lin, squares, cosine, sine, places, q_all, kv_all, grads_all,
+        w_o, gain_all, normed, q_lin, kv_lin, squares, cosine, sine, places, key_pos, q_all, kv_all, grads_all,
     ) = front(
         tokens,
         cotangent,
@@ -1544,39 +1576,15 @@
         lengths,
     )
 
-    pieces = jnp.arange(CTX, dtype=jnp.int32)[:, None] * CTX + deal_perm[0]
-    positions = (pieces[:, :, None] * 12 + jnp.arange(12, dtype=jnp.int32)).reshape(CTX, ROWS)
-    key_pos = positions.reshape(CHIPS, 1, CHUNK).astype(F32)
-    starts = places[:, 1].astype(jnp.int32)
-    whole_from = (jnp.max(starts, axis=1) + CHUNK - 1) // CHUNK
-    chunks = jnp.stack(
-        [jnp.min(starts, axis=1) // CHUNK, jnp.minimum(whole_from, jnp.arange(CHIPS, dtype=jnp.int32))]
-    )
     w_o = w_o.reshape(WIDTH, WIDTH)
     kv_all = kv_all.reshape(KEYS, 128)
-    out_low, out_wide, log_total = attend(q_all, kv_all, key_pos, places, chunks)
+    out_low, out_wide, log_total = attend(q_all, kv_all, key_pos, places, lengths)
     attended, resid, rows_all, meta_all = join_heads(
         out_low, w_o, tokens, gain_all, routes[0].T, gate_logits[0].T
     )
 
-    rows_all, dense_late = lax.optimization_barrier(
-        (rows_all, jnp.concatenate([w_query, w_key, w_value], axis=1))
-    )
-    dense_late = lax.all_gather(dense_late, "exp", axis=0, tiled=True)
-
-    shift = jnp.array([0.0, float(CAP)], F32)[None, None, :, None]
-    spots = meta_all[:, :LOCAL].reshape(PAIRS, 2, LOCAL, ROWS).transpose(0, 2, 1, 3)
-    spots = jnp.where(spots < 0.0, -1.0, spots + shift).reshape(PAIRS, LOCAL, PAIR_ROWS)
-    gates = meta_all[:, LOCAL:].reshape(PAIRS, 2, LOCAL, ROWS).transpose(0, 2, 1, 3)
-    pair_meta = jnp.concatenate([spots, gates.reshape(PAIRS, LOCAL, PAIR_ROWS)], axis=1)
     rows_in, d_rows, act, d_gate, d_up, out_parts, d_parts = experts(
-        rows_all.reshape(PAIRS, PAIR_ROWS, WIDTH),
-        grads_all.reshape(PAIRS, PAIR_ROWS, WIDTH),
-        pair_meta,
-        pair_meta.transpose(0, 2, 1),
-        w_gate,
-        w_up,
-        w_down,
+        rows_all, grads_all, meta_all, w_gate, w_up, w_down
     )
     (
         gate_part, up_part, down_a, down_b, d_resid, d_branch, ffn_gain_grad, d_out, layer_keep, layer_give,
@@ -1593,14 +1601,14 @@
         gain_all,
         w_o,
     )
-    out_part = out_grads(attended, d_branch).reshape(EXP, 2, 64, WIDTH)
-    dq, dkv_mine, dkv_other = attend_back(
-        q_all, kv_all, d_out, out_wide, log_total, key_pos, places, chunks
-    )
     gate_grad, up_grad, down_grad, input_grad, dense, out_grad, layer_got, gain_sums = tail(
-        dq,
-        dkv_mine,
-        dkv_other,
+        q_all,
+        kv_all,
+        d_out,
+        out_wide,
+        log_total,
+        key_pos,
+        places,
         q_lin,
         kv_lin,
         cosine,
@@ -1608,9 +1616,12 @@
         squares,
         gain_all,
         normed,
-        out_part,
+        attended,
+        d_branch,
         layer_give,
-        dense_late.reshape(EXP, 128, 2 * WIDTH),
+        w_query,
+        w_key,
+        w_value,
         tokens,
         d_resid,
         ffn_gain_grad,

time: 349 us -> 323 us (0.926)
  between operations: 14.1 us -> 0.86 us
  other arithmetic: 4.57 us -> 0 us
    pallas_call x1, Pallas kernels: 66.3 us -> 92.6 us  [tail(): pl.pallas_call(body, name='tail', out_shape=[jax.ShapeDtypeStruct((LOCAL,...]
    pallas_call x1 -> x0, Pallas kernels: 19.7 us -> none  [attend_back(): pl.pallas_call(body, name='attend_back', out_shape=[jax.ShapeDtypeStruct(...]
    pallas_call x3 -> x2, Pallas kernels: 49 us -> 39 us  [compute_call(): pl.pallas_call(body, name=name, out_shape=outs, compiler_params=pltpu.Com...]
  transfers between devices with their start and end apart: 1 -> 0, of which waited for: 0 -> 0; matrix products, arithmetic and copies ran while one was open for 1% -> 0% of each run, Pallas kernels for 38% -> 0%
where the time goes in v5:
time: 323 us
  Pallas kernels  322 us (100%)
    pallas_call x1, Pallas kernels, tail(): pl.pallas_call(body, name='tail', out_shape=[jax.ShapeDtypeStruct((LOCAL,...  92.6 us
    pallas_call x1, Pallas kernels, settle_experts(): pl.pallas_call(body, name='settle_experts', out_shape=[jax.ShapeDtypeStru...  66.6 us
    pallas_call x1, Pallas kernels, front(): pl.pallas_call(body, name='front', out_shape=[jax.ShapeDtypeStruct((EXP,...  62.4 us
    pallas_call x1, Pallas kernels, join_heads(): pl.pallas_call(body, name='join_heads', out_shape=[jax.ShapeDtypeStruct((...  43 us
    pallas_call x2, Pallas kernels, compute_call(): pl.pallas_call(body, name=name, out_shape=outs, compiler_params=pltpu.Com...  39 us
    pallas_call x1, Pallas kernels, attend(): pl.pallas_call(body, name='attend', out_shape=[jax.ShapeDtypeStruct((CHIP...  18.6 us

profile of v5, /device:TPU:1, one launch (start us, length us, event | category | flops | bytes accessed | tf_op | source)
XLA Modules:
  0.0 323.0 jit_solution(5119451013716487019)
XLA Ops:
  0.6 62.4 %front.1 = (bf16[8,128,1024]{2,1,0:T(8,128)(2,1)}, f32[8,8,128]{2,1,0:T(8,128)}, bf16[8,192,1024]{2,1,0:T(8,128)(2,1)}, f32[8,192,128]{2,1,0:T(8,128)}, f32[8,19...) custom-call(bf16[192,1024]{1,0:T(8,128)(2,1)} %bitcast.25, ...), custom_call_target="tpu_custom_call" | custom-call | tf_op jit(solution)/shard_map/front/pallas_call | solution.py:1085
  63.1 18.6 %attend.1 = (bf16[8,192,128]{2,1,0:T(8,128)(2,1)}, f32[8,64,384]{2,1,0:T(8,128)}, f32[8,1,384]{2,1,0:T(1,128)}) custom-call(s32[1,4]{1,0:T(1,128)} %at_ref.1, bf16[8,192,128]{2,1,0:T(8,128)(2,1)} %get-tuple-element.71.q_ref, bf16[3072,128]{1,0:T(8,128)(2,1)} %bitcast.30, f32[8,1,384]{2,1,0:T(1,128)} %get-tuple-element.73.kp_ref, ...), custom_call_target="tpu_custom_call" | custom-call | tf_op jit(solution)/shard_map/attend/pallas_call | solution.py:689
  81.7 43.0 %join_heads.1 = (bf16[192,1024]{1,0:T(8,128)(2,1)}, f32[192,1024]{1,0:T(8,128)}, bf16[8,192,1024]{2,1,0:T(8,128)(2,1)}, f32[8,8,192]{2,1,0:T(8,128)}) custom-call(bf16[8,192,128]{2,1,0:T(8,128)(2,1)} %get-tuple-element.75.x_ref, bf16[1024,1024]{1,0:T(8,128)(2,1)} %bitcast.23, bf16[192,1024]{1,0:T(8,128)(2,1)} %bitcast.26, ...), custom_call_target="tpu_custom_call" | custom-call | tf_op jit(solution)/shard_map/join_heads/pallas_call | solution.py:253
  124.7 34.3 %experts.1 = (bf16[4,576,1024]{2,1,0:T(8,128)(2,1)}, bf16[4,576,1024]{2,1,0:T(8,128)(2,1)}, bf16[4,576,512]{2,1,0:T(8,128)(2,1)}, bf16[4,576,512]{2,1,0:T(8,128)...) custom-call(bf16[8,192,1024]{2,1,0:T(8,128)(2,1)} %get-tuple-element.79.x_ref, ...), custom_call_target="tpu_custom_call" | custom-call | tf_op jit(solution)/shard_map/experts/pallas_call | solution.py:560
  159.0 66.6 %settle_experts.1 = (bf16[4,4,64,512]{3,2,1,0:T(8,128)(2,1)}, bf16[2,4,64,512]{3,2,1,0:T(8,128)(2,1)}, bf16[4,2,32,1024]{3,2,1,0:T(8,128)(2,1)}, bf16[2,2,32,102...) custom-call(bf16[4,576,1024]{2,1,0:T(8,128)(2,1)} %get-tuple-element, ...), custom_call_target="tpu_custom_call" | custom-call | tf_op jit(solution)/shard_map/settle_experts/pallas_call | solution.py:501
  225.6 92.6 %tail.1 = (f32[4,64,512]{2,1,0:T(8,128)}, f32[4,64,512]{2,1,0:T(8,128)}, f32[4,32,1024]{2,1,0:T(8,128)}, f32[192,1024]{1,0:T(8,128)}, bf16[2,128,1024]{2,1,0:T(8...) custom-call(bf16[8,192,128]{2,1,0:T(8,128)(2,1)} %get-tuple-element.71.q_ref, ...), custom_call_target="tpu_custom_call" | custom-call | tf_op jit(solution)/shard_map/tail/pallas_call | solution.py:1467
  318.2 4.7 %deliver.1 = (bf16[192,1024]{1,0:T(8,128)(2,1)}, f32[128,1024]{1,0:T(8,128)}, f32[128,512]{1,0:T(8,128)}, f32[128,512]{1,0:T(8,128)}, f32[128,1024]{1,0:T(8,128)...) custom-call(f32[192,1024]{1,0:T(8,128)} %get-tuple-element.78.res_re, ...), custom_call_target="tpu_custom_call" | custom-call | tf_op jit(solution)/shard_map/deliver/pallas_call | solution.py:560

commit v6 on v5

--- a/solution.py
+++ b/solution.py
@@ -21,6 +21,7 @@
 LOCAL = 4
 CAP = 72
 PAIRS = EXP // 2
+LONGEST = 2048
 PAIR_ROWS = 2 * ROWS
 PAIR_CAP = 2 * CAP
 SLOTS = EXP * CAP
@@ -192,10 +193,11 @@
     return pl.ds(pl.multiple_of(index * 128, 128), 128)
 
 
-def join_heads(blocks, w_out, tokens, gains, routes_t, logits_t):
+def attend(q, kv, key_pos, places, cotangent, w_out, tokens, gains, routes_t, logits_t):
     def body(
-        x_ref, w_ref, t_ref, g_ref, r_ref, l_ref,
-        a_ref, res_ref, o_ref, mo_ref, w_v, ffn, m_v, send_sem, recv_sem, local_sem,
+        q_ref, kv_ref, kp_ref, p_ref, cot_ref, w_ref, t_ref, g_ref, r_ref, l_ref,
+        a_ref, ot_ref, lt_ref, res_ref, o_ref, mo_ref, co_ref,
+        keys, values, key_at, done, w_v, ffn, m_v, out_sem, in_sem, send_sem, recv_sem, local_sem,
     ):
         _, chip, core, _ = place()
         ring = ring_of(lax.axis_index("exp"))
@@ -206,8 +208,10 @@
         copier = Copier(send_sem, recv_sem, local_sem)
         load = copier.keep(w_ref, w_v)
         meet([to_chip(p) for p in twins] + [to_exp(p) for p in ring[1:]])
-        arrivals = [copier.send(x_ref.at[p], a_ref.at[:, lanes(chip)], *to_chip(p)) for p in twins]
-        own = copier.keep(x_ref.at[chip], a_ref.at[:, lanes(chip)])
+        extra = relay(copier, cot_ref, lambda s: co_ref.at[s], ROWS, ring, to_exp)
+        next(extra)
+        next(extra)
+        copier.keep(cot_ref, co_ref.at[me])
 
         logits = l_ref[...]
         raised = jnp.exp(logits - jnp.max(logits, axis=0, keepdims=True))
@@ -231,10 +235,75 @@
             copier.send(m_v.at[p], mo_ref.at[me], *to_exp(p))
         copier.keep(m_v.at[me], mo_ref.at[me])
 
+        low = key_lanes()
+
+        def place_keys(p, _):
+            rows = pl.ds(pl.multiple_of(p * CHUNK, CHUNK), CHUNK)
+            both = kv_ref[rows, :].astype(F32)
+            keys[rows, :] = jnp.where(low, both, 0.0).astype(BF16)
+            values[:, rows] = jnp.where(low, pltpu.roll(both, 64, 1), 0.0).T.astype(BF16)
+            key_at[rows, :] = key_columns(kp_ref[p])
+            return 0
+
+        lax.fori_loop(0, CHIPS, place_keys, 0)
+
+        def homeward(target, source):
+            return pltpu.make_async_remote_copy(
+                src_ref=done.at[target],
+                dst_ref=a_ref.at[:, lanes(source)],
+                send_sem=out_sem.at[target],
+                recv_sem=in_sem.at[source],
+                device_id={"ctx": 2 * target + core},
+                device_id_type=MESH,
+            )
+
+        def block(k, _):
+            i = CHIPS - 1 - k
+            wide = q_ref[i].astype(F32)
+            stacked = jnp.concatenate([wide, pltpu.roll(wide, 64, 1)], axis=0).astype(BF16)
+            at_row, start_row = pair_rows(p_ref[i])
+
+            def step(diagonal, p, carry):
+                top, total, acc = carry
+                rows = pl.ds(pl.multiple_of(p * CHUNK, CHUNK), CHUNK)
+                scores = dot(keys[rows, :], stacked, NT)
+                at_key = jnp.concatenate([key_at[rows, :]] * (CHUNK // 128), axis=1)
+                seen = at_key >= start_row
+                if diagonal:
+                    seen = seen & (at_key <= at_row)
+                scores = jnp.where(seen, scores, MASKED)
+                new_top = jnp.maximum(top, jnp.max(scores, axis=0, keepdims=True))
+                probs = jnp.exp(scores - new_top)
+                scale = jnp.exp(top - new_top)
+                total = total * scale + jnp.sum(probs, axis=0, keepdims=True)
+                acc = acc * scale + dot(values[:, rows], probs.astype(BF16))
+                return new_top, total, acc
+
+            none = jnp.zeros((1, 2 * ROWS), F32)
+            carry = (none + MASKED, none, jnp.zeros((128, 2 * ROWS), F32))
+            carry = lax.fori_loop(first_chunk(i, core), i, lambda p, c: step(False, p, c), carry)
+            top, total, acc = step(True, i, carry)
+            turned = acc[0:64, :] / total
+            ot_ref[i] = turned
+            lt_ref[i] = top + jnp.log(total)
+            out = jnp.concatenate([turned, turned], axis=0).T
+            done[i] = jnp.where(low, out[:ROWS], out[ROWS:]).astype(BF16)
+
+            @pl.when(i != chip)
+            def _():
+                homeward(i, chip).start()
+
+            return 0
+
+        for first, last in ((0, 1), (1, 2), (2, 3), (3, 4)):
+            lax.fori_loop(first, last, block, 0)
+            next(extra)
+        lax.fori_loop(4, CHIPS, block, 0)
+        next(extra)
+        a_ref[:, lanes(chip)] = done[chip]
         copier.kept(load)
-        copier.kept(own)
-        for at in arrivals:
-            copier.arrived(at)
+        for p in twins:
+            homeward(chip, p).wait_recv()
         branch = dot(a_ref[...], w_v[...]).astype(BF16).astype(F32)
         resid = t_ref[...].astype(F32) + branch
         res_ref[...] = resid
@@ -246,33 +315,45 @@
         next(rows_out)
         next(rows_out)
         copier.keep(ffn, o_ref.at[me])
+        side_by_side(extra)
         side_by_side(rows_out)
+        for p in twins:
+            homeward(p, chip).wait_send()
         copier.finish()
 
     vmem = pl.BlockSpec(memory_space=pltpu.VMEM)
     return pl.pallas_call(
         body,
-        name="join_heads",
+        name="attend",
         out_shape=[
             jax.ShapeDtypeStruct((ROWS, WIDTH), BF16),
+            jax.ShapeDtypeStruct((CHIPS, 64, 2 * ROWS), F32),
+            jax.ShapeDtypeStruct((CHIPS, 1, 2 * ROWS), F32),
             jax.ShapeDtypeStruct((ROWS, WIDTH), F32),
             jax.ShapeDtypeStruct((EXP, ROWS, WIDTH), BF16),
             jax.ShapeDtypeStruct((EXP, 8, ROWS), F32),
+            jax.ShapeDtypeStruct((EXP, ROWS, WIDTH), BF16),
         ],
-        in_specs=[ANY_SPEC] * 2 + [vmem] * 4,
-        out_specs=[vmem, vmem, ANY_SPEC, ANY_SPEC],
+        in_specs=[vmem] * 5 + [ANY_SPEC] + [vmem] * 4,
+        out_specs=[vmem] * 4 + [ANY_SPEC] * 3,
         scratch_shapes=[
+            pltpu.VMEM((KEYS, 128), BF16),
+            pltpu.VMEM((128, KEYS), BF16),
+            pltpu.VMEM((KEYS, 128), F32),
+            pltpu.VMEM((CHIPS, ROWS, 128), BF16),
             pltpu.VMEM((WIDTH, WIDTH), BF16),
             pltpu.VMEM((ROWS, WIDTH), BF16),
             pltpu.VMEM((EXP, 8, ROWS), F32),
-            pltpu.SemaphoreType.DMA((28,)),
-            pltpu.SemaphoreType.DMA((28,)),
+            pltpu.SemaphoreType.DMA((CHIPS,)),
+            pltpu.SemaphoreType.DMA((CHIPS,)),
+            pltpu.SemaphoreType.DMA((36,)),
+            pltpu.SemaphoreType.DMA((36,)),
             pltpu.SemaphoreType.DMA((8,)),
         ],
         compiler_params=pltpu.CompilerParams(
             collective_id=2, has_side_effects=True, vmem_limit_bytes=60 * MIB
         ),
-    )(blocks, w_out, tokens, gains, routes_t, logits_t)
+    )(q, kv, key_pos, places, cotangent, w_out, tokens, gains, routes_t, logits_t)
 
 
 def settle_experts(
@@ -614,104 +695,22 @@
     return dot(parts, scale, TN)
 
 
+def first_chunk(i, core):
+    return jnp.maximum((2 * i + core) * ROWS - (LONGEST - 1), 0) // CHUNK
+
+
 def pair_rows(places_i):
     return [jnp.concatenate([places_i[k : k + 1, :]] * 2, axis=1) for k in range(2)]
 
 
-def block_chunks(len_ref, i):
-    first_row = (2 * i + lax.rem(lax.axis_index("ctx"), 2)) * ROWS
-    first, last, end = 0, 0, 0
-    for k in range(3):
-        end = end + len_ref[0, k]
-        first = jnp.where(first_row >= end, end, first)
-        last = jnp.where(first_row + ROWS - 1 >= end, end, last)
-    return first // CHUNK, jnp.minimum((last + CHUNK - 1) // CHUNK, i)
-
-
-def attend(q, kv, key_pos, places, lengths):
-    def body(at_ref, q_ref, kv_ref, kp_ref, p_ref, o_ref, ot_ref, l_ref, keys, values, key_at):
-        low = key_lanes()
-
-        def place_keys(p, _):
-            rows = pl.ds(pl.multiple_of(p * CHUNK, CHUNK), CHUNK)
-            both = kv_ref[rows, :].astype(F32)
-            keys[rows, :] = jnp.where(low, both, 0.0).astype(BF16)
-            values[:, rows] = jnp.where(low, pltpu.roll(both, 64, 1), 0.0).T.astype(BF16)
-            key_at[rows, :] = key_columns(kp_ref[p])
-            return 0
-
-        lax.fori_loop(0, CHIPS, place_keys, 0)
-
-        def block(i, _):
-            wide = q_ref[i].astype(F32)
-            stacked = jnp.concatenate([wide, pltpu.roll(wide, 64, 1)], axis=0).astype(BF16)
-            at_row, start_row = pair_rows(p_ref[i])
-
-            def step(masked, diagonal, p, carry):
-                top, total, acc = carry
-                rows = pl.ds(pl.multiple_of(p * CHUNK, CHUNK), CHUNK)
-                scores = dot(keys[rows, :], stacked, NT)
-                if masked:
-                    at_key = jnp.concatenate([key_at[rows, :]] * (CHUNK // 128), axis=1)
-                    seen = at_key >= start_row
-                    if diagonal:
-                        seen = seen & (at_key <= at_row)
-                    scores = jnp.where(seen, scores, MASKED)
-                new_top = jnp.maximum(top, jnp.max(scores, axis=0, keepdims=True))
-                probs = jnp.exp(scores - new_top)
-                scale = jnp.exp(top - new_top)
-                total = total * scale + jnp.sum(probs, axis=0, keepdims=True)
-                acc = acc * scale + dot(values[:, rows], probs.astype(BF16))
-                return new_top, total, acc
-
-            def masked_step(p, carry):
-                return step(True, False, p, carry)
-
-            def plain_step(p, carry):
-                return step(False, False, p, carry)
-
-            none = jnp.zeros((1, 2 * ROWS), F32)
-            carry = (none + MASKED, none, jnp.zeros((128, 2 * ROWS), F32))
-            first, plain = block_chunks(at_ref, i)
-            carry = lax.fori_loop(first, plain, masked_step, carry)
-            carry = lax.fori_loop(plain, i, plain_step, carry)
-            top, total, acc = step(True, True, i, carry)
-            turned = acc[0:64, :] / total
-            ot_ref[i] = turned
-            l_ref[i] = top + jnp.log(total)
-            out = jnp.concatenate([turned, turned], axis=0).T
-            o_ref[i] = jnp.where(low, out[:ROWS], out[ROWS:]).astype(BF16)
-            return 0
-
-        lax.fori_loop(0, CHIPS, block, 0)
-
-    vmem = pl.BlockSpec(memory_space=pltpu.VMEM)
-    return pl.pallas_call(
-        body,
-        name="attend",
-        out_shape=[
-            jax.ShapeDtypeStruct((CHIPS, ROWS, 128), BF16),
-            jax.ShapeDtypeStruct((CHIPS, 64, 2 * ROWS), F32),
-            jax.ShapeDtypeStruct((CHIPS, 1, 2 * ROWS), F32),
-        ],
-        in_specs=[pl.BlockSpec(memory_space=pltpu.SMEM)] + [vmem] * 4,
-        out_specs=[vmem] * 3,
-        scratch_shapes=[
-            pltpu.VMEM((KEYS, 128), BF16),
-            pltpu.VMEM((128, KEYS), BF16),
-            pltpu.VMEM((KEYS, 128), F32),
-        ],
-        compiler_params=pltpu.CompilerParams(vmem_limit_bytes=60 * MIB),
-    )(lengths, q, kv, key_pos, places)
-
-
 def experts(rows, grads, meta, w_gate, w_up, w_down):
     half = SLOTS // 2
+    main, rest = 64, CAP - 64
 
     def body(
         x_ref, g_ref, m_ref, wg_ref, wu_ref, wd_ref,
         xin_ref, dr_ref, act_ref, dg_ref, du_ref, out_ref, dx_ref,
-        x, g, wg, wu, wd, xin, dr, act, dg, du, out, dx, made, back, weight, sems,
+        x, g, wg, wu, wd, xin, dr, act, dg, du, out, dx, made, back, made_rest, back_rest, weight, sems,
     ):
         def pair_in(p):
             at = pl.ds(2 * p, 2)
@@ -742,42 +741,54 @@
 
         for p in range(PAIRS):
             start(pair_in(p))
-        for e in range(LOCAL):
-            start(weights_in(e))
-
-        def pair_meta(p):
-            first, second = m_ref[2 * p], m_ref[2 * p + 1]
-            slots = jnp.where(second[:LOCAL] < 0.0, -1.0, second[:LOCAL] + float(CAP))
-            return jnp.concatenate([first, jnp.concatenate([slots, second[LOCAL:]], axis=0)], axis=1)
-
-        slot_id = lax.broadcasted_iota(jnp.int32, (PAIR_CAP, PAIR_ROWS), 0).astype(F32)
+        start(weights_in(0))
+
+        row_id = lax.broadcasted_iota(jnp.int32, (LOCAL * CAP, ROWS), 0).astype(F32)
+
+        def pick_source(s):
+            meta_s = m_ref[s]
+            chosen = jnp.zeros((LOCAL * CAP, ROWS), F32)
+            gates = jnp.zeros((LOCAL * CAP, ROWS), F32)
+            for k in range(LOCAL):
+                slot = meta_s[k : k + 1, :]
+                spot = jnp.where(slot < main, slot + k * main, slot + (LOCAL * main + k * rest - main))
+                hit = row_id == jnp.where(slot < 0.0, -1.0, spot)
+                chosen = jnp.where(hit, 1.0, chosen)
+                gates = jnp.where(hit, meta_s[4 + k : 5 + k, :], gates)
+            return chosen.astype(BF16), jnp.sum(gates, axis=1, keepdims=True)
 
         def pick(p, _):
             wait(pair_in(p))
-            meta_p = pair_meta(p)
-            parts, gates = [], []
+            found = []
+            for b in range(2):
+                chosen, gates = pick_source(2 * p + b)
+                found.append((dot(chosen, x[2 * p + b]), dot(chosen, g[2 * p + b]) * gates, gates))
+            at_rest = pl.ds(pl.multiple_of(p * PAIR_CAP + 2 * main, 16), 2 * rest)
             for k in range(LOCAL):
-                hit = slot_id == meta_p[k : k + 1, :]
-                parts.append(jnp.where(hit, 1.0, 0.0).astype(BF16))
-                gates.append(jnp.sum(jnp.where(hit, meta_p[4 + k : 5 + k, :], 0.0), axis=1, keepdims=True))
-            chosen = jnp.concatenate(parts, axis=0)
-            at_pair = pl.ds(2 * p, 2)
-            rows_p = dot(chosen, x[at_pair].reshape(PAIR_ROWS, WIDTH)).astype(BF16)
-            grads_p = dot(chosen, g[at_pair].reshape(PAIR_ROWS, WIDTH))
-            at = pl.ds(pl.multiple_of(p * PAIR_CAP, PAIR_CAP), PAIR_CAP)
-            for k in range(LOCAL):
-                piece = slice(k * PAIR_CAP, (k + 1) * PAIR_CAP)
-                xin[k, at, :] = rows_p[piece]
-                dr[k, at, :] = (grads_p[piece] * gates[k]).astype(BF16)
-                weight[k, at, :] = gates[k]
+                last = slice(LOCAL * main + k * rest, LOCAL * main + (k + 1) * rest)
+                for b in range(2):
+                    at = pl.ds(pl.multiple_of(p * PAIR_CAP + b * main, 16), main)
+                    piece = slice(k * main, (k + 1) * main)
+                    xin[k, at, :] = found[b][0][piece].astype(BF16)
+                    dr[k, at, :] = found[b][1][piece].astype(BF16)
+                    weight[k, at, :] = found[b][2][piece]
+                both = [jnp.concatenate([found[0][n][last], found[1][n][last]], axis=0) for n in range(3)]
+                xin[k, at_rest, :] = both[0].astype(BF16)
+                dr[k, at_rest, :] = both[1].astype(BF16)
+                weight[k, at_rest, :] = both[2]
             return 0
 
         lax.fori_loop(0, PAIRS, pick, 0)
-        for e in range(LOCAL):
-            start(rows_out(e))
+        start(weights_in(1))
 
         def expert(e, _):
             wait(weights_in(e))
+
+            @pl.when(e < LOCAL - 2)
+            def _():
+                start(weights_in(e + 2))
+
+            start(rows_out(e))
 
             def work(h, _):
                 at = pl.ds(pl.multiple_of(h * half, half), half)
@@ -795,11 +806,14 @@
                 du[e, at, :] = d_up
                 y = (dot(act_h, wd[e]) * weight[e, at, :]).astype(BF16)
                 dch = (dot(d_gate, wg[e], NT) + dot(d_up, wu[e], NT)).astype(BF16)
-                place_at = pl.ds(pl.multiple_of(e * PAIR_CAP, PAIR_CAP), PAIR_CAP)
+                at_main = pl.ds(pl.multiple_of(e * main, main), main)
+                at_rest = pl.ds(pl.multiple_of(e * 2 * rest, 2 * rest), 2 * rest)
                 for k in range(2):
-                    piece = slice(k * PAIR_CAP, (k + 1) * PAIR_CAP)
-                    made[2 * h + k, place_at, :] = y[piece]
-                    back[2 * h + k, place_at, :] = dch[piece]
+                    for rows_k, whole, last in ((y, made, made_rest), (dch, back, back_rest)):
+                        piece = rows_k[k * PAIR_CAP : (k + 1) * PAIR_CAP]
+                        for b in range(2):
+                            whole[4 * h + 2 * k + b, at_main, :] = piece[b * main : (b + 1) * main]
+                        last[2 * h + k, at_rest, :] = piece[2 * main :]
                 return 0
 
             lax.fori_loop(0, 2, work, 0)
@@ -807,19 +821,27 @@
             return 0
 
         lax.fori_loop(0, LOCAL, expert, 0)
-        lane_id = lax.broadcasted_iota(jnp.int32, (PAIR_ROWS, PAIR_SLOTS), 1).astype(F32)
+        lane_main = lax.broadcasted_iota(jnp.int32, (PAIR_ROWS, LOCAL * main), 1).astype(F32)
+        lane_rest = lax.broadcasted_iota(jnp.int32, (PAIR_ROWS, LOCAL * 2 * rest), 1).astype(F32)
+        second = lax.broadcasted_iota(jnp.int32, (PAIR_ROWS, 1), 0) >= ROWS
 
         def give(p, _):
-            turned = jnp.concatenate([pair_meta(p), jnp.zeros((120, PAIR_ROWS), F32)], axis=0).T
-            chosen = jnp.zeros((PAIR_ROWS, PAIR_SLOTS), F32)
+            both = jnp.concatenate([m_ref[2 * p], m_ref[2 * p + 1]], axis=1)
+            turned = jnp.concatenate([both, jnp.zeros((120, PAIR_ROWS), F32)], axis=0).T
+            in_main = jnp.zeros((PAIR_ROWS, LOCAL * main), F32)
+            in_rest = jnp.zeros((PAIR_ROWS, LOCAL * 2 * rest), F32)
             for k in range(LOCAL):
-                spot = turned[:, k : k + 1]
-                lane = jnp.where(spot < 0.0, -1.0, spot + float(k * PAIR_CAP))
-                chosen = chosen + jnp.where(lane_id == lane, 1.0, 0.0)
-            chosen = chosen.astype(BF16)
-            at_pair = pl.ds(2 * p, 2)
-            dx[at_pair] = dot(chosen, back[p]).astype(BF16).reshape(2, ROWS, WIDTH)
-            out[at_pair] = dot(chosen, made[p]).astype(BF16).reshape(2, ROWS, WIDTH)
+                slot = turned[:, k : k + 1]
+                here = jnp.where((slot >= 0.0) & (slot < main), slot + k * main, -1.0)
+                in_main = jnp.where(lane_main == here, 1.0, in_main)
+                there = slot + (k * 2 * rest - main) + jnp.where(second, float(rest), 0.0)
+                in_rest = jnp.where(lane_rest == jnp.where(slot < main, -1.0, there), 1.0, in_rest)
+            in_main, in_rest = in_main.astype(BF16), in_rest.astype(BF16)
+            for whole, last, to in ((back, back_rest, dx), (made, made_rest, out)):
+                more = dot(in_rest, last[p])
+                for b in range(2):
+                    at = slice(b * ROWS, (b + 1) * ROWS)
+                    to[2 * p + b] = (dot(in_main[at], whole[2 * p + b]) + more[at]).astype(BF16)
             start(pair_out(p))
             return 0
 
@@ -854,8 +876,10 @@
             buf(*narrow),
             buf(*source),
             buf(*source),
-            buf(PAIRS, PAIR_SLOTS, WIDTH),
-            buf(PAIRS, PAIR_SLOTS, WIDTH),
+            buf(EXP, LOCAL * main, WIDTH),
+            buf(EXP, LOCAL * main, WIDTH),
+            buf(PAIRS, LOCAL * 2 * rest, WIDTH),
+            buf(PAIRS, LOCAL * 2 * rest, WIDTH),
             pltpu.VMEM((LOCAL, SLOTS, 1), F32),
             pltpu.SemaphoreType.DMA((5, 4)),
         ],
@@ -889,6 +913,12 @@
         eu[...] = eu_ref[...]
         ed[...] = ed_ref[...]
 
+    def rows(count, width):
+        return pl.BlockSpec((count // LOCAL, width), lambda i: (i, 0))
+
+    def expert(*shape):
+        return pl.BlockSpec((1,) + shape, lambda i: (i, 0, 0))
+
     return compute_call(
         body,
         "deliver",
@@ -906,6 +936,18 @@
         ]
         + [jax.ShapeDtypeStruct(a.shape, F32) for a in expert_sums],
         [resid, layer_keep, layer_got, dense, out_grad, gain_sums, input_grad, *expert_sums],
+        grid=(LOCAL,),
+        in_specs=[rows(ROWS, WIDTH)] * 3
+        + [
+            pl.BlockSpec((2, 128 // LOCAL, WIDTH), lambda i: (0, i, 0)),
+            rows(128, WIDTH),
+            pl.BlockSpec((8, 128), lambda i: (0, 0)),
+            rows(ROWS, WIDTH),
+        ]
+        + [expert(64, FF), expert(64, FF), expert(32, WIDTH)],
+        out_specs=[rows(ROWS, WIDTH), rows(128, WIDTH), rows(128, 512), rows(128, 512), rows(128, WIDTH)]
+        + [pl.BlockSpec((1, n), lambda i: (0, 0)) for n in (128, 128, 64, 128)]
+        + [rows(ROWS, WIDTH), expert(64, FF), expert(64, FF), expert(32, WIDTH)],
     )
 
 
@@ -918,12 +960,12 @@
     return total
 
 
-def front(tokens, cotangent, dense, norms, perm, lengths):
+def front(tokens, dense, norms, perm, lengths):
     half = 64
 
     def body(
-        t_ref, cot_ref, wq_ref, wk_ref, wv_ref, wd_ref, na_ref, nq_ref, nk_ref, nf_ref, perm_ref, len_ref,
-        wo_ref, go_ref, n_ref, ql_ref, kl_ref, s_ref, c_ref, sn_ref, p_ref, kp_ref, q_ref, kv_ref, co_ref,
+        t_ref, wq_ref, wk_ref, wv_ref, wd_ref, na_ref, nq_ref, nk_ref, nf_ref, perm_ref, len_ref,
+        wo_ref, go_ref, n_ref, ql_ref, kl_ref, s_ref, c_ref, sn_ref, p_ref, kp_ref, q_ref, kv_ref,
         g_ref, w_mine, rows, normed, gains_v, w_own, totals, totals_all, kv_half, send_sem, recv_sem, local_sem,
     ):
         _, chip, core, sibling = place()
@@ -972,7 +1014,6 @@
             projected.append(s)
 
         main = relay(copier, t_ref, lambda s: rows.at[s], ROWS, chips, to_chip, landed)
-        extra = relay(copier, cot_ref, lambda s: co_ref.at[s], ROWS, exps, to_exp)
         dense = relay(
             copier,
             wd_ref.at[part],
@@ -987,7 +1028,6 @@
         next(dense)
         next(dense)
         copier.keep(wd_ref, wo_ref.at[me])
-        copier.keep(cot_ref, co_ref.at[me])
         w_own[me] = w_mine[...]
         gains_v[me] = g_ref[...]
 
@@ -1029,8 +1069,6 @@
         next(dense)
         next(main)
         own_sends = [copier.send(w_mine, w_own.at[me], *to_exp(p)) for p in exps[1:]]
-        next(extra)
-        next(extra)
         next(dense)
         next(main)
         next(main)
@@ -1040,8 +1078,6 @@
         for s in projected:
             project(s)
         projected.clear()
-        next(extra)
-        next(extra)
         next(main)
         next(dense)
         for s in projected:
@@ -1054,8 +1090,6 @@
         totals_all[chip] = totals[...]
         side_by_side(dense)
         copier.keep(normed, n_ref)
-        for _ in range(3):
-            next(extra)
         for at in shares:
             copier.arrived(at)
 
@@ -1077,7 +1111,6 @@
         lax.fori_loop(0, CHIPS, turn_one, 0)
         copier.send(kv_half, kv_ref.at[:, core], "ctx", sibling)
         copier.keep(kv_half, kv_ref.at[:, core])
-        side_by_side(extra)
         copier.finish()
 
     vmem = pl.BlockSpec(memory_space=pltpu.VMEM)
@@ -1098,10 +1131,9 @@
             jax.ShapeDtypeStruct((CHIPS, 1, CHUNK), F32),
             jax.ShapeDtypeStruct((CHIPS, ROWS, 128), BF16),
             jax.ShapeDtypeStruct((CHIPS, 2, ROWS, 128), BF16),
-            jax.ShapeDtypeStruct((EXP, ROWS, WIDTH), BF16),
         ],
-        in_specs=[vmem] * 12,
-        out_specs=[ANY_SPEC, vmem, ANY_SPEC] + [vmem] * 8 + [ANY_SPEC] * 2,
+        in_specs=[vmem] * 11,
+        out_specs=[ANY_SPEC, vmem, ANY_SPEC] + [vmem] * 8 + [ANY_SPEC],
         scratch_shapes=[
             pltpu.VMEM((8, 128), F32),
             pltpu.VMEM((128, 256), BF16),
@@ -1112,14 +1144,14 @@
             pltpu.VMEM((CHIPS, 2, ROWS), F32),
             pltpu.VMEM((CHIPS, CHIPS, 2, ROWS), F32),
             pltpu.VMEM((CHIPS, ROWS, 128), BF16),
-            pltpu.SemaphoreType.DMA((71,)),
-            pltpu.SemaphoreType.DMA((71,)),
+            pltpu.SemaphoreType.DMA((57,)),
+            pltpu.SemaphoreType.DMA((57,)),
             pltpu.SemaphoreType.DMA((8,)),
         ],
         compiler_params=pltpu.CompilerParams(
             collective_id=1, has_side_effects=True, vmem_limit_bytes=60 * MIB
         ),
-    )(tokens, cotangent, *dense, *norms, perm, lengths)
+    )(tokens, *dense, *norms, perm, lengths)
 
 
 def apart(pieces):
@@ -1139,9 +1171,9 @@
         q_ref, kv_ref, do_ref, ot_ref, l_ref, kp_ref, p_ref, ql_ref, kl_ref, c_ref, sn_ref, s_ref, g_ref, n_ref, at_ref, br_ref, lp_ref,
         wq_ref, wk_ref, wv_ref, t_ref, r_ref, fg_ref, gp_ref, up_ref, da_ref, db_ref,
         eg_ref, eu_ref, ed_ref, di_ref, dense_ref, og_ref, lo_ref, gs_ref,
-        keys_v, values, acc, key_at, keys_t, dq_v, other_v, w_mine, ql_v, kl_v, c_v, sn_v, n_v, w_v, t_v, r_v,
+        keys_v, values, acc, key_at, keys_t, other_v, w_mine, ql_v, kl_v, c_v, sn_v, n_v, w_v, t_v, r_v,
         got, e_q, e_kv, totals, totals_all, d_lin, home, w_give, w_keep, w_got, joint, traded, done,
-        o_both, o_keep, o_got, o_traded, o_pair, o_half, o_full, a_got, a_done, packet, packets, mine, shared, gate_c, down_c, up_d, down_d, send_sem, recv_sem, local_sem,
+        o_both, o_keep, o_got, o_traded, o_pair, o_half, o_full, a_got, a_done, packet, packets, mine, shared, gate_c, down_c, up_d, down_d, out_sem, in_sem, send_sem, recv_sem, local_sem,
     ):
         ctx, chip, core, sibling = place()
         me = lax.axis_index("exp")
@@ -1211,7 +1243,18 @@
 
         lax.fori_loop(0, CHIPS, place_keys, 0)
 
-        def attend_block(i, _):
+        def swap(i):
+            return pltpu.make_async_remote_copy(
+                src_ref=other_v.at[i],
+                dst_ref=got.at[i],
+                send_sem=out_sem.at[i],
+                recv_sem=in_sem.at[i],
+                device_id={"ctx": sibling},
+                device_id_type=MESH,
+            )
+
+        def attend_block(k, _):
+            i = CHIPS - 1 - k
             q_wide, do_wide = q_ref[i].astype(F32), do_ref[i].astype(F32)
             q_turned, do_turned = pltpu.roll(q_wide, 64, 1), pltpu.roll(do_wide, 64, 1)
             q_rows = jnp.concatenate([q_wide, q_turned], axis=0)
@@ -1237,12 +1280,20 @@
                 acc[rows, :] += dot(jnp.concatenate([d_scores, probs.astype(BF16)], axis=1), right)
                 return dq + dot(keys_t[:, rows], d_scores)
 
-            dq = lax.fori_loop(0, i, lambda p, dq: step(False, p, dq), jnp.zeros((128, 2 * ROWS), F32))
+            dq = jnp.zeros((128, 2 * ROWS), F32)
+            dq = lax.fori_loop(first_chunk(i, core), i, lambda p, dq: step(False, p, dq), dq)
             dq = step(True, i, dq).T * 0.125
-            dq_v[i] = jnp.where(low, dq[:ROWS], pltpu.roll(dq[ROWS:], 64, 1))
+            dq = jnp.where(low, dq[:ROWS], pltpu.roll(dq[ROWS:], 64, 1))
+            e_q[i] = turn(dq, c_v[i], -sn_v[i])
+            other = pl.ds(pl.multiple_of((2 * i + 1 - core) * ROWS, ROWS), ROWS)
+            other_v[i] = acc[other, :].astype(BF16)
+            swap(i).start()
             return 0
 
-        lax.fori_loop(0, 4, attend_block, 0)
+        for at in heads:
+            copier.kept(at)
+
+        lax.fori_loop(0, 1, attend_block, 0)
         next(weights)
         next(weights)
         copier.arrived(o_swap)
@@ -1258,10 +1309,10 @@
             p = lax.rem(x + d, 4)
             for z in range(2):
                 o_trades.append(copier.send(o_keep.at[z * 4 + p], o_traded.at[x, z], "exp", zl * 4 + p))
-        lax.fori_loop(4, 6, attend_block, 0)
+        lax.fori_loop(1, 2, attend_block, 0)
         next(weights)
         next(weights)
-        lax.fori_loop(6, 7, attend_block, 0)
+        lax.fori_loop(2, 3, attend_block, 0)
         next(weights)
         for at in o_trades:
             copier.arrived(at)
@@ -1273,35 +1324,21 @@
         o_half[...] = give.astype(BF16)
         o_full[...] = keep.astype(BF16)
         o_pairs = copier.send(o_half, o_pair, "exp", (1 - zl) * 4 + x)
-        lax.fori_loop(7, CHIPS, attend_block, 0)
+        lax.fori_loop(3, CHIPS, attend_block, 0)
 
         side_by_side(weights)
 
-        def give_other(s, _):
-            other = pl.ds(pl.multiple_of((2 * s + 1 - core) * ROWS, ROWS), ROWS)
-            other_v[s] = acc[other, :].astype(BF16)
-            return 0
-
-        lax.fori_loop(0, CHIPS, give_other, 0)
-        swapped = copier.send(other_v, got, "ctx", sibling)
         copier.arrived(o_pairs)
         o_full[...] = (o_full[...].astype(F32) + o_pair[...].astype(F32)).astype(BF16)
         spread = [copier.send(o_full.at[:, lanes(p)], a_got.at[chip], *to_chip(p)) for p in twins]
         a_got[chip] = o_full[:, lanes(chip)]
         keys = key_lanes()
         gain = g_ref[chip]
-        for at in heads:
-            copier.kept(at)
-
-        def unturn_q(i, _):
-            e_q[i] = turn(dq_v[i], c_v[i], -sn_v[i])
-            return 0
-
-        lax.fori_loop(0, CHIPS, unturn_q, 0)
-        copier.arrived(swapped)
-
-        def unturn_kv(i, carry):
+
+        def unturn_kv(k, carry):
             q_sum, kv_sum = carry
+            i = CHIPS - 1 - k
+            swap(i).wait_recv()
             cos, sin = jnp.where(keys, c_v[i], 1.0), jnp.where(keys, -sn_v[i], 0.0)
             mine_rows = pl.ds(pl.multiple_of((2 * i + core) * ROWS, ROWS), ROWS)
             e = turn(acc[mine_rows, :] + got[i].astype(F32), cos, sin)
@@ -1459,6 +1496,8 @@
         for c in range(1, CTX):
             total = total + shared[c]
         gs_ref[...] = total
+        for i in range(CHIPS):
+            swap(i).wait_send()
         copier.finish()
 
     vmem = pl.BlockSpec(memory_space=pltpu.VMEM)
@@ -1485,7 +1524,6 @@
             pltpu.VMEM((KEYS, 128), F32),
             pltpu.VMEM((KEYS, 128), F32),
             pltpu.VMEM((128, KEYS), BF16),
-            pltpu.VMEM(block, F32),
             pltpu.VMEM(block, BF16),
             pltpu.VMEM((128, 2 * WIDTH), BF16),
             pltpu.VMEM(block, F32),
@@ -1526,8 +1564,10 @@
             pltpu.VMEM((4, 2, 32, WIDTH), BF16),
             pltpu.VMEM((LOCAL, 64, FF), BF16),
             pltpu.VMEM((2, 32, WIDTH), BF16),
-            pltpu.SemaphoreType.DMA((127,)),
-            pltpu.SemaphoreType.DMA((127,)),
+            pltpu.SemaphoreType.DMA((CHIPS,)),
+            pltpu.SemaphoreType.DMA((CHIPS,)),
+            pltpu.SemaphoreType.DMA((126,)),
+            pltpu.SemaphoreType.DMA((126,)),
             pltpu.SemaphoreType.DMA((15,)),
         ],
         compiler_params=pltpu.CompilerParams(
@@ -1566,10 +1606,9 @@
 
     row = lambda v: v.reshape(1, -1)
     (
-        w_o, gain_all, normed, q_lin, kv_lin, squares, cosine, sine, places, key_pos, q_all, kv_all, grads_all,
+        w_o, gain_all, normed, q_lin, kv_lin, squares, cosine, sine, places, key_pos, q_all, kv_all,
     ) = front(
         tokens,
-        cotangent,
         (w_query, w_key, w_value, w_out),
         (row(norm_attn), row(norm_query), row(norm_key), row(norm_ffn)),
         deal_perm[0],
@@ -1578,11 +1617,9 @@
 
     w_o = w_o.reshape(WIDTH, WIDTH)
     kv_all = kv_all.reshape(KEYS, 128)
-    out_low, out_wide, log_total = attend(q_all, kv_all, key_pos, places, lengths)
-    attended, resid, rows_all, meta_all = join_heads(
-        out_low, w_o, tokens, gain_all, routes[0].T, gate_logits[0].T
+    attended, out_turned, log_total, resid, rows_all, meta_all, grads_all = attend(
+        q_all, kv_all, key_pos, places, cotangent, w_o, tokens, gain_all, routes[0].T, gate_logits[0].T
     )
-
     rows_in, d_rows, act, d_gate, d_up, out_parts, d_parts = experts(
         rows_all, grads_all, meta_all, w_gate, w_up, w_down
     )
@@ -1605,7 +1642,7 @@
         q_all,
         kv_all,
         d_out,
-        out_wide,
+        out_turned,
         log_total,
         key_pos,
         places,

time: 323 us -> 310 us (0.960)
  Pallas kernels: 322 us -> 308 us
    pallas_call x1, Pallas kernels: 92.6 us -> 85.4 us  [tail(): pl.pallas_call(body, name='tail', out_shape=[jax.ShapeDtypeStruct((LOCAL,...]
    pallas_call x1, Pallas kernels: 62.4 us -> 55.3 us  [front(): pl.pallas_call(body, name='front', out_shape=[jax.ShapeDtypeStruct((EXP,...]
    pallas_call x1, Pallas kernels: 66.6 us -> 70.2 us  [settle_experts(): pl.pallas_call(body, name='settle_experts', out_shape=[jax.ShapeDtypeStru...]
    pallas_call x2, Pallas kernels: 39 us -> 35.7 us  [compute_call(): pl.pallas_call(body, name=name, out_shape=outs, compiler_params=pltpu.Com...]
    pallas_call x2 -> x1, Pallas kernels: 61.6 us -> 61.7 us  [attend(): pl.pallas_call(body, name='attend', out_shape=[jax.ShapeDtypeStruct((ROWS...]
where the time goes in v6:
time: 310 us; the launch traced here: 309 us
  Pallas kernels  308 us (99%)
    pallas_call x1, Pallas kernels, tail(): pl.pallas_call(body, name='tail', out_shape=[jax.ShapeDtypeStruct((LOCAL,...  85.4 us
    pallas_call x1, Pallas kernels, settle_experts(): pl.pallas_call(body, name='settle_experts', out_shape=[jax.ShapeDtypeStru...  70.2 us
    pallas_call x1, Pallas kernels, attend(): pl.pallas_call(body, name='attend', out_shape=[jax.ShapeDtypeStruct((ROWS...  61.7 us
    pallas_call x1, Pallas kernels, front(): pl.pallas_call(body, name='front', out_shape=[jax.ShapeDtypeStruct((EXP,...  55.3 us
    pallas_call x2, Pallas kernels, compute_call(): pl.pallas_call(body, name=name, out_shape=outs, compiler_params=pltpu.Com...  35.7 us

profile of v6, /device:TPU:1, one launch (start us, length us, event | category | flops | bytes accessed | tf_op | source)
XLA Modules:
  0.0 309.2 jit_solution(1490653608490809319)
XLA Ops:
  0.6 55.3 %front.1 = (bf16[8,128,1024]{2,1,0:T(8,128)(2,1)}, f32[8,8,128]{2,1,0:T(8,128)}, bf16[8,192,1024]{2,1,0:T(8,128)(2,1)}, f32[8,192,128]{2,1,0:T(8,128)}, f32[8,19...) custom-call(bf16[192,1024]{1,0:T(8,128)(2,1)} %bitcast.25, ...), custom_call_target="tpu_custom_call" | custom-call | tf_op jit(solution)/shard_map/front/pallas_call | solution.py:1118
  55.9 61.7 %attend.1 = (bf16[192,1024]{1,0:T(8,128)(2,1)}, f32[8,64,384]{2,1,0:T(8,128)}, f32[8,1,384]{2,1,0:T(1,128)}, f32[192,1024]{1,0:T(8,128)}, bf16[8,192,1024]{2,1,0...) custom-call(bf16[8,192,128]{2,1,0:T(8,128)(2,1)} %get-tuple-element.70.q_ref, ...), custom_call_target="tpu_custom_call" | custom-call | tf_op jit(solution)/shard_map/attend/pallas_call | solution.py:325
  117.7 30.8 %experts.1 = (bf16[4,576,1024]{2,1,0:T(8,128)(2,1)}, bf16[4,576,1024]{2,1,0:T(8,128)(2,1)}, bf16[4,576,512]{2,1,0:T(8,128)(2,1)}, bf16[4,576,512]{2,1,0:T(8,128)...) custom-call(bf16[8,192,1024]{2,1,0:T(8,128)(2,1)} %get-tuple-element.77.x_ref, ...), custom_call_target="tpu_custom_call" | custom-call | tf_op jit(solution)/shard_map/experts/pallas_call | solution.py:641
  148.4 70.2 %settle_experts.1 = (bf16[4,4,64,512]{3,2,1,0:T(8,128)(2,1)}, bf16[2,4,64,512]{3,2,1,0:T(8,128)(2,1)}, bf16[4,2,32,1024]{3,2,1,0:T(8,128)(2,1)}, bf16[2,2,32,102...) custom-call(bf16[4,576,1024]{2,1,0:T(8,128)(2,1)} %get-tuple-element, ...), custom_call_target="tpu_custom_call" | custom-call | tf_op jit(solution)/shard_map/settle_experts/pallas_call | solution.py:582
  218.7 85.4 %tail.1 = (f32[4,64,512]{2,1,0:T(8,128)}, f32[4,64,512]{2,1,0:T(8,128)}, f32[4,32,1024]{2,1,0:T(8,128)}, f32[192,1024]{1,0:T(8,128)}, bf16[2,128,1024]{2,1,0:T(8...) custom-call(bf16[8,192,128]{2,1,0:T(8,128)(2,1)} %get-tuple-element.70.q_ref, ...), custom_call_target="tpu_custom_call" | custom-call | tf_op jit(solution)/shard_map/tail/pallas_call | solution.py:1506
  304.1 4.9 %deliver.1 = (bf16[192,1024]{1,0:T(8,128)(2,1)}, f32[128,1024]{1,0:T(8,128)}, f32[128,512]{1,0:T(8,128)}, f32[128,512]{1,0:T(8,128)}, f32[128,1024]{1,0:T(8,128)...) custom-call(f32[192,1024]{1,0:T(8,128)} %get-tuple-element.76.res_re, ...), custom_call_target="tpu_custom_call" | custom-call | tf_op jit(solution)/shard_map/deliver/pallas_call | solution.py:641

commit v7 on v6

--- a/solution.py
+++ b/solution.py
@@ -22,6 +22,8 @@
 CAP = 72
 PAIRS = EXP // 2
 LONGEST = 2048
+DOWN_A = 1
+DOWN_B = LOCAL - DOWN_A
 PAIR_ROWS = 2 * ROWS
 PAIR_CAP = 2 * CAP
 SLOTS = EXP * CAP
@@ -470,13 +472,13 @@
 
             lax.fori_loop(0, CHIPS, add, 0)
             first_a.append(copier.send(gate.at[core, 1 - zh, :, e], gate_a.at[:, e], *over))
-            if e < 2:
+            if e < DOWN_A:
                 first_a.append(copier.send(down.at[core, 1 - zh, :, e], down_a.at[:, e], *over))
             for c in columns:
                 to = at_ctx(zh, c)
                 first_b.append(copier.send(up.at[core, :, c, e], up_b.at[y, :, e], *to))
-                if e >= 2:
-                    first_b.append(copier.send(down.at[core, :, c, e], down_b.at[y, :, e - 2], *to))
+                if e >= DOWN_A:
+                    first_b.append(copier.send(down.at[core, :, c, e], down_b.at[y, :, e - DOWN_A], *to))
 
         swaps = work(0)
         later = work(1)
@@ -543,7 +545,7 @@
             for e in range(LOCAL):
                 both = gate[core, zh, c, e].astype(F32) + gate_a[c, e].astype(F32)
                 gate_out[c, e] = both.astype(BF16)
-            for e in range(2):
+            for e in range(DOWN_A):
                 both = down[core, zh, c, e].astype(F32) + down_a[c, e].astype(F32)
                 down_a_out[c, e] = both.astype(BF16)
             return 0
@@ -566,13 +568,13 @@
 
         def sum_b_down(e, _):
             for z in range(2):
-                total = down[core, z, y, e + 2].astype(F32)
+                total = down[core, z, y, e + DOWN_A].astype(F32)
                 for c in others:
                     total = total + down_b[c, z, e].astype(F32)
                 down_b_out[z, e] = total.astype(BF16)
             return 0
 
-        lax.fori_loop(0, 2, sum_b_down, 0)
+        lax.fori_loop(0, DOWN_B, sum_b_down, 0)
         sum_up(layer_stage, l_own, l_from, keep_out, give_out)
         copier.finish()
 
@@ -585,8 +587,8 @@
         out_shape=[
             jax.ShapeDtypeStruct((4, LOCAL) + wide, BF16),
             jax.ShapeDtypeStruct((2, LOCAL) + wide, BF16),
-            jax.ShapeDtypeStruct((4, 2) + tall, BF16),
-            jax.ShapeDtypeStruct((2, 2) + tall, BF16),
+            jax.ShapeDtypeStruct((4, DOWN_A) + tall, BF16),
+            jax.ShapeDtypeStruct((2, DOWN_B) + tall, BF16),
             jax.ShapeDtypeStruct((ROWS, WIDTH), F32),
             jax.ShapeDtypeStruct((ROWS, WIDTH), BF16),
             jax.ShapeDtypeStruct((1, WIDTH), F32),
@@ -611,9 +613,9 @@
             buf(2, 4, LOCAL, *wide),
             buf(2, 4, LOCAL, *tall),
             buf(4, LOCAL, *wide),
-            buf(4, 2, *tall),
+            buf(4, DOWN_A, *tall),
             buf(4, 2, LOCAL, *wide),
-            buf(4, 2, 2, *tall),
+            buf(4, 2, DOWN_B, *tall),
             buf(ROWS, WIDTH),
             buf(ROWS, WIDTH),
         ]
@@ -627,8 +629,8 @@
         ]
         * 2
         + [
-            pltpu.SemaphoreType.DMA((56,)),
-            pltpu.SemaphoreType.DMA((56,)),
+            pltpu.SemaphoreType.DMA((58,)),
+            pltpu.SemaphoreType.DMA((58,)),
             pltpu.SemaphoreType.DMA((32,)),
         ],
         compiler_params=pltpu.CompilerParams(
@@ -1314,6 +1316,10 @@
         next(weights)
         lax.fori_loop(2, 3, attend_block, 0)
         next(weights)
+        lax.fori_loop(3, CHIPS, attend_block, 0)
+
+        side_by_side(weights)
+
         for at in o_trades:
             copier.arrived(at)
         keep, give = o_keep[zl * 4 + x].astype(F32), o_keep[(1 - zl) * 4 + x].astype(F32)
@@ -1324,14 +1330,6 @@
         o_half[...] = give.astype(BF16)
         o_full[...] = keep.astype(BF16)
         o_pairs = copier.send(o_half, o_pair, "exp", (1 - zl) * 4 + x)
-        lax.fori_loop(3, CHIPS, attend_block, 0)
-
-        side_by_side(weights)
-
-        copier.arrived(o_pairs)
-        o_full[...] = (o_full[...].astype(F32) + o_pair[...].astype(F32)).astype(BF16)
-        spread = [copier.send(o_full.at[:, lanes(p)], a_got.at[chip], *to_chip(p)) for p in twins]
-        a_got[chip] = o_full[:, lanes(chip)]
         keys = key_lanes()
         gain = g_ref[chip]
 
@@ -1355,16 +1353,10 @@
         q_sum, kv_sum = lax.fori_loop(0, CHIPS, unturn_kv, (none, none))
         shares = [copier.send(totals, totals_all.at[chip], *to_chip(p)) for p in twins]
         totals_all[chip] = totals[...]
-        for at in spread:
-            copier.arrived(at)
-        total = a_got[0].astype(F32)
-        for c in range(1, CHIPS):
-            total = total + a_got[c].astype(F32)
-        a_done[...] = total.astype(BF16)
-        half = pl.ds(pl.multiple_of(core * 64, 64), 64)
-        a_shares = [copier.send(a_done, og_ref.at[half, lanes(chip)], *to_chip(p)) for p in twins]
-        copier.send(a_done, og_ref.at[half, lanes(chip)], "ctx", sibling)
-        copier.keep(a_done, og_ref.at[half, lanes(chip)])
+        copier.arrived(o_pairs)
+        o_full[...] = (o_full[...].astype(F32) + o_pair[...].astype(F32)).astype(BF16)
+        spread = [copier.send(o_full.at[:, lanes(p)], a_got.at[chip], *to_chip(p)) for p in twins]
+        a_got[chip] = o_full[:, lanes(chip)]
         for at in shares:
             copier.arrived(at)
 
@@ -1406,6 +1398,16 @@
         columns_grad(1 - core, w_give)
         w_swap = copier.send(w_give, w_got, "ctx", sibling)
         columns_grad(core, w_keep)
+        for at in spread:
+            copier.arrived(at)
+        total = a_got[0].astype(F32)
+        for c in range(1, CHIPS):
+            total = total + a_got[c].astype(F32)
+        a_done[...] = total.astype(BF16)
+        half = pl.ds(pl.multiple_of(core * 64, 64), 64)
+        a_shares = [copier.send(a_done, og_ref.at[half, lanes(chip)], *to_chip(p)) for p in twins]
+        copier.send(a_done, og_ref.at[half, lanes(chip)], "ctx", sibling)
+        copier.keep(a_done, og_ref.at[half, lanes(chip)])
         copier.arrived(w_swap)
         both = w_keep[...].astype(F32) + w_got[...].astype(F32)
         joint[...] = both.astype(BF16).reshape(EXP, 128, 128)
@@ -1476,12 +1478,13 @@
             return 0
 
         lax.fori_loop(0, LOCAL, add_experts, 0)
-        for e in range(2):
+        for e in range(DOWN_A):
             total = da_ref[y, e].astype(F32)
             for c in columns:
                 total = total + down_c[c, e].astype(F32)
             ed_ref[e] = total
-            ed_ref[e + 2] = db_ref[zh, e].astype(F32) + down_d[e].astype(F32)
+        for e in range(DOWN_B):
+            ed_ref[e + DOWN_A] = db_ref[zh, e].astype(F32) + down_d[e].astype(F32)
         for d, at in zip((2, 6, 4, 1, 3, 5, 7), w_shares):
             copier.arrived(at)
             got_at = dense_ref.at[core, :, lanes(lax.rem(chip + CHIPS - d, CHIPS))]
@@ -1561,9 +1564,9 @@
             pltpu.VMEM((8, 128), F32),
             pltpu.VMEM((CTX, 8, 128), F32),
             pltpu.VMEM((4, LOCAL, 64, FF), BF16),
-            pltpu.VMEM((4, 2, 32, WIDTH), BF16),
+            pltpu.VMEM((4, DOWN_A, 32, WIDTH), BF16),
             pltpu.VMEM((LOCAL, 64, FF), BF16),
-            pltpu.VMEM((2, 32, WIDTH), BF16),
+            pltpu.VMEM((DOWN_B, 32, WIDTH), BF16),
             pltpu.SemaphoreType.DMA((CHIPS,)),
             pltpu.SemaphoreType.DMA((CHIPS,)),
             pltpu.SemaphoreType.DMA((126,)),

time: 310 us -> 302 us (0.974)
  Pallas kernels: 308 us -> 301 us
    pallas_call x1, Pallas kernels: 70.2 us -> 65 us  [settle_experts(): pl.pallas_call(body, name='settle_experts', out_shape=[jax.ShapeDtypeStru...]
where the time goes in v7:
time: 302 us
  Pallas kernels  301 us (100%)
    pallas_call x1, Pallas kernels, tail(): pl.pallas_call(body, name='tail', out_shape=[jax.ShapeDtypeStruct((LOCAL,...  83 us
    pallas_call x1, Pallas kernels, settle_experts(): pl.pallas_call(body, name='settle_experts', out_shape=[jax.ShapeDtypeStru...  65 us
    pallas_call x1, Pallas kernels, attend(): pl.pallas_call(body, name='attend', out_shape=[jax.ShapeDtypeStruct((ROWS...  61.7 us
    pallas_call x1, Pallas kernels, front(): pl.pallas_call(body, name='front', out_shape=[jax.ShapeDtypeStruct((EXP,...  55.3 us
    pallas_call x2, Pallas kernels, compute_call(): pl.pallas_call(body, name=name, out_shape=outs, compiler_params=pltpu.Com...  35.7 us

profile of v7, /device:TPU:1, one launch (start us, length us, event | category | flops | bytes accessed | tf_op | source)
XLA Modules:
  0.0 301.5 jit_solution(7077774639045048967)
XLA Ops:
  0.6 55.3 %front.1 = (bf16[8,128,1024]{2,1,0:T(8,128)(2,1)}, f32[8,8,128]{2,1,0:T(8,128)}, bf16[8,192,1024]{2,1,0:T(8,128)(2,1)}, f32[8,192,128]{2,1,0:T(8,128)}, f32[8,19...) custom-call(bf16[192,1024]{1,0:T(8,128)(2,1)} %bitcast.25, ...), custom_call_target="tpu_custom_call" | custom-call | tf_op jit(solution)/shard_map/front/pallas_call | solution.py:1120
  55.9 61.7 %attend.1 = (bf16[192,1024]{1,0:T(8,128)(2,1)}, f32[8,64,384]{2,1,0:T(8,128)}, f32[8,1,384]{2,1,0:T(1,128)}, f32[192,1024]{1,0:T(8,128)}, bf16[8,192,1024]{2,1,0...) custom-call(bf16[8,192,128]{2,1,0:T(8,128)(2,1)} %get-tuple-element.70.q_ref, ...), custom_call_target="tpu_custom_call" | custom-call | tf_op jit(solution)/shard_map/attend/pallas_call | solution.py:327
  117.6 30.8 %experts.1 = (bf16[4,576,1024]{2,1,0:T(8,128)(2,1)}, bf16[4,576,1024]{2,1,0:T(8,128)(2,1)}, bf16[4,576,512]{2,1,0:T(8,128)(2,1)}, bf16[4,576,512]{2,1,0:T(8,128)...) custom-call(bf16[8,192,1024]{2,1,0:T(8,128)(2,1)} %get-tuple-element.77.x_ref, ...), custom_call_target="tpu_custom_call" | custom-call | tf_op jit(solution)/shard_map/experts/pallas_call | solution.py:643
  148.4 65.0 %settle_experts.1 = (bf16[4,4,64,512]{3,2,1,0:T(8,128)(2,1)}, bf16[2,4,64,512]{3,2,1,0:T(8,128)(2,1)}, bf16[4,1,32,1024]{3,2,1,0:T(8,128)(2,1)}, bf16[2,3,32,102...) custom-call(bf16[4,576,1024]{2,1,0:T(8,128)(2,1)} %get-tuple-element, ...), custom_call_target="tpu_custom_call" | custom-call | tf_op jit(solution)/shard_map/settle_experts/pallas_call | solution.py:584
  213.5 83.0 %tail.1 = (f32[4,64,512]{2,1,0:T(8,128)}, f32[4,64,512]{2,1,0:T(8,128)}, f32[4,32,1024]{2,1,0:T(8,128)}, f32[192,1024]{1,0:T(8,128)}, bf16[2,128,1024]{2,1,0:T(8...) custom-call(bf16[8,192,128]{2,1,0:T(8,128)(2,1)} %get-tuple-element.70.q_ref, ...), custom_call_target="tpu_custom_call" | custom-call | tf_op jit(solution)/shard_map/tail/pallas_call | solution.py:1509
  296.4 4.9 %deliver.1 = (bf16[192,1024]{1,0:T(8,128)(2,1)}, f32[128,1024]{1,0:T(8,128)}, f32[128,512]{1,0:T(8,128)}, f32[128,512]{1,0:T(8,128)}, f32[128,1024]{1,0:T(8,128)...) custom-call(f32[192,1024]{1,0:T(8,128)} %get-tuple-element.76.res_re, ...), custom_call_target="tpu_custom_call" | custom-call | tf_op jit(solution)/shard_map/deliver/pallas_call | solution.py:643
